TPU v7x, 32 devices: a whole 2x2x4 slice. The times are simulated.
32 devices in a mesh: ctx: 8 (over y, x, core), head: 4 (over z).
Axes of the slice: x: 2, y: 2, z: 4, core: 2. Of those that a mesh axis runs over, the one named last changes fastest.
Arguments:
- queries: bfloat16 [8192, 2048], P(('ctx', 'head')), may hold values from -6 to 6
- keys: bfloat16 [8192, 2048], P(('ctx', 'head')), may hold values from -6 to 6
- values: bfloat16 [8192, 2048], P(('ctx', 'head')), may hold values from -6 to 6
- grad_out: bfloat16 [8192, 2048], P(('ctx', 'head')), may hold values from -6 to 6
- gain: float32 [2048], replicated, may hold values from 0.1 to 1.9
- lengths: int32 [4], replicated, may hold values from 1 to 4096, 8192 in all
- block_mask: int32 [16, 6], P('ctx'), may hold values 0 or 1
Outputs:
- output: bfloat16 [8192, 2048], P(('ctx', 'head'))
- grad_queries: bfloat16 [8192, 2048], P(('ctx', 'head'))
- grad_keys: bfloat16 [8192, 2048], P(('ctx', 'head'))
- grad_values: bfloat16 [8192, 2048], P(('ctx', 'head'))
Inputs may be any that keep to these rules, and one draw needn't show every extreme that they name: The lengths of the 4 packed repertoires in order; they sum to 8192.
All inputs are finite; a program needn't handle non-finite values. No bound on the sum of `block_mask` on one device may be relied on, other than what follows from the above.
Results may differ from a plain program's by a relative error of at most 0.0051.
Values may be sent and summed in bfloat16 or wider, within the bound.
No kernel may reach another device: no remote copies, remote signals or barrier semaphores. Data moves between devices by JAX's collectives and lax.ppermute only.
A program may use at most 64 MiB of HBM per device.

v0:
```python
import jax
import jax.numpy as jnp
from jax import lax
from jax.sharding import PartitionSpec as P

HEADS = 16
DH = 128
GROUP = 512


eps_norm = 1e-06
pair_slots = [-1, -1, -1, -1, 0, -1, -1, -1, 1, 2, -1, -1, 3, 4, 5, -1]


def carried_in(part, axis, combine, identity):
    count = lax.axis_size(axis)
    place = lax.axis_index(axis)
    ahead = count - 1 - place
    gathered = jax.tree.map(lambda a: lax.all_gather(a, axis), part)
    state = jax.tree.map(lambda a, e: jnp.zeros_like(a) + jnp.asarray(e, a.dtype), part, identity)

    def one(turn, state):
        source = count - 1 - turn
        return combine(
            state, jax.tree.map(lambda a: lax.dynamic_index_in_dim(a, source, 0, False), gathered)
        )

    return lax.fori_loop(0, ahead, one, state)


def segment_of(position, bounds):
    return jnp.sum((position[..., None] >= bounds).astype(jnp.int32), axis=-1)


def group_weights(mask_row, seg_group):
    full_side = seg_group.shape[0]
    quarter = full_side // 4
    select = (
        lax.broadcasted_iota(jnp.int32, (6, 16), 0)
        == jnp.array(pair_slots, dtype=jnp.int32)[None, :]
    ).astype(jnp.float32)
    blocks = jnp.dot(mask_row.astype(jnp.float32), select).reshape(4, 4) + jnp.eye(
        4, dtype=jnp.float32
    )
    spread = jnp.broadcast_to(blocks[:, None, :, None], (4, quarter, 4, quarter)).reshape(
        full_side, full_side
    )
    row_ids = lax.broadcasted_iota(jnp.int32, (full_side, full_side), 0)
    col_ids = lax.broadcasted_iota(jnp.int32, (full_side, full_side), 1)
    causal = (col_ids <= row_ids).astype(jnp.float32)
    shared = (seg_group[:, None] == seg_group[None, :]).astype(jnp.float32)
    return spread * causal * shared


def link_pair(first_part, second_part):
    return (first_part[0] * second_part[0], second_part[0] * first_part[1] + second_part[1])


def state_before(carry_prod, kv_local):
    keep_flags, kv_all = (
        lax.all_gather(carry_prod[None], "ctx", axis=0, tiled=True),
        lax.all_gather(kv_local[None], "ctx", axis=0, tiled=True),
    )
    rank_ids = lax.iota(jnp.int32, keep_flags.shape[0])
    index_now = lax.axis_index("ctx")
    breaks = 1.0 - keep_flags
    running = jnp.cumsum(breaks)
    below_count = jnp.sum(jnp.where(rank_ids < index_now, breaks, 0.0))
    chosen = jnp.where((rank_ids < index_now) & (below_count - running == 0.0), 1.0, 0.0).astype(
        jnp.float32
    )
    result_state = jnp.tensordot(chosen, kv_all, axes=1, precision=lax.Precision.HIGHEST)
    return result_state


def state_after(carry_prod, grad_local):
    identity = (jnp.ones((), jnp.float32), jnp.zeros_like(grad_local))
    suffix = carried_in((carry_prod, grad_local), "ctx", link_pair, identity)
    return suffix[1]


def local_link(carried, inputs):
    flag_now, update_now = inputs
    return ((carried[0] * flag_now, flag_now * carried[1] + update_now), carried)


def local(queries, keys, values, grad_out, gain, lengths, block_mask):
    q_head, k_head, v_head, d_head = (
        lax.all_to_all(queries, "head", split_axis=1, concat_axis=0, tiled=True),
        lax.all_to_all(keys, "head", split_axis=1, concat_axis=0, tiled=True),
        lax.all_to_all(values, "head", split_axis=1, concat_axis=0, tiled=True),
        lax.all_to_all(grad_out, "head", split_axis=1, concat_axis=0, tiled=True),
    )
    tok_rows = q_head.shape[0]
    local_cols = q_head.shape[1]
    local_heads = local_cols // DH
    group_count = tok_rows // GROUP
    full_width = HEADS * DH
    highest = lax.Precision.HIGHEST

    def blocked(source):
        return source.reshape(group_count, GROUP, local_heads, DH)

    bounds = jnp.cumsum(lengths)[:3]
    positions = lax.axis_index("ctx") * tok_rows + lax.iota(jnp.int32, tok_rows).reshape(
        group_count, GROUP
    )
    seg_ids = segment_of(positions, bounds)
    seg_before = segment_of(positions[:, 0] - 1, bounds)
    seg_after = segment_of(positions[:, -1] + 1, bounds)
    seg_start = seg_ids[:, 0]
    seg_end = seg_ids[:, -1]
    q_blocks = blocked(q_head)
    k_blocks = blocked(k_head)
    v_blocks = blocked(v_head)
    end_mask = (seg_ids == seg_end[:, None]).astype(jnp.bfloat16)
    updates = jnp.einsum(
        "cthi,cthj->chij",
        k_blocks * end_mask[:, :, None, None],
        v_blocks,
        preferred_element_type=jnp.float32,
    )
    carry_flags = (seg_end == seg_before).astype(jnp.float32)
    zero_state = jnp.zeros((local_heads, DH, DH), jnp.float32)
    device_sum, (flags_before, local_before) = lax.scan(
        local_link, (jnp.ones((), jnp.float32), zero_state), (carry_flags, updates)
    )
    kv_device = state_before(device_sum[0], device_sum[1])
    kv_states = flags_before[:, None, None, None] * kv_device[None] + local_before

    def forward_block(inputs):
        q_part, k_part, v_part, mask_row, seg_group, before_seg, kv_state = inputs
        weights = group_weights(mask_row, seg_group)
        before_mask = (seg_group == before_seg).astype(jnp.float32)
        scores = (
            jnp.einsum("thd,shd->hts", q_part, k_part, preferred_element_type=jnp.float32)
            * weights[None]
        )
        prob_bf = scores.astype(jnp.bfloat16)
        intra_term = jnp.einsum("hts,shd->thd", prob_bf, v_part, preferred_element_type=jnp.float32)
        inter_term = jnp.einsum(
            "thi,hij->thj", q_part.astype(jnp.float32), kv_state, precision=highest
        )
        return (intra_term + inter_term * before_mask[:, None, None]).astype(jnp.bfloat16)

    raw_head = lax.map(
        forward_block, (q_blocks, k_blocks, v_blocks, block_mask, seg_ids, seg_before, kv_states)
    ).reshape(tok_rows, local_cols)
    gain_local = lax.dynamic_slice_in_dim(gain, lax.axis_index("head") * local_cols, local_cols)
    raw_float = raw_head.astype(jnp.float32)
    square_total = lax.psum(jnp.sum(raw_float * raw_float, axis=1), "head")
    scale_rms = jnp.sqrt(square_total / full_width + eps_norm)
    normed = raw_float / scale_rms[:, None]
    out_head = (normed * gain_local[None, :]).astype(jnp.bfloat16)
    grad_norm = d_head.astype(jnp.float32) * gain_local[None, :]
    cross_mean = lax.psum(jnp.sum(grad_norm * normed, axis=1), "head") / full_width
    d_flat = ((grad_norm - normed * cross_mean[:, None]) / scale_rms[:, None]).astype(jnp.bfloat16)
    d_blocks = blocked(d_flat)
    start_mask = (seg_ids == seg_start[:, None]).astype(jnp.bfloat16)
    grad_updates = jnp.einsum(
        "cthi,cthj->chij",
        q_blocks * start_mask[:, :, None, None],
        d_blocks,
        preferred_element_type=jnp.float32,
    )
    back_flags = (seg_start == seg_after).astype(jnp.float32)
    device_back, (flags_after, local_after) = lax.scan(
        local_link,
        (jnp.ones((), jnp.float32), zero_state),
        (back_flags, grad_updates),
        reverse=True,
    )
    grad_device = state_after(device_back[0], device_back[1])
    grad_states = flags_after[:, None, None, None] * grad_device[None] + local_after

    def backward_block(inputs):
        (
            q_part,
            k_part,
            v_part,
            d_part,
            mask_row,
            seg_group,
            before_seg,
            after_seg,
            kv_state,
            grad_state,
        ) = inputs
        weights = group_weights(mask_row, seg_group)
        before_mask = (seg_group == before_seg).astype(jnp.float32)
        after_mask = (seg_group == after_seg).astype(jnp.float32)
        prob_bf = (
            jnp.einsum("thd,shd->hts", q_part, k_part, preferred_element_type=jnp.float32)
            * weights[None]
        ).astype(jnp.bfloat16)
        grad_probs = (
            jnp.einsum("thd,shd->hts", d_part, v_part, preferred_element_type=jnp.float32)
            * weights[None]
        ).astype(jnp.bfloat16)
        grad_q = (
            jnp.einsum("hts,shd->thd", grad_probs, k_part, preferred_element_type=jnp.float32)
            + jnp.einsum("thj,hij->thi", d_part.astype(jnp.float32), kv_state, precision=highest)
            * before_mask[:, None, None]
        )
        grad_k = (
            jnp.einsum("hts,thd->shd", grad_probs, q_part, preferred_element_type=jnp.float32)
            + jnp.einsum("shj,hij->shi", v_part.astype(jnp.float32), grad_state, precision=highest)
            * after_mask[:, None, None]
        )
        grad_v = (
            jnp.einsum("hts,thd->shd", prob_bf, d_part, preferred_element_type=jnp.float32)
            + jnp.einsum("shi,hij->shj", k_part.astype(jnp.float32), grad_state, precision=highest)
            * after_mask[:, None, None]
        )
        return (
            grad_q.astype(jnp.bfloat16),
            grad_k.astype(jnp.bfloat16),
            grad_v.astype(jnp.bfloat16),
        )

    grad_blocks = lax.map(
        backward_block,
        (
            q_blocks,
            k_blocks,
            v_blocks,
            d_blocks,
            block_mask,
            seg_ids,
            seg_before,
            seg_after,
            kv_states,
            grad_states,
        ),
    )
    grad_q_head = grad_blocks[0].reshape(tok_rows, local_cols)
    grad_k_head = grad_blocks[1].reshape(tok_rows, local_cols)
    grad_v_head = grad_blocks[2].reshape(tok_rows, local_cols)
    output, back_q, back_k, back_v = (
        lax.all_to_all(out_head, "head", split_axis=0, concat_axis=1, tiled=True),
        lax.all_to_all(grad_q_head, "head", split_axis=0, concat_axis=1, tiled=True),
        lax.all_to_all(grad_k_head, "head", split_axis=0, concat_axis=1, tiled=True),
        lax.all_to_all(grad_v_head, "head", split_axis=0, concat_axis=1, tiled=True),
    )
    return (output, back_q, back_k, back_v)


def solution(mesh):
    placed = (
        P(("ctx", "head"), None),
        P(("ctx", "head"), None),
        P(("ctx", "head"), None),
        P(("ctx", "head"), None),
        P(),
        P(),
        P("ctx", None),
    )
    return jax.shard_map(
        local,
        mesh=mesh,
        in_specs=placed,
        out_specs=(
            P(("ctx", "head"), None),
            P(("ctx", "head"), None),
            P(("ctx", "head"), None),
            P(("ctx", "head"), None),
        ),
        check_vma=False,
    )
```

profile of v0, /device:TPU:1, one launch (start us, length us, event | category | flops | bytes accessed | tf_op | source)
XLA Modules:
  0.0 414.1 jit_solution(11334521217345969317)
XLA Ops:
  7.2 2.4 copy.204
  9.6 5.4 %all-to-all-start = ((bf16[256,4,512]{2,0,1:T(8,128)(2,1)}), bf16[256,4,512]{2,0,1:T(8,128)(2,1)S(1)}, u32[]{:S(2)}, u32[]{:S(2)}) async-start(bf16[256,4,512]{2,0,1:T(8,128)(2,1)} %bitcast.183), calls=%async_computation | async-start | bytes 2097152 | tf_op jit(solution)/shard_map/all_to_all | solution.py:91
  16.0 24.2 %all-to-all-done = bf16[256,4,512]{2,0,1:T(8,128)(2,1)S(1)} async-done(((bf16[256,4,512]{2,0,1:T(8,128)(2,1)}), bf16[256,4,512]{2,0,1:T(8,128)(2,1)S(1)}, u32[]{:S(2)}, u32[]{:S(2)}) %all-to-all-start) | async-done | bytes 1048608 | tf_op jit(solution)/shard_map/all_to_all | solution.py:91
  40.2 3.6 all-to-all-start.2
  43.9 2.3 copy.203
  48.2 20.9 %all-to-all-done.2 = bf16[256,4,512]{2,0,1:T(8,128)(2,1)S(1)} async-done(((bf16[256,4,512]{2,0,1:T(8,128)(2,1)}), bf16[256,4,512]{2,0,1:T(8,128)(2,1)S(1)}, u32[]{:S(2)}, u32[]{:S(2)}) %all-to-all-start.2) | async-done | bytes 1048608 | tf_op jit(solution)/shard_map/all_to_all | solution.py:90
  69.1 3.5 all-to-all-start.1
  77.8 4.3 %while.81 = (s32[]{:T(128)}, f32[]{:T(128)}, f32[4,128,128]{2,1,0:T(8,128)S(1)}, f32[2]{0:T(128)S(1)}, f32[2,4,128,128]{3,2,1,0:T(8,128)S(1)}, /*index=5*/f32[2]...) while((s32[]{:T(128)}, f32[]{:T(128)}, f32[4,128,128]{2,1,0:T(8,128)S(1)}, ...), condition=%wide.region_4.5_spmd.clone, body=%wide.region_3.4_spmd.clone.sunk | while | flops 262148 | bytes 1310888 | solution.py:125
  82.8 2.3 copy.131
  85.1 2.3 copy.132
  87.4 10.3 %all-to-all-done.1 = bf16[256,4,512]{2,0,1:T(8,128)(2,1)S(1)} async-done(((bf16[256,4,512]{2,0,1:T(8,128)(2,1)}), bf16[256,4,512]{2,0,1:T(8,128)(2,1)S(1)}, u32[]{:S(2)}, u32[]{:S(2)}) %all-to-all-start.1) | async-done | bytes 1048608 | tf_op jit(solution)/shard_map/all_to_all | solution.py:89
  98.7 3.5 all-to-all-start.4
  103.9 13.2 %all-reduce = f32[8]{0:T(128)S(1)} all-reduce(f32[8]{0:T(128)S(1)} %dynamic-update-slice), channel_id=1, replica_groups=mesh['ctx'=8,'head'=4] {'ctx'}, use_global_device_ids=true, to_apply=%add | all-reduce | flops 8 | bytes 64
  119.2 8.2 %all-to-all-done.4 = bf16[256,4,512]{2,0,1:T(8,128)(2,1)S(1)} async-done(((bf16[256,4,512]{2,0,1:T(8,128)(2,1)}), bf16[256,4,512]{2,0,1:T(8,128)(2,1)S(1)}, u32[]{:S(2)}, u32[]{:S(2)}) %all-to-all-start.4) | async-done | bytes 1048608 | tf_op jit(solution)/shard_map/all_to_all | solution.py:92
  129.1 2.9 reshape.379
  132.8 3.2 broadcast_multiply_fusion
  136.0 5.1 %fusion.61 = f32[1,4,128,128]{3,0,2,1:T(1,128)S(1)} fusion(f32[8,4,128,128]{3,2,1,0:T(8,128)} %bitcast.299, f32[8,1]{0,1:T(1,128)S(1)} %reduce-window.15, f32[]{:T(128)} %get-tuple-element.752, s32[]{:T(128)S(6)} %axis_index.15), kind=kOutput, calls=%fused_computation.99 | convolution fusion | flops 6291496 | bytes 2359336 | tf_op jit(solution)/shard_map/dot_general | solution.py:72
  143.3 21.9 %while.79 = (s32[]{:T(128)}, bf16[2,512,4,128]{3,2,1,0:T(4,128)(2,1)}, bf16[2,512,4,128]{3,2,1,0:T(4,128)(2,1)}, bf16[2,512,4,128]{3,2,1,0:T(4,128)(2,1)}, bf16[...) while((s32[]{:T(128)}, ...), condition=%wide.region_8.9_spmd.clone, body=%wide.region_7.8_spmd.sunk.clone.sunk | while | flops 943457600 | bytes 23870580 | solution.py:146
  147.7 2.4 fusion.130
  158.7 2.4 fusion.130
  165.2 2.6 reshape.378
  169.8 6.9 %psum.14 = f32[1024]{0:T(1024)S(1)} all-reduce(f32[1024]{0:T(1024)S(1)} %bitcast.315), channel_id=1, replica_groups=mesh['ctx'=8,'head'=4] {'head'}, use_global_device_ids=true, to_apply=%region_10.11 | all-reduce | flops 1024 | bytes 8192 | tf_op jit(solution)/shard_map/psum | solution.py:151
  176.8 3.4 fusion.60
  180.2 8.1 %psum.15 = f32[1024]{0:T(1024)S(1)} all-reduce(f32[1024]{0:T(1024)S(1)} %bitcast.316), channel_id=1, replica_groups=mesh['ctx'=8,'head'=4] {'head'}, use_global_device_ids=true, to_apply=%region_12.13 | all-reduce | flops 1024 | bytes 8192 | tf_op jit(solution)/shard_map/psum | solution.py:156
  188.3 5.6 %fusion.63 = bf16[2,512,4,128]{3,2,1,0:T(4,128)(2,1)S(1)} fusion(f32[2,512,4,128]{3,2,1,0:T(4,128)} %reshape.379, bf16[2,512,4,128]{3,2,1,0:T(4,128)(2,1)S(1)} %copy-done.13, f32[2,512]{1,0:T(2,128)S(1)} %mul.231, f32[2,512]{1,0:T(2,128)S(1)} %div.36, f32[4,128]{1,0:T(4,128)S(1)} %dynamic-slice_bitcast_fusion), kind=kLoop, calls=%fused_computation.104 | loop fusion | flops 3670016 | bytes 4204544 | tf_op jit(solution)/shard_map/convert_element_type | solution.py:157
  195.5 4.2 %while.82 = (s32[]{:T(128)}, f32[]{:T(128)}, f32[4,128,128]{2,1,0:T(8,128)S(1)}, f32[2]{0:T(128)S(1)}, f32[2,4,128,128]{3,2,1,0:T(8,128)S(1)}, /*index=5*/f32[2]...) while((s32[]{:T(128)}, f32[]{:T(128)}, f32[4,128,128]{2,1,0:T(8,128)S(1)}, ...), condition=%wide.region_15.16_spmd.clone, body=%wide.region_14.15_spmd.clone.sunk | while | flops 262149 | bytes 1310900 | solution.py:167
  200.4 2.4 copy.124
  204.7 4.2 %all-to-all-start.3 = ((bf16[4,256,512]{2,1,0:T(8,128)(2,1)}), bf16[4,256,512]{2,1,0:T(8,128)(2,1)}, u32[]{:S(2)}, u32[]{:S(2)}) async-start(bf16[4,256,512]{2,1,0:T(8,128)(2,1)} %get-tuple-element.747), calls=%async_computation.3 | async-start | bytes 2097152 | tf_op jit(solution)/shard_map/all_to_all | solution.py:240
  209.0 16.8 %all-reduce.1 = f32[8]{0:T(128)S(1)} all-reduce(f32[8]{0:T(128)S(1)} %dynamic-update-slice.1), channel_id=1, replica_groups=mesh['ctx'=8,'head'=4] {'ctx'}, use_global_device_ids=true, to_apply=%add.1 | all-reduce | flops 8 | bytes 64
  225.7 6.9 %all-gather.7.cloned.1.call-done = f32[32,128,128]{2,1,0:T(8,128)} async-done(((f32[4,128,128]{2,1,0:T(8,128)}), f32[32,128,128]{2,1,0:T(8,128)}) %all-gather.7.cloned.1.call-update) | async-done | bytes 2097168 | tf_op jit(solution)/shard_map/all_gather | solution.py:19
  232.6 13.8 %while.78 = (s32[]{:T(128)}, f32[4,128,128]{2,1,0:T(8,128)S(1)}, s32[]{:T(128)}, f32[8]{0:T(128)S(1)}, f32[8,4,128,128]{3,2,1,0:T(8,128)}, /*index=5*/s32[]{:T(128)}, s32[]{:T(128)}, s32[]{:T(128)}, s32[]{:T(128)}) while((s32[]{:T(128)}, f32[4,128,128]{2,1,0:T(8,128)S(1)}, s32[]{:T(128)}, f32[8]{0:T(128)S(1)}, ...), condition=%wide.region_17.18_spmd, body=%wide.region_16.17_spmd.sunk | while | flops 131078 | bytes 786599 | solution.py:28
  251.1 64.9 %while.80 = (s32[]{:T(128)}, bf16[2,512,4,128]{3,2,1,0:T(4,128)(2,1)}, bf16[2,512,4,128]{3,2,1,0:T(4,128)(2,1)}, bf16[2,512,4,128]{3,2,1,0:T(4,128)(2,1)}, bf16[...) while((s32[]{:T(128)}, ...), condition=%wide.region_19.20_spmd.clone, body=%wide.region_18.19_spmd.sunk.clone.sunk | while | flops 2557741568 | bytes 67395960 | solution.py:221
  270.0 2.2 copy.226
  272.1 3.4 fusion.153
  275.5 3.0 fusion.154
  302.4 2.2 copy.226
  304.6 3.4 fusion.153
  308.0 3.0 fusion.154
  316.0 2.3 all_to_all.114
  318.3 4.3 %all-to-all-start.5 = ((bf16[4,256,512]{2,1,0:T(8,128)(2,1)}), bf16[4,256,512]{2,1,0:T(8,128)(2,1)S(1)}, u32[]{:S(2)}, u32[]{:S(2)}) async-start(bf16[4,256,512]{2,1,0:T(8,128)(2,1)} %all_to_all.114), calls=%async_computation.5 | async-start | bytes 2097152 | tf_op jit(solution)/shard_map/all_to_all | solution.py:241
  323.9 24.0 %all-to-all-done.5 = bf16[4,256,512]{2,1,0:T(8,128)(2,1)S(1)} async-done(((bf16[4,256,512]{2,1,0:T(8,128)(2,1)}), bf16[4,256,512]{2,1,0:T(8,128)(2,1)S(1)}, u32[]{:S(2)}, u32[]{:S(2)}) %all-to-all-start.5) | async-done | bytes 1048608 | tf_op jit(solution)/shard_map/all_to_all | solution.py:241
  347.9 3.5 all-to-all-start.6
  352.6 23.9 %all-to-all-done.6 = bf16[4,256,512]{2,1,0:T(8,128)(2,1)S(1)} async-done(((bf16[4,256,512]{2,1,0:T(8,128)(2,1)}), bf16[4,256,512]{2,1,0:T(8,128)(2,1)S(1)}, u32[]{:S(2)}, u32[]{:S(2)}) %all-to-all-start.6) | async-done | bytes 1048608 | tf_op jit(solution)/shard_map/all_to_all | solution.py:242
  376.6 3.5 all-to-all-start.7
  380.1 2.3 copy.130
  382.4 2.3 copy.145
  385.9 2.3 copy.146
  390.1 15.1 %all-to-all-done.7 = bf16[4,256,512]{2,1,0:T(8,128)(2,1)S(1)} async-done(((bf16[4,256,512]{2,1,0:T(8,128)(2,1)}), bf16[4,256,512]{2,1,0:T(8,128)(2,1)S(1)}, u32[]{:S(2)}, u32[]{:S(2)}) %all-to-all-start.7) | async-done | bytes 1048608 | tf_op jit(solution)/shard_map/all_to_all | solution.py:243
  (244 shorter events, 120.8 us)
Async XLA Ops:
  7.2 7.8 %copy-start.24 = (bf16[256,2048]{1,0:T(8,128)(2,1)S(1)}, bf16[256,2048]{1,0:T(8,128)(2,1)}, u32[]{:S(2)}) copy-start(bf16[256,2048]{1,0:T(8,128)(2,1)} %param.20) | copy-start | bytes 3145732
  9.6 30.7 %all-to-all-start = ((bf16[256,4,512]{2,0,1:T(8,128)(2,1)}), bf16[256,4,512]{2,0,1:T(8,128)(2,1)S(1)}, u32[]{:S(2)}, u32[]{:S(2)}) async-start(bf16[256,4,512]{2,0,1:T(8,128)(2,1)} %bitcast.183), calls=%async_computation | async-start | bytes 2097152 | tf_op jit(solution)/shard_map/all_to_all | solution.py:91
  40.2 6.1 %copy-start.28 = (s32[4]{0:T(128)S(1)}, s32[4]{0:T(128)}, u32[]{:S(2)}) copy-start(s32[4]{0:T(128)} %param.24) | copy-start | bytes 52
  40.2 28.8 %all-to-all-start.2 = ((bf16[256,4,512]{2,0,1:T(8,128)(2,1)}), bf16[256,4,512]{2,0,1:T(8,128)(2,1)S(1)}, u32[]{:S(2)}, u32[]{:S(2)}) async-start(bf16[256,4,512]{2,0,1:T(8,128)(2,1)} %bitcast.181), calls=%async_computation.2 | async-start | bytes 2097152 | tf_op jit(solution)/shard_map/all_to_all | solution.py:90
  69.0 3.6 copy-start.16
  69.1 28.7 %all-to-all-start.1 = ((bf16[256,4,512]{2,0,1:T(8,128)(2,1)}), bf16[256,4,512]{2,0,1:T(8,128)(2,1)S(1)}, u32[]{:S(2)}, u32[]{:S(2)}) async-start(bf16[256,4,512]{2,0,1:T(8,128)(2,1)} %bitcast.182), calls=%async_computation.1 | async-start | bytes 2097152 | tf_op jit(solution)/shard_map/all_to_all | solution.py:89
  72.6 63.4 %all-gather.5.cloned.1.call-start = ((), (), s32[]{:S(2)}) async-start(), calls=%async_computation.8 | async-start | bytes 2359296 | tf_op jit(solution)/shard_map/all_gather | solution.py:62
  82.1 5.3 %copy-start.21 = (f32[2,4,128,128]{3,2,1,0:T(8,128)}, f32[2,4,128,128]{3,2,1,0:T(8,128)S(1)}, u32[]{:S(2)}) copy-start(f32[2,4,128,128]{3,2,1,0:T(8,128)S(1)} %get-tuple-element.406) | copy-start | bytes 1572868
  85.1 17.2 %copy-start.26 = (f32[2048]{0:T(1024)S(1)}, f32[2048]{0:T(1024)}, u32[]{:S(2)}) copy-start(f32[2048]{0:T(1024)} %param.23) | copy-start | bytes 24580
  85.1 17.3 %copy-start.29 = (u32[32]{0:T(128)S(1)}, u32[32]{0:T(128)}, u32[]{:S(2)}) copy-start(u32[32]{0:T(128)} %constant.166) | copy-start | bytes 388
  98.7 28.7 %all-to-all-start.4 = ((bf16[256,4,512]{2,0,1:T(8,128)(2,1)}), bf16[256,4,512]{2,0,1:T(8,128)(2,1)S(1)}, u32[]{:S(2)}, u32[]{:S(2)}) async-start(bf16[256,4,512]{2,0,1:T(8,128)(2,1)} %copy.132), calls=%async_computation.4 | async-start | bytes 2097152 | tf_op jit(solution)/shard_map/all_to_all | solution.py:92
  102.3 130.4 %all-gather.7.cloned.1.call-start = ((), (), s32[]{:S(2)}) async-start(), calls=%async_computation.9 | async-start | bytes 2359296 | tf_op jit(solution)/shard_map/all_gather | solution.py:19
  127.4 4.6 %copy-start.14 = (bf16[256,4,512]{2,0,1:T(8,128)(2,1)}, bf16[256,4,512]{2,0,1:T(8,128)(2,1)S(1)}, u32[]{:S(2)}) copy-start(bf16[256,4,512]{2,0,1:T(8,128)(2,1)S(1)} %all-to-all-done.4) | copy-start | bytes 3145732
  132.8 8.3 %copy-start.22 = (f32[2,4,128,128]{3,2,1,0:T(8,128)S(1)}, f32[2,4,128,128]{3,2,1,0:T(8,128)}, u32[]{:S(2)}) copy-start(f32[2,4,128,128]{3,2,1,0:T(8,128)} %copy-done.21) | copy-start | bytes 1572868
  136.0 7.3 %copy-start.25 = (s32[16]{0:T(128)S(1)}, s32[16]{0:T(128)}, u32[]{:S(2)}) copy-start(s32[16]{0:T(128)} %constant.162.clone..sunk.4) | copy-start | bytes 196
  136.0 7.3 %copy-start.27 = (s32[2,6]{1,0:T(2,128)S(1)}, s32[2,6]{1,0:T(2,128)}, u32[]{:S(2)}) copy-start(s32[2,6]{1,0:T(2,128)} %param.25) | copy-start | bytes 148
  143.3 2.1 copy-start.3
  152.9 1.3 copy-start.4
  154.2 2.1 copy-start.3
  163.9 1.3 copy-start.4
  165.2 2.6 copy-start.13
  188.3 6.6 %copy-start.23 = (bf16[2,512,4,128]{3,2,1,0:T(4,128)(2,1)S(1)}, bf16[2,512,4,128]{3,2,1,0:T(4,128)(2,1)}, u32[]{:S(2)}) copy-start(bf16[2,512,4,128]{3,2,1,0:T(4,128)(2,1)} %broadcast_multiply_fusion) | copy-start | bytes 3145732
  193.9 1.0 copy-start.19
  199.7 3.1 copy-start.20
  204.7 113.6 %all-to-all-start.3 = ((bf16[4,256,512]{2,1,0:T(8,128)(2,1)}), bf16[4,256,512]{2,1,0:T(8,128)(2,1)}, u32[]{:S(2)}, u32[]{:S(2)}) async-start(bf16[4,256,512]{2,1,0:T(8,128)(2,1)} %get-tuple-element.747), calls=%async_computation.3 | async-start | bytes 2097152 | tf_op jit(solution)/shard_map/all_to_all | solution.py:240
  251.1 1.0 copy-start.5
  251.1 1.6 copy-start.1
  251.1 1.9 copy-start.7
  257.9 4.5 %copy-start.2 = (bf16[2,512,4,128]{3,1,2,0:T(8,128)(2,1)S(1)}, bf16[2,512,4,128]{3,1,2,0:T(8,128)(2,1)}, u32[]{:S(2)}) copy-start(bf16[2,512,4,128]{3,1,2,0:T(8,128)(2,1)} %get-tuple-element.1177) | copy-start | bytes 3145732 | tf_op jit(solution)/shard_map/while
  257.9 4.5 %copy-start.11 = (f32[2,4,128,128]{3,2,1,0:T(8,128)S(1)}, f32[2,4,128,128]{3,2,1,0:T(8,128)}, u32[]{:S(2)}) copy-start(f32[2,4,128,128]{3,2,1,0:T(8,128)} %get-tuple-element.1181) | copy-start | bytes 1572868 | tf_op jit(solution)/shard_map/while
  275.5 4.4 %copy-start = (bf16[1,512,4,128]{1,3,2,0:T(8,128)(2,1)S(1)}, bf16[1,512,4,128]{1,3,2,0:T(8,128)(2,1)}, u32[]{:S(2)}) copy-start(bf16[1,512,4,128]{1,3,2,0:T(8,128)(2,1)} %copy.226) | copy-start | bytes 1572868 | tf_op jit(solution)/shard_map/while
  279.9 1.2 copy-start.8
  279.9 1.3 copy-start.12
  281.9 1.7 copy-start.6
  283.5 1.0 copy-start.5
  283.5 1.6 copy-start.1
  283.5 1.9 copy-start.7
  290.3 4.5 %copy-start.2 = (bf16[2,512,4,128]{3,1,2,0:T(8,128)(2,1)S(1)}, bf16[2,512,4,128]{3,1,2,0:T(8,128)(2,1)}, u32[]{:S(2)}) copy-start(bf16[2,512,4,128]{3,1,2,0:T(8,128)(2,1)} %get-tuple-element.1177) | copy-start | bytes 3145732 | tf_op jit(solution)/shard_map/while
  290.3 4.5 %copy-start.11 = (f32[2,4,128,128]{3,2,1,0:T(8,128)S(1)}, f32[2,4,128,128]{3,2,1,0:T(8,128)}, u32[]{:S(2)}) copy-start(f32[2,4,128,128]{3,2,1,0:T(8,128)} %get-tuple-element.1181) | copy-start | bytes 1572868 | tf_op jit(solution)/shard_map/while
  308.0 4.4 %copy-start = (bf16[1,512,4,128]{1,3,2,0:T(8,128)(2,1)S(1)}, bf16[1,512,4,128]{1,3,2,0:T(8,128)(2,1)}, u32[]{:S(2)}) copy-start(bf16[1,512,4,128]{1,3,2,0:T(8,128)(2,1)} %copy.226) | copy-start | bytes 1572868 | tf_op jit(solution)/shard_map/while
  312.4 1.2 copy-start.8
  312.4 1.3 copy-start.12
  314.3 1.7 copy-start.6
  316.0 6.7 %copy-start.17 = (bf16[2,512,4,128]{3,2,1,0:T(4,128)(2,1)S(1)}, bf16[2,512,4,128]{3,2,1,0:T(4,128)(2,1)}, u32[]{:S(2)}) copy-start(bf16[2,512,4,128]{3,2,1,0:T(4,128)(2,1)} %get-tuple-element.414) | copy-start | bytes 3145732
  318.3 29.5 %all-to-all-start.5 = ((bf16[4,256,512]{2,1,0:T(8,128)(2,1)}), bf16[4,256,512]{2,1,0:T(8,128)(2,1)S(1)}, u32[]{:S(2)}, u32[]{:S(2)}) async-start(bf16[4,256,512]{2,1,0:T(8,128)(2,1)} %all_to_all.114), calls=%async_computation.5 | async-start | bytes 2097152 | tf_op jit(solution)/shard_map/all_to_all | solution.py:241
  322.7 28.7 %copy-start.18 = (bf16[2,512,4,128]{3,2,1,0:T(4,128)(2,1)S(1)}, bf16[2,512,4,128]{3,2,1,0:T(4,128)(2,1)}, u32[]{:S(2)}) copy-start(bf16[2,512,4,128]{3,2,1,0:T(4,128)(2,1)} %get-tuple-element.415) | copy-start | bytes 3145732
  347.9 28.7 %all-to-all-start.6 = ((bf16[4,256,512]{2,1,0:T(8,128)(2,1)}), bf16[4,256,512]{2,1,0:T(8,128)(2,1)S(1)}, u32[]{:S(2)}, u32[]{:S(2)}) async-start(bf16[4,256,512]{2,1,0:T(8,128)(2,1)} %all_to_all.118), calls=%async_computation.6 | async-start | bytes 2097152 | tf_op jit(solution)/shard_map/all_to_all | solution.py:242
  376.6 28.7 %all-to-all-start.7 = ((bf16[4,256,512]{2,1,0:T(8,128)(2,1)}), bf16[4,256,512]{2,1,0:T(8,128)(2,1)S(1)}, u32[]{:S(2)}, u32[]{:S(2)}) async-start(bf16[4,256,512]{2,1,0:T(8,128)(2,1)} %all_to_all.122), calls=%async_computation.7 | async-start | bytes 2097152 | tf_op jit(solution)/shard_map/all_to_all | solution.py:243
  (3 other events, 2.4 us)
Sparse Core Ops, SparseCore 0:
  83.0 30.5 all-gather.4
  200.6 32.0 all-gather.6
where the time goes:
time: 418 us; the launch traced here: 414 us
  waiting for transfers between devices  134 us (32%)
  local copies, waits for them, and re-layouts  108 us (26%)
  blocking collectives  44.9 us (11%)
  other arithmetic  39.1 us (9%)
  matrix products  39 us (9%)
  starting transfers between devices  31.8 us (8%)
  between operations  14.3 us (3%)
    unnamed x2, blocking collectives  29.9 us
    dynamic_slice x24, local copies, waits for them, and re-layouts, local(): lax.map(forward_block, (q_blocks, k_blocks, v_blocks, block_mask, seg_ids...  27.9 us
    all_to_all x1, waiting for transfers between devices, local(): lax.all_to_all(values, 'head', split_axis=1, concat_axis=0, tiled=True)  24.2 us
    all_to_all x1, waiting for transfers between devices, local(): lax.all_to_all(grad_q_head, 'head', split_axis=0, concat_axis=1, tiled=True)  24 us
    all_to_all x1, waiting for transfers between devices, local(): lax.all_to_all(grad_k_head, 'head', split_axis=0, concat_axis=1, tiled=True)  23.9 us
    all_to_all x1, waiting for transfers between devices, local(): lax.all_to_all(keys, 'head', split_axis=1, concat_axis=0, tiled=True)  20.9 us
    dynamic_update_slice x14, local copies, waits for them, and re-layouts, local(): lax.map(forward_block, (q_blocks, k_blocks, v_blocks, block_mask, seg_ids...  16.8 us
    unnamed x51, local copies, waits for them, and re-layouts  16.4 us
  transfers between devices with their start and end apart: 10, of which 8 were waited for; matrix products, arithmetic and copies ran while one was open for 30% of the time, Pallas kernels for 0%

commit v1 on v0

v1 whole, which is shorter than its diff:
```python
import functools

import jax
import jax.numpy as jnp
from jax import lax
from jax.experimental import pallas as pl
from jax.experimental.pallas import tpu as pltpu
from jax.sharding import PartitionSpec as P

DH = 128
GROUP = 512
BLOCK = 128
UNROLL = 4

eps_norm = 1e-06
BF = jnp.bfloat16
F32 = jnp.float32
AXES = ("ctx", "head")

NN = (((1,), (0,)), ((), ()))
NT = (((1,), (1,)), ((), ()))
TN = (((0,), (0,)), ((), ()))


def dot(a, b, dims):
    return lax.dot_general(a, b, dims, preferred_element_type=F32)


def bounds_of(len_ref):
    bounds, total = [], None
    for k in range(len_ref.shape[0] - 1):
        total = len_ref[k] if total is None else total + len_ref[k]
        bounds.append(total)
    return bounds


def segment(position, bounds):
    result = (position >= bounds[0]).astype(jnp.int32)
    for bound in bounds[1:]:
        result = result + (position >= bound).astype(jnp.int32)
    return result


def same(a, b):
    return (a == b).astype(F32)


class Place:
    def __init__(self, len_ref, rows, mask_ref=None):
        self.rows = rows
        self.blocks = rows // BLOCK
        self.devices = GROUP // rows
        self.bounds = bounds_of(len_ref)
        spot = lax.axis_index("head")
        index = lax.axis_index("ctx") * lax.axis_size("head") + spot
        self.first = index * rows
        self.part = lax.rem(spot, self.devices)
        self.group = lax.div(spot, self.devices)
        self.group_first = self.first - self.part * rows
        self.mask_ref = mask_ref

    def seg(self, position):
        return segment(position, self.bounds)

    def row_segments(self, block=None):
        count, start = (self.rows, 0) if block is None else (BLOCK, block * BLOCK)
        rows = lax.broadcasted_iota(jnp.int32, (count, 1), 0)
        return self.seg(rows + (self.first + start))

    def pair(self, i, j):
        slot = jnp.clip(lax.div(i * (i - 1), 2) + j, 0, self.mask_ref.shape[1] - 1)
        return self.mask_ref[self.group, slot].astype(F32)

    def weights(self):
        rows = self.rows
        t = lax.broadcasted_iota(jnp.int32, (rows, rows), 0)
        s = lax.broadcasted_iota(jnp.int32, (rows, rows), 1)
        keep = (s <= t) & (self.seg(t + self.first) == self.seg(s + self.first))
        result = jnp.where(keep, 1.0, 0.0)
        for i in range(1, self.blocks):
            for j in range(i):
                bit = self.pair(self.part * self.blocks + i, self.part * self.blocks + j)
                inside = (
                    (t >= i * BLOCK)
                    & (t < (i + 1) * BLOCK)
                    & (s >= j * BLOCK)
                    & (s < (j + 1) * BLOCK)
                )
                result = jnp.where(inside, result * bit, result)
        return result

    def before(self, block):
        own = self.part * self.blocks + block
        edge = self.seg(self.first + block * BLOCK - 1)
        carried = same(self.seg(self.group_first - 1), edge)
        peers = []
        for away in range(1, self.devices):
            there = (self.part >= away).astype(F32)
            for j in range(self.blocks):
                other = (self.part - away) * self.blocks + j
                last = self.first - away * self.rows + (j + 1) * BLOCK - 1
                peers.append(self.pair(own, other) * same(self.seg(last), edge) * there)
        reach = self.row_segments(block) == edge
        return carried, peers, reach

    def after(self, block):
        own = self.part * self.blocks + block
        edge = self.seg(self.first + (block + 1) * BLOCK)
        carried = same(self.seg(self.group_first + GROUP), edge)
        peers = []
        for away in range(1, self.devices):
            there = (self.part + away < self.devices).astype(F32)
            for i in range(self.blocks):
                other = (self.part + away) * self.blocks + i
                start = self.first + away * self.rows + i * BLOCK
                peers.append(self.pair(other, own) * same(self.seg(start), edge) * there)
        reach = self.row_segments(block) == edge
        return carried, peers, reach


def mixed(state_ref, peer_refs, factors, blocks, head):
    carried, peers, _ = factors
    total = state_ref[head].astype(F32) * carried
    for at, factor in enumerate(peers):
        total = total + peer_refs[at // blocks][at % blocks, head].astype(F32) * factor
    return total.astype(BF)


def columns(head):
    return pl.ds(pl.multiple_of(head * DH, DH), DH)


def each_head(heads, body, carry=()):
    step = UNROLL if heads % UNROLL == 0 else 1

    def some(turn, carry):
        for k in range(step):
            carry = body(turn * step + k, carry)
        return carry

    return lax.fori_loop(0, heads // step, some, carry)


def rows_of(block):
    return pl.ds(block * BLOCK, BLOCK)


def state_kernel(len_ref, k_ref, v_ref, u_ref, t_ref):
    rows, width = k_ref.shape
    place = Place(len_ref, rows)
    last = place.seg(place.first + rows - 1)
    ends = [place.seg(place.first + (b + 1) * BLOCK - 1) for b in range(place.blocks)]
    masks = [(place.row_segments(b) == ends[b]).astype(BF) for b in range(place.blocks)]
    into = [same(e, last) for e in ends]

    def one(head, carry):
        total = jnp.zeros((DH, DH), F32)
        for b in range(place.blocks):
            k = k_ref[rows_of(b), columns(head)] * masks[b]
            update = dot(k, v_ref[rows_of(b), columns(head)], TN)
            u_ref[b, head] = update.astype(BF)
            total = total + update * into[b]
        t_ref[head] = total.astype(BF)
        return carry

    each_head(width // DH, one)


def inner_kernel(len_ref, mask_ref, q_ref, k_ref, v_ref, raw_ref, weight_ref):
    rows, width = q_ref.shape
    weight_ref[...] = Place(len_ref, rows, mask_ref).weights()

    def one(head, carry):
        at = columns(head)
        probs = (dot(q_ref[:, at], k_ref[:, at], NT) * weight_ref[...]).astype(BF)
        raw_ref[:, at] = dot(probs, v_ref[:, at], NN)
        return carry

    each_head(width // DH, one)


def scan_kernel(len_ref, t_ref, out_ref, *, rows, backward):
    count = t_ref.shape[0]
    devices = GROUP // rows
    bounds = bounds_of(len_ref)

    def one(turn, acc):
        group = count // devices - 1 - turn if backward else turn
        for k in range(devices):
            out_ref[group * devices + k] = acc.astype(BF)
        for k in range(devices):
            index = group * devices + (devices - 1 - k if backward else k)
            first = index * rows
            if backward:
                keep = same(segment(first, bounds), segment(first + rows, bounds))
            else:
                keep = same(segment(first - 1, bounds), segment(first + rows - 1, bounds))
            acc = acc * keep + t_ref[index].astype(F32)
        return acc

    lax.fori_loop(0, count // devices, one, jnp.zeros(t_ref.shape[1:], F32))


def norm_kernel(len_ref, mask_ref, gain_ref, q_ref, raw_ref, grad_ref, kv_ref, *rest, peers):
    peer_refs, (out_ref, d_ref, w_ref, t_ref, held_ref) = rest[:peers], rest[peers:]
    rows, width = q_ref.shape
    heads = width // DH
    place = Place(len_ref, rows, mask_ref)
    starts = [place.seg(place.first + b * BLOCK) for b in range(place.blocks)]
    into = [same(s, starts[0]) for s in starts]
    for b in range(place.blocks):
        factors = place.before(b)
        reach = factors[2].astype(F32)
        begin = (place.row_segments(b) == starts[b]).astype(BF)
        at_rows = rows_of(b)

        def add_up(head, carry):
            squares, cross = carry
            at = columns(head)
            state = mixed(kv_ref, peer_refs, factors, place.blocks, head)
            raw = raw_ref[at_rows, at] + dot(q_ref[at_rows, at], state, NN) * reach
            raw = raw.astype(BF)
            held_ref[at_rows, at] = raw
            raw = raw.astype(F32)
            scaled = grad_ref[at_rows, at].astype(F32) * gain_ref[:, at]
            return squares + raw * raw, cross + scaled * raw

        zero = jnp.zeros((BLOCK, DH), F32)
        squares, cross = each_head(heads, add_up, (zero, zero))
        rms = jnp.sqrt(jnp.sum(squares, axis=1, keepdims=True) / width + eps_norm)
        inverse = 1.0 / rms
        cross = jnp.sum(cross, axis=1, keepdims=True) * inverse / width

        def give(head, carry):
            at = columns(head)
            gain = gain_ref[:, at]
            normed = held_ref[at_rows, at].astype(F32) * inverse
            out_ref[at_rows, at] = (normed * gain).astype(BF)
            scaled = grad_ref[at_rows, at].astype(F32) * gain
            grad = ((scaled - normed * cross) * inverse).astype(BF)
            d_ref[at_rows, at] = grad
            update = dot(q_ref[at_rows, at] * begin, grad, TN)
            w_ref[b, head] = update.astype(BF)
            if b == 0:
                held = update
            else:
                held = t_ref[head].astype(F32) + update * into[b]
            t_ref[head] = held.astype(t_ref.dtype)
            return carry

        each_head(heads, give)


def grads_kernel(len_ref, mask_ref, q_ref, k_ref, v_ref, d_ref, kv_ref, *rest, peers):
    peer_refs, (gq_ref, gk_ref, gv_ref, weight_ref) = rest[:peers], rest[peers:]
    rows, width = q_ref.shape
    place = Place(len_ref, rows, mask_ref)
    weight_ref[...] = place.weights()
    factors = [place.before(b) for b in range(place.blocks)]

    def one(head, carry):
        at = columns(head)
        q, k, v, d = q_ref[:, at], k_ref[:, at], v_ref[:, at], d_ref[:, at]
        probs = (dot(q, k, NT) * weight_ref[...]).astype(BF)
        grad_probs = (dot(d, v, NT) * weight_ref[...]).astype(BF)
        inner = dot(grad_probs, k, NN)
        for b in range(place.blocks):
            state = mixed(kv_ref, peer_refs, factors[b], place.blocks, head)
            outer = dot(d_ref[rows_of(b), at], state, NT) * factors[b][2].astype(F32)
            part = inner[b * BLOCK : (b + 1) * BLOCK] + outer
            gq_ref[rows_of(b), at] = part.astype(BF)
        gk_ref[:, at] = dot(grad_probs, q, TN)
        gv_ref[:, at] = dot(probs, d, TN)
        return carry

    each_head(width // DH, one)


def last_kernel(len_ref, mask_ref, k_ref, v_ref, gk_in, gv_in, gs_ref, *rest, peers):
    peer_refs, (gk_ref, gv_ref) = rest[:peers], rest[peers:]
    rows, width = k_ref.shape
    place = Place(len_ref, rows, mask_ref)
    factors = [place.after(b) for b in range(place.blocks)]

    def one(head, carry):
        at = columns(head)
        for b in range(place.blocks):
            at_rows = rows_of(b)
            state = mixed(gs_ref, peer_refs, factors[b], place.blocks, head)
            reach = factors[b][2].astype(F32)
            gk = gk_in[at_rows, at] + dot(v_ref[at_rows, at], state, NT) * reach
            gv = gv_in[at_rows, at] + dot(k_ref[at_rows, at], state, NN) * reach
            gk_ref[at_rows, at] = gk.astype(BF)
            gv_ref[at_rows, at] = gv.astype(BF)
        return carry

    each_head(width // DH, one)


SMEM = pl.BlockSpec(memory_space=pltpu.SMEM)
VMEM = pl.BlockSpec(memory_space=pltpu.VMEM)


def call(kernel, name, scalars, arrays, outs, scratch=(), flops=0):
    moved = sum(a.size * a.dtype.itemsize for a in arrays)
    moved += sum(o.size * o.dtype.itemsize for o in outs)
    single = len(outs) == 1
    return pl.pallas_call(
        kernel,
        name=name,
        in_specs=[SMEM] * len(scalars) + [VMEM] * len(arrays),
        out_specs=VMEM if single else [VMEM] * len(outs),
        out_shape=outs[0] if single else outs,
        scratch_shapes=scratch,
        compiler_params=pltpu.CompilerParams(vmem_limit_bytes=32 * 1024 * 1024),
        cost_estimate=pl.CostEstimate(flops=flops, bytes_accessed=moved, transcendentals=0),
    )(*scalars, *arrays)


def local(queries, keys, values, grad_out, gain, lengths, block_mask):
    rows, width = queries.shape
    heads = width // DH
    blocks = rows // BLOCK
    devices = GROUP // rows
    head_count = lax.axis_size("head")
    total = lax.axis_size("ctx") * head_count
    shape = jax.ShapeDtypeStruct
    state = shape((heads, DH, DH), BF)
    block_states = shape((blocks, heads, DH, DH), BF)
    tokens = shape((rows, width), BF)
    partial = shape((rows, width), F32)
    square = [pltpu.VMEM((rows, rows), F32)]
    unit = 2 * rows * width * DH
    inner = 2 * rows * rows * width

    def to_peers(states, backward):
        result = []
        for away in range(1, devices):
            pairs = [
                (z, z + away) for z in range(head_count - away) if z % devices + away < devices
            ]
            if backward:
                pairs = [(b, a) for a, b in pairs]
            result.append(lax.ppermute(states, "head", pairs))
        return result

    def scanned(sums, backward):
        slices = sums.reshape(total, heads * DH // total, DH)
        slices = lax.all_to_all(slices, AXES, split_axis=0, concat_axis=0, tiled=True)
        kernel = functools.partial(scan_kernel, rows=rows, backward=backward)
        slices = call(
            kernel, "scan", [lengths], [slices], [shape(slices.shape, BF)]
        )
        slices = lax.all_to_all(slices, AXES, split_axis=0, concat_axis=0, tiled=True)
        return slices.reshape(heads, DH, DH)

    gain_row = gain.reshape(1, width)
    block_kv, sum_kv = call(
        state_kernel, "states", [lengths], [keys, values], [block_states, state], flops=unit
    )
    kv_state = scanned(sum_kv, False)
    peer_kv = to_peers(block_kv, False)
    raw_inner = call(
        inner_kernel,
        "inner",
        [lengths, block_mask],
        [queries, keys, values],
        [partial],
        square,
        flops=2 * inner,
    )
    peers = len(peer_kv)
    output, grad_raw, block_grad, sum_grad = call(
        functools.partial(norm_kernel, peers=peers),
        "norm",
        [lengths, block_mask],
        [gain_row, queries, raw_inner, grad_out, kv_state, *peer_kv],
        [tokens, tokens, block_states, state],
        [pltpu.VMEM((rows, width), BF)],
        flops=2 * unit,
    )
    grad_state = scanned(sum_grad, True)
    peer_grad = to_peers(block_grad, True)
    grad_q, part_k, part_v = call(
        functools.partial(grads_kernel, peers=peers),
        "grads",
        [lengths, block_mask],
        [queries, keys, values, grad_raw, kv_state, *peer_kv],
        [tokens, partial, partial],
        square,
        flops=5 * inner + unit,
    )
    grad_k, grad_v = call(
        functools.partial(last_kernel, peers=peers),
        "last",
        [lengths, block_mask],
        [keys, values, part_k, part_v, grad_state, *peer_grad],
        [tokens, tokens],
        flops=2 * unit,
    )
    return output, grad_q, grad_k, grad_v


def solution(mesh):
    tokens = P(AXES, None)
    return jax.shard_map(
        local,
        mesh=mesh,
        in_specs=(tokens, tokens, tokens, tokens, P(), P(), P("ctx", None)),
        out_specs=(tokens, tokens, tokens, tokens),
        check_vma=False,
    )
```

time: 418 us -> 127 us (0.30)
  local copies, waits for them, and re-layouts: 108 us -> 20.4 us
  waiting for transfers between devices: 134 us -> 50.1 us
  blocking collectives: 44.9 us -> 0 us
  other arithmetic: 39.1 us -> 0 us
  matrix products: 39 us -> 0 us
  Pallas kernels: 0 us -> 27.7 us
  between operations: 14.3 us -> 0.81 us
  starting transfers between devices: 31.8 us -> 26.4 us
    all_to_all x8 -> x4, waiting for transfers between devices: 127 us -> 41.1 us  [scanned(): lax.all_to_all(slices, AXES, split_axis=0, concat_axis=0, tiled=True)]
    dot_general x25 -> x0, matrix products: 39 us -> none  [the longest x2 6.82 us: backward_block(): jnp.einsum('hts,thd->shd', prob_bf, d_part, preferred_element_type=jnp.fl...]
    dynamic_slice x35 -> x0, local copies, waits for them, and re-layouts: 33.9 us -> none  [the longest x24 27.9 us: local(): lax.map(forward_block, (q_blocks, k_blocks, v_blocks, block_mask, seg_ids...]
    unnamed x2 -> x0, blocking collectives: 29.9 us -> none
    pallas_call x0 -> x7, Pallas kernels: none -> 27.7 us  [call(): pl.pallas_call(kernel, name=name, in_specs=[SMEM] * len(scalars) + [VMEM]...]
    all_to_all x11 -> x0, local copies, waits for them, and re-layouts: 17.4 us -> none  [the longest x2 3.63 us: local(): lax.all_to_all(grad_q_head, 'head', split_axis=0, concat_axis=1, tiled=True)]
    dynamic_update_slice x18 -> x0, local copies, waits for them, and re-layouts: 17.3 us -> none  [the longest x14 16.8 us: local(): lax.map(forward_block, (q_blocks, k_blocks, v_blocks, block_mask, seg_ids...]
    psum x2 -> x0, blocking collectives: 15 us -> none  [the longest x1 8.09 us: local(): lax.psum(jnp.sum(grad_norm * normed, axis=1), 'head') / full_width]
  transfers between devices with their start and end apart: 10 -> 6, of which waited for: 8 -> 6; matrix products, arithmetic and copies ran while one was open for 30% -> 0% of each run, Pallas kernels for 0% -> 12%
where the time goes in v1:
time: 127 us; the launch traced here: 126 us
  waiting for transfers between devices  50.1 us (39%)
  Pallas kernels  27.7 us (22%)
  starting transfers between devices  26.4 us (21%)
  local copies, waits for them, and re-layouts  20.4 us (16%)
    all_to_all x4, waiting for transfers between devices, scanned(): lax.all_to_all(slices, AXES, split_axis=0, concat_axis=0, tiled=True)  41.1 us
    pallas_call x7, Pallas kernels, call(): pl.pallas_call(kernel, name=name, in_specs=[SMEM] * len(scalars) + [VMEM]...  27.7 us
    all_to_all x4, starting transfers between devices, scanned(): lax.all_to_all(slices, AXES, split_axis=0, concat_axis=0, tiled=True)  20.9 us
    unnamed x48, local copies, waits for them, and re-layouts  20.4 us
    ppermute x2, waiting for transfers between devices, to_peers(): result.append(lax.ppermute(states, 'head', pairs))  9 us
    ppermute x2, starting transfers between devices, to_peers(): result.append(lax.ppermute(states, 'head', pairs))  5.59 us
  transfers between devices with their start and end apart: 6, of which 6 were waited for; matrix products, arithmetic and copies ran while one was open for 0% of the time, Pallas kernels for 12%

profile of v1, /device:TPU:1, one launch (start us, length us, event | category | flops | bytes accessed | tf_op | source)
XLA Modules:
  0.0 125.6 jit_solution(10566458942587459129)
XLA Ops:
  0.6 0.0 copy-start
  0.6 1.2 copy-done
  1.9 1.2 copy-done.2
  3.1 0.7 copy-done.18
  3.7 1.9 %states.1 = (bf16[2,16,128,128]{3,2,1,0:T(8,128)(2,1)S(1)}, bf16[16,128,128]{2,1,0:T(8,128)(2,1)S(1)}) custom-call(s32[4]{0:T(128)S(1)} %copy-done.18, bf16[256,2048]{1,0:T(8,128)(2,1)S(1)} %copy-done, bf16[256,2048]{1,0:T(8,128)(2,1)S(1)} %copy-done.2), custom_call_target="tpu_custom_call" | custom-call | flops 134217728 | bytes 3670016 | tf_op jit(solution)/shard_map/states/pallas_call | solution.py:308
  5.6 0.0 copy-start.17
  5.6 0.8 copy-done.17
  6.4 1.0 copy-done.23
  7.4 7.2 %all-to-all-start = ((bf16[32,64,128]{2,1,0:T(8,128)(2,1)}), bf16[32,64,128]{2,1,0:T(8,128)(2,1)}, u32[]{:S(2)}, u32[]{:S(2)}) async-start(bf16[32,64,128]{2,1,0:T(8,128)(2,1)} %bitcast.6), calls=%async_computation | async-start | bytes 1048576 | tf_op jit(solution)/shard_map/all_to_all | solution.py:349
  14.6 4.3 %collective-permute-start = (bf16[2,16,128,128]{3,2,1,0:T(8,128)(2,1)}, bf16[2,16,128,128]{3,2,1,0:T(8,128)(2,1)}, u32[]{:S(2)}, u32[]{:S(2)}) collective-permute-start(bf16[2,16,128,128]{3,2,1,0:T(8,128)(2,1)} %copy-done.23), channel_id=1, source_target_pairs={{0,1},{2,3},{4,5},{6,7},{8,9},{10,11},{12,13},{14,15},{16,17},{18,... | collective-permute-start | bytes 3145736 | tf_op jit(solution)/shard_map/ppermute | solution.py:344
  18.9 11.0 %all-to-all-done.t_ref = bf16[32,64,128]{2,1,0:T(8,128)(2,1)} async-done(((bf16[32,64,128]{2,1,0:T(8,128)(2,1)}), bf16[32,64,128]{2,1,0:T(8,128)(2,1)}, u32[]{:S(2)}, u32[]{:S(2)}) %all-to-all-start) | async-done | bytes 524320 | tf_op jit(solution)/shard_map/all_to_all | solution.py:349
  29.9 0.0 copy-done.19
  29.9 1.4 %scan.2 = bf16[32,64,128]{2,1,0:T(8,128)(2,1)S(1)} custom-call(s32[4]{0:T(128)S(1)} %copy-done.19, bf16[32,64,128]{2,1,0:T(8,128)(2,1)} %all-to-all-done.t_ref), custom_call_target="tpu_custom_call" | custom-call | bytes 1048576 | tf_op jit(solution)/shard_map/scan/pallas_call | solution.py:308
  31.3 0.0 copy-start.8
  31.3 0.8 copy-done.8
  32.1 3.2 %all-to-all-start.1 = ((bf16[32,64,128]{2,1,0:T(8,128)(2,1)}), bf16[32,64,128]{2,1,0:T(8,128)(2,1)}, u32[]{:S(2)}, u32[]{:S(2)}) async-start(bf16[32,64,128]{2,1,0:T(8,128)(2,1)} %copy-done.8), calls=%async_computation.1 | async-start | bytes 1048576 | tf_op jit(solution)/shard_map/all_to_all | solution.py:354
  35.4 0.0 copy-done.1
  35.4 0.0 copy-done.3
  35.4 0.0 copy-done.4
  35.4 0.0 copy-done.20
  35.4 0.0 copy-start.21
  35.4 3.3 %inner.1.raw_ref = f32[256,2048]{1,0:T(8,128)S(1)} custom-call(s32[4]{0:T(128)S(1)} %copy-done.19, s32[2,6]{1,0:T(2,128)S(1)} %copy-done.20, bf16[256,2048]{1,0:T(8,128)(2,1)S(1)} %copy-done.4, bf16[256,2048]{1,0:T(8,128)(2,1)S(1)} %copy-done.1, bf16[256,2048]{1,0:T(8,128)(2,1)S(1)} %copy-done.3), custom_call_target="tpu_custom_call" | custom-call | flops 536870912 | bytes 5242880 | tf_op jit(solution)/shard_map/inner/pallas_call | solution.py:308
  38.7 1.3 %copy-done.5 = f32[256,2048]{1,0:T(8,128)} copy-done((f32[256,2048]{1,0:T(8,128)}, f32[256,2048]{1,0:T(8,128)S(1)}, u32[]{:S(2)}) %copy-start.5) | copy-done | bytes 2097176
  40.1 5.8 %collective-permute-done.rest_0_ = bf16[2,16,128,128]{3,2,1,0:T(8,128)(2,1)} collective-permute-done((bf16[2,16,128,128]{3,2,1,0:T(8,128)(2,1)}, bf16[2,16,128,128]{3,2,1,0:T(8,128)(2,1)}, u32[]{:S(2)}, u32[]{:S(2)}) %collective-permute-start) | collective-permute-done | bytes 1048608 | tf_op jit(solution)/shard_map/ppermute | solution.py:344
  45.8 8.3 %all-to-all-done.1 = bf16[32,64,128]{2,1,0:T(8,128)(2,1)} async-done(((bf16[32,64,128]{2,1,0:T(8,128)(2,1)}), bf16[32,64,128]{2,1,0:T(8,128)(2,1)}, u32[]{:S(2)}, u32[]{:S(2)}) %all-to-all-start.1) | async-done | bytes 524320 | tf_op jit(solution)/shard_map/all_to_all | solution.py:354
  54.1 0.0 copy-done.21
  54.1 1.6 %copy-done.6 = f32[256,2048]{1,0:T(8,128)S(1)} copy-done((f32[256,2048]{1,0:T(8,128)S(1)}, f32[256,2048]{1,0:T(8,128)}, u32[]{:S(2)}) %copy-start.6) | copy-done | bytes 2097176
  55.7 1.2 copy-done.13
  57.0 7.0 %norm.1 = (bf16[256,2048]{1,0:T(8,128)(2,1)}, bf16[256,2048]{1,0:T(8,128)(2,1)S(1)}, bf16[2,16,128,128]{3,2,1,0:T(8,128)(2,1)S(1)}, bf16[16,128,128]{2,1,0:T(8,128)(2,1)S(1)}) custom-call(s32[4]{0:T(128)S(1)} %copy-done.19, s32[2,6]{1,0:T(2,128)S(1)} %copy-done.20, f32[1,2048]{1,0:T(1,128)S(1)} %bitcast.7, bf16[256,2048]{1,0:T(8,128)(2,1)S(1)} %copy-done.4, ...), custom_call_target="tpu_custom_call" | custom-call | flops 268435456 | bytes 9445376 | tf_op jit(solution)/shard_map/norm/pallas_call | solution.py:308
  63.9 1.0 copy-done.14
  64.9 0.8 copy-done.16
  65.7 1.0 copy-done.22
  66.7 7.3 %all-to-all-start.2 = ((bf16[32,64,128]{2,1,0:T(8,128)(2,1)}), bf16[32,64,128]{2,1,0:T(8,128)(2,1)}, u32[]{:S(2)}, u32[]{:S(2)}) async-start(bf16[32,64,128]{2,1,0:T(8,128)(2,1)} %bitcast.5), calls=%async_computation.2 | async-start | bytes 1048576 | tf_op jit(solution)/shard_map/all_to_all | solution.py:349
  74.0 1.3 %collective-permute-start.1 = (bf16[2,16,128,128]{3,2,1,0:T(8,128)(2,1)}, bf16[2,16,128,128]{3,2,1,0:T(8,128)(2,1)}, u32[]{:S(2)}, u32[]{:S(2)}) collective-permute-start(bf16[2,16,128,128]{3,2,1,0:T(8,128)(2,1)} %copy-done.22), channel_id=1, source_target_pairs={{1,0},{3,2},{5,4},{7,6},{9,8},{11,10},{13,12},{15,14},{17,16},{19,... | collective-permute-start | bytes 3145736 | tf_op jit(solution)/shard_map/ppermute | solution.py:344
  75.3 14.1 %all-to-all-done.2.t_ref = bf16[32,64,128]{2,1,0:T(8,128)(2,1)} async-done(((bf16[32,64,128]{2,1,0:T(8,128)(2,1)}), bf16[32,64,128]{2,1,0:T(8,128)(2,1)}, u32[]{:S(2)}, u32[]{:S(2)}) %all-to-all-start.2) | async-done | bytes 524320 | tf_op jit(solution)/shard_map/all_to_all | solution.py:349
  89.3 1.3 %scan.3 = bf16[32,64,128]{2,1,0:T(8,128)(2,1)S(1)} custom-call(s32[4]{0:T(128)S(1)} %copy-done.19, bf16[32,64,128]{2,1,0:T(8,128)(2,1)} %all-to-all-done.2.t_ref), custom_call_target="tpu_custom_call" | custom-call | bytes 1048576 | tf_op jit(solution)/shard_map/scan/pallas_call | solution.py:308
  90.7 0.8 copy-done.7
  91.5 3.2 %all-to-all-start.3 = ((bf16[32,64,128]{2,1,0:T(8,128)(2,1)}), bf16[32,64,128]{2,1,0:T(8,128)(2,1)}, u32[]{:S(2)}, u32[]{:S(2)}) async-start(bf16[32,64,128]{2,1,0:T(8,128)(2,1)} %copy-done.7), calls=%async_computation.3 | async-start | bytes 1048576 | tf_op jit(solution)/shard_map/all_to_all | solution.py:354
  94.7 0.0 copy-start.15
  94.7 1.2 copy-done.15
  95.9 8.5 %grads.1 = (bf16[256,2048]{1,0:T(8,128)(2,1)}, f32[256,2048]{1,0:T(8,128)S(1)}, f32[256,2048]{1,0:T(8,128)S(1)}) custom-call(s32[4]{0:T(128)S(1)} %copy-done.19, s32[2,6]{1,0:T(2,128)S(1)} %copy-done.20, bf16[256,2048]{1,0:T(8,128)(2,1)S(1)} %copy-done.4, bf16[256,2048]{1,0:T(8,128)(2,1)S(1)} %copy-done.1, bf16[256,2048]{1,0:T(8,128)(2,1)S(1)} %copy-done.3, ...), custom_call_target="tpu_custom_call" | custom-call | flops 1476395008 | bytes 11010048 | tf_op jit(solution)/shard_map/grads/pallas_call | solution.py:308
  104.4 1.4 %copy-done.9 = f32[256,2048]{1,0:T(8,128)} copy-done((f32[256,2048]{1,0:T(8,128)}, f32[256,2048]{1,0:T(8,128)S(1)}, u32[]{:S(2)}) %copy-start.9) | copy-done | bytes 2097176
  105.7 1.3 %copy-done.11 = f32[256,2048]{1,0:T(8,128)} copy-done((f32[256,2048]{1,0:T(8,128)}, f32[256,2048]{1,0:T(8,128)S(1)}, u32[]{:S(2)}) %copy-start.11) | copy-done | bytes 2097176
  107.1 3.2 %collective-permute-done.1.rest_0_ = bf16[2,16,128,128]{3,2,1,0:T(8,128)(2,1)} collective-permute-done((bf16[2,16,128,128]{3,2,1,0:T(8,128)(2,1)}, bf16[2,16,128,128]{3,2,1,0:T(8,128)(2,1)}, u32[]{:S(2)}, u32[]{:S(2)}) %collective-permute-start.1) | collective-permute-done | bytes 1048608 | tf_op jit(solution)/shard_map/ppermute | solution.py:344
  110.3 7.7 %all-to-all-done.3 = bf16[32,64,128]{2,1,0:T(8,128)(2,1)} async-done(((bf16[32,64,128]{2,1,0:T(8,128)(2,1)}), bf16[32,64,128]{2,1,0:T(8,128)(2,1)}, u32[]{:S(2)}, u32[]{:S(2)}) %all-to-all-start.3) | async-done | bytes 524320 | tf_op jit(solution)/shard_map/all_to_all | solution.py:354
  118.0 1.6 %copy-done.10 = f32[256,2048]{1,0:T(8,128)S(1)} copy-done((f32[256,2048]{1,0:T(8,128)S(1)}, f32[256,2048]{1,0:T(8,128)}, u32[]{:S(2)}) %copy-start.10) | copy-done | bytes 2097176
  119.6 1.6 %copy-done.12 = f32[256,2048]{1,0:T(8,128)S(1)} copy-done((f32[256,2048]{1,0:T(8,128)S(1)}, f32[256,2048]{1,0:T(8,128)}, u32[]{:S(2)}) %copy-start.12) | copy-done | bytes 2097176
  121.2 4.4 %last.1 = (bf16[256,2048]{1,0:T(8,128)(2,1)}, bf16[256,2048]{1,0:T(8,128)(2,1)}) custom-call(s32[4]{0:T(128)S(1)} %copy-done.19, s32[2,6]{1,0:T(2,128)S(1)} %copy-done.20, bf16[256,2048]{1,0:T(8,128)(2,1)S(1)} %copy-done.1, bf16[256,2048]{1,0:T(8,128)(2,1)S(1)} %copy-done.3, f32[256,2048]{1,0:T(8,128)S(1)} %copy-done.10, f32[256,2048]{1,0:T(8,128)S(1)} %copy-done.12, ...), custom_call_target="tpu_custom_call" | custom-call | flops 268435456 | bytes 9961472 | tf_op jit(solution)/shard_map/last/pallas_call | solution.py:308
  (19 shorter events, 0.0 us)
Async XLA Ops:
  0.6 1.2 copy-start
  1.9 1.2 copy-start.2
  3.1 0.7 copy-start.18
  3.7 26.2 %copy-start.19 = (s32[4]{0:T(128)S(1)}, s32[4]{0:T(128)}, u32[]{:S(2)}) copy-start(s32[4]{0:T(128)} %len_ref.13) | copy-start | bytes 52
  5.6 0.8 copy-start.17
  6.4 1.0 copy-start.23
  7.4 27.9 %copy-start.1 = (bf16[256,2048]{1,0:T(8,128)(2,1)S(1)}, bf16[256,2048]{1,0:T(8,128)(2,1)}, u32[]{:S(2)}) copy-start(bf16[256,2048]{1,0:T(8,128)(2,1)} %k_ref.7) | copy-start | bytes 3145732
  7.4 28.0 %copy-start.3 = (bf16[256,2048]{1,0:T(8,128)(2,1)S(1)}, bf16[256,2048]{1,0:T(8,128)(2,1)}, u32[]{:S(2)}) copy-start(bf16[256,2048]{1,0:T(8,128)(2,1)} %v_ref.7) | copy-start | bytes 3145732
  7.4 28.0 %copy-start.4 = (bf16[256,2048]{1,0:T(8,128)(2,1)S(1)}, bf16[256,2048]{1,0:T(8,128)(2,1)}, u32[]{:S(2)}) copy-start(bf16[256,2048]{1,0:T(8,128)(2,1)} %q_ref.5) | copy-start | bytes 3145732
  7.4 28.0 %copy-start.20 = (s32[2,6]{1,0:T(2,128)S(1)}, s32[2,6]{1,0:T(2,128)}, u32[]{:S(2)}) copy-start(s32[2,6]{1,0:T(2,128)} %mask_ref.7) | copy-start | bytes 148
  7.4 22.5 %all-to-all-start = ((bf16[32,64,128]{2,1,0:T(8,128)(2,1)}), bf16[32,64,128]{2,1,0:T(8,128)(2,1)}, u32[]{:S(2)}, u32[]{:S(2)}) async-start(bf16[32,64,128]{2,1,0:T(8,128)(2,1)} %bitcast.6), calls=%async_computation | async-start | bytes 1048576 | tf_op jit(solution)/shard_map/all_to_all | solution.py:349
  14.6 31.2 %collective-permute-start = (bf16[2,16,128,128]{3,2,1,0:T(8,128)(2,1)}, bf16[2,16,128,128]{3,2,1,0:T(8,128)(2,1)}, u32[]{:S(2)}, u32[]{:S(2)}) collective-permute-start(bf16[2,16,128,128]{3,2,1,0:T(8,128)(2,1)} %copy-done.23), channel_id=1, source_target_pairs={{0,1},{2,3},{4,5},{6,7},{8,9},{10,11},{12,13},{14,15},{16,17},{18,... | collective-permute-start | bytes 3145736 | tf_op jit(solution)/shard_map/ppermute | solution.py:344
  31.3 0.8 copy-start.8
  32.1 22.0 %all-to-all-start.1 = ((bf16[32,64,128]{2,1,0:T(8,128)(2,1)}), bf16[32,64,128]{2,1,0:T(8,128)(2,1)}, u32[]{:S(2)}, u32[]{:S(2)}) async-start(bf16[32,64,128]{2,1,0:T(8,128)(2,1)} %copy-done.8), calls=%async_computation.1 | async-start | bytes 1048576 | tf_op jit(solution)/shard_map/all_to_all | solution.py:354
  35.4 18.8 %copy-start.21 = (f32[2048]{0:T(1024)S(1)}, f32[2048]{0:T(1024)}, u32[]{:S(2)}) copy-start(f32[2048]{0:T(1024)} %param.11) | copy-start | bytes 24580
  38.7 1.4 %copy-start.5 = (f32[256,2048]{1,0:T(8,128)}, f32[256,2048]{1,0:T(8,128)S(1)}, u32[]{:S(2)}) copy-start(f32[256,2048]{1,0:T(8,128)S(1)} %inner.1.raw_ref) | copy-start | bytes 6291460
  54.1 1.6 %copy-start.6 = (f32[256,2048]{1,0:T(8,128)S(1)}, f32[256,2048]{1,0:T(8,128)}, u32[]{:S(2)}) copy-start(f32[256,2048]{1,0:T(8,128)} %copy-done.5) | copy-start | bytes 6291460
  55.7 1.2 copy-start.13
  63.9 1.0 copy-start.14
  64.9 0.8 copy-start.16
  65.7 1.0 copy-start.22
  66.7 22.7 %all-to-all-start.2 = ((bf16[32,64,128]{2,1,0:T(8,128)(2,1)}), bf16[32,64,128]{2,1,0:T(8,128)(2,1)}, u32[]{:S(2)}, u32[]{:S(2)}) async-start(bf16[32,64,128]{2,1,0:T(8,128)(2,1)} %bitcast.5), calls=%async_computation.2 | async-start | bytes 1048576 | tf_op jit(solution)/shard_map/all_to_all | solution.py:349
  74.0 36.4 %collective-permute-start.1 = (bf16[2,16,128,128]{3,2,1,0:T(8,128)(2,1)}, bf16[2,16,128,128]{3,2,1,0:T(8,128)(2,1)}, u32[]{:S(2)}, u32[]{:S(2)}) collective-permute-start(bf16[2,16,128,128]{3,2,1,0:T(8,128)(2,1)} %copy-done.22), channel_id=1, source_target_pairs={{1,0},{3,2},{5,4},{7,6},{9,8},{11,10},{13,12},{15,14},{17,16},{19,... | collective-permute-start | bytes 3145736 | tf_op jit(solution)/shard_map/ppermute | solution.py:344
  90.7 0.8 copy-start.7
  91.5 26.5 %all-to-all-start.3 = ((bf16[32,64,128]{2,1,0:T(8,128)(2,1)}), bf16[32,64,128]{2,1,0:T(8,128)(2,1)}, u32[]{:S(2)}, u32[]{:S(2)}) async-start(bf16[32,64,128]{2,1,0:T(8,128)(2,1)} %copy-done.7), calls=%async_computation.3 | async-start | bytes 1048576 | tf_op jit(solution)/shard_map/all_to_all | solution.py:354
  94.7 1.2 copy-start.15
  104.4 1.4 %copy-start.9 = (f32[256,2048]{1,0:T(8,128)}, f32[256,2048]{1,0:T(8,128)S(1)}, u32[]{:S(2)}) copy-start(f32[256,2048]{1,0:T(8,128)S(1)} %get-tuple-element.20.gk_in) | copy-start | bytes 6291460
  105.7 1.3 %copy-start.11 = (f32[256,2048]{1,0:T(8,128)}, f32[256,2048]{1,0:T(8,128)S(1)}, u32[]{:S(2)}) copy-start(f32[256,2048]{1,0:T(8,128)S(1)} %get-tuple-element.21.gv_in) | copy-start | bytes 6291460
  118.0 1.6 %copy-start.10 = (f32[256,2048]{1,0:T(8,128)S(1)}, f32[256,2048]{1,0:T(8,128)}, u32[]{:S(2)}) copy-start(f32[256,2048]{1,0:T(8,128)} %copy-done.9) | copy-start | bytes 6291460
  119.6 1.6 %copy-start.12 = (f32[256,2048]{1,0:T(8,128)S(1)}, f32[256,2048]{1,0:T(8,128)}, u32[]{:S(2)}) copy-start(f32[256,2048]{1,0:T(8,128)} %copy-done.11) | copy-start | bytes 6291460

commit v2 on v1

v2 whole, which is shorter than its diff:
```python
import functools

import jax
import jax.numpy as jnp
from jax import lax
from jax.experimental import pallas as pl
from jax.experimental.pallas import tpu as pltpu
from jax.sharding import PartitionSpec as P

DH = 128
GROUP = 512
BLOCK = 128
HEADS_AT_ONCE = 4

eps_norm = 1e-06
BF = jnp.bfloat16
F32 = jnp.float32
AXES = ("ctx", "head")

NN = (((1,), (0,)), ((), ()))
NT = (((1,), (1,)), ((), ()))
TN = (((0,), (0,)), ((), ()))


def dot(a, b, dims):
    return lax.dot_general(a, b, dims, preferred_element_type=F32)


def bounds_of(len_ref):
    bounds, total = [], None
    for k in range(len_ref.shape[0] - 1):
        total = len_ref[k] if total is None else total + len_ref[k]
        bounds.append(total)
    return bounds


def segment(position, bounds):
    result = (position >= bounds[0]).astype(jnp.int32)
    for bound in bounds[1:]:
        result = result + (position >= bound).astype(jnp.int32)
    return result


def same(a, b):
    return (a == b).astype(F32)


class Place:
    def __init__(self, len_ref, rows, mask_ref=None):
        self.rows = rows
        self.blocks = rows // BLOCK
        self.devices = GROUP // rows
        self.bounds = bounds_of(len_ref)
        spot = lax.axis_index("head")
        index = lax.axis_index("ctx") * lax.axis_size("head") + spot
        self.first = index * rows
        self.part = lax.rem(spot, self.devices)
        self.group = lax.div(spot, self.devices)
        self.group_first = self.first - self.part * rows
        self.mask_ref = mask_ref

    def seg(self, position):
        return segment(position, self.bounds)

    def start(self, block):
        return self.first + block * BLOCK

    def row_segments(self, block):
        rows = lax.broadcasted_iota(jnp.int32, (BLOCK, 1), 0)
        return self.seg(rows + self.start(block))

    def pair(self, i, j):
        slot = jnp.clip(lax.div(i * (i - 1), 2) + j, 0, self.mask_ref.shape[1] - 1)
        return self.mask_ref[self.group, slot].astype(F32)

    def weights(self):
        rows = self.rows
        t = lax.broadcasted_iota(jnp.int32, (rows, rows), 0)
        s = lax.broadcasted_iota(jnp.int32, (rows, rows), 1)
        keep = (s <= t) & (self.seg(t + self.first) == self.seg(s + self.first))
        result = jnp.where(keep, 1.0, 0.0)
        for i in range(1, self.blocks):
            for j in range(i):
                bit = self.pair(self.part * self.blocks + i, self.part * self.blocks + j)
                inside = (
                    (t >= i * BLOCK)
                    & (t < (i + 1) * BLOCK)
                    & (s >= j * BLOCK)
                    & (s < (j + 1) * BLOCK)
                )
                result = jnp.where(inside, result * bit, result)
        return result

    def to_later(self, away, block):
        there = (self.part + away) * self.blocks + block
        edge = self.seg(self.start(block) + away * self.rows - 1)
        return [
            self.pair(there, self.part * self.blocks + j) * same(self.seg(self.start(j + 1) - 1), edge)
            for j in range(self.blocks)
        ]

    def before(self, block):
        edge = self.seg(self.start(block) - 1)
        carried = same(self.seg(self.group_first - 1), edge)
        peers = [(self.part >= away).astype(F32) for away in range(1, self.devices)]
        return carried, peers, (self.row_segments(block) == edge).astype(F32)

    def after(self, block):
        own = self.part * self.blocks + block
        edge = self.seg(self.start(block + 1))
        carried = same(self.seg(self.group_first + GROUP), edge)
        peers = []
        for i in range(self.blocks):
            for away in range(1, self.devices):
                there = (self.part + away < self.devices).astype(F32)
                other = (self.part + away) * self.blocks + i
                start = self.start(i) + away * self.rows
                peers.append(self.pair(other, own) * same(self.seg(start), edge) * there)
        return carried, peers, (self.row_segments(block) == edge).astype(F32)


def mixed(state_ref, peer_refs, factors, head):
    carried, peers, _ = factors
    total = state_ref[head].astype(F32) * carried
    for ref, factor in zip(peer_refs, peers, strict=True):
        total = total + ref[head].astype(F32) * factor
    return total.astype(BF)


def columns(head):
    return pl.ds(head * DH, DH)


def rows_of(block):
    return pl.ds(block * BLOCK, BLOCK)


def state_kernel(len_ref, mask_ref, k_ref, v_ref, t_ref, *x_refs):
    rows, width = k_ref.shape
    place = Place(len_ref, rows, mask_ref)
    last = place.seg(place.start(place.blocks) - 1)
    ends = [place.seg(place.start(b + 1) - 1) for b in range(place.blocks)]
    masks = [(place.row_segments(b) == ends[b]).astype(BF) for b in range(place.blocks)]
    wanted = [[same(e, last) for e in ends]]
    for b in range(place.blocks):
        for away in range(1, place.devices):
            wanted.append(place.to_later(away, b))
    for head in range(width // DH):
        updates = []
        for b in range(place.blocks):
            k = k_ref[rows_of(b), columns(head)] * masks[b]
            updates.append(dot(k, v_ref[rows_of(b), columns(head)], TN))
        for ref, factors in zip((t_ref, *x_refs), wanted, strict=True):
            total = updates[0] * factors[0]
            for update, factor in zip(updates[1:], factors[1:], strict=True):
                total = total + update * factor
            ref[head] = total.astype(BF)


def inner_kernel(len_ref, mask_ref, q_ref, k_ref, v_ref, raw_ref, weight_ref):
    rows, width = q_ref.shape

    @pl.when(pl.program_id(0) == 0)
    def _():
        weight_ref[...] = Place(len_ref, rows, mask_ref).weights()

    for head in range(width // DH):
        at = columns(head)
        probs = (dot(q_ref[:, at], k_ref[:, at], NT) * weight_ref[...]).astype(BF)
        raw_ref[:, at] = dot(probs, v_ref[:, at], NN)


def scan_kernel(len_ref, t_ref, out_ref, *, rows, backward):
    count = t_ref.shape[0]
    devices = GROUP // rows
    bounds = bounds_of(len_ref)

    def one(turn, acc):
        group = count // devices - 1 - turn if backward else turn
        for k in range(devices):
            out_ref[group * devices + k] = acc.astype(BF)
        for k in range(devices):
            index = group * devices + (devices - 1 - k if backward else k)
            first = index * rows
            if backward:
                keep = same(segment(first, bounds), segment(first + rows, bounds))
            else:
                keep = same(segment(first - 1, bounds), segment(first + rows - 1, bounds))
            acc = acc * keep + t_ref[index].astype(F32)
        return acc

    lax.fori_loop(0, count // devices, one, jnp.zeros(t_ref.shape[1:], F32))


def norm_kernel(len_ref, mask_ref, gain_ref, q_ref, raw_ref, grad_ref, kv_ref, *rest, rows, block, peers):
    peer_refs, rest = rest[:peers], rest[peers:]
    earlier_refs, rest = rest[:block], rest[block:]
    scale_ref, held_out_ref, d_ref, w_ref = rest[:4]
    held_ref, squares_ref, cross_ref = rest[-3:]
    width = q_ref.shape[1]
    heads = width // DH
    chunk = pl.program_id(1)
    chunks = pl.num_programs(1)
    place = Place(len_ref, rows, mask_ref)

    @pl.when(pl.program_id(0) == 0)
    def _():
        factors = place.before(block)
        squares = cross = None
        for head in range(heads):
            at = columns(head)
            state = mixed(kv_ref, peer_refs, factors, head)
            raw = raw_ref[:, at] + dot(q_ref[:, at], state, NN) * factors[2]
            raw = raw.astype(BF)
            held_ref[chunk, :, at] = raw
            held_out_ref[:, at] = raw
            raw = raw.astype(F32)
            scaled = grad_ref[:, at].astype(F32) * gain_ref[:, at]
            squares = raw * raw if head == 0 else squares + raw * raw
            cross = scaled * raw if head == 0 else cross + scaled * raw
        fresh = chunk == 0
        squares = squares + jnp.where(fresh, 0.0, squares_ref[...])
        cross = cross + jnp.where(fresh, 0.0, cross_ref[...])
        squares_ref[...] = squares
        cross_ref[...] = cross

        @pl.when(chunk == chunks - 1)
        def _():
            full = width * chunks
            total = jnp.sum(squares, axis=1, keepdims=True)
            inverse = 1.0 / jnp.sqrt(total / full + eps_norm)
            mean = jnp.sum(cross, axis=1, keepdims=True) * inverse / full
            squares_ref[...] = jnp.broadcast_to(inverse, squares_ref.shape)
            cross_ref[...] = jnp.broadcast_to(mean, cross_ref.shape)
            scale_ref[...] = squares_ref[...]

    @pl.when(pl.program_id(0) == 1)
    def _():
        inverse, mean = squares_ref[...], cross_ref[...]
        own = place.seg(place.start(block))
        begin = (place.row_segments(block) == own).astype(BF)
        into = [same(place.seg(place.start(b)), place.seg(place.first)) for b in range(block + 1)]
        for head in range(heads):
            at = columns(head)
            normed = held_ref[chunk, :, at].astype(F32) * inverse
            scaled = grad_ref[:, at].astype(F32) * gain_ref[:, at]
            grad = ((scaled - normed * mean) * inverse).astype(BF)
            d_ref[:, at] = grad
            update = dot(q_ref[:, at] * begin, grad, TN)
            w_ref[head] = update.astype(BF)
            if len(rest) > 7:
                total = update * into[block]
                for ref, factor in zip(earlier_refs, into[:block], strict=True):
                    total = total + ref[head].astype(F32) * factor
                rest[4][head] = total.astype(BF)


def grads_kernel(len_ref, mask_ref, gain_ref, q_ref, k_ref, v_ref, kv_ref, *rest, blocks, peers):
    ins = 3 * blocks + blocks * peers
    d_refs, raw_refs, scale_refs = rest[:blocks], rest[blocks : 2 * blocks], rest[2 * blocks : 3 * blocks]
    peer_refs = rest[3 * blocks : ins]
    out_ref, gq_ref, gk_ref, gv_ref, weight_ref = rest[ins:]
    rows, width = q_ref.shape
    place = Place(len_ref, rows, mask_ref)

    @pl.when(pl.program_id(0) == 0)
    def _():
        weight_ref[...] = place.weights()

    factors = [place.before(b) for b in range(blocks)]
    for head in range(width // DH):
        at = columns(head)
        q, k, v = q_ref[:, at], k_ref[:, at], v_ref[:, at]
        d = jnp.concatenate([ref[:, at] for ref in d_refs], axis=0)
        probs = (dot(q, k, NT) * weight_ref[...]).astype(BF)
        grad_probs = (dot(d, v, NT) * weight_ref[...]).astype(BF)
        inner = dot(grad_probs, k, NN)
        for b in range(blocks):
            state = mixed(kv_ref, peer_refs[b * peers : (b + 1) * peers], factors[b], head)
            outer = dot(d_refs[b][:, at], state, NT) * factors[b][2]
            part = inner[b * BLOCK : (b + 1) * BLOCK] + outer
            gq_ref[rows_of(b), at] = part.astype(BF)
            normed = raw_refs[b][:, at].astype(F32) * scale_refs[b][...]
            out_ref[rows_of(b), at] = (normed * gain_ref[:, at]).astype(BF)
        gk_ref[:, at] = dot(grad_probs, q, TN)
        gv_ref[:, at] = dot(probs, d, TN)


def last_kernel(len_ref, mask_ref, k_ref, v_ref, gk_in, gv_in, gs_ref, *rest):
    peer_refs, (gk_ref, gv_ref) = rest[:-2], rest[-2:]
    rows, width = k_ref.shape
    place = Place(len_ref, rows, mask_ref)
    factors = [place.after(b) for b in range(place.blocks)]
    for head in range(width // DH):
        at = columns(head)
        for b in range(place.blocks):
            at_rows = rows_of(b)
            state = mixed(gs_ref, peer_refs, factors[b], head)
            reach = factors[b][2]
            gk = gk_in[at_rows, at] + dot(v_ref[at_rows, at], state, NT) * reach
            gv = gv_in[at_rows, at] + dot(k_ref[at_rows, at], state, NN) * reach
            gk_ref[at_rows, at] = gk.astype(BF)
            gv_ref[at_rows, at] = gv.astype(BF)


SMEM = pl.BlockSpec(memory_space=pltpu.SMEM)


def call(kernel, name, grid, scalars, arrays, outs, scratch=(), flops=0):
    moved = sum(a.size * a.dtype.itemsize for a, _ in (*arrays, *outs))
    return pl.pallas_call(
        kernel,
        name=name,
        grid=grid,
        in_specs=[SMEM] * len(scalars) + [spec for _, spec in arrays],
        out_specs=[spec for _, spec in outs],
        out_shape=[shape for shape, _ in outs],
        scratch_shapes=scratch,
        compiler_params=pltpu.CompilerParams(vmem_limit_bytes=48 * 1024 * 1024),
        cost_estimate=pl.CostEstimate(flops=flops, bytes_accessed=moved, transcendentals=0),
    )(*scalars, *[a for a, _ in arrays])


def local(queries, keys, values, grad_out, gain, lengths, block_mask):
    rows, width = queries.shape
    heads = width // DH
    blocks = rows // BLOCK
    devices = GROUP // rows
    peers = devices - 1
    head_count = lax.axis_size("head")
    total = lax.axis_size("ctx") * head_count
    shape = jax.ShapeDtypeStruct
    state = shape((heads, DH, DH), BF)
    tokens = shape((rows, width), BF)
    partial = shape((rows, width), F32)
    block_tokens = shape((BLOCK, width), BF)
    square = [pltpu.VMEM((rows, rows), F32)]
    unit = 2 * rows * width * DH
    inner = 2 * rows * rows * width
    scalars = [lengths, block_mask]
    group_heads = HEADS_AT_ONCE if heads % HEADS_AT_ONCE == 0 else heads
    chunks = heads // group_heads
    span = group_heads * DH

    wide = pl.BlockSpec((rows, span), lambda c: (0, c))
    block_wide = pl.BlockSpec((BLOCK, span), lambda c: (0, c))
    state_part = pl.BlockSpec((group_heads, DH, DH), lambda c: (c, 0, 0))
    gain_part = pl.BlockSpec((1, span), lambda c: (0, c))
    scale_whole = pl.BlockSpec((BLOCK, DH), lambda c: (0, 0))

    def to_peers(states, away, backward):
        pairs = [(z, z + away) for z in range(head_count - away) if z % devices + away < devices]
        if backward:
            pairs = [(b, a) for a, b in pairs]
        return lax.ppermute(states, "head", pairs)

    def scanned(sums, backward):
        height = heads * DH // total
        slices = sums.reshape(total, height, DH)
        slices = lax.all_to_all(slices, AXES, split_axis=0, concat_axis=0, tiled=True)
        part = 16 if height % 16 == 0 else height
        spec = pl.BlockSpec((total, part, DH), lambda c: (0, c, 0))
        (slices,) = call(
            functools.partial(scan_kernel, rows=rows, backward=backward),
            "scan",
            (height // part,),
            [lengths],
            [(slices, spec)],
            [(shape(slices.shape, BF), spec)],
        )
        slices = lax.all_to_all(slices, AXES, split_axis=0, concat_axis=0, tiled=True)
        return slices.reshape(heads, DH, DH)

    gain_row = gain.reshape(1, width)
    sum_kv, *later = call(
        state_kernel,
        "states",
        (chunks,),
        scalars,
        [(keys, wide), (values, wide)],
        [(state, state_part)] * (1 + blocks * peers),
        flops=unit,
    )
    kv_state = scanned(sum_kv, False)
    from_peers = [to_peers(x, 1 + at % peers, False) for at, x in enumerate(later)]
    (raw_inner,) = call(
        inner_kernel,
        "inner",
        (chunks,),
        scalars,
        [(queries, wide), (keys, wide), (values, wide)],
        [(partial, wide)],
        square,
        flops=2 * inner,
    )

    def norm(block, own_peers, earlier):
        first = lambda p, c: c * (1 - p) + (chunks - 1) * p
        second = lambda p, c: c * p
        both_rows = pl.BlockSpec((BLOCK, span), lambda p, c: (block, c))
        first_rows = pl.BlockSpec((BLOCK, span), lambda p, c: (block, first(p, c)))
        first_block = pl.BlockSpec((BLOCK, span), lambda p, c: (0, first(p, c)))
        second_block = pl.BlockSpec((BLOCK, span), lambda p, c: (0, second(p, c)))
        first_state = pl.BlockSpec((group_heads, DH, DH), lambda p, c: (first(p, c), 0, 0))
        second_state = pl.BlockSpec((group_heads, DH, DH), lambda p, c: (second(p, c), 0, 0))
        ends = [(state, second_state)] if block == blocks - 1 and blocks > 1 else []
        return call(
            functools.partial(norm_kernel, rows=rows, block=block, peers=peers),
            "norm",
            (2, chunks),
            scalars,
            [
                (gain_row, pl.BlockSpec((1, span), lambda p, c: (0, c))),
                (queries, both_rows),
                (raw_inner, first_rows),
                (grad_out, both_rows),
                (kv_state, first_state),
                *[(x, first_state) for x in own_peers],
                *[(w, second_state) for w in earlier],
            ],
            [
                (shape((BLOCK, DH), F32), pl.BlockSpec((BLOCK, DH), lambda p, c: (0, 0))),
                (block_tokens, first_block),
                (block_tokens, second_block),
                (state, second_state),
                *ends,
            ],
            [
                pltpu.VMEM((chunks, BLOCK, span), BF),
                pltpu.VMEM((BLOCK, DH), F32),
                pltpu.VMEM((BLOCK, DH), F32),
            ],
            flops=2 * unit // blocks,
        )

    scales, raws, grads, updates, back = [], [], [], [], []
    for b in range(blocks):
        scale, raw, grad, update, *ends = norm(b, from_peers[b * peers : (b + 1) * peers], updates)
        scales.append(scale)
        raws.append(raw)
        grads.append(grad)
        updates.append(update)
        back += [to_peers(update, away, True) for away in range(1, devices)]
    grad_state = scanned(ends[0] if ends else updates[0], True)
    output, grad_q, part_k, part_v = call(
        functools.partial(grads_kernel, blocks=blocks, peers=peers),
        "grads",
        (chunks,),
        scalars,
        [
            (gain_row, gain_part),
            (queries, wide),
            (keys, wide),
            (values, wide),
            (kv_state, state_part),
            *[(d, block_wide) for d in grads],
            *[(r, block_wide) for r in raws],
            *[(s, scale_whole) for s in scales],
            *[(x, state_part) for x in from_peers],
        ],
        [(tokens, wide), (tokens, wide), (partial, wide), (partial, wide)],
        square,
        flops=5 * inner + unit,
    )
    grad_k, grad_v = call(
        last_kernel,
        "last",
        (chunks,),
        scalars,
        [
            (keys, wide),
            (values, wide),
            (part_k, wide),
            (part_v, wide),
            (grad_state, state_part),
            *[(w, state_part) for w in back],
        ],
        [(tokens, wide), (tokens, wide)],
        flops=2 * unit,
    )
    return output, grad_q, grad_k, grad_v


def solution(mesh):
    tokens = P(AXES, None)
    return jax.shard_map(
        local,
        mesh=mesh,
        in_specs=(tokens, tokens, tokens, tokens, P(), P(), P("ctx", None)),
        out_specs=(tokens, tokens, tokens, tokens),
        check_vma=False,
    )
```

time: 127 us -> 147 us (1.16)
  blocking collectives: 0 us -> 44.4 us
  waiting for transfers between devices: 50.1 us -> 26.1 us
  starting transfers between devices: 26.4 us -> 14.5 us
  Pallas kernels: 27.7 us -> 36.6 us
  local copies, waits for them, and re-layouts: 20.4 us -> 22.7 us
    all_to_all x0 -> x2, blocking collectives: none -> 44.4 us  [scanned(): lax.all_to_all(slices, AXES, split_axis=0, concat_axis=0, tiled=True)]
    all_to_all x4 -> x2, waiting for transfers between devices: 41.1 us -> 0.01 us  [scanned(): lax.all_to_all(slices, AXES, split_axis=0, concat_axis=0, tiled=True)]
    ppermute x2 -> x4, waiting for transfers between devices: 9 us -> 26.1 us  [to_peers(): return lax.ppermute(states, 'head', pairs)]
    all_to_all x4 -> x2, starting transfers between devices: 20.9 us -> 6.42 us  [scanned(): lax.all_to_all(slices, AXES, split_axis=0, concat_axis=0, tiled=True)]
    pallas_call x7 -> x8, Pallas kernels: 27.7 us -> 36.6 us  [call(): pl.pallas_call(kernel, name=name, grid=grid, in_specs=[SMEM] * len(scalar...]
    ppermute x2 -> x4, starting transfers between devices: 5.59 us -> 8.05 us  [to_peers(): return lax.ppermute(states, 'head', pairs)]
    unnamed x48 -> x64, local copies, waits for them, and re-layouts: 20.4 us -> 22.7 us
  transfers between devices with their start and end apart: 6 -> 6, of which waited for: 6 -> 4; matrix products, arithmetic and copies ran while one was open for 0% -> 0% of each run, Pallas kernels for 12% -> 12%
where the time goes in v2:
time: 147 us; the launch traced here: 145 us
  blocking collectives  44.4 us (30%)
  Pallas kernels  36.6 us (25%)
  waiting for transfers between devices  26.1 us (18%)
  local copies, waits for them, and re-layouts  22.7 us (15%)
  starting transfers between devices  14.5 us (10%)
    all_to_all x2, blocking collectives, scanned(): lax.all_to_all(slices, AXES, split_axis=0, concat_axis=0, tiled=True)  44.4 us
    pallas_call x8, Pallas kernels, call(): pl.pallas_call(kernel, name=name, grid=grid, in_specs=[SMEM] * len(scalar...  36.6 us
    ppermute x4, waiting for transfers between devices, to_peers(): return lax.ppermute(states, 'head', pairs)  26.1 us
    unnamed x64, local copies, waits for them, and re-layouts  22.7 us
    ppermute x4, starting transfers between devices, to_peers(): return lax.ppermute(states, 'head', pairs)  8.05 us
    all_to_all x2, starting transfers between devices, scanned(): lax.all_to_all(slices, AXES, split_axis=0, concat_axis=0, tiled=True)  6.42 us
  transfers between devices with their start and end apart: 6, of which 4 were waited for; matrix products, arithmetic and copies ran while one was open for 0% of the time, Pallas kernels for 12%

profile of v2, /device:TPU:1, one launch (start us, length us, event | category | flops | bytes accessed | tf_op | source)
XLA Modules:
  0.0 145.1 jit_solution(9822808744323446803)
XLA Ops:
  0.6 0.0 copy-start.1
  0.6 1.2 copy-done.1
  1.9 1.2 copy-done.3
  3.1 0.7 copy-done.26
  3.8 0.7 copy-done.28
  4.4 2.2 %states.1 = (bf16[16,128,128]{2,1,0:T(8,128)(2,1)S(1)}, bf16[16,128,128]{2,1,0:T(8,128)(2,1)S(1)}, bf16[16,128,128]{2,1,0:T(8,128)(2,1)S(1)}) custom-call(s32[4]{0:T(128)S(1)} %copy-done.28, s32[2,6]{1,0:T(2,128)S(1)} %copy-done.26, bf16[256,2048]{1,0:T(8,128)(2,1)S(1)} %copy-done.1, bf16[256,2048]{1,0:T(8,128)(2,1)S(1)} %copy-done.3), custom_call_target="tpu_custom_call" | custom-call | flops 134217728 | bytes 3670016 | tf_op jit(solution)/shard_map/states/pallas_call | solution.py:311
  6.6 0.0 copy-start.30
  6.6 0.0 copy-start.4
  6.6 0.0 copy-start.6
  6.7 22.2 %all_to_all.20.t_ref = bf16[32,64,128]{2,1,0:T(8,128)(2,1)S(1)} all-to-all(bf16[32,64,128]{2,1,0:T(8,128)(2,1)S(1)} %bitcast.6), channel_id=1, replica_groups=mesh['ctx'=8,'head'=4] {'ctx','head'}, dimensions={0} | all-to-all | bytes 1048576 | tf_op jit(solution)/shard_map/all_to_all | solution.py:360
  28.9 2.1 %scan.2 = bf16[32,64,128]{2,1,0:T(8,128)(2,1)S(1)} custom-call(s32[4]{0:T(128)S(1)} %copy-done.28, bf16[32,64,128]{2,1,0:T(8,128)(2,1)S(1)} %all_to_all.20.t_ref), custom_call_target="tpu_custom_call" | custom-call | bytes 1048576 | tf_op jit(solution)/shard_map/scan/pallas_call | solution.py:311
  31.0 0.0 copy-start.11
  31.0 0.8 copy-done.11
  31.8 3.2 %all-to-all-start.1 = ((bf16[32,64,128]{2,1,0:T(8,128)(2,1)}), bf16[32,64,128]{2,1,0:T(8,128)(2,1)}, u32[]{:S(2)}, u32[]{:S(2)}) async-start(bf16[32,64,128]{2,1,0:T(8,128)(2,1)} %copy-done.11), calls=%async_computation.1 | async-start | bytes 1048576 | tf_op jit(solution)/shard_map/all_to_all | solution.py:371
  35.0 3.3 %collective-permute-start = (bf16[16,128,128]{2,1,0:T(8,128)(2,1)}, bf16[16,128,128]{2,1,0:T(8,128)(2,1)S(1)}, u32[]{:S(2)}, u32[]{:S(2)}) collective-permute-start(bf16[16,128,128]{2,1,0:T(8,128)(2,1)} %copy-done.31), channel_id=1, source_target_pairs={{0,1},{2,3},{4,5},{6,7},{8,9},{10,11},{12,13},{14,15},{16,17},{18,... | collective-permute-start | bytes 1572872 | tf_op jit(solution)/shard_map/ppermute | solution.py:355
  38.4 2.1 %collective-permute-start.1 = (bf16[16,128,128]{2,1,0:T(8,128)(2,1)}, bf16[16,128,128]{2,1,0:T(8,128)(2,1)}, u32[]{:S(2)}, u32[]{:S(2)}) collective-permute-start(bf16[16,128,128]{2,1,0:T(8,128)(2,1)} %copy-done.30), channel_id=1, source_target_pairs={{0,1},{2,3},{4,5},{6,7},{8,9},{10,11},{12,13},{14,15},{16,17},{18,... | collective-permute-start | bytes 1572872 | tf_op jit(solution)/shard_map/ppermute | solution.py:355
  40.5 3.6 %inner.1.raw_ref = f32[256,2048]{1,0:T(8,128)S(1)} custom-call(s32[4]{0:T(128)S(1)} %copy-done.29, s32[2,6]{1,0:T(2,128)S(1)} %copy-done.27, bf16[256,2048]{1,0:T(8,128)(2,1)S(1)} %copy-done.6, bf16[256,2048]{1,0:T(8,128)(2,1)S(1)} %copy-done.2, bf16[256,2048]{1,0:T(8,128)(2,1)S(1)} %copy-done.4), custom_call_target="tpu_custom_call" | custom-call | flops 536870912 | bytes 5242880 | tf_op jit(solution)/shard_map/inner/pallas_call | solution.py:311
  44.2 1.3 copy-done
  45.5 9.5 %collective-permute-done.rest_0_.rest_6_ = bf16[16,128,128]{2,1,0:T(8,128)(2,1)S(1)} collective-permute-done((bf16[16,128,128]{2,1,0:T(8,128)(2,1)}, bf16[16,128,128]{2,1,0:T(8,128)(2,1)S(1)}, u32[]{:S(2)}, u32[]{:S(2)}) %collective-permute-start) | collective-permute-done | bytes 524320 | tf_op jit(solution)/shard_map/ppermute | solution.py:355
  55.0 0.8 copy-done.8
  55.8 1.2 copy-done.7
  57.1 1.0 copy-done.9
  58.1 5.6 %norm.2 = (f32[128,128]{1,0:T(8,128)S(1)}, bf16[128,2048]{1,0:T(8,128)(2,1)S(1)}, bf16[128,2048]{1,0:T(8,128)(2,1)S(1)}, bf16[16,128,128]{2,1,0:T(8,128)(2,1)}) custom-call(s32[4]{0:T(128)S(1)} %copy-done.29, s32[2,6]{1,0:T(2,128)S(1)} %copy-done.27, f32[1,2048]{1,0:T(1,128)S(1)} %bitcast.7, bf16[256,2048]{1,0:T(8,128)(2,1)S(1)} %copy-done.6, ...), custom_call_target="tpu_custom_call" | custom-call | flops 134217728 | bytes 6889472 | tf_op jit(solution)/shard_map/norm/pallas_call | solution.py:311
  63.7 0.8 copy-done.13
  64.5 0.8 copy-done.15
  65.3 1.0 collective-permute-done.1.rest_0_.rest_7_
  66.3 6.6 %norm.3 = (f32[128,128]{1,0:T(8,128)S(1)}, bf16[128,2048]{1,0:T(8,128)(2,1)S(1)}, bf16[128,2048]{1,0:T(8,128)(2,1)S(1)}, bf16[16,128,128]{2,1,0:T(8,128)(2,1)}, bf16[16,128,128]{2,1,0:T(8,128)(2,1)S(1)}) custom-call(s32[4]{0:T(128)S(1)} %copy-done.29, s32[2,6]{1,0:T(2,128)S(1)} %copy-done.27, f32[1,2048]{1,0:T(1,128)S(1)} %bitcast.8, ...), custom_call_target="tpu_custom_call" | custom-call | flops 134217728 | bytes 7938048 | tf_op jit(solution)/shard_map/norm/pallas_call | solution.py:311
  72.8 0.8 copy-done.19
  73.7 0.8 copy-done.21
  74.5 22.2 %all_to_all.21.t_ref = bf16[32,64,128]{2,1,0:T(8,128)(2,1)S(1)} all-to-all(bf16[32,64,128]{2,1,0:T(8,128)(2,1)S(1)} %bitcast.5), channel_id=1, replica_groups=mesh['ctx'=8,'head'=4] {'ctx','head'}, dimensions={0} | all-to-all | bytes 1048576 | tf_op jit(solution)/shard_map/all_to_all | solution.py:360
  96.7 2.9 %scan.3 = bf16[32,64,128]{2,1,0:T(8,128)(2,1)} custom-call(s32[4]{0:T(128)S(1)} %copy-done.29, bf16[32,64,128]{2,1,0:T(8,128)(2,1)S(1)} %all_to_all.21.t_ref), custom_call_target="tpu_custom_call" | custom-call | bytes 1048576 | tf_op jit(solution)/shard_map/scan/pallas_call | solution.py:311
  99.6 3.2 %all-to-all-start.3 = ((bf16[32,64,128]{2,1,0:T(8,128)(2,1)}), bf16[32,64,128]{2,1,0:T(8,128)(2,1)}, u32[]{:S(2)}, u32[]{:S(2)}) async-start(bf16[32,64,128]{2,1,0:T(8,128)(2,1)} %scan.3), calls=%async_computation.3 | async-start | bytes 1048576 | tf_op jit(solution)/shard_map/all_to_all | solution.py:371
  102.8 1.3 collective-permute-start.3
  104.1 1.3 collective-permute-start.2
  105.4 1.0 copy-done.10
  106.4 1.0 copy-done.14
  107.5 1.0 copy-done.16
  108.5 1.0 copy-done.20
  109.6 1.0 copy-done.22
  110.6 8.8 %grads.1 = (bf16[256,2048]{1,0:T(8,128)(2,1)}, bf16[256,2048]{1,0:T(8,128)(2,1)}, f32[256,2048]{1,0:T(8,128)}, f32[256,2048]{1,0:T(8,128)}) custom-call(s32[4]{0:T(128)S(1)} %copy-done.29, s32[2,6]{1,0:T(2,128)S(1)} %copy-done.27, f32[1,2048]{1,0:T(1,128)S(1)} %bitcast.9, bf16[256,2048]{1,0:T(8,128)(2,1)S(1)} %copy-done.6, bf16[256,2048]{1,0:T(8,128)(2,1)S(1)} %copy-done.2, ...), custom_call_target="tpu_custom_call" | custom-call | flops 1476395008 | bytes 13246464 | tf_op jit(solution)/shard_map/grads/pallas_call | solution.py:311
  119.4 5.2 %collective-permute-done.3.rest_1_ = bf16[16,128,128]{2,1,0:T(8,128)(2,1)S(1)} collective-permute-done((bf16[16,128,128]{2,1,0:T(8,128)(2,1)}, bf16[16,128,128]{2,1,0:T(8,128)(2,1)S(1)}, u32[]{:S(2)}, u32[]{:S(2)}) %collective-permute-start.3) | collective-permute-done | bytes 524320 | tf_op jit(solution)/shard_map/ppermute | solution.py:355
  124.6 0.8 copy-done.17
  125.4 10.4 %collective-permute-done.2.rest_0_ = bf16[16,128,128]{2,1,0:T(8,128)(2,1)S(1)} collective-permute-done((bf16[16,128,128]{2,1,0:T(8,128)(2,1)}, bf16[16,128,128]{2,1,0:T(8,128)(2,1)S(1)}, u32[]{:S(2)}, u32[]{:S(2)}) %collective-permute-start.2) | collective-permute-done | bytes 524320 | tf_op jit(solution)/shard_map/ppermute | solution.py:355
  135.9 0.8 copy-done.23
  136.7 1.6 %copy-done.12 = f32[256,2048]{1,0:T(8,128)S(1)} copy-done((f32[256,2048]{1,0:T(8,128)S(1)}, f32[256,2048]{1,0:T(8,128)}, u32[]{:S(2)}) %copy-start.12) | copy-done | bytes 2097176
  138.3 1.0 copy-done.18
  139.3 1.0 copy-done.24
  140.4 4.8 %last.1 = (bf16[256,2048]{1,0:T(8,128)(2,1)}, bf16[256,2048]{1,0:T(8,128)(2,1)}) custom-call(s32[4]{0:T(128)S(1)} %copy-done.29, s32[2,6]{1,0:T(2,128)S(1)} %copy-done.27, bf16[256,2048]{1,0:T(8,128)(2,1)S(1)} %copy-done.2, bf16[256,2048]{1,0:T(8,128)(2,1)S(1)} %copy-done.5, f32[256,2048]{1,0:T(8,128)S(1)} %copy-done.12, ...), custom_call_target="tpu_custom_call" | custom-call | flops 268435456 | bytes 9961472 | tf_op jit(solution)/shard_map/last/pallas_call | solution.py:311
  (38 shorter events, 0.1 us)
Async XLA Ops:
  0.6 1.2 copy-start.1
  1.9 1.2 copy-start.3
  3.1 0.7 copy-start.26
  3.8 0.7 copy-start.28
  6.6 22.3 %copy-start.30 = (bf16[16,128,128]{2,1,0:T(8,128)(2,1)}, bf16[16,128,128]{2,1,0:T(8,128)(2,1)S(1)}, u32[]{:S(2)}) copy-start(bf16[16,128,128]{2,1,0:T(8,128)(2,1)S(1)} %get-tuple-element.25) | copy-start | bytes 1572868
  6.6 22.3 %copy-start.31 = (bf16[16,128,128]{2,1,0:T(8,128)(2,1)}, bf16[16,128,128]{2,1,0:T(8,128)(2,1)S(1)}, u32[]{:S(2)}) copy-start(bf16[16,128,128]{2,1,0:T(8,128)(2,1)S(1)} %get-tuple-element.23) | copy-start | bytes 1572868
  6.6 33.9 %copy-start.2 = (bf16[256,2048]{1,0:T(8,128)(2,1)S(1)}, bf16[256,2048]{1,0:T(8,128)(2,1)}, u32[]{:S(2)}) copy-start(bf16[256,2048]{1,0:T(8,128)(2,1)} %k_ref.7) | copy-start | bytes 3145732
  6.6 33.9 %copy-start.4 = (bf16[256,2048]{1,0:T(8,128)(2,1)S(1)}, bf16[256,2048]{1,0:T(8,128)(2,1)}, u32[]{:S(2)}) copy-start(bf16[256,2048]{1,0:T(8,128)(2,1)} %v_ref.7) | copy-start | bytes 3145732
  6.6 33.9 %copy-start.6 = (bf16[256,2048]{1,0:T(8,128)(2,1)S(1)}, bf16[256,2048]{1,0:T(8,128)(2,1)}, u32[]{:S(2)}) copy-start(bf16[256,2048]{1,0:T(8,128)(2,1)} %q_ref.7) | copy-start | bytes 3145732
  6.6 33.9 %copy-start.27 = (s32[2,6]{1,0:T(2,128)S(1)}, s32[2,6]{1,0:T(2,128)}, u32[]{:S(2)}) copy-start(s32[2,6]{1,0:T(2,128)} %mask_ref.11) | copy-start | bytes 148
  6.7 33.9 %copy-start.29 = (s32[4]{0:T(128)S(1)}, s32[4]{0:T(128)}, u32[]{:S(2)}) copy-start(s32[4]{0:T(128)} %len_ref.15) | copy-start | bytes 52
  31.0 0.8 copy-start.11
  31.8 24.0 %all-to-all-start.1 = ((bf16[32,64,128]{2,1,0:T(8,128)(2,1)}), bf16[32,64,128]{2,1,0:T(8,128)(2,1)}, u32[]{:S(2)}, u32[]{:S(2)}) async-start(bf16[32,64,128]{2,1,0:T(8,128)(2,1)} %copy-done.11), calls=%async_computation.1 | async-start | bytes 1048576 | tf_op jit(solution)/shard_map/all_to_all | solution.py:371
  35.0 20.0 %collective-permute-start = (bf16[16,128,128]{2,1,0:T(8,128)(2,1)}, bf16[16,128,128]{2,1,0:T(8,128)(2,1)S(1)}, u32[]{:S(2)}, u32[]{:S(2)}) collective-permute-start(bf16[16,128,128]{2,1,0:T(8,128)(2,1)} %copy-done.31), channel_id=1, source_target_pairs={{0,1},{2,3},{4,5},{6,7},{8,9},{10,11},{12,13},{14,15},{16,17},{18,... | collective-permute-start | bytes 1572872 | tf_op jit(solution)/shard_map/ppermute | solution.py:355
  38.4 17.5 %copy-start.25 = (f32[2048]{0:T(1024)S(1)}, f32[2048]{0:T(1024)}, u32[]{:S(2)}) copy-start(f32[2048]{0:T(1024)} %param.11) | copy-start | bytes 24580
  38.4 27.9 %collective-permute-start.1 = (bf16[16,128,128]{2,1,0:T(8,128)(2,1)}, bf16[16,128,128]{2,1,0:T(8,128)(2,1)}, u32[]{:S(2)}, u32[]{:S(2)}) collective-permute-start(bf16[16,128,128]{2,1,0:T(8,128)(2,1)} %copy-done.30), channel_id=1, source_target_pairs={{0,1},{2,3},{4,5},{6,7},{8,9},{10,11},{12,13},{14,15},{16,17},{18,... | collective-permute-start | bytes 1572872 | tf_op jit(solution)/shard_map/ppermute | solution.py:355
  44.2 1.4 copy-start
  55.0 0.8 copy-start.8
  55.8 1.2 copy-start.7
  57.1 1.0 copy-start.9
  63.7 0.8 copy-start.13
  64.5 0.8 copy-start.15
  72.8 0.8 copy-start.19
  73.7 0.8 copy-start.21
  99.6 37.1 %all-to-all-start.3 = ((bf16[32,64,128]{2,1,0:T(8,128)(2,1)}), bf16[32,64,128]{2,1,0:T(8,128)(2,1)}, u32[]{:S(2)}, u32[]{:S(2)}) async-start(bf16[32,64,128]{2,1,0:T(8,128)(2,1)} %scan.3), calls=%async_computation.3 | async-start | bytes 1048576 | tf_op jit(solution)/shard_map/all_to_all | solution.py:371
  102.8 21.9 %collective-permute-start.3 = (bf16[16,128,128]{2,1,0:T(8,128)(2,1)}, bf16[16,128,128]{2,1,0:T(8,128)(2,1)S(1)}, u32[]{:S(2)}, u32[]{:S(2)}) collective-permute-start(bf16[16,128,128]{2,1,0:T(8,128)(2,1)} %get-tuple-element.37), channel_id=1, source_target_pairs={{1,0},{3,2},{5,4},{7,6},{9,8},{11,10},{13,12},{15,14},{17,16},{19,... | collective-permute-start | bytes 1572872 | tf_op jit(solution)/shard_map/ppermute | solution.py:355
  104.1 31.8 %collective-permute-start.2 = (bf16[16,128,128]{2,1,0:T(8,128)(2,1)}, bf16[16,128,128]{2,1,0:T(8,128)(2,1)S(1)}, u32[]{:S(2)}, u32[]{:S(2)}) collective-permute-start(bf16[16,128,128]{2,1,0:T(8,128)(2,1)} %get-tuple-element.26.rest_1_), channel_id=1, source_target_pairs={{1,0},{3,2},{5,4},{7,6},{9,8},{11,10},{13,12},{15,14},{17,16},{19,... | collective-permute-start | bytes 1572872 | tf_op jit(solution)/shard_map/ppermute | solution.py:355
  105.4 1.0 copy-start.10
  106.4 1.0 copy-start.14
  107.5 1.0 copy-start.16
  108.5 1.0 copy-start.20
  109.6 1.0 copy-start.22
  110.6 26.1 %copy-start.5 = (bf16[256,2048]{1,0:T(8,128)(2,1)S(1)}, bf16[256,2048]{1,0:T(8,128)(2,1)}, u32[]{:S(2)}) copy-start(bf16[256,2048]{1,0:T(8,128)(2,1)} %v_ref.7) | copy-start | bytes 3145732
  124.6 0.8 copy-start.17
  135.9 0.8 copy-start.23
  136.7 1.6 %copy-start.12 = (f32[256,2048]{1,0:T(8,128)S(1)}, f32[256,2048]{1,0:T(8,128)}, u32[]{:S(2)}) copy-start(f32[256,2048]{1,0:T(8,128)} %get-tuple-element.34.gk_in) | copy-start | bytes 6291460
  138.3 1.0 copy-start.18
  139.3 1.0 copy-start.24

commit v3 on v2

v3 whole, which is shorter than its diff:
```python
import functools

import jax
import jax.numpy as jnp
from jax import lax
from jax.experimental import pallas as pl
from jax.experimental.pallas import tpu as pltpu
from jax.sharding import PartitionSpec as P

DH = 128
GROUP = 512
BLOCK = 128
CHUNKS = 4
VMEM_BYTES = 60 * 1024 * 1024

eps_norm = 1e-06
BF = jnp.bfloat16
F32 = jnp.float32
AXES = ("ctx", "head")

NN = (((1,), (0,)), ((), ()))
NT = (((1,), (1,)), ((), ()))
TN = (((0,), (0,)), ((), ()))


def dot(a, b, dims):
    return lax.dot_general(a, b, dims, preferred_element_type=F32)


def bounds_of(len_ref):
    bounds, total = [], None
    for k in range(len_ref.shape[0] - 1):
        total = len_ref[k] if total is None else total + len_ref[k]
        bounds.append(total)
    return bounds


def segment(position, bounds):
    result = (position >= bounds[0]).astype(jnp.int32)
    for bound in bounds[1:]:
        result = result + (position >= bound).astype(jnp.int32)
    return result


def same(a, b):
    return (a == b).astype(F32)


class Place:
    def __init__(self, len_ref, rows, mask_ref=None):
        self.rows = rows
        self.blocks = rows // BLOCK
        self.devices = GROUP // rows
        self.bounds = bounds_of(len_ref)
        spot = lax.axis_index("head")
        index = lax.axis_index("ctx") * lax.axis_size("head") + spot
        self.first = index * rows
        self.part = lax.rem(spot, self.devices)
        self.group = lax.div(spot, self.devices)
        self.group_first = self.first - self.part * rows
        self.mask_ref = mask_ref

    def seg(self, position):
        return segment(position, self.bounds)

    def start(self, block):
        return self.first + block * BLOCK

    def row_segments(self, block):
        rows = lax.broadcasted_iota(jnp.int32, (BLOCK, 1), 0)
        return self.seg(rows + self.start(block))

    def pair(self, i, j):
        slot = jnp.clip(lax.div(i * (i - 1), 2) + j, 0, self.mask_ref.shape[1] - 1)
        return self.mask_ref[self.group, slot].astype(F32)

    def weights(self):
        rows = self.rows
        t = lax.broadcasted_iota(jnp.int32, (rows, rows), 0)
        s = lax.broadcasted_iota(jnp.int32, (rows, rows), 1)
        keep = (s <= t) & (self.seg(t + self.first) == self.seg(s + self.first))
        result = jnp.where(keep, 1.0, 0.0)
        for i in range(1, self.blocks):
            for j in range(i):
                bit = self.pair(self.part * self.blocks + i, self.part * self.blocks + j)
                inside = (
                    (t >= i * BLOCK)
                    & (t < (i + 1) * BLOCK)
                    & (s >= j * BLOCK)
                    & (s < (j + 1) * BLOCK)
                )
                result = jnp.where(inside, result * bit, result)
        return result

    def to_later(self, away, block):
        there = (self.part + away) * self.blocks + block
        edge = self.seg(self.start(block) + away * self.rows - 1)
        return [
            self.pair(there, self.part * self.blocks + j) * same(self.seg(self.start(j + 1) - 1), edge)
            for j in range(self.blocks)
        ]

    def before(self, block):
        edge = self.seg(self.start(block) - 1)
        carried = same(self.seg(self.group_first - 1), edge)
        peers = [(self.part >= away).astype(F32) for away in range(1, self.devices)]
        return carried, peers, (self.row_segments(block) == edge).astype(F32)

    def after(self, block):
        own = self.part * self.blocks + block
        edge = self.seg(self.start(block + 1))
        carried = same(self.seg(self.group_first + GROUP), edge)
        peers = []
        for i in range(self.blocks):
            for away in range(1, self.devices):
                there = (self.part + away < self.devices).astype(F32)
                other = (self.part + away) * self.blocks + i
                start = self.start(i) + away * self.rows
                peers.append(self.pair(other, own) * same(self.seg(start), edge) * there)
        return carried, peers, (self.row_segments(block) == edge).astype(F32)


def mixed(state_ref, peer_refs, factors, head):
    carried, peers, _ = factors
    total = state_ref[head].astype(F32) * carried
    for ref, factor in zip(peer_refs, peers, strict=True):
        total = total + ref[head].astype(F32) * factor
    return total.astype(BF)


def columns(head):
    return pl.ds(head * DH, DH)


def rows_of(block):
    return pl.ds(block * BLOCK, BLOCK)


def state_body(place_of, ins, outs, scratch, arrive, leave, chunks):
    k_ref, v_ref = ins
    rows, width = k_ref.shape
    place = place_of(rows)
    last = place.seg(place.start(place.blocks) - 1)
    ends = [place.seg(place.start(b + 1) - 1) for b in range(place.blocks)]
    masks = [(place.row_segments(b) == ends[b]).astype(BF) for b in range(place.blocks)]
    wanted = [[same(e, last) for e in ends]]
    for b in range(place.blocks):
        for away in range(1, place.devices):
            wanted.append(place.to_later(away, b))
    for c, heads in enumerate(chunks):
        arrive(c)
        for head in heads:
            updates = []
            for b in range(place.blocks):
                k = k_ref[rows_of(b), columns(head)] * masks[b]
                updates.append(dot(k, v_ref[rows_of(b), columns(head)], TN))
            for ref, factors in zip(outs, wanted, strict=True):
                total = updates[0] * factors[0]
                for update, factor in zip(updates[1:], factors[1:], strict=True):
                    total = total + update * factor
                ref[head] = total.astype(BF)
        leave(c)


def inner_body(place_of, ins, outs, scratch, arrive, leave, chunks):
    q_ref, k_ref, v_ref = ins
    (raw_ref,), (weight_ref,) = outs, scratch
    weight_ref[...] = place_of(q_ref.shape[0]).weights()
    for c, heads in enumerate(chunks):
        arrive(c)
        for head in heads:
            at = columns(head)
            probs = (dot(q_ref[:, at], k_ref[:, at], NT) * weight_ref[...]).astype(BF)
            raw_ref[:, at] = dot(probs, v_ref[:, at], NN)
        leave(c)


def scan_body(place_of, ins, outs, scratch, arrive, leave, chunks, *, rows, backward):
    (t_ref,), (out_ref,) = ins, outs
    count, height, _ = t_ref.shape
    devices = GROUP // rows
    bounds = place_of(rows).bounds
    part = height // len(chunks)

    for c in range(len(chunks)):
        arrive(c)
        at = pl.ds(c * part, part)

        def one(turn, acc):
            group = count // devices - 1 - turn if backward else turn
            for k in range(devices):
                out_ref[group * devices + k, at] = acc.astype(BF)
            for k in range(devices):
                index = group * devices + (devices - 1 - k if backward else k)
                first = index * rows
                if backward:
                    keep = same(segment(first, bounds), segment(first + rows, bounds))
                else:
                    keep = same(segment(first - 1, bounds), segment(first + rows - 1, bounds))
                acc = acc * keep + t_ref[index, at].astype(F32)
            return acc

        lax.fori_loop(0, count // devices, one, jnp.zeros((part, DH), F32))
        leave(c)


def norm_body(place_of, ins, outs, scratch, arrive, leave, chunks, *, rows, block, peers):
    gain_ref, q_ref, raw_ref, grad_ref, kv_ref = ins[:5]
    peer_refs, earlier_refs = ins[5 : 5 + peers], ins[5 + peers :]
    scale_ref, held_ref, d_ref, w_ref, *t_refs = outs
    width = q_ref.shape[1]
    place = place_of(rows)
    factors = place.before(block)
    squares = cross = jnp.zeros((BLOCK, DH), F32)
    for c, heads in enumerate(chunks):
        arrive(c)
        for head in heads:
            at = columns(head)
            state = mixed(kv_ref, peer_refs, factors, head)
            raw = raw_ref[:, at] + dot(q_ref[:, at], state, NN) * factors[2]
            raw = raw.astype(BF)
            held_ref[:, at] = raw
            raw = raw.astype(F32)
            scaled = grad_ref[:, at].astype(F32) * gain_ref[:, at]
            squares = squares + raw * raw
            cross = cross + scaled * raw
        leave(c, [1])
    total = jnp.sum(squares, axis=1, keepdims=True)
    inverse = 1.0 / jnp.sqrt(total / width + eps_norm)
    mean = jnp.sum(cross, axis=1, keepdims=True) * inverse / width
    scale_ref[...] = jnp.broadcast_to(inverse, scale_ref.shape)
    leave(0, [0])
    own = place.seg(place.start(block))
    begin = (place.row_segments(block) == own).astype(BF)
    into = [same(place.seg(place.start(b)), place.seg(place.first)) for b in range(block + 1)]
    for c, heads in enumerate(chunks):
        for head in heads:
            at = columns(head)
            normed = held_ref[:, at].astype(F32) * inverse
            scaled = grad_ref[:, at].astype(F32) * gain_ref[:, at]
            grad = ((scaled - normed * mean) * inverse).astype(BF)
            d_ref[:, at] = grad
            update = dot(q_ref[:, at] * begin, grad, TN)
            w_ref[head] = update.astype(BF)
            for t_ref in t_refs:
                sums = update * into[block]
                for ref, factor in zip(earlier_refs, into[:block], strict=True):
                    sums = sums + ref[head].astype(F32) * factor
                t_ref[head] = sums.astype(BF)
        leave(c, range(2, len(outs)))


def grads_body(place_of, ins, outs, scratch, arrive, leave, chunks, *, peers):
    gain_ref, q_ref, k_ref, v_ref, kv_ref = ins[:5]
    rows, width = q_ref.shape
    place = place_of(rows)
    blocks = place.blocks
    rest = ins[5:]
    d_refs, raw_refs, scale_refs = rest[:blocks], rest[blocks : 2 * blocks], rest[2 * blocks : 3 * blocks]
    peer_refs = rest[3 * blocks :]
    out_ref, gq_ref, gk_ref, gv_ref = outs
    (weight_ref,) = scratch
    weight_ref[...] = place.weights()
    factors = [place.before(b) for b in range(blocks)]
    for c, heads in enumerate(chunks):
        arrive(c)
        for head in heads:
            at = columns(head)
            q, k, v = q_ref[:, at], k_ref[:, at], v_ref[:, at]
            d = jnp.concatenate([ref[:, at] for ref in d_refs], axis=0)
            probs = (dot(q, k, NT) * weight_ref[...]).astype(BF)
            grad_probs = (dot(d, v, NT) * weight_ref[...]).astype(BF)
            inner = dot(grad_probs, k, NN)
            for b in range(blocks):
                state = mixed(kv_ref, peer_refs[b * peers : (b + 1) * peers], factors[b], head)
                outer = dot(d_refs[b][:, at], state, NT) * factors[b][2]
                part = inner[b * BLOCK : (b + 1) * BLOCK] + outer
                gq_ref[rows_of(b), at] = part.astype(BF)
                normed = raw_refs[b][:, at].astype(F32) * scale_refs[b][...]
                out_ref[rows_of(b), at] = (normed * gain_ref[:, at]).astype(BF)
            gk_ref[:, at] = dot(grad_probs, q, TN)
            gv_ref[:, at] = dot(probs, d, TN)
        leave(c)


def last_body(place_of, ins, outs, scratch, arrive, leave, chunks):
    k_ref, v_ref, gk_in, gv_in, gs_ref = ins[:5]
    peer_refs, (gk_ref, gv_ref) = ins[5:], outs
    place = place_of(k_ref.shape[0])
    factors = [place.after(b) for b in range(place.blocks)]
    for c, heads in enumerate(chunks):
        arrive(c)
        for head in heads:
            at = columns(head)
            for b in range(place.blocks):
                at_rows = rows_of(b)
                state = mixed(gs_ref, peer_refs, factors[b], head)
                reach = factors[b][2]
                gk = gk_in[at_rows, at] + dot(v_ref[at_rows, at], state, NT) * reach
                gv = gv_in[at_rows, at] + dot(k_ref[at_rows, at], state, NN) * reach
                gk_ref[at_rows, at] = gk.astype(BF)
                gv_ref[at_rows, at] = gv.astype(BF)
        leave(c)


class Part:
    def __init__(self, array, axis=None, block=None):
        self.array, self.axis, self.block = array, axis, block
        self.shape = array.shape if block is None else (BLOCK, *array.shape[1:])

    def pieces(self, far, near, sems, count):
        far = far if self.block is None else far.at[rows_of(self.block)]
        if self.axis is None:
            return [(far, near, sems.at[0])]
        size = self.shape[self.axis] // count
        result = []
        for c in range(count):
            at = [slice(None)] * len(self.shape)
            at[self.axis] = pl.ds(c * size, size)
            result.append((far.at[tuple(at)], near.at[tuple(at)], sems.at[c]))
        return result


def call(body, name, scalars, ins, outs, heads, chunks, scratch=(), flops=0, after=()):
    sizes = (len(scalars), len(ins), len(after), len(outs), len(ins), len(outs), 2, len(scratch))

    def kernel(*refs):
        split, at = [], 0
        for size in sizes:
            split.append(refs[at : at + size])
            at += size
        settings, far_in, _, far_out, near_in, near_out, (in_sems, out_sems), rest = split
        coming = [
            part.pieces(far, near, in_sems.at[i], chunks)
            for i, (part, far, near) in enumerate(zip(ins, far_in, near_in, strict=True))
        ]
        going = [
            part.pieces(far, near, out_sems.at[i], chunks)
            for i, (part, far, near) in enumerate(zip(outs, far_out, near_out, strict=True))
        ]

        def copies(parts, c, which=None):
            for i, pieces in enumerate(parts):
                if c < len(pieces) and (which is None or i in which):
                    yield pieces[c]

        def arrive(c):
            for far, near, sem in copies(coming, c):
                pltpu.make_async_copy(far, near, sem).wait()

        def leave(c, which=None):
            for far, near, sem in copies(going, c, which):
                pltpu.make_async_copy(near, far, sem).start()

        for c in range(chunks):
            for far, near, sem in copies(coming, c):
                pltpu.make_async_copy(far, near, sem).start()
        each = heads // chunks
        turns = [range(c * each, (c + 1) * each) for c in range(chunks)]
        place_of = lambda rows: Place(settings[0], rows, *settings[1:])
        body(place_of, near_in, near_out, rest, arrive, leave, turns)
        for c in range(chunks):
            for far, near, sem in copies(going, c):
                pltpu.make_async_copy(near, far, sem).wait()

    everything = [p.array for p in (*ins, *outs)]
    anywhere = pl.BlockSpec(memory_space=pl.ANY)
    return pl.pallas_call(
        kernel,
        name=name,
        in_specs=[pl.BlockSpec(memory_space=pltpu.SMEM)] * len(scalars) + [anywhere] * (len(ins) + len(after)),
        out_specs=[anywhere] * len(outs),
        out_shape=[p.array for p in outs],
        scratch_shapes=[
            *[pltpu.VMEM(p.shape, p.array.dtype) for p in (*ins, *outs)],
            pltpu.SemaphoreType.DMA((len(ins), chunks)),
            pltpu.SemaphoreType.DMA((len(outs), chunks)),
            *scratch,
        ],
        compiler_params=pltpu.CompilerParams(vmem_limit_bytes=VMEM_BYTES),
        cost_estimate=pl.CostEstimate(
            flops=flops,
            bytes_accessed=sum(a.size * a.dtype.itemsize for a in everything),
            transcendentals=0,
        ),
    )(*scalars, *[p.array for p in ins], *after)


def local(queries, keys, values, grad_out, gain, lengths, block_mask):
    rows, width = queries.shape
    heads = width // DH
    blocks = rows // BLOCK
    devices = GROUP // rows
    peers = devices - 1
    head_count = lax.axis_size("head")
    total = lax.axis_size("ctx") * head_count
    chunks = CHUNKS if heads % CHUNKS == 0 else 1
    shape = jax.ShapeDtypeStruct
    state = shape((heads, DH, DH), BF)
    tokens = shape((rows, width), BF)
    partial = shape((rows, width), F32)
    block_tokens = shape((BLOCK, width), BF)
    square = [pltpu.VMEM((rows, rows), F32)]
    unit = 2 * rows * width * DH
    inner = 2 * rows * rows * width
    scalars = [lengths, block_mask]

    def wide(array, block=None):
        return Part(array, 1, block)

    def states(array):
        return Part(array, 0)

    def to_peers(array, away, backward):
        pairs = [(z, z + away) for z in range(head_count - away) if z % devices + away < devices]
        if backward:
            pairs = [(b, a) for a, b in pairs]
        return lax.ppermute(array, "head", pairs)

    def scanned(sums, backward, after):
        height = heads * DH // total
        slices = sums.reshape(total, height, DH)
        slices = lax.all_to_all(slices, AXES, split_axis=0, concat_axis=0, tiled=True)
        (slices,) = call(
            functools.partial(scan_body, rows=rows, backward=backward),
            "scan",
            [lengths],
            [Part(slices, 1)],
            [Part(shape(slices.shape, BF), 1)],
            heads,
            2 if height % 32 == 0 else 1,
            after=after,
        )
        slices = lax.all_to_all(slices, AXES, split_axis=0, concat_axis=0, tiled=True)
        return slices.reshape(heads, DH, DH)

    gain_row = Part(gain.reshape(1, width))
    sum_kv, *later = call(
        state_body,
        "states",
        scalars,
        [wide(keys), wide(values)],
        [states(state)] * (1 + blocks * peers),
        heads,
        chunks,
        flops=unit,
    )
    from_peers = [to_peers(x, 1 + at % peers, False) for at, x in enumerate(later)]
    (raw_inner,) = call(
        inner_body,
        "inner",
        scalars,
        [wide(queries), wide(keys), wide(values)],
        [wide(partial)],
        heads,
        chunks,
        square,
        flops=2 * inner,
    )
    kv_state = scanned(sum_kv, False, [raw_inner])

    scales, raws, grads, updates, back = [], [], [], [], []
    for b in range(blocks):
        ends = [states(state)] if b == blocks - 1 and blocks > 1 else []
        scale, raw, grad, update, *sums = call(
            functools.partial(norm_body, rows=rows, block=b, peers=peers),
            "norm",
            scalars,
            [
                gain_row,
                wide(queries, b),
                wide(raw_inner, b),
                wide(grad_out, b),
                states(kv_state),
                *[states(x) for x in from_peers[b * peers : (b + 1) * peers]],
                *[states(w) for w in (updates if ends else [])],
            ],
            [Part(shape((BLOCK, DH), F32)), wide(block_tokens), wide(block_tokens), states(state), *ends],
            heads,
            chunks,
            flops=2 * unit // blocks,
        )
        scales.append(scale)
        raws.append(raw)
        grads.append(grad)
        updates.append(update)
        back += [to_peers(update, away, True) for away in range(1, devices)]
    output, grad_q, part_k, part_v = call(
        functools.partial(grads_body, peers=peers),
        "grads",
        scalars,
        [
            gain_row,
            wide(queries),
            wide(keys),
            wide(values),
            states(kv_state),
            *[wide(d) for d in grads],
            *[wide(r) for r in raws],
            *[Part(s) for s in scales],
            *[states(x) for x in from_peers],
        ],
        [wide(tokens), wide(tokens), wide(partial), wide(partial)],
        heads,
        chunks,
        square,
        flops=5 * inner + unit,
    )
    grad_state = scanned(sums[0] if sums else updates[0], True, [part_v])
    grad_k, grad_v = call(
        last_body,
        "last",
        scalars,
        [
            wide(keys),
            wide(values),
            wide(part_k),
            wide(part_v),
            states(grad_state),
            *[states(w) for w in back],
        ],
        [wide(tokens), wide(tokens)],
        heads,
        chunks,
        flops=2 * unit,
    )
    return output, grad_q, grad_k, grad_v


def solution(mesh):
    tokens = P(AXES, None)
    return jax.shard_map(
        local,
        mesh=mesh,
        in_specs=(tokens, tokens, tokens, tokens, P(), P(), P("ctx", None)),
        out_specs=(tokens, tokens, tokens, tokens),
        check_vma=False,
    )
```

time: 147 us -> 142 us (0.966)
  blocking collectives: 44.4 us -> 0 us
  waiting for transfers between devices: 26.1 us -> 66.8 us
  local copies, waits for them, and re-layouts: 22.7 us -> 4.39 us
  starting transfers between devices: 14.5 us -> 27.8 us
  Pallas kernels: 36.6 us -> 40.6 us
    all_to_all x2 -> x0, blocking collectives: 44.4 us -> none  [scanned(): lax.all_to_all(slices, AXES, split_axis=0, concat_axis=0, tiled=True)]
    ppermute x4, waiting for transfers between devices: 26.1 us -> 51.4 us  [to_peers(): return lax.ppermute(array, 'head', pairs)]
    unnamed x64 -> x24, local copies, waits for them, and re-layouts: 22.7 us -> 4.39 us
    all_to_all x2 -> x4, waiting for transfers between devices: 0.01 us -> 15.4 us  [scanned(): lax.all_to_all(slices, AXES, split_axis=0, concat_axis=0, tiled=True)]
    all_to_all x2 -> x4, starting transfers between devices: 6.42 us -> 20.6 us  [scanned(): lax.all_to_all(slices, AXES, split_axis=0, concat_axis=0, tiled=True)]
    pallas_call x8, Pallas kernels: 36.6 us -> 40.6 us  [call(): pl.pallas_call(kernel, name=name, in_specs=[pl.BlockSpec(memory_space=plt...]
  transfers between devices with their start and end apart: 6 -> 8, of which waited for: 4 -> 6; matrix products, arithmetic and copies ran while one was open for 0% -> 0% of each run, Pallas kernels for 12% -> 14%
where the time goes in v3:
time: 142 us; the launch traced here: 141 us
  waiting for transfers between devices  66.8 us (47%)
  Pallas kernels  40.6 us (29%)
  starting transfers between devices  27.8 us (20%)
  local copies, waits for them, and re-layouts  4.39 us (3%)
    ppermute x4, waiting for transfers between devices, to_peers(): return lax.ppermute(array, 'head', pairs)  51.4 us
    pallas_call x8, Pallas kernels, call(): pl.pallas_call(kernel, name=name, in_specs=[pl.BlockSpec(memory_space=plt...  40.6 us
    all_to_all x4, starting transfers between devices, scanned(): lax.all_to_all(slices, AXES, split_axis=0, concat_axis=0, tiled=True)  20.6 us
    all_to_all x4, waiting for transfers between devices, scanned(): lax.all_to_all(slices, AXES, split_axis=0, concat_axis=0, tiled=True)  15.4 us
    ppermute x4, starting transfers between devices, to_peers(): return lax.ppermute(array, 'head', pairs)  7.23 us
    unnamed x24, local copies, waits for them, and re-layouts  4.39 us
  transfers between devices with their start and end apart: 8, of which 6 were waited for; matrix products, arithmetic and copies ran while one was open for 0% of the time, Pallas kernels for 14%

profile of v3, /device:TPU:1, one launch (start us, length us, event | category | flops | bytes accessed | tf_op | source)
XLA Modules:
  0.0 140.6 jit_solution(8751611515972165963)
XLA Ops:
  0.6 3.8 %states.1 = (bf16[16,128,128]{2,1,0:T(8,128)(2,1)}, bf16[16,128,128]{2,1,0:T(8,128)(2,1)}, bf16[16,128,128]{2,1,0:T(8,128)(2,1)}) custom-call(s32[4]{0:T(128)} %refs_0_.15, s32[2,6]{1,0:T(2,128)} %refs_1_.11, bf16[256,2048]{1,0:T(8,128)(2,1)} %refs_2_.5, bf16[256,2048]{1,0:T(8,128)(2,1)} %refs_3_.11), custom_call_target="tpu_custom_call" | custom-call | flops 134217728 | bytes 3670016 | tf_op jit(solution)/shard_map/states/pallas_call | solution.py:368
  4.5 7.1 %all-to-all-start = ((bf16[32,64,128]{2,1,0:T(8,128)(2,1)}), bf16[32,64,128]{2,1,0:T(8,128)(2,1)S(1)}, u32[]{:S(2)}, u32[]{:S(2)}) async-start(bf16[32,64,128]{2,1,0:T(8,128)(2,1)} %bitcast.10), calls=%async_computation | async-start | bytes 1048576 | tf_op jit(solution)/shard_map/all_to_all | solution.py:423
  11.6 5.1 %inner.1.refs_2_.refs_4_ = f32[256,2048]{1,0:T(8,128)} custom-call(s32[4]{0:T(128)} %refs_0_.15, s32[2,6]{1,0:T(2,128)} %refs_1_.11, bf16[256,2048]{1,0:T(8,128)(2,1)} %refs_3_.10, bf16[256,2048]{1,0:T(8,128)(2,1)} %refs_2_.5, bf16[256,2048]{1,0:T(8,128)(2,1)} %refs_3_.11), custom_call_target="tpu_custom_call" | custom-call | flops 536870912 | bytes 5242880 | tf_op jit(solution)/shard_map/inner/pallas_call | solution.py:368
  16.6 0.0 copy-start.11
  16.6 0.0 copy-start.10
  16.7 10.2 %all-to-all-done.refs_1_ = bf16[32,64,128]{2,1,0:T(8,128)(2,1)S(1)} async-done(((bf16[32,64,128]{2,1,0:T(8,128)(2,1)}), bf16[32,64,128]{2,1,0:T(8,128)(2,1)S(1)}, u32[]{:S(2)}, u32[]{:S(2)}) %all-to-all-start) | async-done | bytes 524320 | tf_op jit(solution)/shard_map/all_to_all | solution.py:423
  26.9 0.0 copy-start.5
  26.9 0.8 copy-done.5
  27.7 3.0 %scan.2 = bf16[32,64,128]{2,1,0:T(8,128)(2,1)} custom-call(s32[4]{0:T(128)} %refs_0_.15, bf16[32,64,128]{2,1,0:T(8,128)(2,1)} %copy-done.5, f32[256,2048]{1,0:T(8,128)} %inner.1.refs_2_.refs_4_), custom_call_target="tpu_custom_call" | custom-call | bytes 1048576 | tf_op jit(solution)/shard_map/scan/pallas_call | solution.py:368
  30.7 3.2 %all-to-all-start.1 = ((bf16[32,64,128]{2,1,0:T(8,128)(2,1)}), bf16[32,64,128]{2,1,0:T(8,128)(2,1)S(1)}, u32[]{:S(2)}, u32[]{:S(2)}) async-start(bf16[32,64,128]{2,1,0:T(8,128)(2,1)} %scan.2), calls=%async_computation.1 | async-start | bytes 1048576 | tf_op jit(solution)/shard_map/all_to_all | solution.py:434
  33.8 0.0 copy-done.11
  33.8 3.3 %collective-permute-start = (bf16[16,128,128]{2,1,0:T(8,128)(2,1)S(1)}, bf16[16,128,128]{2,1,0:T(8,128)(2,1)S(1)}, u32[]{:S(2)}, u32[]{:S(2)}) collective-permute-start(bf16[16,128,128]{2,1,0:T(8,128)(2,1)S(1)} %copy-done.11), channel_id=1, source_target_pairs={{0,1},{2,3},{4,5},{6,7},{8,9},{10,11},{12,13},{14,15},{16,17},{18,... | collective-permute-start | bytes 1572872 | tf_op jit(solution)/shard_map/ppermute | solution.py:418
  37.2 0.0 copy-done.10
  37.2 1.3 collective-permute-start.1
  38.5 15.3 %collective-permute-done.refs_7_.refs_13_ = bf16[16,128,128]{2,1,0:T(8,128)(2,1)S(1)} collective-permute-done((bf16[16,128,128]{2,1,0:T(8,128)(2,1)S(1)}, bf16[16,128,128]{2,1,0:T(8,128)(2,1)S(1)}, u32[]{:S(2)}, u32[]{:S(2)}) %collective-permute-start) | collective-permute-done | bytes 524320 | tf_op jit(solution)/shard_map/ppermute | solution.py:418
  53.8 0.0 copy-start.1
  53.8 0.0 all-to-all-done.1
  53.8 0.0 copy-start
  53.8 0.8 copy-done.1
  54.6 0.2 copy-done
  54.8 4.6 %norm.2 = (f32[128,128]{1,0:T(8,128)}, bf16[128,2048]{1,0:T(8,128)(2,1)}, bf16[128,2048]{1,0:T(8,128)(2,1)}, bf16[16,128,128]{2,1,0:T(8,128)(2,1)}) custom-call(s32[4]{0:T(128)} %refs_0_.15, s32[2,6]{1,0:T(2,128)} %refs_1_.11, f32[1,2048]{1,0:T(1,128)} %bitcast.11, bf16[256,2048]{1,0:T(8,128)(2,1)} %refs_3_.10, f32[256,2048]{1,0:T(8,128)} %inner.1.refs_2_.refs_4_, ...), custom_call_target="tpu_custom_call" | custom-call | flops 134217728 | bytes 6889472 | tf_op jit(solution)/shard_map/norm/pallas_call | solution.py:368
  59.4 5.6 %collective-permute-done.1.refs_7_.refs_14_ = bf16[16,128,128]{2,1,0:T(8,128)(2,1)S(1)} collective-permute-done((bf16[16,128,128]{2,1,0:T(8,128)(2,1)S(1)}, bf16[16,128,128]{2,1,0:T(8,128)(2,1)S(1)}, u32[]{:S(2)}, u32[]{:S(2)}) %collective-permute-start.1) | collective-permute-done | bytes 524320 | tf_op jit(solution)/shard_map/ppermute | solution.py:418
  65.0 0.0 copy-start.2
  65.0 0.8 copy-done.2
  65.8 5.1 %norm.3 = (f32[128,128]{1,0:T(8,128)}, bf16[128,2048]{1,0:T(8,128)(2,1)}, bf16[128,2048]{1,0:T(8,128)(2,1)}, bf16[16,128,128]{2,1,0:T(8,128)(2,1)}, bf16[16,128,128]{2,1,0:T(8,128)(2,1)}) custom-call(s32[4]{0:T(128)} %refs_0_.15, s32[2,6]{1,0:T(2,128)} %refs_1_.11, f32[1,2048]{1,0:T(1,128)} %bitcast.12, bf16[256,2048]{1,0:T(8,128)(2,1)} %refs_3_.10, ...), custom_call_target="tpu_custom_call" | custom-call | flops 134217728 | bytes 7938048 | tf_op jit(solution)/shard_map/norm/pallas_call | solution.py:368
  71.0 7.1 %all-to-all-start.2 = ((bf16[32,64,128]{2,1,0:T(8,128)(2,1)}), bf16[32,64,128]{2,1,0:T(8,128)(2,1)S(1)}, u32[]{:S(2)}, u32[]{:S(2)}) async-start(bf16[32,64,128]{2,1,0:T(8,128)(2,1)} %bitcast.9), calls=%async_computation.2 | async-start | bytes 1048576 | tf_op jit(solution)/shard_map/all_to_all | solution.py:423
  78.2 10.1 %grads.1 = (bf16[256,2048]{1,0:T(8,128)(2,1)}, bf16[256,2048]{1,0:T(8,128)(2,1)}, f32[256,2048]{1,0:T(8,128)}, f32[256,2048]{1,0:T(8,128)}) custom-call(s32[4]{0:T(128)} %refs_0_.15, s32[2,6]{1,0:T(2,128)} %refs_1_.11, f32[1,2048]{1,0:T(1,128)} %bitcast.13, bf16[256,2048]{1,0:T(8,128)(2,1)} %refs_3_.10, bf16[256,2048]{1,0:T(8,128)(2,1)} %refs_2_.5, ...), custom_call_target="tpu_custom_call" | custom-call | flops 1476395008 | bytes 13246464 | tf_op jit(solution)/shard_map/grads/pallas_call | solution.py:368
  88.3 5.2 %all-to-all-done.2.refs_1_ = bf16[32,64,128]{2,1,0:T(8,128)(2,1)S(1)} async-done(((bf16[32,64,128]{2,1,0:T(8,128)(2,1)}), bf16[32,64,128]{2,1,0:T(8,128)(2,1)S(1)}, u32[]{:S(2)}, u32[]{:S(2)}) %all-to-all-start.2) | async-done | bytes 524320 | tf_op jit(solution)/shard_map/all_to_all | solution.py:423
  93.4 0.0 copy-start.4
  93.4 0.8 copy-done.4
  94.2 0.0 copy-start.9
  94.2 0.0 copy-start.6
  94.2 3.1 %scan.3 = bf16[32,64,128]{2,1,0:T(8,128)(2,1)} custom-call(s32[4]{0:T(128)} %refs_0_.15, bf16[32,64,128]{2,1,0:T(8,128)(2,1)} %copy-done.4, f32[256,2048]{1,0:T(8,128)} %get-tuple-element.35.refs_2_.refs_5_), custom_call_target="tpu_custom_call" | custom-call | bytes 1048576 | tf_op jit(solution)/shard_map/scan/pallas_call | solution.py:368
  97.3 3.2 %all-to-all-start.3 = ((bf16[32,64,128]{2,1,0:T(8,128)(2,1)}), bf16[32,64,128]{2,1,0:T(8,128)(2,1)S(1)}, u32[]{:S(2)}, u32[]{:S(2)}) async-start(bf16[32,64,128]{2,1,0:T(8,128)(2,1)} %scan.3), calls=%async_computation.3 | async-start | bytes 1048576 | tf_op jit(solution)/shard_map/all_to_all | solution.py:434
  100.5 0.0 copy-done.9
  100.5 1.3 collective-permute-start.3
  101.8 0.0 copy-done.6
  101.8 1.3 collective-permute-start.2
  103.1 19.3 %collective-permute-done.3.refs_8_ = bf16[16,128,128]{2,1,0:T(8,128)(2,1)S(1)} collective-permute-done((bf16[16,128,128]{2,1,0:T(8,128)(2,1)S(1)}, bf16[16,128,128]{2,1,0:T(8,128)(2,1)S(1)}, u32[]{:S(2)}, u32[]{:S(2)}) %collective-permute-start.3) | collective-permute-done | bytes 524320 | tf_op jit(solution)/shard_map/ppermute | solution.py:418
  122.4 0.0 copy-start.7
  122.4 11.2 %collective-permute-done.2.refs_7_ = bf16[16,128,128]{2,1,0:T(8,128)(2,1)S(1)} collective-permute-done((bf16[16,128,128]{2,1,0:T(8,128)(2,1)S(1)}, bf16[16,128,128]{2,1,0:T(8,128)(2,1)S(1)}, u32[]{:S(2)}, u32[]{:S(2)}) %collective-permute-start.2) | collective-permute-done | bytes 524320 | tf_op jit(solution)/shard_map/ppermute | solution.py:418
  133.6 0.0 copy-start.8
  133.6 0.0 all-to-all-done.3
  133.6 0.0 copy-start.3
  133.6 0.0 copy-done.7
  133.6 0.8 copy-done.8
  134.4 0.2 copy-done.3
  134.6 5.8 %last.1 = (bf16[256,2048]{1,0:T(8,128)(2,1)}, bf16[256,2048]{1,0:T(8,128)(2,1)}) custom-call(s32[4]{0:T(128)} %refs_0_.15, s32[2,6]{1,0:T(2,128)} %refs_1_.11, bf16[256,2048]{1,0:T(8,128)(2,1)} %refs_2_.5, bf16[256,2048]{1,0:T(8,128)(2,1)} %refs_3_.11, f32[256,2048]{1,0:T(8,128)} %get-tuple-element.34.refs_4_, ...), custom_call_target="tpu_custom_call" | custom-call | flops 268435456 | bytes 9961472 | tf_op jit(solution)/shard_map/last/pallas_call | solution.py:368
Async XLA Ops:
  4.5 22.4 %all-to-all-start = ((bf16[32,64,128]{2,1,0:T(8,128)(2,1)}), bf16[32,64,128]{2,1,0:T(8,128)(2,1)S(1)}, u32[]{:S(2)}, u32[]{:S(2)}) async-start(bf16[32,64,128]{2,1,0:T(8,128)(2,1)} %bitcast.10), calls=%async_computation | async-start | bytes 1048576 | tf_op jit(solution)/shard_map/all_to_all | solution.py:423
  16.6 17.2 %copy-start.11 = (bf16[16,128,128]{2,1,0:T(8,128)(2,1)S(1)}, bf16[16,128,128]{2,1,0:T(8,128)(2,1)}, u32[]{:S(2)}) copy-start(bf16[16,128,128]{2,1,0:T(8,128)(2,1)} %get-tuple-element.23) | copy-start | bytes 1572868
  16.6 20.5 %copy-start.10 = (bf16[16,128,128]{2,1,0:T(8,128)(2,1)S(1)}, bf16[16,128,128]{2,1,0:T(8,128)(2,1)}, u32[]{:S(2)}) copy-start(bf16[16,128,128]{2,1,0:T(8,128)(2,1)} %get-tuple-element.25) | copy-start | bytes 1572868
  26.9 0.8 copy-start.5
  30.7 23.1 %all-to-all-start.1 = ((bf16[32,64,128]{2,1,0:T(8,128)(2,1)}), bf16[32,64,128]{2,1,0:T(8,128)(2,1)S(1)}, u32[]{:S(2)}, u32[]{:S(2)}) async-start(bf16[32,64,128]{2,1,0:T(8,128)(2,1)} %scan.2), calls=%async_computation.1 | async-start | bytes 1048576 | tf_op jit(solution)/shard_map/all_to_all | solution.py:434
  33.8 19.9 %collective-permute-start = (bf16[16,128,128]{2,1,0:T(8,128)(2,1)S(1)}, bf16[16,128,128]{2,1,0:T(8,128)(2,1)S(1)}, u32[]{:S(2)}, u32[]{:S(2)}) collective-permute-start(bf16[16,128,128]{2,1,0:T(8,128)(2,1)S(1)} %copy-done.11), channel_id=1, source_target_pairs={{0,1},{2,3},{4,5},{6,7},{8,9},{10,11},{12,13},{14,15},{16,17},{18,... | collective-permute-start | bytes 1572872 | tf_op jit(solution)/shard_map/ppermute | solution.py:418
  37.2 27.8 %collective-permute-start.1 = (bf16[16,128,128]{2,1,0:T(8,128)(2,1)S(1)}, bf16[16,128,128]{2,1,0:T(8,128)(2,1)S(1)}, u32[]{:S(2)}, u32[]{:S(2)}) collective-permute-start(bf16[16,128,128]{2,1,0:T(8,128)(2,1)S(1)} %copy-done.10), channel_id=1, source_target_pairs={{0,1},{2,3},{4,5},{6,7},{8,9},{10,11},{12,13},{14,15},{16,17},{18,... | collective-permute-start | bytes 1572872 | tf_op jit(solution)/shard_map/ppermute | solution.py:418
  53.8 0.8 copy-start.1
  53.8 1.0 copy-start
  65.0 0.8 copy-start.2
  71.0 22.4 %all-to-all-start.2 = ((bf16[32,64,128]{2,1,0:T(8,128)(2,1)}), bf16[32,64,128]{2,1,0:T(8,128)(2,1)S(1)}, u32[]{:S(2)}, u32[]{:S(2)}) async-start(bf16[32,64,128]{2,1,0:T(8,128)(2,1)} %bitcast.9), calls=%async_computation.2 | async-start | bytes 1048576 | tf_op jit(solution)/shard_map/all_to_all | solution.py:423
  93.4 0.8 copy-start.4
  94.2 6.2 %copy-start.9 = (bf16[16,128,128]{2,1,0:T(8,128)(2,1)S(1)}, bf16[16,128,128]{2,1,0:T(8,128)(2,1)}, u32[]{:S(2)}) copy-start(bf16[16,128,128]{2,1,0:T(8,128)(2,1)} %get-tuple-element.37) | copy-start | bytes 1572868
  94.2 7.5 %copy-start.6 = (bf16[16,128,128]{2,1,0:T(8,128)(2,1)S(1)}, bf16[16,128,128]{2,1,0:T(8,128)(2,1)}, u32[]{:S(2)}) copy-start(bf16[16,128,128]{2,1,0:T(8,128)(2,1)} %get-tuple-element.26.refs_8_) | copy-start | bytes 1572868
  97.3 36.3 %all-to-all-start.3 = ((bf16[32,64,128]{2,1,0:T(8,128)(2,1)}), bf16[32,64,128]{2,1,0:T(8,128)(2,1)S(1)}, u32[]{:S(2)}, u32[]{:S(2)}) async-start(bf16[32,64,128]{2,1,0:T(8,128)(2,1)} %scan.3), calls=%async_computation.3 | async-start | bytes 1048576 | tf_op jit(solution)/shard_map/all_to_all | solution.py:434
  100.5 21.9 %collective-permute-start.3 = (bf16[16,128,128]{2,1,0:T(8,128)(2,1)S(1)}, bf16[16,128,128]{2,1,0:T(8,128)(2,1)S(1)}, u32[]{:S(2)}, u32[]{:S(2)}) collective-permute-start(bf16[16,128,128]{2,1,0:T(8,128)(2,1)S(1)} %copy-done.9), channel_id=1, source_target_pairs={{1,0},{3,2},{5,4},{7,6},{9,8},{11,10},{13,12},{15,14},{17,16},{19,... | collective-permute-start | bytes 1572872 | tf_op jit(solution)/shard_map/ppermute | solution.py:418
  101.8 31.8 %collective-permute-start.2 = (bf16[16,128,128]{2,1,0:T(8,128)(2,1)S(1)}, bf16[16,128,128]{2,1,0:T(8,128)(2,1)S(1)}, u32[]{:S(2)}, u32[]{:S(2)}) collective-permute-start(bf16[16,128,128]{2,1,0:T(8,128)(2,1)S(1)} %copy-done.6), channel_id=1, source_target_pairs={{1,0},{3,2},{5,4},{7,6},{9,8},{11,10},{13,12},{15,14},{17,16},{19,... | collective-permute-start | bytes 1572872 | tf_op jit(solution)/shard_map/ppermute | solution.py:418
  122.4 11.2 %copy-start.7 = (bf16[16,128,128]{2,1,0:T(8,128)(2,1)}, bf16[16,128,128]{2,1,0:T(8,128)(2,1)S(1)}, u32[]{:S(2)}) copy-start(bf16[16,128,128]{2,1,0:T(8,128)(2,1)S(1)} %collective-permute-done.3.refs_8_) | copy-start | bytes 1572868
  133.6 0.8 copy-start.8
  133.6 1.0 copy-start.3

commit v4 on v3

--- a/solution.py
+++ b/solution.py
@@ -10,7 +10,8 @@
 DH = 128
 GROUP = 512
 BLOCK = 128
-CHUNKS = 4
+CHUNKS = 8
+LONG = 40_000_000_000
 VMEM_BYTES = 60 * 1024 * 1024
 
 eps_norm = 1e-06
@@ -200,7 +201,12 @@
                 acc = acc * keep + t_ref[index, at].astype(F32)
             return acc
 
-        lax.fori_loop(0, count // devices, one, jnp.zeros((part, DH), F32))
+        acc = jnp.zeros((part, DH), F32)
+        if count <= 32:
+            for turn in range(count // devices):
+                acc = one(turn, acc)
+        else:
+            lax.fori_loop(0, count // devices, one, acc)
         leave(c)
 
 
@@ -250,15 +256,15 @@
         leave(c, range(2, len(outs)))
 
 
-def grads_body(place_of, ins, outs, scratch, arrive, leave, chunks, *, peers):
-    gain_ref, q_ref, k_ref, v_ref, kv_ref = ins[:5]
-    rows, width = q_ref.shape
+def query_grads_body(place_of, ins, outs, scratch, arrive, leave, chunks, *, peers):
+    gain_ref, k_ref, v_ref, kv_ref = ins[:4]
+    rows, width = k_ref.shape
     place = place_of(rows)
     blocks = place.blocks
-    rest = ins[5:]
+    rest = ins[4:]
     d_refs, raw_refs, scale_refs = rest[:blocks], rest[blocks : 2 * blocks], rest[2 * blocks : 3 * blocks]
     peer_refs = rest[3 * blocks :]
-    out_ref, gq_ref, gk_ref, gv_ref = outs
+    out_ref, gq_ref = outs
     (weight_ref,) = scratch
     weight_ref[...] = place.weights()
     factors = [place.before(b) for b in range(blocks)]
@@ -266,11 +272,9 @@
         arrive(c)
         for head in heads:
             at = columns(head)
-            q, k, v = q_ref[:, at], k_ref[:, at], v_ref[:, at]
             d = jnp.concatenate([ref[:, at] for ref in d_refs], axis=0)
-            probs = (dot(q, k, NT) * weight_ref[...]).astype(BF)
-            grad_probs = (dot(d, v, NT) * weight_ref[...]).astype(BF)
-            inner = dot(grad_probs, k, NN)
+            grad_probs = (dot(d, v_ref[:, at], NT) * weight_ref[...]).astype(BF)
+            inner = dot(grad_probs, k_ref[:, at], NN)
             for b in range(blocks):
                 state = mixed(kv_ref, peer_refs[b * peers : (b + 1) * peers], factors[b], head)
                 outer = dot(d_refs[b][:, at], state, NT) * factors[b][2]
@@ -278,6 +282,22 @@
                 gq_ref[rows_of(b), at] = part.astype(BF)
                 normed = raw_refs[b][:, at].astype(F32) * scale_refs[b][...]
                 out_ref[rows_of(b), at] = (normed * gain_ref[:, at]).astype(BF)
+        leave(c)
+
+
+def key_grads_body(place_of, ins, outs, scratch, arrive, leave, chunks):
+    q_ref, k_ref, v_ref, *d_refs = ins
+    place = place_of(q_ref.shape[0])
+    gk_ref, gv_ref = outs
+    (weight_ref,) = scratch
+    weight_ref[...] = place.weights()
+    for c, heads in enumerate(chunks):
+        arrive(c)
+        for head in heads:
+            at = columns(head)
+            q, d = q_ref[:, at], jnp.concatenate([ref[:, at] for ref in d_refs], axis=0)
+            probs = (dot(q, k_ref[:, at], NT) * weight_ref[...]).astype(BF)
+            grad_probs = (dot(d, v_ref[:, at], NT) * weight_ref[...]).astype(BF)
             gk_ref[:, at] = dot(grad_probs, q, TN)
             gv_ref[:, at] = dot(probs, d, TN)
         leave(c)
@@ -417,10 +437,12 @@
             pairs = [(b, a) for a, b in pairs]
         return lax.ppermute(array, "head", pairs)
 
-    def scanned(sums, backward, after):
+    def exchanged(slices):
+        return lax.all_to_all(slices, AXES, split_axis=0, concat_axis=0, tiled=True)
+
+    def scanned(sums, backward, after=()):
         height = heads * DH // total
-        slices = sums.reshape(total, height, DH)
-        slices = lax.all_to_all(slices, AXES, split_axis=0, concat_axis=0, tiled=True)
+        slices = exchanged(sums.reshape(total, height, DH))
         (slices,) = call(
             functools.partial(scan_body, rows=rows, backward=backward),
             "scan",
@@ -431,8 +453,7 @@
             2 if height % 32 == 0 else 1,
             after=after,
         )
-        slices = lax.all_to_all(slices, AXES, split_axis=0, concat_axis=0, tiled=True)
-        return slices.reshape(heads, DH, DH)
+        return slices
 
     gain_row = Part(gain.reshape(1, width))
     sum_kv, *later = call(
@@ -446,6 +467,7 @@
         flops=unit,
     )
     from_peers = [to_peers(x, 1 + at % peers, False) for at, x in enumerate(later)]
+    slices = scanned(sum_kv, False)
     (raw_inner,) = call(
         inner_body,
         "inner",
@@ -455,9 +477,10 @@
         heads,
         chunks,
         square,
-        flops=2 * inner,
+        flops=LONG,
+        after=[slices, *from_peers[:peers]],
     )
-    kv_state = scanned(sum_kv, False, [raw_inner])
+    kv_state = exchanged(slices).reshape(heads, DH, DH)
 
     scales, raws, grads, updates, back = [], [], [], [], []
     for b in range(blocks):
@@ -478,20 +501,19 @@
             [Part(shape((BLOCK, DH), F32)), wide(block_tokens), wide(block_tokens), states(state), *ends],
             heads,
             chunks,
-            flops=2 * unit // blocks,
+            flops=LONG if b > 0 else 2 * unit // blocks,
         )
         scales.append(scale)
         raws.append(raw)
         grads.append(grad)
         updates.append(update)
         back += [to_peers(update, away, True) for away in range(1, devices)]
-    output, grad_q, part_k, part_v = call(
-        functools.partial(grads_body, peers=peers),
-        "grads",
+    output, grad_q = call(
+        functools.partial(query_grads_body, peers=peers),
+        "query_grads",
         scalars,
         [
             gain_row,
-            wide(queries),
             wide(keys),
             wide(values),
             states(kv_state),
@@ -500,13 +522,27 @@
             *[Part(s) for s in scales],
             *[states(x) for x in from_peers],
         ],
-        [wide(tokens), wide(tokens), wide(partial), wide(partial)],
+        [wide(tokens), wide(tokens)],
         heads,
         chunks,
         square,
-        flops=5 * inner + unit,
+        flops=LONG,
+        after=back[:peers],
     )
-    grad_state = scanned(sums[0] if sums else updates[0], True, [part_v])
+    slices = scanned(sums[0] if sums else updates[0], True, [grad_q])
+    part_k, part_v = call(
+        key_grads_body,
+        "key_grads",
+        scalars,
+        [wide(queries), wide(keys), wide(values), *[wide(d) for d in grads]],
+        [wide(partial), wide(partial)],
+        heads,
+        chunks,
+        square,
+        flops=LONG,
+        after=[slices, *back[peers:]],
+    )
+    grad_state = exchanged(slices).reshape(heads, DH, DH)
     grad_k, grad_v = call(
         last_body,
         "last",

time: 142 us -> 119 us (0.84)
  waiting for transfers between devices: 66.8 us -> 30.8 us
  Pallas kernels: 40.6 us -> 51.3 us
  local copies, waits for them, and re-layouts: 4.39 us -> 6.35 us
    ppermute x4, waiting for transfers between devices: 51.4 us -> 0.1 us  [to_peers(): return lax.ppermute(array, 'head', pairs)]
    all_to_all x4, waiting for transfers between devices: 15.4 us -> 30.7 us  [exchanged(): return lax.all_to_all(slices, AXES, split_axis=0, concat_axis=0, tiled=True)]
    pallas_call x8 -> x9, Pallas kernels: 40.6 us -> 51.3 us  [call(): pl.pallas_call(kernel, name=name, in_specs=[pl.BlockSpec(memory_space=plt...]
    unnamed x24 -> x16, local copies, waits for them, and re-layouts: 4.39 us -> 6.35 us
  transfers between devices with their start and end apart: 8 -> 8, of which waited for: 6 -> 5; matrix products, arithmetic and copies ran while one was open for 0% -> 0% of each run, Pallas kernels for 14% -> 34%
where the time goes in v4:
time: 119 us; the launch traced here: 118 us
  Pallas kernels  51.3 us (43%)
  waiting for transfers between devices  30.8 us (26%)
  starting transfers between devices  28.8 us (24%)
  local copies, waits for them, and re-layouts  6.35 us (5%)
    pallas_call x9, Pallas kernels, call(): pl.pallas_call(kernel, name=name, in_specs=[pl.BlockSpec(memory_space=plt...  51.3 us
    all_to_all x4, waiting for transfers between devices, exchanged(): return lax.all_to_all(slices, AXES, split_axis=0, concat_axis=0, tiled=True)  30.7 us
    all_to_all x4, starting transfers between devices, exchanged(): return lax.all_to_all(slices, AXES, split_axis=0, concat_axis=0, tiled=True)  21.4 us
    ppermute x4, starting transfers between devices, to_peers(): return lax.ppermute(array, 'head', pairs)  7.41 us
    unnamed x16, local copies, waits for them, and re-layouts  6.35 us
  transfers between devices with their start and end apart: 8, of which 5 were waited for; matrix products, arithmetic and copies ran while one was open for 0% of the time, Pallas kernels for 34%

profile of v4, /device:TPU:1, one launch (start us, length us, event | category | flops | bytes accessed | tf_op | source)
XLA Modules:
  0.0 118.1 jit_solution(2211682839664863440)
XLA Ops:
  0.6 4.6 %states.1 = (bf16[16,128,128]{2,1,0:T(8,128)(2,1)}, bf16[16,128,128]{2,1,0:T(8,128)(2,1)}, bf16[16,128,128]{2,1,0:T(8,128)(2,1)}) custom-call(s32[4]{0:T(128)} %refs_0_.17, s32[2,6]{1,0:T(2,128)} %refs_1_.13, bf16[256,2048]{1,0:T(8,128)(2,1)} %refs_2_.7, bf16[256,2048]{1,0:T(8,128)(2,1)} %refs_3_.13), custom_call_target="tpu_custom_call" | custom-call | flops 134217728 | bytes 3670016 | tf_op jit(solution)/shard_map/states/pallas_call | solution.py:388
  5.2 7.1 %all-to-all-start = ((bf16[32,64,128]{2,1,0:T(8,128)(2,1)}), bf16[32,64,128]{2,1,0:T(8,128)(2,1)S(1)}, u32[]{:S(2)}, u32[]{:S(2)}) async-start(bf16[32,64,128]{2,1,0:T(8,128)(2,1)} %bitcast.10), calls=%async_computation | async-start | bytes 1048576 | tf_op jit(solution)/shard_map/all_to_all | solution.py:441
  12.3 3.3 %collective-permute-start = (bf16[16,128,128]{2,1,0:T(8,128)(2,1)}, bf16[16,128,128]{2,1,0:T(8,128)(2,1)S(1)}, u32[]{:S(2)}, u32[]{:S(2)}) collective-permute-start(bf16[16,128,128]{2,1,0:T(8,128)(2,1)} %get-tuple-element.23), channel_id=1, source_target_pairs={{0,1},{2,3},{4,5},{6,7},{8,9},{10,11},{12,13},{14,15},{16,17},{18,... | collective-permute-start | bytes 1572872 | tf_op jit(solution)/shard_map/ppermute | solution.py:438
  15.7 1.3 %collective-permute-start.1 = (bf16[16,128,128]{2,1,0:T(8,128)(2,1)}, bf16[16,128,128]{2,1,0:T(8,128)(2,1)S(1)}, u32[]{:S(2)}, u32[]{:S(2)}) collective-permute-start(bf16[16,128,128]{2,1,0:T(8,128)(2,1)} %get-tuple-element.25), channel_id=1, source_target_pairs={{0,1},{2,3},{4,5},{6,7},{8,9},{10,11},{12,13},{14,15},{16,17},{18,... | collective-permute-start | bytes 1572872 | tf_op jit(solution)/shard_map/ppermute | solution.py:438
  17.0 10.6 %all-to-all-done.refs_1_ = bf16[32,64,128]{2,1,0:T(8,128)(2,1)S(1)} async-done(((bf16[32,64,128]{2,1,0:T(8,128)(2,1)}), bf16[32,64,128]{2,1,0:T(8,128)(2,1)S(1)}, u32[]{:S(2)}, u32[]{:S(2)}) %all-to-all-start) | async-done | bytes 524320 | tf_op jit(solution)/shard_map/all_to_all | solution.py:441
  27.6 0.0 copy-start.3
  27.6 0.8 copy-done.3
  28.4 2.6 %scan.2.refs_5_ = bf16[32,64,128]{2,1,0:T(8,128)(2,1)} custom-call(s32[4]{0:T(128)} %refs_0_.17, bf16[32,64,128]{2,1,0:T(8,128)(2,1)} %copy-done.3), custom_call_target="tpu_custom_call" | custom-call | bytes 1048576 | tf_op jit(solution)/shard_map/scan/pallas_call | solution.py:388
  31.0 3.2 %all-to-all-start.1 = ((bf16[32,64,128]{2,1,0:T(8,128)(2,1)}), bf16[32,64,128]{2,1,0:T(8,128)(2,1)S(1)}, u32[]{:S(2)}, u32[]{:S(2)}) async-start(bf16[32,64,128]{2,1,0:T(8,128)(2,1)} %scan.2.refs_5_), calls=%async_computation.1 | async-start | bytes 1048576 | tf_op jit(solution)/shard_map/all_to_all | solution.py:441
  34.2 0.0 collective-permute-done.refs_6_.refs_7_.refs_12_
  34.2 0.0 copy-start.5
  34.2 0.8 copy-done.5
  35.0 6.2 %inner.1.refs_4_ = f32[256,2048]{1,0:T(8,128)} custom-call(s32[4]{0:T(128)} %refs_0_.17, s32[2,6]{1,0:T(2,128)} %refs_1_.13, bf16[256,2048]{1,0:T(8,128)(2,1)} %refs_2_.6, bf16[256,2048]{1,0:T(8,128)(2,1)} %refs_2_.7, bf16[256,2048]{1,0:T(8,128)(2,1)} %refs_3_.13, bf16[32,64,128]{2,1,0:T(8,128)(2,1)} %scan.2.refs_5_, bf16[16,128,128]{2,1,0:T(8,128)(2,1)} %copy-done.5), custom_call_target="tpu_custom_call" | custom-call | flops 40000000000 | bytes 5242880 | tf_op jit(solution)/shard_map/inner/pallas_call | solution.py:388
  41.2 10.8 %all-to-all-done.1 = bf16[32,64,128]{2,1,0:T(8,128)(2,1)S(1)} async-done(((bf16[32,64,128]{2,1,0:T(8,128)(2,1)}), bf16[32,64,128]{2,1,0:T(8,128)(2,1)S(1)}, u32[]{:S(2)}, u32[]{:S(2)}) %all-to-all-start.1) | async-done | bytes 524320 | tf_op jit(solution)/shard_map/all_to_all | solution.py:441
  52.0 0.0 copy-start
  52.0 0.8 copy-done
  52.7 5.4 %norm.2 = (f32[128,128]{1,0:T(8,128)}, bf16[128,2048]{1,0:T(8,128)(2,1)}, bf16[128,2048]{1,0:T(8,128)(2,1)}, bf16[16,128,128]{2,1,0:T(8,128)(2,1)}) custom-call(s32[4]{0:T(128)} %refs_0_.17, s32[2,6]{1,0:T(2,128)} %refs_1_.13, f32[1,2048]{1,0:T(1,128)} %bitcast.11, bf16[256,2048]{1,0:T(8,128)(2,1)} %refs_2_.6, f32[256,2048]{1,0:T(8,128)} %inner.1.refs_4_, ...), custom_call_target="tpu_custom_call" | custom-call | flops 134217728 | bytes 6889472 | tf_op jit(solution)/shard_map/norm/pallas_call | solution.py:388
  58.2 1.3 %collective-permute-start.2 = (bf16[16,128,128]{2,1,0:T(8,128)(2,1)}, bf16[16,128,128]{2,1,0:T(8,128)(2,1)S(1)}, u32[]{:S(2)}, u32[]{:S(2)}) collective-permute-start(bf16[16,128,128]{2,1,0:T(8,128)(2,1)} %get-tuple-element.26.refs_8_), channel_id=1, source_target_pairs={{1,0},{3,2},{5,4},{7,6},{9,8},{11,10},{13,12},{15,14},{17,16},{19,... | collective-permute-start | bytes 1572872 | tf_op jit(solution)/shard_map/ppermute | solution.py:438
  59.5 0.0 collective-permute-done.1.refs_7_.refs_13_
  59.5 0.0 copy-start.7
  59.5 0.8 copy-done.7
  60.3 5.8 %norm.3 = (f32[128,128]{1,0:T(8,128)}, bf16[128,2048]{1,0:T(8,128)(2,1)}, bf16[128,2048]{1,0:T(8,128)(2,1)}, bf16[16,128,128]{2,1,0:T(8,128)(2,1)}, bf16[16,128,128]{2,1,0:T(8,128)(2,1)}) custom-call(s32[4]{0:T(128)} %refs_0_.17, s32[2,6]{1,0:T(2,128)} %refs_1_.13, f32[1,2048]{1,0:T(1,128)} %bitcast.12, bf16[256,2048]{1,0:T(8,128)(2,1)} %refs_2_.6, ...), custom_call_target="tpu_custom_call" | custom-call | flops 40000000000 | bytes 7938048 | tf_op jit(solution)/shard_map/norm/pallas_call | solution.py:388
  66.1 8.0 %all-to-all-start.2 = ((bf16[32,64,128]{2,1,0:T(8,128)(2,1)}), bf16[32,64,128]{2,1,0:T(8,128)(2,1)S(1)}, u32[]{:S(2)}, u32[]{:S(2)}) async-start(bf16[32,64,128]{2,1,0:T(8,128)(2,1)} %bitcast.9), calls=%async_computation.2 | async-start | bytes 1048576 | tf_op jit(solution)/shard_map/all_to_all | solution.py:441
  74.0 1.5 %collective-permute-start.3 = (bf16[16,128,128]{2,1,0:T(8,128)(2,1)}, bf16[16,128,128]{2,1,0:T(8,128)(2,1)S(1)}, u32[]{:S(2)}, u32[]{:S(2)}) collective-permute-start(bf16[16,128,128]{2,1,0:T(8,128)(2,1)} %get-tuple-element.35), channel_id=1, source_target_pairs={{1,0},{3,2},{5,4},{7,6},{9,8},{11,10},{13,12},{15,14},{17,16},{19,... | collective-permute-start | bytes 1572872 | tf_op jit(solution)/shard_map/ppermute | solution.py:438
  75.5 0.0 collective-permute-done.2.refs_14_.refs_7_
  75.5 0.0 copy-start.4
  75.5 0.8 copy-done.4
  76.3 8.4 %query_grads.1 = (bf16[256,2048]{1,0:T(8,128)(2,1)}, bf16[256,2048]{1,0:T(8,128)(2,1)}) custom-call(s32[4]{0:T(128)} %refs_0_.17, s32[2,6]{1,0:T(2,128)} %refs_1_.13, f32[1,2048]{1,0:T(1,128)} %bitcast.13, bf16[256,2048]{1,0:T(8,128)(2,1)} %refs_2_.7, bf16[256,2048]{1,0:T(8,128)(2,1)} %refs_3_.13, bf16[16,128,128]{2,1,0:T(8,128)(2,1)} %bitcast.7, ...), custom_call_target="tpu_custom_call" | custom-call | flops 40000000000 | bytes 8003584 | tf_op jit(solution)/shard_map/query_grads/pallas_call | solution.py:388
  84.8 4.6 %all-to-all-done.2.refs_1_ = bf16[32,64,128]{2,1,0:T(8,128)(2,1)S(1)} async-done(((bf16[32,64,128]{2,1,0:T(8,128)(2,1)}), bf16[32,64,128]{2,1,0:T(8,128)(2,1)S(1)}, u32[]{:S(2)}, u32[]{:S(2)}) %all-to-all-start.2) | async-done | bytes 524320 | tf_op jit(solution)/shard_map/all_to_all | solution.py:441
  89.3 0.0 copy-start.1
  89.3 0.8 copy-done.1
  90.1 2.6 %scan.3.refs_7_ = bf16[32,64,128]{2,1,0:T(8,128)(2,1)} custom-call(s32[4]{0:T(128)} %refs_0_.17, bf16[32,64,128]{2,1,0:T(8,128)(2,1)} %copy-done.1, bf16[256,2048]{1,0:T(8,128)(2,1)} %get-tuple-element.19.refs_2_), custom_call_target="tpu_custom_call" | custom-call | bytes 1048576 | tf_op jit(solution)/shard_map/scan/pallas_call | solution.py:388
  92.7 3.1 %all-to-all-start.3 = ((bf16[32,64,128]{2,1,0:T(8,128)(2,1)}), bf16[32,64,128]{2,1,0:T(8,128)(2,1)S(1)}, u32[]{:S(2)}, u32[]{:S(2)}) async-start(bf16[32,64,128]{2,1,0:T(8,128)(2,1)} %scan.3.refs_7_), calls=%async_computation.3 | async-start | bytes 1048576 | tf_op jit(solution)/shard_map/all_to_all | solution.py:441
  95.9 0.1 collective-permute-done.3.refs_8_
  95.9 0.0 copy-start.6
  95.9 0.8 copy-done.6
  96.8 9.7 %key_grads.1 = (f32[256,2048]{1,0:T(8,128)}, f32[256,2048]{1,0:T(8,128)}) custom-call(s32[4]{0:T(128)} %refs_0_.17, s32[2,6]{1,0:T(2,128)} %refs_1_.13, bf16[256,2048]{1,0:T(8,128)(2,1)} %refs_2_.6, bf16[256,2048]{1,0:T(8,128)(2,1)} %refs_2_.7, bf16[256,2048]{1,0:T(8,128)(2,1)} %refs_3_.13, bf16[128,2048]{1,0:T(8,128)(2,1)} %get-tuple-element.24.refs_6_.refs_5_, ...), custom_call_target="tpu_custom_call" | custom-call | flops 40000000000 | bytes 8388608 | tf_op jit(solution)/shard_map/key_grads/pallas_call | solution.py:388
  106.5 4.7 %all-to-all-done.3 = bf16[32,64,128]{2,1,0:T(8,128)(2,1)S(1)} async-done(((bf16[32,64,128]{2,1,0:T(8,128)(2,1)}), bf16[32,64,128]{2,1,0:T(8,128)(2,1)S(1)}, u32[]{:S(2)}, u32[]{:S(2)}) %all-to-all-start.3) | async-done | bytes 524320 | tf_op jit(solution)/shard_map/all_to_all | solution.py:441
  111.2 0.0 copy-start.2
  111.2 0.8 copy-done.2
  112.0 6.0 %last.1 = (bf16[256,2048]{1,0:T(8,128)(2,1)}, bf16[256,2048]{1,0:T(8,128)(2,1)}) custom-call(s32[4]{0:T(128)} %refs_0_.17, s32[2,6]{1,0:T(2,128)} %refs_1_.13, bf16[256,2048]{1,0:T(8,128)(2,1)} %refs_2_.7, bf16[256,2048]{1,0:T(8,128)(2,1)} %refs_3_.13, f32[256,2048]{1,0:T(8,128)} %get-tuple-element.36.refs_4_, f32[256,2048]{1,0:T(8,128)} %get-tuple-element.37.refs_5_, ...), custom_call_target="tpu_custom_call" | custom-call | flops 268435456 | bytes 9961472 | tf_op jit(solution)/shard_map/last/pallas_call | solution.py:388
Async XLA Ops:
  5.2 22.4 %all-to-all-start = ((bf16[32,64,128]{2,1,0:T(8,128)(2,1)}), bf16[32,64,128]{2,1,0:T(8,128)(2,1)S(1)}, u32[]{:S(2)}, u32[]{:S(2)}) async-start(bf16[32,64,128]{2,1,0:T(8,128)(2,1)} %bitcast.10), calls=%async_computation | async-start | bytes 1048576 | tf_op jit(solution)/shard_map/all_to_all | solution.py:441
  12.3 21.8 %collective-permute-start = (bf16[16,128,128]{2,1,0:T(8,128)(2,1)}, bf16[16,128,128]{2,1,0:T(8,128)(2,1)S(1)}, u32[]{:S(2)}, u32[]{:S(2)}) collective-permute-start(bf16[16,128,128]{2,1,0:T(8,128)(2,1)} %get-tuple-element.23), channel_id=1, source_target_pairs={{0,1},{2,3},{4,5},{6,7},{8,9},{10,11},{12,13},{14,15},{16,17},{18,... | collective-permute-start | bytes 1572872 | tf_op jit(solution)/shard_map/ppermute | solution.py:438
  15.7 43.8 %collective-permute-start.1 = (bf16[16,128,128]{2,1,0:T(8,128)(2,1)}, bf16[16,128,128]{2,1,0:T(8,128)(2,1)S(1)}, u32[]{:S(2)}, u32[]{:S(2)}) collective-permute-start(bf16[16,128,128]{2,1,0:T(8,128)(2,1)} %get-tuple-element.25), channel_id=1, source_target_pairs={{0,1},{2,3},{4,5},{6,7},{8,9},{10,11},{12,13},{14,15},{16,17},{18,... | collective-permute-start | bytes 1572872 | tf_op jit(solution)/shard_map/ppermute | solution.py:438
  27.6 0.8 copy-start.3
  31.0 21.0 %all-to-all-start.1 = ((bf16[32,64,128]{2,1,0:T(8,128)(2,1)}), bf16[32,64,128]{2,1,0:T(8,128)(2,1)S(1)}, u32[]{:S(2)}, u32[]{:S(2)}) async-start(bf16[32,64,128]{2,1,0:T(8,128)(2,1)} %scan.2.refs_5_), calls=%async_computation.1 | async-start | bytes 1048576 | tf_op jit(solution)/shard_map/all_to_all | solution.py:441
  34.2 0.8 copy-start.5
  52.0 0.8 copy-start
  58.2 17.4 %collective-permute-start.2 = (bf16[16,128,128]{2,1,0:T(8,128)(2,1)}, bf16[16,128,128]{2,1,0:T(8,128)(2,1)S(1)}, u32[]{:S(2)}, u32[]{:S(2)}) collective-permute-start(bf16[16,128,128]{2,1,0:T(8,128)(2,1)} %get-tuple-element.26.refs_8_), channel_id=1, source_target_pairs={{1,0},{3,2},{5,4},{7,6},{9,8},{11,10},{13,12},{15,14},{17,16},{19,... | collective-permute-start | bytes 1572872 | tf_op jit(solution)/shard_map/ppermute | solution.py:438
  59.5 0.8 copy-start.7
  66.1 23.3 %all-to-all-start.2 = ((bf16[32,64,128]{2,1,0:T(8,128)(2,1)}), bf16[32,64,128]{2,1,0:T(8,128)(2,1)S(1)}, u32[]{:S(2)}, u32[]{:S(2)}) async-start(bf16[32,64,128]{2,1,0:T(8,128)(2,1)} %bitcast.9), calls=%async_computation.2 | async-start | bytes 1048576 | tf_op jit(solution)/shard_map/all_to_all | solution.py:441
  74.0 21.9 %collective-permute-start.3 = (bf16[16,128,128]{2,1,0:T(8,128)(2,1)}, bf16[16,128,128]{2,1,0:T(8,128)(2,1)S(1)}, u32[]{:S(2)}, u32[]{:S(2)}) collective-permute-start(bf16[16,128,128]{2,1,0:T(8,128)(2,1)} %get-tuple-element.35), channel_id=1, source_target_pairs={{1,0},{3,2},{5,4},{7,6},{9,8},{11,10},{13,12},{15,14},{17,16},{19,... | collective-permute-start | bytes 1572872 | tf_op jit(solution)/shard_map/ppermute | solution.py:438
  75.5 0.8 copy-start.4
  89.3 0.8 copy-start.1
  92.7 18.4 %all-to-all-start.3 = ((bf16[32,64,128]{2,1,0:T(8,128)(2,1)}), bf16[32,64,128]{2,1,0:T(8,128)(2,1)S(1)}, u32[]{:S(2)}, u32[]{:S(2)}) async-start(bf16[32,64,128]{2,1,0:T(8,128)(2,1)} %scan.3.refs_7_), calls=%async_computation.3 | async-start | bytes 1048576 | tf_op jit(solution)/shard_map/all_to_all | solution.py:441
  95.9 0.8 copy-start.6
  111.2 0.8 copy-start.2

commit v5 on v4

--- a/solution.py
+++ b/solution.py
@@ -10,9 +10,10 @@
 DH = 128
 GROUP = 512
 BLOCK = 128
-CHUNKS = 8
+CHUNKS = 4
 LONG = 40_000_000_000
 VMEM_BYTES = 60 * 1024 * 1024
+SOME_BYTES = 24 * 1024 * 1024
 
 eps_norm = 1e-06
 BF = jnp.bfloat16
@@ -177,12 +178,12 @@
 
 
 def scan_body(place_of, ins, outs, scratch, arrive, leave, chunks, *, rows, backward):
-    (t_ref,), (out_ref,) = ins, outs
+    (t_ref,), (out_ref, token_ref) = ins, outs
+    token_ref[...] = jnp.zeros_like(token_ref)
     count, height, _ = t_ref.shape
     devices = GROUP // rows
     bounds = place_of(rows).bounds
     part = height // len(chunks)
-
     for c in range(len(chunks)):
         arrive(c)
         at = pl.ds(c * part, part)
@@ -264,8 +265,9 @@
     rest = ins[4:]
     d_refs, raw_refs, scale_refs = rest[:blocks], rest[blocks : 2 * blocks], rest[2 * blocks : 3 * blocks]
     peer_refs = rest[3 * blocks :]
-    out_ref, gq_ref = outs
+    out_ref, gq_ref, token_ref = outs
     (weight_ref,) = scratch
+    token_ref[...] = jnp.zeros_like(token_ref)
     weight_ref[...] = place.weights()
     factors = [place.before(b) for b in range(blocks)]
     for c, heads in enumerate(chunks):
@@ -288,7 +290,7 @@
 def key_grads_body(place_of, ins, outs, scratch, arrive, leave, chunks):
     q_ref, k_ref, v_ref, *d_refs = ins
     place = place_of(q_ref.shape[0])
-    gk_ref, gv_ref = outs
+    gk_ref, gv_ref, k_out, v_out = outs
     (weight_ref,) = scratch
     weight_ref[...] = place.weights()
     for c, heads in enumerate(chunks):
@@ -300,6 +302,8 @@
             grad_probs = (dot(d, v_ref[:, at], NT) * weight_ref[...]).astype(BF)
             gk_ref[:, at] = dot(grad_probs, q, TN)
             gv_ref[:, at] = dot(probs, d, TN)
+            k_out[:, at] = k_ref[:, at]
+            v_out[:, at] = v_ref[:, at]
         leave(c)
 
 
@@ -324,9 +328,10 @@
 
 
 class Part:
-    def __init__(self, array, axis=None, block=None):
-        self.array, self.axis, self.block = array, axis, block
+    def __init__(self, array, axis=None, block=None, near=False):
+        self.array, self.axis, self.block, self.near = array, axis, block, near
         self.shape = array.shape if block is None else (BLOCK, *array.shape[1:])
+        self.spec = pl.BlockSpec(memory_space=pltpu.VMEM if near else pltpu.HBM)
 
     def pieces(self, far, near, sems, count):
         far = far if self.block is None else far.at[rows_of(self.block)]
@@ -341,23 +346,27 @@
         return result
 
 
-def call(body, name, scalars, ins, outs, heads, chunks, scratch=(), flops=0, after=()):
-    sizes = (len(scalars), len(ins), len(after), len(outs), len(ins), len(outs), 2, len(scratch))
+def call(body, name, scalars, ins, outs, heads, chunks, scratch=(), flops=0, after=(), limit=VMEM_BYTES):
+    far = [p for p in (*ins, *outs) if not p.near]
+    sizes = (len(scalars), len(ins), len(after), len(outs), len(far), 2, len(scratch))
 
     def kernel(*refs):
         split, at = [], 0
         for size in sizes:
             split.append(refs[at : at + size])
             at += size
-        settings, far_in, _, far_out, near_in, near_out, (in_sems, out_sems), rest = split
-        coming = [
-            part.pieces(far, near, in_sems.at[i], chunks)
-            for i, (part, far, near) in enumerate(zip(ins, far_in, near_in, strict=True))
-        ]
-        going = [
-            part.pieces(far, near, out_sems.at[i], chunks)
-            for i, (part, far, near) in enumerate(zip(outs, far_out, near_out, strict=True))
-        ]
+        settings, in_refs, _, out_refs, buffers, (in_sems, out_sems), rest = split
+        buffers = iter(buffers)
+
+        def opened(parts, given, sems):
+            refs, pieces = [], []
+            for i, (part, ref) in enumerate(zip(parts, given, strict=True)):
+                refs.append(ref if part.near else next(buffers))
+                pieces.append([] if part.near else part.pieces(ref, refs[-1], sems.at[i], chunks))
+            return refs, pieces
+
+        near_in, coming = opened(ins, in_refs, in_sems)
+        near_out, going = opened(outs, out_refs, out_sems)
 
         def copies(parts, c, which=None):
             for i, pieces in enumerate(parts):
@@ -383,24 +392,27 @@
             for far, near, sem in copies(going, c):
                 pltpu.make_async_copy(near, far, sem).wait()
 
-    everything = [p.array for p in (*ins, *outs)]
     anywhere = pl.BlockSpec(memory_space=pl.ANY)
     return pl.pallas_call(
         kernel,
         name=name,
-        in_specs=[pl.BlockSpec(memory_space=pltpu.SMEM)] * len(scalars) + [anywhere] * (len(ins) + len(after)),
-        out_specs=[anywhere] * len(outs),
+        in_specs=[
+            *[pl.BlockSpec(memory_space=pltpu.SMEM)] * len(scalars),
+            *[p.spec for p in ins],
+            *[anywhere] * len(after),
+        ],
+        out_specs=[p.spec for p in outs],
         out_shape=[p.array for p in outs],
         scratch_shapes=[
-            *[pltpu.VMEM(p.shape, p.array.dtype) for p in (*ins, *outs)],
+            *[pltpu.VMEM(p.shape, p.array.dtype) for p in far],
             pltpu.SemaphoreType.DMA((len(ins), chunks)),
             pltpu.SemaphoreType.DMA((len(outs), chunks)),
             *scratch,
         ],
-        compiler_params=pltpu.CompilerParams(vmem_limit_bytes=VMEM_BYTES),
+        compiler_params=pltpu.CompilerParams(vmem_limit_bytes=limit),
         cost_estimate=pl.CostEstimate(
             flops=flops,
-            bytes_accessed=sum(a.size * a.dtype.itemsize for a in everything),
+            bytes_accessed=sum(p.array.size * p.array.dtype.itemsize for p in (*ins, *outs)),
             transcendentals=0,
         ),
     )(*scalars, *[p.array for p in ins], *after)
@@ -424,6 +436,7 @@
     unit = 2 * rows * width * DH
     inner = 2 * rows * rows * width
     scalars = [lengths, block_mask]
+    token_part = Part(shape((8, DH), F32), near=True)
 
     def wide(array, block=None):
         return Part(array, 1, block)
@@ -443,17 +456,18 @@
     def scanned(sums, backward, after=()):
         height = heads * DH // total
         slices = exchanged(sums.reshape(total, height, DH))
-        (slices,) = call(
+        slices, token = call(
             functools.partial(scan_body, rows=rows, backward=backward),
             "scan",
             [lengths],
-            [Part(slices, 1)],
-            [Part(shape(slices.shape, BF), 1)],
+            [Part(slices, near=True)],
+            [Part(shape(slices.shape, BF), 1), token_part],
             heads,
             2 if height % 32 == 0 else 1,
             after=after,
+            limit=SOME_BYTES,
         )
-        return slices
+        return slices, token
 
     gain_row = Part(gain.reshape(1, width))
     sum_kv, *later = call(
@@ -467,7 +481,7 @@
         flops=unit,
     )
     from_peers = [to_peers(x, 1 + at % peers, False) for at, x in enumerate(later)]
-    slices = scanned(sum_kv, False)
+    slices, token = scanned(sum_kv, False)
     (raw_inner,) = call(
         inner_body,
         "inner",
@@ -478,7 +492,7 @@
         chunks,
         square,
         flops=LONG,
-        after=[slices, *from_peers[:peers]],
+        after=[token, *from_peers[:peers]],
     )
     kv_state = exchanged(slices).reshape(heads, DH, DH)
 
@@ -508,7 +522,7 @@
         grads.append(grad)
         updates.append(update)
         back += [to_peers(update, away, True) for away in range(1, devices)]
-    output, grad_q = call(
+    output, grad_q, token = call(
         functools.partial(query_grads_body, peers=peers),
         "query_grads",
         scalars,
@@ -522,25 +536,26 @@
             *[Part(s) for s in scales],
             *[states(x) for x in from_peers],
         ],
-        [wide(tokens), wide(tokens)],
+        [wide(tokens), wide(tokens), token_part],
         heads,
         chunks,
         square,
         flops=LONG,
         after=back[:peers],
     )
-    slices = scanned(sums[0] if sums else updates[0], True, [grad_q])
-    part_k, part_v = call(
+    slices, token = scanned(sums[0] if sums else updates[0], True, [token])
+    part_k, part_v, near_k, near_v = call(
         key_grads_body,
         "key_grads",
         scalars,
         [wide(queries), wide(keys), wide(values), *[wide(d) for d in grads]],
-        [wide(partial), wide(partial)],
+        [Part(a, near=True) for a in (partial, partial, tokens, tokens)],
         heads,
         chunks,
         square,
         flops=LONG,
-        after=[slices, *back[peers:]],
+        after=[token, *back[peers:]],
+        limit=SOME_BYTES,
     )
     grad_state = exchanged(slices).reshape(heads, DH, DH)
     grad_k, grad_v = call(
@@ -548,17 +563,15 @@
         "last",
         scalars,
         [
-            wide(keys),
-            wide(values),
-            wide(part_k),
-            wide(part_v),
-            states(grad_state),
-            *[states(w) for w in back],
+            *[Part(a, near=True) for a in (near_k, near_v, part_k, part_v)],
+            Part(grad_state, near=True),
+            *[Part(w, near=True) for w in back],
         ],
         [wide(tokens), wide(tokens)],
         heads,
         chunks,
         flops=2 * unit,
+        limit=SOME_BYTES,
     )
     return output, grad_q, grad_k, grad_v
 

time: 119 us -> 123 us (1.034); the launches traced: 118 us -> 121 us
  local copies, waits for them, and re-layouts: 6.35 us -> 20.5 us
  Pallas kernels: 51.3 us -> 40.9 us
    unnamed x16 -> x48, local copies, waits for them, and re-layouts: 6.35 us -> 20.5 us
    pallas_call x9, Pallas kernels: 51.3 us -> 40.9 us  [call(): pl.pallas_call(kernel, name=name, in_specs=[*[pl.BlockSpec(memory_space=p...]
    all_to_all x4, waiting for transfers between devices: 30.7 us -> 27.9 us  [exchanged(): return lax.all_to_all(slices, AXES, split_axis=0, concat_axis=0, tiled=True)]
    ppermute x4, waiting for transfers between devices: 0.1 us -> 1.84 us  [to_peers(): return lax.ppermute(array, 'head', pairs)]
  transfers between devices with their start and end apart: 8 -> 8, of which waited for: 5 -> 5; matrix products, arithmetic and copies ran while one was open for 0% -> 0% of each run, Pallas kernels for 34% -> 28%
where the time goes in v5:
time: 123 us; the launch traced here: 121 us
  Pallas kernels  40.9 us (33%)
  waiting for transfers between devices  29.7 us (24%)
  starting transfers between devices  28.6 us (23%)
  local copies, waits for them, and re-layouts  20.5 us (17%)
    pallas_call x9, Pallas kernels, call(): pl.pallas_call(kernel, name=name, in_specs=[*[pl.BlockSpec(memory_space=p...  40.9 us
    all_to_all x4, waiting for transfers between devices, exchanged(): return lax.all_to_all(slices, AXES, split_axis=0, concat_axis=0, tiled=True)  27.9 us
    all_to_all x4, starting transfers between devices, exchanged(): return lax.all_to_all(slices, AXES, split_axis=0, concat_axis=0, tiled=True)  21.4 us
    unnamed x48, local copies, waits for them, and re-layouts  20.5 us
    ppermute x4, starting transfers between devices, to_peers(): return lax.ppermute(array, 'head', pairs)  7.23 us
  transfers between devices with their start and end apart: 8, of which 5 were waited for; matrix products, arithmetic and copies ran while one was open for 0% of the time, Pallas kernels for 28%

profile of v5, /device:TPU:1, one launch (start us, length us, event | category | flops | bytes accessed | tf_op | source)
XLA Modules:
  0.0 120.6 jit_solution(9870113537806788111)
XLA Ops:
  0.6 0.0 copy-start.14
  0.6 3.9 %states.1 = (bf16[16,128,128]{2,1,0:T(8,128)(2,1)}, bf16[16,128,128]{2,1,0:T(8,128)(2,1)}, bf16[16,128,128]{2,1,0:T(8,128)(2,1)}) custom-call(s32[4]{0:T(128)} %refs_0_.17, s32[2,6]{1,0:T(2,128)} %refs_1_.13, bf16[256,2048]{1,0:T(8,128)(2,1)} %refs_3_.11, bf16[256,2048]{1,0:T(8,128)(2,1)} %refs_4_.5), custom_call_target="tpu_custom_call" | custom-call | flops 134217728 | bytes 3670016 | tf_op jit(solution)/shard_map/states/pallas_call | solution.py:396
  4.6 7.1 %all-to-all-start = ((bf16[32,64,128]{2,1,0:T(8,128)(2,1)}), bf16[32,64,128]{2,1,0:T(8,128)(2,1)S(1)}, u32[]{:S(2)}, u32[]{:S(2)}) async-start(bf16[32,64,128]{2,1,0:T(8,128)(2,1)} %bitcast.10), calls=%async_computation | async-start | bytes 1048576 | tf_op jit(solution)/shard_map/all_to_all | solution.py:454
  11.7 3.3 %collective-permute-start = (bf16[16,128,128]{2,1,0:T(8,128)(2,1)}, bf16[16,128,128]{2,1,0:T(8,128)(2,1)S(1)}, u32[]{:S(2)}, u32[]{:S(2)}) collective-permute-start(bf16[16,128,128]{2,1,0:T(8,128)(2,1)} %get-tuple-element.32), channel_id=1, source_target_pairs={{0,1},{2,3},{4,5},{6,7},{8,9},{10,11},{12,13},{14,15},{16,17},{18,... | collective-permute-start | bytes 1572872 | tf_op jit(solution)/shard_map/ppermute | solution.py:451
  15.0 1.3 %collective-permute-start.1 = (bf16[16,128,128]{2,1,0:T(8,128)(2,1)}, bf16[16,128,128]{2,1,0:T(8,128)(2,1)S(1)}, u32[]{:S(2)}, u32[]{:S(2)}) collective-permute-start(bf16[16,128,128]{2,1,0:T(8,128)(2,1)} %get-tuple-element.34), channel_id=1, source_target_pairs={{0,1},{2,3},{4,5},{6,7},{8,9},{10,11},{12,13},{14,15},{16,17},{18,... | collective-permute-start | bytes 1572872 | tf_op jit(solution)/shard_map/ppermute | solution.py:451
  16.4 10.6 %all-to-all-done.refs_1_ = bf16[32,64,128]{2,1,0:T(8,128)(2,1)S(1)} async-done(((bf16[32,64,128]{2,1,0:T(8,128)(2,1)}), bf16[32,64,128]{2,1,0:T(8,128)(2,1)S(1)}, u32[]{:S(2)}, u32[]{:S(2)}) %all-to-all-start) | async-done | bytes 524320 | tf_op jit(solution)/shard_map/all_to_all | solution.py:454
  27.0 1.5 %scan.2 = (bf16[32,64,128]{2,1,0:T(8,128)(2,1)}, f32[8,128]{1,0:T(8,128)S(1)}) custom-call(s32[4]{0:T(128)S(1)} %copy-done.14, bf16[32,64,128]{2,1,0:T(8,128)(2,1)S(1)} %all-to-all-done.refs_1_), custom_call_target="tpu_custom_call" | custom-call | bytes 1052672 | tf_op jit(solution)/shard_map/scan/pallas_call | solution.py:396
  28.5 0.0 copy-start.19
  28.5 0.6 copy-done.19
  29.1 3.2 %all-to-all-start.1 = ((bf16[32,64,128]{2,1,0:T(8,128)(2,1)}), bf16[32,64,128]{2,1,0:T(8,128)(2,1)S(1)}, u32[]{:S(2)}, u32[]{:S(2)}) async-start(bf16[32,64,128]{2,1,0:T(8,128)(2,1)} %get-tuple-element.30), calls=%async_computation.1 | async-start | bytes 1048576 | tf_op jit(solution)/shard_map/all_to_all | solution.py:454
  32.3 0.0 collective-permute-done.refs_6_.refs_7_.refs_12_
  32.3 0.0 copy-start.22
  32.3 0.8 copy-done.22
  33.1 5.1 %inner.1.refs_4_ = f32[256,2048]{1,0:T(8,128)} custom-call(s32[4]{0:T(128)} %refs_0_.17, s32[2,6]{1,0:T(2,128)} %refs_1_.13, bf16[256,2048]{1,0:T(8,128)(2,1)} %refs_2_.5, bf16[256,2048]{1,0:T(8,128)(2,1)} %refs_3_.11, bf16[256,2048]{1,0:T(8,128)(2,1)} %refs_4_.5, f32[8,128]{1,0:T(8,128)} %copy-done.19, bf16[16,128,128]{2,1,0:T(8,128)(2,1)} %copy-done.22), custom_call_target="tpu_custom_call" | custom-call | flops 40000000000 | bytes 5242880 | tf_op jit(solution)/shard_map/inner/pallas_call | solution.py:396
  38.2 13.1 %all-to-all-done.1 = bf16[32,64,128]{2,1,0:T(8,128)(2,1)S(1)} async-done(((bf16[32,64,128]{2,1,0:T(8,128)(2,1)}), bf16[32,64,128]{2,1,0:T(8,128)(2,1)S(1)}, u32[]{:S(2)}, u32[]{:S(2)}) %all-to-all-start.1) | async-done | bytes 524320 | tf_op jit(solution)/shard_map/all_to_all | solution.py:454
  51.3 0.8 copy-done.21
  52.1 4.6 %norm.2 = (f32[128,128]{1,0:T(8,128)}, bf16[128,2048]{1,0:T(8,128)(2,1)}, bf16[128,2048]{1,0:T(8,128)(2,1)}, bf16[16,128,128]{2,1,0:T(8,128)(2,1)}) custom-call(s32[4]{0:T(128)} %refs_0_.17, s32[2,6]{1,0:T(2,128)} %refs_1_.13, f32[1,2048]{1,0:T(1,128)} %bitcast.11, bf16[256,2048]{1,0:T(8,128)(2,1)} %refs_2_.5, f32[256,2048]{1,0:T(8,128)} %inner.1.refs_4_, ...), custom_call_target="tpu_custom_call" | custom-call | flops 134217728 | bytes 6889472 | tf_op jit(solution)/shard_map/norm/pallas_call | solution.py:396
  56.7 1.3 %collective-permute-start.2 = (bf16[16,128,128]{2,1,0:T(8,128)(2,1)}, bf16[16,128,128]{2,1,0:T(8,128)(2,1)S(1)}, u32[]{:S(2)}, u32[]{:S(2)}) collective-permute-start(bf16[16,128,128]{2,1,0:T(8,128)(2,1)} %get-tuple-element.35.refs_8_), channel_id=1, source_target_pairs={{1,0},{3,2},{5,4},{7,6},{9,8},{11,10},{13,12},{15,14},{17,16},{19,... | collective-permute-start | bytes 1572872 | tf_op jit(solution)/shard_map/ppermute | solution.py:451
  58.0 0.0 collective-permute-done.1.refs_7_.refs_13_
  58.0 0.8 copy-done.23
  58.8 5.0 %norm.3 = (f32[128,128]{1,0:T(8,128)}, bf16[128,2048]{1,0:T(8,128)(2,1)}, bf16[128,2048]{1,0:T(8,128)(2,1)}, bf16[16,128,128]{2,1,0:T(8,128)(2,1)}, bf16[16,128,128]{2,1,0:T(8,128)(2,1)}) custom-call(s32[4]{0:T(128)} %refs_0_.17, s32[2,6]{1,0:T(2,128)} %refs_1_.13, f32[1,2048]{1,0:T(1,128)} %bitcast.12, bf16[256,2048]{1,0:T(8,128)(2,1)} %refs_2_.5, ...), custom_call_target="tpu_custom_call" | custom-call | flops 40000000000 | bytes 7938048 | tf_op jit(solution)/shard_map/norm/pallas_call | solution.py:396
  63.9 7.9 %all-to-all-start.2 = ((bf16[32,64,128]{2,1,0:T(8,128)(2,1)}), bf16[32,64,128]{2,1,0:T(8,128)(2,1)S(1)}, u32[]{:S(2)}, u32[]{:S(2)}) async-start(bf16[32,64,128]{2,1,0:T(8,128)(2,1)} %bitcast.9), calls=%async_computation.2 | async-start | bytes 1048576 | tf_op jit(solution)/shard_map/all_to_all | solution.py:454
  71.8 1.3 %collective-permute-start.3 = (bf16[16,128,128]{2,1,0:T(8,128)(2,1)}, bf16[16,128,128]{2,1,0:T(8,128)(2,1)S(1)}, u32[]{:S(2)}, u32[]{:S(2)}) collective-permute-start(bf16[16,128,128]{2,1,0:T(8,128)(2,1)} %get-tuple-element.46), channel_id=1, source_target_pairs={{1,0},{3,2},{5,4},{7,6},{9,8},{11,10},{13,12},{15,14},{17,16},{19,... | collective-permute-start | bytes 1572872 | tf_op jit(solution)/shard_map/ppermute | solution.py:451
  73.1 0.6 collective-permute-done.2.refs_14_.refs_7_
  73.8 0.8 copy-done.9
  74.6 8.5 %query_grads.1 = (bf16[256,2048]{1,0:T(8,128)(2,1)}, bf16[256,2048]{1,0:T(8,128)(2,1)}, f32[8,128]{1,0:T(8,128)}) custom-call(s32[4]{0:T(128)} %refs_0_.17, s32[2,6]{1,0:T(2,128)} %refs_1_.13, f32[1,2048]{1,0:T(1,128)} %bitcast.13, bf16[256,2048]{1,0:T(8,128)(2,1)} %refs_3_.11, bf16[256,2048]{1,0:T(8,128)(2,1)} %refs_4_.5, bf16[16,128,128]{2,1,0:T(8,128)(2,1)} %bitcast.8, ...), custom_call_target="tpu_custom_call" | custom-call | flops 40000000000 | bytes 8007680 | tf_op jit(solution)/shard_map/query_grads/pallas_call | solution.py:396
  83.0 4.1 %all-to-all-done.2.refs_1_ = bf16[32,64,128]{2,1,0:T(8,128)(2,1)S(1)} async-done(((bf16[32,64,128]{2,1,0:T(8,128)(2,1)}), bf16[32,64,128]{2,1,0:T(8,128)(2,1)S(1)}, u32[]{:S(2)}, u32[]{:S(2)}) %all-to-all-start.2) | async-done | bytes 524320 | tf_op jit(solution)/shard_map/all_to_all | solution.py:454
  87.2 0.7 copy-done.17
  87.8 1.5 %scan.3 = (bf16[32,64,128]{2,1,0:T(8,128)(2,1)}, f32[8,128]{1,0:T(8,128)S(1)}) custom-call(s32[4]{0:T(128)S(1)} %copy-done.15, bf16[32,64,128]{2,1,0:T(8,128)(2,1)S(1)} %all-to-all-done.2.refs_1_, f32[8,128]{1,0:T(8,128)S(1)} %copy-done.17), custom_call_target="tpu_custom_call" | custom-call | bytes 1052672 | tf_op jit(solution)/shard_map/scan/pallas_call | solution.py:396
  89.4 3.1 %all-to-all-start.3 = ((bf16[32,64,128]{2,1,0:T(8,128)(2,1)}), bf16[32,64,128]{2,1,0:T(8,128)(2,1)S(1)}, u32[]{:S(2)}, u32[]{:S(2)}) async-start(bf16[32,64,128]{2,1,0:T(8,128)(2,1)} %get-tuple-element.51), calls=%async_computation.3 | async-start | bytes 1048576 | tf_op jit(solution)/shard_map/all_to_all | solution.py:454
  92.5 1.2 %collective-permute-done.3.refs_8_ = bf16[16,128,128]{2,1,0:T(8,128)(2,1)S(1)} collective-permute-done((bf16[16,128,128]{2,1,0:T(8,128)(2,1)}, bf16[16,128,128]{2,1,0:T(8,128)(2,1)S(1)}, u32[]{:S(2)}, u32[]{:S(2)}) %collective-permute-start.3) | collective-permute-done | bytes 524320 | tf_op jit(solution)/shard_map/ppermute | solution.py:451
  93.8 0.8 copy-done.11
  94.6 1.2 %copy-done.6 = bf16[256,2048]{1,0:T(8,128)(2,1)S(1)} copy-done((bf16[256,2048]{1,0:T(8,128)(2,1)S(1)}, bf16[256,2048]{1,0:T(8,128)(2,1)}, u32[]{:S(2)}) %copy-start.6) | copy-done | bytes 1048600
  95.8 1.2 %copy-done.7 = bf16[256,2048]{1,0:T(8,128)(2,1)S(1)} copy-done((bf16[256,2048]{1,0:T(8,128)(2,1)S(1)}, bf16[256,2048]{1,0:T(8,128)(2,1)}, u32[]{:S(2)}) %copy-start.7) | copy-done | bytes 1048600
  97.0 1.2 %copy-done.8 = bf16[256,2048]{1,0:T(8,128)(2,1)S(1)} copy-done((bf16[256,2048]{1,0:T(8,128)(2,1)S(1)}, bf16[256,2048]{1,0:T(8,128)(2,1)}, u32[]{:S(2)}) %copy-start.8) | copy-done | bytes 1048600
  98.2 1.0 copy-done.12
  99.3 1.0 copy-done.18
  100.3 1.0 copy-done.20
  101.4 7.7 %key_grads.1 = (f32[256,2048]{1,0:T(8,128)S(1)}, f32[256,2048]{1,0:T(8,128)S(1)}, bf16[256,2048]{1,0:T(8,128)(2,1)S(1)}, bf16[256,2048]{1,0:T(8,128)(2,1)S(1)}) custom-call(s32[4]{0:T(128)S(1)} %copy-done.15, s32[2,6]{1,0:T(2,128)S(1)} %copy-done.16, bf16[256,2048]{1,0:T(8,128)(2,1)S(1)} %copy-done.8, bf16[256,2048]{1,0:T(8,128)(2,1)S(1)} %copy-done.6, ...), custom_call_target="tpu_custom_call" | custom-call | flops 40000000000 | bytes 10485760 | tf_op jit(solution)/shard_map/key_grads/pallas_call | solution.py:396
  109.1 1.4 %copy-done = f32[256,2048]{1,0:T(8,128)} copy-done((f32[256,2048]{1,0:T(8,128)}, f32[256,2048]{1,0:T(8,128)S(1)}, u32[]{:S(2)}) %copy-start) | copy-done | bytes 2097176
  110.4 1.0 copy-done.2
  111.4 1.0 copy-done.4
  112.4 0.0 all-to-all-done.3
  112.4 1.6 %copy-done.1 = f32[256,2048]{1,0:T(8,128)S(1)} copy-done((f32[256,2048]{1,0:T(8,128)S(1)}, f32[256,2048]{1,0:T(8,128)}, u32[]{:S(2)}) %copy-start.1) | copy-done | bytes 2097176
  114.0 1.2 %copy-done.3 = bf16[256,2048]{1,0:T(8,128)(2,1)S(1)} copy-done((bf16[256,2048]{1,0:T(8,128)(2,1)S(1)}, bf16[256,2048]{1,0:T(8,128)(2,1)}, u32[]{:S(2)}) %copy-start.3) | copy-done | bytes 1048600
  115.2 1.2 %copy-done.5 = bf16[256,2048]{1,0:T(8,128)(2,1)S(1)} copy-done((bf16[256,2048]{1,0:T(8,128)(2,1)S(1)}, bf16[256,2048]{1,0:T(8,128)(2,1)}, u32[]{:S(2)}) %copy-start.5) | copy-done | bytes 1048600
  116.4 1.0 copy-done.13
  117.4 3.0 %last.1 = (bf16[256,2048]{1,0:T(8,128)(2,1)}, bf16[256,2048]{1,0:T(8,128)(2,1)}) custom-call(s32[4]{0:T(128)S(1)} %copy-done.15, s32[2,6]{1,0:T(2,128)S(1)} %copy-done.16, bf16[256,2048]{1,0:T(8,128)(2,1)S(1)} %copy-done.3, bf16[256,2048]{1,0:T(8,128)(2,1)S(1)} %copy-done.5, f32[256,2048]{1,0:T(8,128)S(1)} %get-tuple-element.49.refs_4_, ...), custom_call_target="tpu_custom_call" | custom-call | flops 268435456 | bytes 9961472 | tf_op jit(solution)/shard_map/last/pallas_call | solution.py:396
  (25 shorter events, 0.0 us)
Async XLA Ops:
  0.6 26.4 %copy-start.14 = (s32[4]{0:T(128)S(1)}, s32[4]{0:T(128)}, u32[]{:S(2)}) copy-start(s32[4]{0:T(128)} %refs_0_.17) | copy-start | bytes 52
  4.6 22.4 %all-to-all-start = ((bf16[32,64,128]{2,1,0:T(8,128)(2,1)}), bf16[32,64,128]{2,1,0:T(8,128)(2,1)S(1)}, u32[]{:S(2)}, u32[]{:S(2)}) async-start(bf16[32,64,128]{2,1,0:T(8,128)(2,1)} %bitcast.10), calls=%async_computation | async-start | bytes 1048576 | tf_op jit(solution)/shard_map/all_to_all | solution.py:454
  11.7 20.6 %collective-permute-start = (bf16[16,128,128]{2,1,0:T(8,128)(2,1)}, bf16[16,128,128]{2,1,0:T(8,128)(2,1)S(1)}, u32[]{:S(2)}, u32[]{:S(2)}) collective-permute-start(bf16[16,128,128]{2,1,0:T(8,128)(2,1)} %get-tuple-element.32), channel_id=1, source_target_pairs={{0,1},{2,3},{4,5},{6,7},{8,9},{10,11},{12,13},{14,15},{16,17},{18,... | collective-permute-start | bytes 1572872 | tf_op jit(solution)/shard_map/ppermute | solution.py:451
  15.0 43.0 %collective-permute-start.1 = (bf16[16,128,128]{2,1,0:T(8,128)(2,1)}, bf16[16,128,128]{2,1,0:T(8,128)(2,1)S(1)}, u32[]{:S(2)}, u32[]{:S(2)}) collective-permute-start(bf16[16,128,128]{2,1,0:T(8,128)(2,1)} %get-tuple-element.34), channel_id=1, source_target_pairs={{0,1},{2,3},{4,5},{6,7},{8,9},{10,11},{12,13},{14,15},{16,17},{18,... | collective-permute-start | bytes 1572872 | tf_op jit(solution)/shard_map/ppermute | solution.py:451
  28.5 0.6 copy-start.19
  29.1 22.2 %all-to-all-start.1 = ((bf16[32,64,128]{2,1,0:T(8,128)(2,1)}), bf16[32,64,128]{2,1,0:T(8,128)(2,1)S(1)}, u32[]{:S(2)}, u32[]{:S(2)}) async-start(bf16[32,64,128]{2,1,0:T(8,128)(2,1)} %get-tuple-element.30), calls=%async_computation.1 | async-start | bytes 1048576 | tf_op jit(solution)/shard_map/all_to_all | solution.py:454
  32.3 0.8 copy-start.22
  51.3 0.8 copy-start.21
  56.7 17.0 %collective-permute-start.2 = (bf16[16,128,128]{2,1,0:T(8,128)(2,1)}, bf16[16,128,128]{2,1,0:T(8,128)(2,1)S(1)}, u32[]{:S(2)}, u32[]{:S(2)}) collective-permute-start(bf16[16,128,128]{2,1,0:T(8,128)(2,1)} %get-tuple-element.35.refs_8_), channel_id=1, source_target_pairs={{1,0},{3,2},{5,4},{7,6},{9,8},{11,10},{13,12},{15,14},{17,16},{19,... | collective-permute-start | bytes 1572872 | tf_op jit(solution)/shard_map/ppermute | solution.py:451
  58.0 0.8 copy-start.23
  63.9 23.3 %all-to-all-start.2 = ((bf16[32,64,128]{2,1,0:T(8,128)(2,1)}), bf16[32,64,128]{2,1,0:T(8,128)(2,1)S(1)}, u32[]{:S(2)}, u32[]{:S(2)}) async-start(bf16[32,64,128]{2,1,0:T(8,128)(2,1)} %bitcast.9), calls=%async_computation.2 | async-start | bytes 1048576 | tf_op jit(solution)/shard_map/all_to_all | solution.py:454
  71.8 21.9 %collective-permute-start.3 = (bf16[16,128,128]{2,1,0:T(8,128)(2,1)}, bf16[16,128,128]{2,1,0:T(8,128)(2,1)S(1)}, u32[]{:S(2)}, u32[]{:S(2)}) collective-permute-start(bf16[16,128,128]{2,1,0:T(8,128)(2,1)} %get-tuple-element.46), channel_id=1, source_target_pairs={{1,0},{3,2},{5,4},{7,6},{9,8},{11,10},{13,12},{15,14},{17,16},{19,... | collective-permute-start | bytes 1572872 | tf_op jit(solution)/shard_map/ppermute | solution.py:451
  73.8 0.8 copy-start.9
  74.6 12.6 %copy-start.15 = (s32[4]{0:T(128)S(1)}, s32[4]{0:T(128)}, u32[]{:S(2)}) copy-start(s32[4]{0:T(128)} %refs_0_.17) | copy-start | bytes 52
  74.6 20.0 %copy-start.16 = (s32[2,6]{1,0:T(2,128)S(1)}, s32[2,6]{1,0:T(2,128)}, u32[]{:S(2)}) copy-start(s32[2,6]{1,0:T(2,128)} %refs_1_.13) | copy-start | bytes 148
  87.2 0.7 copy-start.17
  89.4 23.0 %all-to-all-start.3 = ((bf16[32,64,128]{2,1,0:T(8,128)(2,1)}), bf16[32,64,128]{2,1,0:T(8,128)(2,1)S(1)}, u32[]{:S(2)}, u32[]{:S(2)}) async-start(bf16[32,64,128]{2,1,0:T(8,128)(2,1)} %get-tuple-element.51), calls=%async_computation.3 | async-start | bytes 1048576 | tf_op jit(solution)/shard_map/all_to_all | solution.py:454
  93.7 0.8 copy-start.11
  94.6 1.2 %copy-start.6 = (bf16[256,2048]{1,0:T(8,128)(2,1)S(1)}, bf16[256,2048]{1,0:T(8,128)(2,1)}, u32[]{:S(2)}) copy-start(bf16[256,2048]{1,0:T(8,128)(2,1)} %refs_3_.11) | copy-start | bytes 3145732
  95.8 1.2 %copy-start.7 = (bf16[256,2048]{1,0:T(8,128)(2,1)S(1)}, bf16[256,2048]{1,0:T(8,128)(2,1)}, u32[]{:S(2)}) copy-start(bf16[256,2048]{1,0:T(8,128)(2,1)} %refs_4_.5) | copy-start | bytes 3145732
  97.0 1.2 %copy-start.8 = (bf16[256,2048]{1,0:T(8,128)(2,1)S(1)}, bf16[256,2048]{1,0:T(8,128)(2,1)}, u32[]{:S(2)}) copy-start(bf16[256,2048]{1,0:T(8,128)(2,1)} %refs_2_.5) | copy-start | bytes 3145732
  98.2 1.0 copy-start.12
  99.3 1.0 copy-start.18
  100.3 1.0 copy-start.20
  101.4 11.0 %copy-start.10 = (bf16[16,128,128]{2,1,0:T(8,128)(2,1)S(1)}, bf16[16,128,128]{2,1,0:T(8,128)(2,1)}, u32[]{:S(2)}) copy-start(bf16[16,128,128]{2,1,0:T(8,128)(2,1)} %copy-done.9) | copy-start | bytes 1572868
  109.1 1.4 %copy-start = (f32[256,2048]{1,0:T(8,128)}, f32[256,2048]{1,0:T(8,128)S(1)}, u32[]{:S(2)}) copy-start(f32[256,2048]{1,0:T(8,128)S(1)} %get-tuple-element.50.refs_5_) | copy-start | bytes 6291460
  110.4 1.0 copy-start.2
  111.4 1.0 copy-start.4
  112.4 1.6 %copy-start.1 = (f32[256,2048]{1,0:T(8,128)S(1)}, f32[256,2048]{1,0:T(8,128)}, u32[]{:S(2)}) copy-start(f32[256,2048]{1,0:T(8,128)} %copy-done) | copy-start | bytes 6291460
  114.0 1.2 %copy-start.3 = (bf16[256,2048]{1,0:T(8,128)(2,1)S(1)}, bf16[256,2048]{1,0:T(8,128)(2,1)}, u32[]{:S(2)}) copy-start(bf16[256,2048]{1,0:T(8,128)(2,1)} %copy-done.2) | copy-start | bytes 3145732
  115.2 1.2 %copy-start.5 = (bf16[256,2048]{1,0:T(8,128)(2,1)S(1)}, bf16[256,2048]{1,0:T(8,128)(2,1)}, u32[]{:S(2)}) copy-start(bf16[256,2048]{1,0:T(8,128)(2,1)} %copy-done.4) | copy-start | bytes 3145732
  116.4 1.0 copy-start.13

commit v6 on v5

--- a/solution.py
+++ b/solution.py
@@ -122,10 +122,9 @@
         return carried, peers, (self.row_segments(block) == edge).astype(F32)
 
 
-def mixed(state_ref, peer_refs, factors, head):
-    carried, peers, _ = factors
-    total = state_ref[head].astype(F32) * carried
-    for ref, factor in zip(peer_refs, peers, strict=True):
+def mixed(refs, factors, head):
+    total = refs[0][head].astype(F32) * factors[0]
+    for ref, factor in zip(refs[1:], factors[1:], strict=True):
         total = total + ref[head].astype(F32) * factor
     return total.astype(BF)
 
@@ -164,16 +163,24 @@
         leave(c)
 
 
-def inner_body(place_of, ins, outs, scratch, arrive, leave, chunks):
-    q_ref, k_ref, v_ref = ins
+def inner_body(place_of, ins, outs, scratch, arrive, leave, chunks, *, peers):
+    q_ref, k_ref, v_ref, *x_refs = ins
     (raw_ref,), (weight_ref,) = outs, scratch
-    weight_ref[...] = place_of(q_ref.shape[0]).weights()
+    place = place_of(q_ref.shape[0])
+    weight_ref[...] = place.weights()
+    factors = [place.before(b) for b in range(place.blocks)]
     for c, heads in enumerate(chunks):
         arrive(c)
         for head in heads:
             at = columns(head)
             probs = (dot(q_ref[:, at], k_ref[:, at], NT) * weight_ref[...]).astype(BF)
-            raw_ref[:, at] = dot(probs, v_ref[:, at], NN)
+            raw = dot(probs, v_ref[:, at], NN)
+            for b in range(place.blocks):
+                part = raw[b * BLOCK : (b + 1) * BLOCK]
+                if peers:
+                    state = mixed(x_refs[b * peers : (b + 1) * peers], factors[b][1], head)
+                    part = part + dot(q_ref[rows_of(b), at], state, NN) * factors[b][2]
+                raw_ref[rows_of(b), at] = part
         leave(c)
 
 
@@ -211,20 +218,19 @@
         leave(c)
 
 
-def norm_body(place_of, ins, outs, scratch, arrive, leave, chunks, *, rows, block, peers):
-    gain_ref, q_ref, raw_ref, grad_ref, kv_ref = ins[:5]
-    peer_refs, earlier_refs = ins[5 : 5 + peers], ins[5 + peers :]
+def norm_body(place_of, ins, outs, scratch, arrive, leave, chunks, *, rows, block):
+    gain_ref, q_ref, raw_ref, grad_ref, kv_ref, *earlier_refs = ins
     scale_ref, held_ref, d_ref, w_ref, *t_refs = outs
     width = q_ref.shape[1]
     place = place_of(rows)
-    factors = place.before(block)
+    carried, _, reach = place.before(block)
+    reach = reach * carried
     squares = cross = jnp.zeros((BLOCK, DH), F32)
     for c, heads in enumerate(chunks):
         arrive(c)
         for head in heads:
             at = columns(head)
-            state = mixed(kv_ref, peer_refs, factors, head)
-            raw = raw_ref[:, at] + dot(q_ref[:, at], state, NN) * factors[2]
+            raw = raw_ref[:, at] + dot(q_ref[:, at], kv_ref[head], NN) * reach
             raw = raw.astype(BF)
             held_ref[:, at] = raw
             raw = raw.astype(F32)
@@ -278,7 +284,8 @@
             grad_probs = (dot(d, v_ref[:, at], NT) * weight_ref[...]).astype(BF)
             inner = dot(grad_probs, k_ref[:, at], NN)
             for b in range(blocks):
-                state = mixed(kv_ref, peer_refs[b * peers : (b + 1) * peers], factors[b], head)
+                carried, there, _ = factors[b]
+                state = mixed([kv_ref, *peer_refs[b * peers : (b + 1) * peers]], [carried, *there], head)
                 outer = dot(d_refs[b][:, at], state, NT) * factors[b][2]
                 part = inner[b * BLOCK : (b + 1) * BLOCK] + outer
                 gq_ref[rows_of(b), at] = part.astype(BF)
@@ -287,12 +294,15 @@
         leave(c)
 
 
-def key_grads_body(place_of, ins, outs, scratch, arrive, leave, chunks):
-    q_ref, k_ref, v_ref, *d_refs = ins
+def key_grads_body(place_of, ins, outs, scratch, arrive, leave, chunks, *, peers):
+    q_ref, k_ref, v_ref, *rest = ins
     place = place_of(q_ref.shape[0])
-    gk_ref, gv_ref, k_out, v_out = outs
+    blocks = place.blocks
+    d_refs, w_refs = rest[:blocks], rest[blocks:]
+    gk_ref, gv_ref = outs
     (weight_ref,) = scratch
     weight_ref[...] = place.weights()
+    factors = [place.after(b) for b in range(blocks)]
     for c, heads in enumerate(chunks):
         arrive(c)
         for head in heads:
@@ -300,30 +310,34 @@
             q, d = q_ref[:, at], jnp.concatenate([ref[:, at] for ref in d_refs], axis=0)
             probs = (dot(q, k_ref[:, at], NT) * weight_ref[...]).astype(BF)
             grad_probs = (dot(d, v_ref[:, at], NT) * weight_ref[...]).astype(BF)
-            gk_ref[:, at] = dot(grad_probs, q, TN)
-            gv_ref[:, at] = dot(probs, d, TN)
-            k_out[:, at] = k_ref[:, at]
-            v_out[:, at] = v_ref[:, at]
+            gk = dot(grad_probs, q, TN)
+            gv = dot(probs, d, TN)
+            for b in range(blocks):
+                at_rows, here = rows_of(b), slice(b * BLOCK, (b + 1) * BLOCK)
+                part_k, part_v = gk[here], gv[here]
+                if peers:
+                    state = mixed(w_refs, factors[b][1], head)
+                    part_k = part_k + dot(v_ref[at_rows, at], state, NT) * factors[b][2]
+                    part_v = part_v + dot(k_ref[at_rows, at], state, NN) * factors[b][2]
+                gk_ref[at_rows, at] = part_k
+                gv_ref[at_rows, at] = part_v
         leave(c)
 
 
 def last_body(place_of, ins, outs, scratch, arrive, leave, chunks):
-    k_ref, v_ref, gk_in, gv_in, gs_ref = ins[:5]
-    peer_refs, (gk_ref, gv_ref) = ins[5:], outs
+    k_ref, v_ref, gk_in, gv_in, gs_ref = ins
+    gk_ref, gv_ref = outs
     place = place_of(k_ref.shape[0])
     factors = [place.after(b) for b in range(place.blocks)]
+    reach = jnp.concatenate([reach * carried for carried, _, reach in factors], axis=0)
     for c, heads in enumerate(chunks):
         arrive(c)
         for head in heads:
             at = columns(head)
-            for b in range(place.blocks):
-                at_rows = rows_of(b)
-                state = mixed(gs_ref, peer_refs, factors[b], head)
-                reach = factors[b][2]
-                gk = gk_in[at_rows, at] + dot(v_ref[at_rows, at], state, NT) * reach
-                gv = gv_in[at_rows, at] + dot(k_ref[at_rows, at], state, NN) * reach
-                gk_ref[at_rows, at] = gk.astype(BF)
-                gv_ref[at_rows, at] = gv.astype(BF)
+            gk = gk_in[:, at] + dot(v_ref[:, at], gs_ref[head], NT) * reach
+            gv = gv_in[:, at] + dot(k_ref[:, at], gs_ref[head], NN) * reach
+            gk_ref[:, at] = gk.astype(BF)
+            gv_ref[:, at] = gv.astype(BF)
         leave(c)
 
 
@@ -483,16 +497,16 @@
     from_peers = [to_peers(x, 1 + at % peers, False) for at, x in enumerate(later)]
     slices, token = scanned(sum_kv, False)
     (raw_inner,) = call(
-        inner_body,
+        functools.partial(inner_body, peers=peers),
         "inner",
         scalars,
-        [wide(queries), wide(keys), wide(values)],
+        [wide(queries), wide(keys), wide(values), *[states(x) for x in from_peers]],
         [wide(partial)],
         heads,
         chunks,
         square,
         flops=LONG,
-        after=[token, *from_peers[:peers]],
+        after=[token],
     )
     kv_state = exchanged(slices).reshape(heads, DH, DH)
 
@@ -500,7 +514,7 @@
     for b in range(blocks):
         ends = [states(state)] if b == blocks - 1 and blocks > 1 else []
         scale, raw, grad, update, *sums = call(
-            functools.partial(norm_body, rows=rows, block=b, peers=peers),
+            functools.partial(norm_body, rows=rows, block=b),
             "norm",
             scalars,
             [
@@ -509,7 +523,6 @@
                 wide(raw_inner, b),
                 wide(grad_out, b),
                 states(kv_state),
-                *[states(x) for x in from_peers[b * peers : (b + 1) * peers]],
                 *[states(w) for w in (updates if ends else [])],
             ],
             [Part(shape((BLOCK, DH), F32)), wide(block_tokens), wide(block_tokens), states(state), *ends],
@@ -544,34 +557,34 @@
         after=back[:peers],
     )
     slices, token = scanned(sums[0] if sums else updates[0], True, [token])
-    part_k, part_v, near_k, near_v = call(
-        key_grads_body,
+    part_k, part_v = call(
+        functools.partial(key_grads_body, peers=peers),
         "key_grads",
         scalars,
-        [wide(queries), wide(keys), wide(values), *[wide(d) for d in grads]],
-        [Part(a, near=True) for a in (partial, partial, tokens, tokens)],
+        [
+            wide(queries),
+            wide(keys),
+            wide(values),
+            *[wide(d) for d in grads],
+            *[states(w) for w in back],
+        ],
+        [wide(partial), wide(partial)],
         heads,
         chunks,
         square,
         flops=LONG,
-        after=[token, *back[peers:]],
-        limit=SOME_BYTES,
+        after=[token],
     )
     grad_state = exchanged(slices).reshape(heads, DH, DH)
     grad_k, grad_v = call(
         last_body,
         "last",
         scalars,
-        [
-            *[Part(a, near=True) for a in (near_k, near_v, part_k, part_v)],
-            Part(grad_state, near=True),
-            *[Part(w, near=True) for w in back],
-        ],
+        [wide(keys), wide(values), wide(part_k), wide(part_v), states(grad_state)],
         [wide(tokens), wide(tokens)],
         heads,
         chunks,
         flops=2 * unit,
-        limit=SOME_BYTES,
     )
     return output, grad_q, grad_k, grad_v
 

time: 123 us -> 117 us (0.951); the launches traced: 121 us -> 116 us
  local copies, waits for them, and re-layouts: 20.5 us -> 5.87 us
  Pallas kernels: 40.9 us -> 47.1 us
  starting transfers between devices: 28.6 us -> 31.8 us
    unnamed x48 -> x22, local copies, waits for them, and re-layouts: 20.5 us -> 5.87 us
    ppermute x4, waiting for transfers between devices: 1.84 us -> 11.3 us  [to_peers(): return lax.ppermute(array, 'head', pairs)]
    all_to_all x4, waiting for transfers between devices: 27.9 us -> 19.4 us  [exchanged(): return lax.all_to_all(slices, AXES, split_axis=0, concat_axis=0, tiled=True)]
    pallas_call x9, Pallas kernels: 40.9 us -> 47.1 us  [call(): pl.pallas_call(kernel, name=name, in_specs=[*[pl.BlockSpec(memory_space=p...]
    all_to_all x4, starting transfers between devices: 21.4 us -> 24.4 us  [exchanged(): return lax.all_to_all(slices, AXES, split_axis=0, concat_axis=0, tiled=True)]
  transfers between devices with their start and end apart: 8 -> 8, of which waited for: 5 -> 6; matrix products, arithmetic and copies ran while one was open for 0% -> 0% of each run, Pallas kernels for 28% -> 29%
where the time goes in v6:
time: 117 us; the launch traced here: 116 us
  Pallas kernels  47.1 us (40%)
  starting transfers between devices  31.8 us (27%)
  waiting for transfers between devices  30.7 us (26%)
  local copies, waits for them, and re-layouts  5.87 us (5%)
    pallas_call x9, Pallas kernels, call(): pl.pallas_call(kernel, name=name, in_specs=[*[pl.BlockSpec(memory_space=p...  47.1 us
    all_to_all x4, starting transfers between devices, exchanged(): return lax.all_to_all(slices, AXES, split_axis=0, concat_axis=0, tiled=True)  24.4 us
    all_to_all x4, waiting for transfers between devices, exchanged(): return lax.all_to_all(slices, AXES, split_axis=0, concat_axis=0, tiled=True)  19.4 us
    ppermute x4, waiting for transfers between devices, to_peers(): return lax.ppermute(array, 'head', pairs)  11.3 us
    ppermute x4, starting transfers between devices, to_peers(): return lax.ppermute(array, 'head', pairs)  7.41 us
    unnamed x22, local copies, waits for them, and re-layouts  5.87 us
  transfers between devices with their start and end apart: 8, of which 6 were waited for; matrix products, arithmetic and copies ran while one was open for 0% of the time, Pallas kernels for 29%

profile of v6, /device:TPU:1, one launch (start us, length us, event | category | flops | bytes accessed | tf_op | source)
XLA Modules:
  0.0 116.4 jit_solution(382894190250820730)
XLA Ops:
  0.6 0.0 copy-start
  0.6 3.9 %states.1 = (bf16[16,128,128]{2,1,0:T(8,128)(2,1)}, bf16[16,128,128]{2,1,0:T(8,128)(2,1)}, bf16[16,128,128]{2,1,0:T(8,128)(2,1)}) custom-call(s32[4]{0:T(128)} %refs_0_.17, s32[2,6]{1,0:T(2,128)} %refs_1_.13, bf16[256,2048]{1,0:T(8,128)(2,1)} %refs_2_.7, bf16[256,2048]{1,0:T(8,128)(2,1)} %refs_3_.13), custom_call_target="tpu_custom_call" | custom-call | flops 134217728 | bytes 3670016 | tf_op jit(solution)/shard_map/states/pallas_call | solution.py:410
  4.6 7.1 %all-to-all-start = ((bf16[32,64,128]{2,1,0:T(8,128)(2,1)}), bf16[32,64,128]{2,1,0:T(8,128)(2,1)S(1)}, u32[]{:S(2)}, u32[]{:S(2)}) async-start(bf16[32,64,128]{2,1,0:T(8,128)(2,1)} %bitcast.10), calls=%async_computation | async-start | bytes 1048576 | tf_op jit(solution)/shard_map/all_to_all | solution.py:468
  11.7 3.3 %collective-permute-start = (bf16[16,128,128]{2,1,0:T(8,128)(2,1)}, bf16[16,128,128]{2,1,0:T(8,128)(2,1)S(1)}, u32[]{:S(2)}, u32[]{:S(2)}) collective-permute-start(bf16[16,128,128]{2,1,0:T(8,128)(2,1)} %get-tuple-element.29), channel_id=1, source_target_pairs={{0,1},{2,3},{4,5},{6,7},{8,9},{10,11},{12,13},{14,15},{16,17},{18,... | collective-permute-start | bytes 1572872 | tf_op jit(solution)/shard_map/ppermute | solution.py:465
  15.0 1.3 %collective-permute-start.1 = (bf16[16,128,128]{2,1,0:T(8,128)(2,1)}, bf16[16,128,128]{2,1,0:T(8,128)(2,1)S(1)}, u32[]{:S(2)}, u32[]{:S(2)}) collective-permute-start(bf16[16,128,128]{2,1,0:T(8,128)(2,1)} %get-tuple-element.30), channel_id=1, source_target_pairs={{0,1},{2,3},{4,5},{6,7},{8,9},{10,11},{12,13},{14,15},{16,17},{18,... | collective-permute-start | bytes 1572872 | tf_op jit(solution)/shard_map/ppermute | solution.py:465
  16.4 10.6 %all-to-all-done.refs_1_ = bf16[32,64,128]{2,1,0:T(8,128)(2,1)S(1)} async-done(((bf16[32,64,128]{2,1,0:T(8,128)(2,1)}), bf16[32,64,128]{2,1,0:T(8,128)(2,1)S(1)}, u32[]{:S(2)}, u32[]{:S(2)}) %all-to-all-start) | async-done | bytes 524320 | tf_op jit(solution)/shard_map/all_to_all | solution.py:468
  27.0 0.0 copy-done
  27.0 1.5 %scan.2 = (bf16[32,64,128]{2,1,0:T(8,128)(2,1)}, f32[8,128]{1,0:T(8,128)S(1)}) custom-call(s32[4]{0:T(128)S(1)} %copy-done, bf16[32,64,128]{2,1,0:T(8,128)(2,1)S(1)} %all-to-all-done.refs_1_), custom_call_target="tpu_custom_call" | custom-call | bytes 1052672 | tf_op jit(solution)/shard_map/scan/pallas_call | solution.py:410
  28.5 0.0 copy-start.4
  28.5 0.6 copy-done.4
  29.1 3.2 %all-to-all-start.1 = ((bf16[32,64,128]{2,1,0:T(8,128)(2,1)}), bf16[32,64,128]{2,1,0:T(8,128)(2,1)S(1)}, u32[]{:S(2)}, u32[]{:S(2)}) async-start(bf16[32,64,128]{2,1,0:T(8,128)(2,1)} %get-tuple-element.28), calls=%async_computation.1 | async-start | bytes 1048576 | tf_op jit(solution)/shard_map/all_to_all | solution.py:468
  32.3 0.0 collective-permute-done.refs_5_.refs_12_
  32.3 0.0 copy-start.7
  32.3 10.7 %collective-permute-done.1.refs_6_.refs_13_ = bf16[16,128,128]{2,1,0:T(8,128)(2,1)S(1)} collective-permute-done((bf16[16,128,128]{2,1,0:T(8,128)(2,1)}, bf16[16,128,128]{2,1,0:T(8,128)(2,1)S(1)}, u32[]{:S(2)}, u32[]{:S(2)}) %collective-permute-start.1) | collective-permute-done | bytes 524320 | tf_op jit(solution)/shard_map/ppermute | solution.py:465
  43.0 0.0 copy-start.8
  43.0 0.0 copy-done.7
  43.0 0.8 copy-done.8
  43.8 7.1 %inner.1.refs_4_ = f32[256,2048]{1,0:T(8,128)} custom-call(s32[4]{0:T(128)} %refs_0_.17, s32[2,6]{1,0:T(2,128)} %refs_1_.13, bf16[256,2048]{1,0:T(8,128)(2,1)} %refs_2_.6, bf16[256,2048]{1,0:T(8,128)(2,1)} %refs_2_.7, bf16[256,2048]{1,0:T(8,128)(2,1)} %refs_3_.13, bf16[16,128,128]{2,1,0:T(8,128)(2,1)} %copy-done.7, bf16[16,128,128]{2,1,0:T(8,128)(2,1)} %copy-done.8, ...), custom_call_target="tpu_custom_call" | custom-call | flops 40000000000 | bytes 6291456 | tf_op jit(solution)/shard_map/inner/pallas_call | solution.py:410
  50.9 0.4 all-to-all-done.1
  51.3 0.0 copy-start.6
  51.3 0.8 copy-done.6
  52.1 4.4 %norm.2 = (f32[128,128]{1,0:T(8,128)}, bf16[128,2048]{1,0:T(8,128)(2,1)}, bf16[128,2048]{1,0:T(8,128)(2,1)}, bf16[16,128,128]{2,1,0:T(8,128)(2,1)}) custom-call(s32[4]{0:T(128)} %refs_0_.17, s32[2,6]{1,0:T(2,128)} %refs_1_.13, f32[1,2048]{1,0:T(1,128)} %bitcast.11, bf16[256,2048]{1,0:T(8,128)(2,1)} %refs_2_.6, f32[256,2048]{1,0:T(8,128)} %inner.1.refs_4_, ...), custom_call_target="tpu_custom_call" | custom-call | flops 134217728 | bytes 6365184 | tf_op jit(solution)/shard_map/norm/pallas_call | solution.py:410
  56.6 1.3 %collective-permute-start.2 = (bf16[16,128,128]{2,1,0:T(8,128)(2,1)}, bf16[16,128,128]{2,1,0:T(8,128)(2,1)S(1)}, u32[]{:S(2)}, u32[]{:S(2)}) collective-permute-start(bf16[16,128,128]{2,1,0:T(8,128)(2,1)} %get-tuple-element.33.refs_7_), channel_id=1, source_target_pairs={{1,0},{3,2},{5,4},{7,6},{9,8},{11,10},{13,12},{15,14},{17,16},{19,... | collective-permute-start | bytes 1572872 | tf_op jit(solution)/shard_map/ppermute | solution.py:465
  57.9 4.9 %norm.3 = (f32[128,128]{1,0:T(8,128)}, bf16[128,2048]{1,0:T(8,128)(2,1)}, bf16[128,2048]{1,0:T(8,128)(2,1)}, bf16[16,128,128]{2,1,0:T(8,128)(2,1)}, bf16[16,128,128]{2,1,0:T(8,128)(2,1)}) custom-call(s32[4]{0:T(128)} %refs_0_.17, s32[2,6]{1,0:T(2,128)} %refs_1_.13, f32[1,2048]{1,0:T(1,128)} %bitcast.12, bf16[256,2048]{1,0:T(8,128)(2,1)} %refs_2_.6, ...), custom_call_target="tpu_custom_call" | custom-call | flops 40000000000 | bytes 7413760 | tf_op jit(solution)/shard_map/norm/pallas_call | solution.py:410
  62.7 11.0 %all-to-all-start.2 = ((bf16[32,64,128]{2,1,0:T(8,128)(2,1)}), bf16[32,64,128]{2,1,0:T(8,128)(2,1)S(1)}, u32[]{:S(2)}, u32[]{:S(2)}) async-start(bf16[32,64,128]{2,1,0:T(8,128)(2,1)} %bitcast.9), calls=%async_computation.2 | async-start | bytes 1048576 | tf_op jit(solution)/shard_map/all_to_all | solution.py:468
  73.7 1.5 %collective-permute-start.3 = (bf16[16,128,128]{2,1,0:T(8,128)(2,1)}, bf16[16,128,128]{2,1,0:T(8,128)(2,1)S(1)}, u32[]{:S(2)}, u32[]{:S(2)}) collective-permute-start(bf16[16,128,128]{2,1,0:T(8,128)(2,1)} %get-tuple-element.41), channel_id=1, source_target_pairs={{1,0},{3,2},{5,4},{7,6},{9,8},{11,10},{13,12},{15,14},{17,16},{19,... | collective-permute-start | bytes 1572872 | tf_op jit(solution)/shard_map/ppermute | solution.py:465
  75.2 0.0 collective-permute-done.2.refs_14_.refs_7_
  75.2 0.0 copy-start.9
  75.2 0.8 copy-done.9
  76.0 0.0 copy-start.1
  76.0 8.4 %query_grads.1 = (bf16[256,2048]{1,0:T(8,128)(2,1)}, bf16[256,2048]{1,0:T(8,128)(2,1)}, f32[8,128]{1,0:T(8,128)}) custom-call(s32[4]{0:T(128)} %refs_0_.17, s32[2,6]{1,0:T(2,128)} %refs_1_.13, f32[1,2048]{1,0:T(1,128)} %bitcast.13, bf16[256,2048]{1,0:T(8,128)(2,1)} %refs_2_.7, bf16[256,2048]{1,0:T(8,128)(2,1)} %refs_3_.13, bf16[16,128,128]{2,1,0:T(8,128)(2,1)} %bitcast.8, ...), custom_call_target="tpu_custom_call" | custom-call | flops 40000000000 | bytes 8007680 | tf_op jit(solution)/shard_map/query_grads/pallas_call | solution.py:410
  84.4 4.6 %all-to-all-done.2.refs_1_ = bf16[32,64,128]{2,1,0:T(8,128)(2,1)S(1)} async-done(((bf16[32,64,128]{2,1,0:T(8,128)(2,1)}), bf16[32,64,128]{2,1,0:T(8,128)(2,1)S(1)}, u32[]{:S(2)}, u32[]{:S(2)}) %all-to-all-start.2) | async-done | bytes 524320 | tf_op jit(solution)/shard_map/all_to_all | solution.py:468
  89.0 0.0 copy-done.1
  89.0 0.0 copy-start.2
  89.0 0.7 copy-done.2
  89.7 1.5 %scan.3 = (bf16[32,64,128]{2,1,0:T(8,128)(2,1)}, f32[8,128]{1,0:T(8,128)S(1)}) custom-call(s32[4]{0:T(128)S(1)} %copy-done.1, bf16[32,64,128]{2,1,0:T(8,128)(2,1)S(1)} %all-to-all-done.2.refs_1_, f32[8,128]{1,0:T(8,128)S(1)} %copy-done.2), custom_call_target="tpu_custom_call" | custom-call | bytes 1052672 | tf_op jit(solution)/shard_map/scan/pallas_call | solution.py:410
  91.2 0.0 copy-start.3
  91.2 0.6 copy-done.3
  91.8 3.1 %all-to-all-start.3 = ((bf16[32,64,128]{2,1,0:T(8,128)(2,1)}), bf16[32,64,128]{2,1,0:T(8,128)(2,1)S(1)}, u32[]{:S(2)}, u32[]{:S(2)}) async-start(bf16[32,64,128]{2,1,0:T(8,128)(2,1)} %get-tuple-element.47), calls=%async_computation.3 | async-start | bytes 1048576 | tf_op jit(solution)/shard_map/all_to_all | solution.py:468
  95.0 0.7 collective-permute-done.3.refs_8_
  95.6 0.0 copy-start.10
  95.6 0.8 copy-done.10
  96.4 10.1 %key_grads.1 = (f32[256,2048]{1,0:T(8,128)}, f32[256,2048]{1,0:T(8,128)}) custom-call(s32[4]{0:T(128)} %refs_0_.17, s32[2,6]{1,0:T(2,128)} %refs_1_.13, bf16[256,2048]{1,0:T(8,128)(2,1)} %refs_2_.6, bf16[256,2048]{1,0:T(8,128)(2,1)} %refs_2_.7, bf16[256,2048]{1,0:T(8,128)(2,1)} %refs_3_.13, bf16[128,2048]{1,0:T(8,128)(2,1)} %get-tuple-element.32.refs_6_.refs_5_, ...), custom_call_target="tpu_custom_call" | custom-call | flops 40000000000 | bytes 9437184 | tf_op jit(solution)/shard_map/key_grads/pallas_call | solution.py:410
  106.5 3.8 %all-to-all-done.3 = bf16[32,64,128]{2,1,0:T(8,128)(2,1)S(1)} async-done(((bf16[32,64,128]{2,1,0:T(8,128)(2,1)}), bf16[32,64,128]{2,1,0:T(8,128)(2,1)S(1)}, u32[]{:S(2)}, u32[]{:S(2)}) %all-to-all-start.3) | async-done | bytes 524320 | tf_op jit(solution)/shard_map/all_to_all | solution.py:468
  110.2 0.0 copy-start.5
  110.3 0.8 copy-done.5
  111.1 5.2 %last.1 = (bf16[256,2048]{1,0:T(8,128)(2,1)}, bf16[256,2048]{1,0:T(8,128)(2,1)}) custom-call(s32[4]{0:T(128)} %refs_0_.17, s32[2,6]{1,0:T(2,128)} %refs_1_.13, bf16[256,2048]{1,0:T(8,128)(2,1)} %refs_2_.7, bf16[256,2048]{1,0:T(8,128)(2,1)} %refs_3_.13, f32[256,2048]{1,0:T(8,128)} %get-tuple-element.45.refs_4_, f32[256,2048]{1,0:T(8,128)} %get-tuple-element.46.refs_5_, ...), custom_call_target="tpu_custom_call" | custom-call | flops 268435456 | bytes 8912896 | tf_op jit(solution)/shard_map/last/pallas_call | solution.py:410
Async XLA Ops:
  0.6 26.4 %copy-start = (s32[4]{0:T(128)S(1)}, s32[4]{0:T(128)}, u32[]{:S(2)}) copy-start(s32[4]{0:T(128)} %refs_0_.17) | copy-start | bytes 52
  4.6 22.4 %all-to-all-start = ((bf16[32,64,128]{2,1,0:T(8,128)(2,1)}), bf16[32,64,128]{2,1,0:T(8,128)(2,1)S(1)}, u32[]{:S(2)}, u32[]{:S(2)}) async-start(bf16[32,64,128]{2,1,0:T(8,128)(2,1)} %bitcast.10), calls=%async_computation | async-start | bytes 1048576 | tf_op jit(solution)/shard_map/all_to_all | solution.py:468
  11.7 20.6 %collective-permute-start = (bf16[16,128,128]{2,1,0:T(8,128)(2,1)}, bf16[16,128,128]{2,1,0:T(8,128)(2,1)S(1)}, u32[]{:S(2)}, u32[]{:S(2)}) collective-permute-start(bf16[16,128,128]{2,1,0:T(8,128)(2,1)} %get-tuple-element.29), channel_id=1, source_target_pairs={{0,1},{2,3},{4,5},{6,7},{8,9},{10,11},{12,13},{14,15},{16,17},{18,... | collective-permute-start | bytes 1572872 | tf_op jit(solution)/shard_map/ppermute | solution.py:465
  15.0 28.0 %collective-permute-start.1 = (bf16[16,128,128]{2,1,0:T(8,128)(2,1)}, bf16[16,128,128]{2,1,0:T(8,128)(2,1)S(1)}, u32[]{:S(2)}, u32[]{:S(2)}) collective-permute-start(bf16[16,128,128]{2,1,0:T(8,128)(2,1)} %get-tuple-element.30), channel_id=1, source_target_pairs={{0,1},{2,3},{4,5},{6,7},{8,9},{10,11},{12,13},{14,15},{16,17},{18,... | collective-permute-start | bytes 1572872 | tf_op jit(solution)/shard_map/ppermute | solution.py:465
  28.5 0.6 copy-start.4
  29.1 22.2 %all-to-all-start.1 = ((bf16[32,64,128]{2,1,0:T(8,128)(2,1)}), bf16[32,64,128]{2,1,0:T(8,128)(2,1)S(1)}, u32[]{:S(2)}, u32[]{:S(2)}) async-start(bf16[32,64,128]{2,1,0:T(8,128)(2,1)} %get-tuple-element.28), calls=%async_computation.1 | async-start | bytes 1048576 | tf_op jit(solution)/shard_map/all_to_all | solution.py:468
  32.3 10.7 %copy-start.7 = (bf16[16,128,128]{2,1,0:T(8,128)(2,1)}, bf16[16,128,128]{2,1,0:T(8,128)(2,1)S(1)}, u32[]{:S(2)}) copy-start(bf16[16,128,128]{2,1,0:T(8,128)(2,1)S(1)} %collective-permute-done.refs_5_.refs_12_) | copy-start | bytes 1572868
  43.0 0.8 copy-start.8
  51.3 0.8 copy-start.6
  56.6 18.6 %collective-permute-start.2 = (bf16[16,128,128]{2,1,0:T(8,128)(2,1)}, bf16[16,128,128]{2,1,0:T(8,128)(2,1)S(1)}, u32[]{:S(2)}, u32[]{:S(2)}) collective-permute-start(bf16[16,128,128]{2,1,0:T(8,128)(2,1)} %get-tuple-element.33.refs_7_), channel_id=1, source_target_pairs={{1,0},{3,2},{5,4},{7,6},{9,8},{11,10},{13,12},{15,14},{17,16},{19,... | collective-permute-start | bytes 1572872 | tf_op jit(solution)/shard_map/ppermute | solution.py:465
  62.7 26.3 %all-to-all-start.2 = ((bf16[32,64,128]{2,1,0:T(8,128)(2,1)}), bf16[32,64,128]{2,1,0:T(8,128)(2,1)S(1)}, u32[]{:S(2)}, u32[]{:S(2)}) async-start(bf16[32,64,128]{2,1,0:T(8,128)(2,1)} %bitcast.9), calls=%async_computation.2 | async-start | bytes 1048576 | tf_op jit(solution)/shard_map/all_to_all | solution.py:468
  73.7 21.9 %collective-permute-start.3 = (bf16[16,128,128]{2,1,0:T(8,128)(2,1)}, bf16[16,128,128]{2,1,0:T(8,128)(2,1)S(1)}, u32[]{:S(2)}, u32[]{:S(2)}) collective-permute-start(bf16[16,128,128]{2,1,0:T(8,128)(2,1)} %get-tuple-element.41), channel_id=1, source_target_pairs={{1,0},{3,2},{5,4},{7,6},{9,8},{11,10},{13,12},{15,14},{17,16},{19,... | collective-permute-start | bytes 1572872 | tf_op jit(solution)/shard_map/ppermute | solution.py:465
  75.2 0.8 copy-start.9
  76.0 13.0 %copy-start.1 = (s32[4]{0:T(128)S(1)}, s32[4]{0:T(128)}, u32[]{:S(2)}) copy-start(s32[4]{0:T(128)} %refs_0_.17) | copy-start | bytes 52
  89.0 0.7 copy-start.2
  91.2 0.6 copy-start.3
  91.8 18.4 %all-to-all-start.3 = ((bf16[32,64,128]{2,1,0:T(8,128)(2,1)}), bf16[32,64,128]{2,1,0:T(8,128)(2,1)S(1)}, u32[]{:S(2)}, u32[]{:S(2)}) async-start(bf16[32,64,128]{2,1,0:T(8,128)(2,1)} %get-tuple-element.47), calls=%async_computation.3 | async-start | bytes 1048576 | tf_op jit(solution)/shard_map/all_to_all | solution.py:468
  95.6 0.8 copy-start.10
  110.2 0.8 copy-start.5

commit v7 on v6

--- a/solution.py
+++ b/solution.py
@@ -163,24 +163,16 @@
         leave(c)
 
 
-def inner_body(place_of, ins, outs, scratch, arrive, leave, chunks, *, peers):
-    q_ref, k_ref, v_ref, *x_refs = ins
+def inner_body(place_of, ins, outs, scratch, arrive, leave, chunks):
+    q_ref, k_ref, v_ref = ins
     (raw_ref,), (weight_ref,) = outs, scratch
-    place = place_of(q_ref.shape[0])
-    weight_ref[...] = place.weights()
-    factors = [place.before(b) for b in range(place.blocks)]
+    weight_ref[...] = place_of(q_ref.shape[0]).weights()
     for c, heads in enumerate(chunks):
         arrive(c)
         for head in heads:
             at = columns(head)
             probs = (dot(q_ref[:, at], k_ref[:, at], NT) * weight_ref[...]).astype(BF)
-            raw = dot(probs, v_ref[:, at], NN)
-            for b in range(place.blocks):
-                part = raw[b * BLOCK : (b + 1) * BLOCK]
-                if peers:
-                    state = mixed(x_refs[b * peers : (b + 1) * peers], factors[b][1], head)
-                    part = part + dot(q_ref[rows_of(b), at], state, NN) * factors[b][2]
-                raw_ref[rows_of(b), at] = part
+            raw_ref[:, at] = dot(probs, v_ref[:, at], NN)
         leave(c)
 
 
@@ -218,19 +210,20 @@
         leave(c)
 
 
-def norm_body(place_of, ins, outs, scratch, arrive, leave, chunks, *, rows, block):
-    gain_ref, q_ref, raw_ref, grad_ref, kv_ref, *earlier_refs = ins
+def norm_body(place_of, ins, outs, scratch, arrive, leave, chunks, *, rows, block, peers):
+    gain_ref, q_ref, raw_ref, grad_ref = ins[:4]
+    state_refs, earlier_refs = ins[4 : 5 + peers], ins[5 + peers :]
     scale_ref, held_ref, d_ref, w_ref, *t_refs = outs
     width = q_ref.shape[1]
     place = place_of(rows)
-    carried, _, reach = place.before(block)
-    reach = reach * carried
+    carried, there, reach = place.before(block)
     squares = cross = jnp.zeros((BLOCK, DH), F32)
     for c, heads in enumerate(chunks):
         arrive(c)
         for head in heads:
             at = columns(head)
-            raw = raw_ref[:, at] + dot(q_ref[:, at], kv_ref[head], NN) * reach
+            state = mixed(state_refs, [carried, *there], head)
+            raw = raw_ref[:, at] + dot(q_ref[:, at], state, NN) * reach
             raw = raw.astype(BF)
             held_ref[:, at] = raw
             raw = raw.astype(F32)
@@ -497,16 +490,16 @@
     from_peers = [to_peers(x, 1 + at % peers, False) for at, x in enumerate(later)]
     slices, token = scanned(sum_kv, False)
     (raw_inner,) = call(
-        functools.partial(inner_body, peers=peers),
+        inner_body,
         "inner",
         scalars,
-        [wide(queries), wide(keys), wide(values), *[states(x) for x in from_peers]],
+        [wide(queries), wide(keys), wide(values)],
         [wide(partial)],
         heads,
         chunks,
         square,
         flops=LONG,
-        after=[token],
+        after=[token, *from_peers[:peers]],
     )
     kv_state = exchanged(slices).reshape(heads, DH, DH)
 
@@ -514,7 +507,7 @@
     for b in range(blocks):
         ends = [states(state)] if b == blocks - 1 and blocks > 1 else []
         scale, raw, grad, update, *sums = call(
-            functools.partial(norm_body, rows=rows, block=b),
+            functools.partial(norm_body, rows=rows, block=b, peers=peers),
             "norm",
             scalars,
             [
@@ -523,6 +516,7 @@
                 wide(raw_inner, b),
                 wide(grad_out, b),
                 states(kv_state),
+                *[states(x) for x in from_peers[b * peers : (b + 1) * peers]],
                 *[states(w) for w in (updates if ends else [])],
             ],
             [Part(shape((BLOCK, DH), F32)), wide(block_tokens), wide(block_tokens), states(state), *ends],

time: 117 us -> 116 us (level)
  starting transfers between devices: 31.8 us -> 28.6 us
  waiting for transfers between devices: 30.7 us -> 32.9 us
  Pallas kernels: 47.1 us -> 45.5 us
    all_to_all x4, waiting for transfers between devices: 19.4 us -> 31.7 us  [exchanged(): return lax.all_to_all(slices, AXES, split_axis=0, concat_axis=0, tiled=True)]
    ppermute x4, waiting for transfers between devices: 11.3 us -> 1.21 us  [to_peers(): return lax.ppermute(array, 'head', pairs)]
    all_to_all x4, starting transfers between devices: 24.4 us -> 21.4 us  [exchanged(): return lax.all_to_all(slices, AXES, split_axis=0, concat_axis=0, tiled=True)]
    pallas_call x9, Pallas kernels: 47.1 us -> 45.5 us  [call(): pl.pallas_call(kernel, name=name, in_specs=[*[pl.BlockSpec(memory_space=p...]
  transfers between devices with their start and end apart: 8 -> 8, of which waited for: 6 -> 6; matrix products, arithmetic and copies ran while one was open for 0% -> 0% of each run, Pallas kernels for 29% -> 32%
where the time goes in v7:
time: 116 us; the launch traced here: 115 us
  Pallas kernels  45.5 us (39%)
  waiting for transfers between devices  32.9 us (28%)
  starting transfers between devices  28.6 us (25%)
  local copies, waits for them, and re-layouts  6.65 us (6%)
    pallas_call x9, Pallas kernels, call(): pl.pallas_call(kernel, name=name, in_specs=[*[pl.BlockSpec(memory_space=p...  45.5 us
    all_to_all x4, waiting for transfers between devices, exchanged(): return lax.all_to_all(slices, AXES, split_axis=0, concat_axis=0, tiled=True)  31.7 us
    all_to_all x4, starting transfers between devices, exchanged(): return lax.all_to_all(slices, AXES, split_axis=0, concat_axis=0, tiled=True)  21.4 us
    ppermute x4, starting transfers between devices, to_peers(): return lax.ppermute(array, 'head', pairs)  7.23 us
    unnamed x22, local copies, waits for them, and re-layouts  6.65 us
  transfers between devices with their start and end apart: 8, of which 6 were waited for; matrix products, arithmetic and copies ran while one was open for 0% of the time, Pallas kernels for 32%

profile of v7, /device:TPU:1, one launch (start us, length us, event | category | flops | bytes accessed | tf_op | source)
XLA Modules:
  0.0 114.6 jit_solution(8359852998586771068)
XLA Ops:
  0.6 0.0 copy-start
  0.6 3.9 %states.1 = (bf16[16,128,128]{2,1,0:T(8,128)(2,1)}, bf16[16,128,128]{2,1,0:T(8,128)(2,1)}, bf16[16,128,128]{2,1,0:T(8,128)(2,1)}) custom-call(s32[4]{0:T(128)} %refs_0_.17, s32[2,6]{1,0:T(2,128)} %refs_1_.13, bf16[256,2048]{1,0:T(8,128)(2,1)} %refs_2_.7, bf16[256,2048]{1,0:T(8,128)(2,1)} %refs_3_.13), custom_call_target="tpu_custom_call" | custom-call | flops 134217728 | bytes 3670016 | tf_op jit(solution)/shard_map/states/pallas_call | solution.py:403
  4.6 7.1 %all-to-all-start = ((bf16[32,64,128]{2,1,0:T(8,128)(2,1)}), bf16[32,64,128]{2,1,0:T(8,128)(2,1)S(1)}, u32[]{:S(2)}, u32[]{:S(2)}) async-start(bf16[32,64,128]{2,1,0:T(8,128)(2,1)} %bitcast.10), calls=%async_computation | async-start | bytes 1048576 | tf_op jit(solution)/shard_map/all_to_all | solution.py:461
  11.7 3.3 %collective-permute-start = (bf16[16,128,128]{2,1,0:T(8,128)(2,1)}, bf16[16,128,128]{2,1,0:T(8,128)(2,1)S(1)}, u32[]{:S(2)}, u32[]{:S(2)}) collective-permute-start(bf16[16,128,128]{2,1,0:T(8,128)(2,1)} %get-tuple-element.30), channel_id=1, source_target_pairs={{0,1},{2,3},{4,5},{6,7},{8,9},{10,11},{12,13},{14,15},{16,17},{18,... | collective-permute-start | bytes 1572872 | tf_op jit(solution)/shard_map/ppermute | solution.py:458
  15.0 1.3 %collective-permute-start.1 = (bf16[16,128,128]{2,1,0:T(8,128)(2,1)}, bf16[16,128,128]{2,1,0:T(8,128)(2,1)S(1)}, u32[]{:S(2)}, u32[]{:S(2)}) collective-permute-start(bf16[16,128,128]{2,1,0:T(8,128)(2,1)} %get-tuple-element.32), channel_id=1, source_target_pairs={{0,1},{2,3},{4,5},{6,7},{8,9},{10,11},{12,13},{14,15},{16,17},{18,... | collective-permute-start | bytes 1572872 | tf_op jit(solution)/shard_map/ppermute | solution.py:458
  16.4 10.6 %all-to-all-done.refs_1_ = bf16[32,64,128]{2,1,0:T(8,128)(2,1)S(1)} async-done(((bf16[32,64,128]{2,1,0:T(8,128)(2,1)}), bf16[32,64,128]{2,1,0:T(8,128)(2,1)S(1)}, u32[]{:S(2)}, u32[]{:S(2)}) %all-to-all-start) | async-done | bytes 524320 | tf_op jit(solution)/shard_map/all_to_all | solution.py:461
  27.0 0.0 copy-done
  27.0 1.5 %scan.2 = (bf16[32,64,128]{2,1,0:T(8,128)(2,1)}, f32[8,128]{1,0:T(8,128)S(1)}) custom-call(s32[4]{0:T(128)S(1)} %copy-done, bf16[32,64,128]{2,1,0:T(8,128)(2,1)S(1)} %all-to-all-done.refs_1_), custom_call_target="tpu_custom_call" | custom-call | bytes 1052672 | tf_op jit(solution)/shard_map/scan/pallas_call | solution.py:403
  28.5 0.0 copy-start.4
  28.5 0.6 copy-done.4
  29.1 3.2 %all-to-all-start.1 = ((bf16[32,64,128]{2,1,0:T(8,128)(2,1)}), bf16[32,64,128]{2,1,0:T(8,128)(2,1)S(1)}, u32[]{:S(2)}, u32[]{:S(2)}) async-start(bf16[32,64,128]{2,1,0:T(8,128)(2,1)} %get-tuple-element.28), calls=%async_computation.1 | async-start | bytes 1048576 | tf_op jit(solution)/shard_map/all_to_all | solution.py:461
  32.3 0.0 collective-permute-done.refs_6_.refs_7_.refs_12_
  32.3 0.0 copy-start.7
  32.3 0.8 copy-done.7
  33.1 5.1 %inner.1.refs_4_ = f32[256,2048]{1,0:T(8,128)} custom-call(s32[4]{0:T(128)} %refs_0_.17, s32[2,6]{1,0:T(2,128)} %refs_1_.13, bf16[256,2048]{1,0:T(8,128)(2,1)} %refs_2_.6, bf16[256,2048]{1,0:T(8,128)(2,1)} %refs_2_.7, bf16[256,2048]{1,0:T(8,128)(2,1)} %refs_3_.13, f32[8,128]{1,0:T(8,128)} %copy-done.4, bf16[16,128,128]{2,1,0:T(8,128)(2,1)} %copy-done.7), custom_call_target="tpu_custom_call" | custom-call | flops 40000000000 | bytes 5242880 | tf_op jit(solution)/shard_map/inner/pallas_call | solution.py:403
  38.2 13.1 %all-to-all-done.1 = bf16[32,64,128]{2,1,0:T(8,128)(2,1)S(1)} async-done(((bf16[32,64,128]{2,1,0:T(8,128)(2,1)}), bf16[32,64,128]{2,1,0:T(8,128)(2,1)S(1)}, u32[]{:S(2)}, u32[]{:S(2)}) %all-to-all-start.1) | async-done | bytes 524320 | tf_op jit(solution)/shard_map/all_to_all | solution.py:461
  51.3 0.0 copy-start.5
  51.3 0.8 copy-done.5
  52.1 4.6 %norm.2 = (f32[128,128]{1,0:T(8,128)}, bf16[128,2048]{1,0:T(8,128)(2,1)}, bf16[128,2048]{1,0:T(8,128)(2,1)}, bf16[16,128,128]{2,1,0:T(8,128)(2,1)}) custom-call(s32[4]{0:T(128)} %refs_0_.17, s32[2,6]{1,0:T(2,128)} %refs_1_.13, f32[1,2048]{1,0:T(1,128)} %bitcast.11, bf16[256,2048]{1,0:T(8,128)(2,1)} %refs_2_.6, f32[256,2048]{1,0:T(8,128)} %inner.1.refs_4_, ...), custom_call_target="tpu_custom_call" | custom-call | flops 134217728 | bytes 6889472 | tf_op jit(solution)/shard_map/norm/pallas_call | solution.py:403
  56.7 1.3 %collective-permute-start.2 = (bf16[16,128,128]{2,1,0:T(8,128)(2,1)}, bf16[16,128,128]{2,1,0:T(8,128)(2,1)S(1)}, u32[]{:S(2)}, u32[]{:S(2)}) collective-permute-start(bf16[16,128,128]{2,1,0:T(8,128)(2,1)} %get-tuple-element.33.refs_8_), channel_id=1, source_target_pairs={{1,0},{3,2},{5,4},{7,6},{9,8},{11,10},{13,12},{15,14},{17,16},{19,... | collective-permute-start | bytes 1572872 | tf_op jit(solution)/shard_map/ppermute | solution.py:458
  58.0 0.0 collective-permute-done.1.refs_7_.refs_13_
  58.0 0.0 copy-start.8
  58.0 0.8 copy-done.8
  58.8 5.1 %norm.3 = (f32[128,128]{1,0:T(8,128)}, bf16[128,2048]{1,0:T(8,128)(2,1)}, bf16[128,2048]{1,0:T(8,128)(2,1)}, bf16[16,128,128]{2,1,0:T(8,128)(2,1)}, bf16[16,128,128]{2,1,0:T(8,128)(2,1)}) custom-call(s32[4]{0:T(128)} %refs_0_.17, s32[2,6]{1,0:T(2,128)} %refs_1_.13, f32[1,2048]{1,0:T(1,128)} %bitcast.12, bf16[256,2048]{1,0:T(8,128)(2,1)} %refs_2_.6, ...), custom_call_target="tpu_custom_call" | custom-call | flops 40000000000 | bytes 7938048 | tf_op jit(solution)/shard_map/norm/pallas_call | solution.py:403
  63.9 8.0 %all-to-all-start.2 = ((bf16[32,64,128]{2,1,0:T(8,128)(2,1)}), bf16[32,64,128]{2,1,0:T(8,128)(2,1)S(1)}, u32[]{:S(2)}, u32[]{:S(2)}) async-start(bf16[32,64,128]{2,1,0:T(8,128)(2,1)} %bitcast.9), calls=%async_computation.2 | async-start | bytes 1048576 | tf_op jit(solution)/shard_map/all_to_all | solution.py:461
  71.9 1.3 %collective-permute-start.3 = (bf16[16,128,128]{2,1,0:T(8,128)(2,1)}, bf16[16,128,128]{2,1,0:T(8,128)(2,1)S(1)}, u32[]{:S(2)}, u32[]{:S(2)}) collective-permute-start(bf16[16,128,128]{2,1,0:T(8,128)(2,1)} %get-tuple-element.41), channel_id=1, source_target_pairs={{1,0},{3,2},{5,4},{7,6},{9,8},{11,10},{13,12},{15,14},{17,16},{19,... | collective-permute-start | bytes 1572872 | tf_op jit(solution)/shard_map/ppermute | solution.py:458
  73.2 0.6 collective-permute-done.2.refs_14_.refs_7_
  73.8 0.0 copy-start.9
  73.8 0.8 copy-done.9
  74.5 0.0 copy-start.1
  74.6 8.4 %query_grads.1 = (bf16[256,2048]{1,0:T(8,128)(2,1)}, bf16[256,2048]{1,0:T(8,128)(2,1)}, f32[8,128]{1,0:T(8,128)}) custom-call(s32[4]{0:T(128)} %refs_0_.17, s32[2,6]{1,0:T(2,128)} %refs_1_.13, f32[1,2048]{1,0:T(1,128)} %bitcast.13, bf16[256,2048]{1,0:T(8,128)(2,1)} %refs_2_.7, bf16[256,2048]{1,0:T(8,128)(2,1)} %refs_3_.13, bf16[16,128,128]{2,1,0:T(8,128)(2,1)} %bitcast.7, ...), custom_call_target="tpu_custom_call" | custom-call | flops 40000000000 | bytes 8007680 | tf_op jit(solution)/shard_map/query_grads/pallas_call | solution.py:403
  83.0 4.2 %all-to-all-done.2.refs_1_ = bf16[32,64,128]{2,1,0:T(8,128)(2,1)S(1)} async-done(((bf16[32,64,128]{2,1,0:T(8,128)(2,1)}), bf16[32,64,128]{2,1,0:T(8,128)(2,1)S(1)}, u32[]{:S(2)}, u32[]{:S(2)}) %all-to-all-start.2) | async-done | bytes 524320 | tf_op jit(solution)/shard_map/all_to_all | solution.py:461
  87.2 0.0 copy-done.1
  87.2 0.0 copy-start.2
  87.2 0.7 copy-done.2
  87.9 1.5 %scan.3 = (bf16[32,64,128]{2,1,0:T(8,128)(2,1)}, f32[8,128]{1,0:T(8,128)S(1)}) custom-call(s32[4]{0:T(128)S(1)} %copy-done.1, bf16[32,64,128]{2,1,0:T(8,128)(2,1)S(1)} %all-to-all-done.2.refs_1_, f32[8,128]{1,0:T(8,128)S(1)} %copy-done.2), custom_call_target="tpu_custom_call" | custom-call | bytes 1052672 | tf_op jit(solution)/shard_map/scan/pallas_call | solution.py:403
  89.4 0.0 copy-start.3
  89.4 0.6 copy-done.3
  90.0 3.1 %all-to-all-start.3 = ((bf16[32,64,128]{2,1,0:T(8,128)(2,1)}), bf16[32,64,128]{2,1,0:T(8,128)(2,1)S(1)}, u32[]{:S(2)}, u32[]{:S(2)}) async-start(bf16[32,64,128]{2,1,0:T(8,128)(2,1)} %get-tuple-element.47), calls=%async_computation.3 | async-start | bytes 1048576 | tf_op jit(solution)/shard_map/all_to_all | solution.py:461
  93.2 0.6 collective-permute-done.3.refs_8_
  93.8 0.0 copy-start.10
  93.8 0.8 copy-done.10
  94.6 10.1 %key_grads.1 = (f32[256,2048]{1,0:T(8,128)}, f32[256,2048]{1,0:T(8,128)}) custom-call(s32[4]{0:T(128)} %refs_0_.17, s32[2,6]{1,0:T(2,128)} %refs_1_.13, bf16[256,2048]{1,0:T(8,128)(2,1)} %refs_2_.6, bf16[256,2048]{1,0:T(8,128)(2,1)} %refs_2_.7, bf16[256,2048]{1,0:T(8,128)(2,1)} %refs_3_.13, bf16[128,2048]{1,0:T(8,128)(2,1)} %get-tuple-element.31.refs_6_.refs_5_, ...), custom_call_target="tpu_custom_call" | custom-call | flops 40000000000 | bytes 9437184 | tf_op jit(solution)/shard_map/key_grads/pallas_call | solution.py:403
  104.7 3.8 %all-to-all-done.3 = bf16[32,64,128]{2,1,0:T(8,128)(2,1)S(1)} async-done(((bf16[32,64,128]{2,1,0:T(8,128)(2,1)}), bf16[32,64,128]{2,1,0:T(8,128)(2,1)S(1)}, u32[]{:S(2)}, u32[]{:S(2)}) %all-to-all-start.3) | async-done | bytes 524320 | tf_op jit(solution)/shard_map/all_to_all | solution.py:461
  108.4 0.0 copy-start.6
  108.4 0.8 copy-done.6
  109.3 5.2 %last.1 = (bf16[256,2048]{1,0:T(8,128)(2,1)}, bf16[256,2048]{1,0:T(8,128)(2,1)}) custom-call(s32[4]{0:T(128)} %refs_0_.17, s32[2,6]{1,0:T(2,128)} %refs_1_.13, bf16[256,2048]{1,0:T(8,128)(2,1)} %refs_2_.7, bf16[256,2048]{1,0:T(8,128)(2,1)} %refs_3_.13, f32[256,2048]{1,0:T(8,128)} %get-tuple-element.45.refs_4_, f32[256,2048]{1,0:T(8,128)} %get-tuple-element.46.refs_5_, ...), custom_call_target="tpu_custom_call" | custom-call | flops 268435456 | bytes 8912896 | tf_op jit(solution)/shard_map/last/pallas_call | solution.py:403
Async XLA Ops:
  0.6 26.4 %copy-start = (s32[4]{0:T(128)S(1)}, s32[4]{0:T(128)}, u32[]{:S(2)}) copy-start(s32[4]{0:T(128)} %refs_0_.17) | copy-start | bytes 52
  4.6 22.4 %all-to-all-start = ((bf16[32,64,128]{2,1,0:T(8,128)(2,1)}), bf16[32,64,128]{2,1,0:T(8,128)(2,1)S(1)}, u32[]{:S(2)}, u32[]{:S(2)}) async-start(bf16[32,64,128]{2,1,0:T(8,128)(2,1)} %bitcast.10), calls=%async_computation | async-start | bytes 1048576 | tf_op jit(solution)/shard_map/all_to_all | solution.py:461
  11.7 20.6 %collective-permute-start = (bf16[16,128,128]{2,1,0:T(8,128)(2,1)}, bf16[16,128,128]{2,1,0:T(8,128)(2,1)S(1)}, u32[]{:S(2)}, u32[]{:S(2)}) collective-permute-start(bf16[16,128,128]{2,1,0:T(8,128)(2,1)} %get-tuple-element.30), channel_id=1, source_target_pairs={{0,1},{2,3},{4,5},{6,7},{8,9},{10,11},{12,13},{14,15},{16,17},{18,... | collective-permute-start | bytes 1572872 | tf_op jit(solution)/shard_map/ppermute | solution.py:458
  15.0 43.0 %collective-permute-start.1 = (bf16[16,128,128]{2,1,0:T(8,128)(2,1)}, bf16[16,128,128]{2,1,0:T(8,128)(2,1)S(1)}, u32[]{:S(2)}, u32[]{:S(2)}) collective-permute-start(bf16[16,128,128]{2,1,0:T(8,128)(2,1)} %get-tuple-element.32), channel_id=1, source_target_pairs={{0,1},{2,3},{4,5},{6,7},{8,9},{10,11},{12,13},{14,15},{16,17},{18,... | collective-permute-start | bytes 1572872 | tf_op jit(solution)/shard_map/ppermute | solution.py:458
  28.5 0.6 copy-start.4
  29.1 22.2 %all-to-all-start.1 = ((bf16[32,64,128]{2,1,0:T(8,128)(2,1)}), bf16[32,64,128]{2,1,0:T(8,128)(2,1)S(1)}, u32[]{:S(2)}, u32[]{:S(2)}) async-start(bf16[32,64,128]{2,1,0:T(8,128)(2,1)} %get-tuple-element.28), calls=%async_computation.1 | async-start | bytes 1048576 | tf_op jit(solution)/shard_map/all_to_all | solution.py:461
  32.3 0.8 copy-start.7
  51.3 0.8 copy-start.5
  56.7 17.0 %collective-permute-start.2 = (bf16[16,128,128]{2,1,0:T(8,128)(2,1)}, bf16[16,128,128]{2,1,0:T(8,128)(2,1)S(1)}, u32[]{:S(2)}, u32[]{:S(2)}) collective-permute-start(bf16[16,128,128]{2,1,0:T(8,128)(2,1)} %get-tuple-element.33.refs_8_), channel_id=1, source_target_pairs={{1,0},{3,2},{5,4},{7,6},{9,8},{11,10},{13,12},{15,14},{17,16},{19,... | collective-permute-start | bytes 1572872 | tf_op jit(solution)/shard_map/ppermute | solution.py:458
  58.0 0.8 copy-start.8
  63.9 23.3 %all-to-all-start.2 = ((bf16[32,64,128]{2,1,0:T(8,128)(2,1)}), bf16[32,64,128]{2,1,0:T(8,128)(2,1)S(1)}, u32[]{:S(2)}, u32[]{:S(2)}) async-start(bf16[32,64,128]{2,1,0:T(8,128)(2,1)} %bitcast.9), calls=%async_computation.2 | async-start | bytes 1048576 | tf_op jit(solution)/shard_map/all_to_all | solution.py:461
  71.9 21.9 %collective-permute-start.3 = (bf16[16,128,128]{2,1,0:T(8,128)(2,1)}, bf16[16,128,128]{2,1,0:T(8,128)(2,1)S(1)}, u32[]{:S(2)}, u32[]{:S(2)}) collective-permute-start(bf16[16,128,128]{2,1,0:T(8,128)(2,1)} %get-tuple-element.41), channel_id=1, source_target_pairs={{1,0},{3,2},{5,4},{7,6},{9,8},{11,10},{13,12},{15,14},{17,16},{19,... | collective-permute-start | bytes 1572872 | tf_op jit(solution)/shard_map/ppermute | solution.py:458
  73.8 0.8 copy-start.9
  74.5 12.7 %copy-start.1 = (s32[4]{0:T(128)S(1)}, s32[4]{0:T(128)}, u32[]{:S(2)}) copy-start(s32[4]{0:T(128)} %refs_0_.17) | copy-start | bytes 52
  87.2 0.7 copy-start.2
  89.4 0.6 copy-start.3
  90.0 18.4 %all-to-all-start.3 = ((bf16[32,64,128]{2,1,0:T(8,128)(2,1)}), bf16[32,64,128]{2,1,0:T(8,128)(2,1)S(1)}, u32[]{:S(2)}, u32[]{:S(2)}) async-start(bf16[32,64,128]{2,1,0:T(8,128)(2,1)} %get-tuple-element.47), calls=%async_computation.3 | async-start | bytes 1048576 | tf_op jit(solution)/shard_map/all_to_all | solution.py:461
  93.8 0.8 copy-start.10
  108.4 0.8 copy-start.6

commit v8 on v7

--- a/solution.py
+++ b/solution.py
@@ -11,8 +11,9 @@
 GROUP = 512
 BLOCK = 128
 CHUNKS = 4
-LONG = 40_000_000_000
+LONG = 400_000_000_000
 VMEM_BYTES = 60 * 1024 * 1024
+NARROW_BYTES = 53 * 1024 * 1024
 SOME_BYTES = 24 * 1024 * 1024
 
 eps_norm = 1e-06
@@ -579,6 +580,7 @@
         heads,
         chunks,
         flops=2 * unit,
+        limit=NARROW_BYTES,
     )
     return output, grad_q, grad_k, grad_v
 

time: 116 us -> 115 us (level)
  local copies, waits for them, and re-layouts: 6.65 us -> 2.66 us
  starting transfers between devices: 28.6 us -> 30.5 us
    unnamed x22 -> x16, local copies, waits for them, and re-layouts: 6.65 us -> 2.66 us
    all_to_all x4, waiting for transfers between devices: 31.7 us -> 32.9 us  [exchanged(): return lax.all_to_all(slices, AXES, split_axis=0, concat_axis=0, tiled=True)]
  transfers between devices with their start and end apart: 8 -> 8, of which waited for: 6 -> 5; matrix products, arithmetic and copies ran while one was open for 0% -> 0% of each run, Pallas kernels for 32% -> 32%
where the time goes in v8:
time: 115 us; the launch traced here: 114 us
  Pallas kernels  45.9 us (40%)
  waiting for transfers between devices  33.6 us (29%)
  starting transfers between devices  30.5 us (27%)
  local copies, waits for them, and re-layouts  2.66 us (2%)
    pallas_call x9, Pallas kernels, call(): pl.pallas_call(kernel, name=name, in_specs=[*[pl.BlockSpec(memory_space=p...  45.9 us
    all_to_all x4, waiting for transfers between devices, exchanged(): return lax.all_to_all(slices, AXES, split_axis=0, concat_axis=0, tiled=True)  32.9 us
    all_to_all x4, starting transfers between devices, exchanged(): return lax.all_to_all(slices, AXES, split_axis=0, concat_axis=0, tiled=True)  22.5 us
    ppermute x4, starting transfers between devices, to_peers(): return lax.ppermute(array, 'head', pairs)  8 us
    unnamed x16, local copies, waits for them, and re-layouts  2.66 us
  transfers between devices with their start and end apart: 8, of which 5 were waited for; matrix products, arithmetic and copies ran while one was open for 0% of the time, Pallas kernels for 32%

profile of v8, /device:TPU:1, one launch (start us, length us, event | category | flops | bytes accessed | tf_op | source)
XLA Modules:
  0.0 113.6 jit_solution(12274141028819585490)
XLA Ops:
  0.6 0.0 copy-start
  0.6 3.9 %states.1 = (bf16[16,128,128]{2,1,0:T(8,128)(2,1)}, bf16[16,128,128]{2,1,0:T(8,128)(2,1)}, bf16[16,128,128]{2,1,0:T(8,128)(2,1)}) custom-call(s32[4]{0:T(128)} %refs_0_.17, s32[2,6]{1,0:T(2,128)} %refs_1_.13, bf16[256,2048]{1,0:T(8,128)(2,1)} %refs_2_.7, bf16[256,2048]{1,0:T(8,128)(2,1)} %refs_3_.13), custom_call_target="tpu_custom_call" | custom-call | flops 134217728 | bytes 3670016 | tf_op jit(solution)/shard_map/states/pallas_call | solution.py:404
  4.6 7.1 %all-to-all-start = ((bf16[32,64,128]{2,1,0:T(8,128)(2,1)}), bf16[32,64,128]{2,1,0:T(8,128)(2,1)S(1)}, u32[]{:S(2)}, u32[]{:S(2)}) async-start(bf16[32,64,128]{2,1,0:T(8,128)(2,1)} %bitcast.6), calls=%async_computation | async-start | bytes 1048576 | tf_op jit(solution)/shard_map/all_to_all | solution.py:462
  11.7 3.3 %collective-permute-start = (bf16[16,128,128]{2,1,0:T(8,128)(2,1)}, bf16[16,128,128]{2,1,0:T(8,128)(2,1)S(1)}, u32[]{:S(2)}, u32[]{:S(2)}) collective-permute-start(bf16[16,128,128]{2,1,0:T(8,128)(2,1)} %get-tuple-element.30), channel_id=1, source_target_pairs={{0,1},{2,3},{4,5},{6,7},{8,9},{10,11},{12,13},{14,15},{16,17},{18,... | collective-permute-start | bytes 1572872 | tf_op jit(solution)/shard_map/ppermute | solution.py:459
  15.0 2.1 %collective-permute-start.1 = (bf16[16,128,128]{2,1,0:T(8,128)(2,1)}, bf16[16,128,128]{2,1,0:T(8,128)(2,1)}, u32[]{:S(2)}, u32[]{:S(2)}) collective-permute-start(bf16[16,128,128]{2,1,0:T(8,128)(2,1)} %get-tuple-element.32), channel_id=1, source_target_pairs={{0,1},{2,3},{4,5},{6,7},{8,9},{10,11},{12,13},{14,15},{16,17},{18,... | collective-permute-start | bytes 1572872 | tf_op jit(solution)/shard_map/ppermute | solution.py:459
  17.1 9.9 %all-to-all-done.refs_1_ = bf16[32,64,128]{2,1,0:T(8,128)(2,1)S(1)} async-done(((bf16[32,64,128]{2,1,0:T(8,128)(2,1)}), bf16[32,64,128]{2,1,0:T(8,128)(2,1)S(1)}, u32[]{:S(2)}, u32[]{:S(2)}) %all-to-all-start) | async-done | bytes 524320 | tf_op jit(solution)/shard_map/all_to_all | solution.py:462
  27.0 0.0 copy-done
  27.0 1.5 %scan.2 = (bf16[32,64,128]{2,1,0:T(8,128)(2,1)}, f32[8,128]{1,0:T(8,128)S(1)}) custom-call(s32[4]{0:T(128)S(1)} %copy-done, bf16[32,64,128]{2,1,0:T(8,128)(2,1)S(1)} %all-to-all-done.refs_1_), custom_call_target="tpu_custom_call" | custom-call | bytes 1052672 | tf_op jit(solution)/shard_map/scan/pallas_call | solution.py:404
  28.5 0.0 copy-start.6
  28.5 0.6 copy-done.6
  29.1 3.2 %all-to-all-start.1 = ((bf16[32,64,128]{2,1,0:T(8,128)(2,1)}), bf16[32,64,128]{2,1,0:T(8,128)(2,1)}, u32[]{:S(2)}, u32[]{:S(2)}) async-start(bf16[32,64,128]{2,1,0:T(8,128)(2,1)} %get-tuple-element.28), calls=%async_computation.1 | async-start | bytes 1048576 | tf_op jit(solution)/shard_map/all_to_all | solution.py:462
  32.4 0.0 collective-permute-done.refs_6_.refs_7_.refs_12_
  32.4 0.0 copy-start.7
  32.4 0.8 copy-done.7
  33.2 5.1 %inner.1.refs_4_ = f32[256,2048]{1,0:T(8,128)} custom-call(s32[4]{0:T(128)} %refs_0_.17, s32[2,6]{1,0:T(2,128)} %refs_1_.13, bf16[256,2048]{1,0:T(8,128)(2,1)} %refs_2_.6, bf16[256,2048]{1,0:T(8,128)(2,1)} %refs_2_.7, bf16[256,2048]{1,0:T(8,128)(2,1)} %refs_3_.13, f32[8,128]{1,0:T(8,128)} %copy-done.6, bf16[16,128,128]{2,1,0:T(8,128)(2,1)} %copy-done.7), custom_call_target="tpu_custom_call" | custom-call | flops 399999991808 | bytes 5242880 | tf_op jit(solution)/shard_map/inner/pallas_call | solution.py:404
  38.3 13.1 %all-to-all-done.1 = bf16[32,64,128]{2,1,0:T(8,128)(2,1)} async-done(((bf16[32,64,128]{2,1,0:T(8,128)(2,1)}), bf16[32,64,128]{2,1,0:T(8,128)(2,1)}, u32[]{:S(2)}, u32[]{:S(2)}) %all-to-all-start.1) | async-done | bytes 524320 | tf_op jit(solution)/shard_map/all_to_all | solution.py:462
  51.3 4.6 %norm.2 = (f32[128,128]{1,0:T(8,128)}, bf16[128,2048]{1,0:T(8,128)(2,1)}, bf16[128,2048]{1,0:T(8,128)(2,1)}, bf16[16,128,128]{2,1,0:T(8,128)(2,1)}) custom-call(s32[4]{0:T(128)} %refs_0_.17, s32[2,6]{1,0:T(2,128)} %refs_1_.13, f32[1,2048]{1,0:T(1,128)} %bitcast.7, bf16[256,2048]{1,0:T(8,128)(2,1)} %refs_2_.6, f32[256,2048]{1,0:T(8,128)} %inner.1.refs_4_, ...), custom_call_target="tpu_custom_call" | custom-call | flops 134217728 | bytes 6889472 | tf_op jit(solution)/shard_map/norm/pallas_call | solution.py:404
  55.9 1.3 %collective-permute-start.2 = (bf16[16,128,128]{2,1,0:T(8,128)(2,1)}, bf16[16,128,128]{2,1,0:T(8,128)(2,1)}, u32[]{:S(2)}, u32[]{:S(2)}) collective-permute-start(bf16[16,128,128]{2,1,0:T(8,128)(2,1)} %get-tuple-element.33.refs_8_), channel_id=1, source_target_pairs={{1,0},{3,2},{5,4},{7,6},{9,8},{11,10},{13,12},{15,14},{17,16},{19,... | collective-permute-start | bytes 1572872 | tf_op jit(solution)/shard_map/ppermute | solution.py:459
  57.2 0.0 collective-permute-done.1.refs_7_.refs_13_
  57.2 5.1 %norm.3 = (f32[128,128]{1,0:T(8,128)}, bf16[128,2048]{1,0:T(8,128)(2,1)}, bf16[128,2048]{1,0:T(8,128)(2,1)}, bf16[16,128,128]{2,1,0:T(8,128)(2,1)}, bf16[16,128,128]{2,1,0:T(8,128)(2,1)}) custom-call(s32[4]{0:T(128)} %refs_0_.17, s32[2,6]{1,0:T(2,128)} %refs_1_.13, f32[1,2048]{1,0:T(1,128)} %bitcast.8, bf16[256,2048]{1,0:T(8,128)(2,1)} %refs_2_.6, ...), custom_call_target="tpu_custom_call" | custom-call | flops 399999991808 | bytes 7938048 | tf_op jit(solution)/shard_map/norm/pallas_call | solution.py:404
  62.3 8.9 %all-to-all-start.2 = ((bf16[32,64,128]{2,1,0:T(8,128)(2,1)}), bf16[32,64,128]{2,1,0:T(8,128)(2,1)}, u32[]{:S(2)}, u32[]{:S(2)}) async-start(bf16[32,64,128]{2,1,0:T(8,128)(2,1)} %bitcast.5), calls=%async_computation.2 | async-start | bytes 1048576 | tf_op jit(solution)/shard_map/all_to_all | solution.py:462
  71.2 1.3 %collective-permute-start.3 = (bf16[16,128,128]{2,1,0:T(8,128)(2,1)}, bf16[16,128,128]{2,1,0:T(8,128)(2,1)}, u32[]{:S(2)}, u32[]{:S(2)}) collective-permute-start(bf16[16,128,128]{2,1,0:T(8,128)(2,1)} %get-tuple-element.41), channel_id=1, source_target_pairs={{1,0},{3,2},{5,4},{7,6},{9,8},{11,10},{13,12},{15,14},{17,16},{19,... | collective-permute-start | bytes 1572872 | tf_op jit(solution)/shard_map/ppermute | solution.py:459
  72.5 0.7 collective-permute-done.2.refs_14_.refs_7_
  73.2 0.0 copy-start.1
  73.2 8.5 %query_grads.1 = (bf16[256,2048]{1,0:T(8,128)(2,1)}, bf16[256,2048]{1,0:T(8,128)(2,1)}, f32[8,128]{1,0:T(8,128)}) custom-call(s32[4]{0:T(128)} %refs_0_.17, s32[2,6]{1,0:T(2,128)} %refs_1_.13, f32[1,2048]{1,0:T(1,128)} %bitcast.9, bf16[256,2048]{1,0:T(8,128)(2,1)} %refs_2_.7, bf16[256,2048]{1,0:T(8,128)(2,1)} %refs_3_.13, ...), custom_call_target="tpu_custom_call" | custom-call | flops 399999991808 | bytes 8007680 | tf_op jit(solution)/shard_map/query_grads/pallas_call | solution.py:404
  81.6 4.9 %all-to-all-done.2.refs_1_ = bf16[32,64,128]{2,1,0:T(8,128)(2,1)} async-done(((bf16[32,64,128]{2,1,0:T(8,128)(2,1)}), bf16[32,64,128]{2,1,0:T(8,128)(2,1)}, u32[]{:S(2)}, u32[]{:S(2)}) %all-to-all-start.2) | async-done | bytes 524320 | tf_op jit(solution)/shard_map/all_to_all | solution.py:462
  86.6 0.0 copy-done.1
  86.6 0.0 copy-start.4
  86.6 0.7 copy-done.4
  87.2 2.0 %scan.3 = (bf16[32,64,128]{2,1,0:T(8,128)(2,1)}, f32[8,128]{1,0:T(8,128)S(1)}) custom-call(s32[4]{0:T(128)S(1)} %copy-done.1, bf16[32,64,128]{2,1,0:T(8,128)(2,1)} %all-to-all-done.2.refs_1_, f32[8,128]{1,0:T(8,128)S(1)} %copy-done.4), custom_call_target="tpu_custom_call" | custom-call | bytes 1052672 | tf_op jit(solution)/shard_map/scan/pallas_call | solution.py:404
  89.3 0.0 copy-start.5
  89.3 0.6 copy-done.5
  89.9 3.3 %all-to-all-start.3 = ((bf16[32,64,128]{2,1,0:T(8,128)(2,1)}), bf16[32,64,128]{2,1,0:T(8,128)(2,1)}, u32[]{:S(2)}, u32[]{:S(2)}) async-start(bf16[32,64,128]{2,1,0:T(8,128)(2,1)} %get-tuple-element.47), calls=%async_computation.3 | async-start | bytes 1048576 | tf_op jit(solution)/shard_map/all_to_all | solution.py:462
  93.1 0.0 collective-permute-done.3.refs_8_
  93.2 0.0 copy-start.2
  93.2 0.0 copy-start.3
  93.2 10.2 %key_grads.1 = (f32[256,2048]{1,0:T(8,128)}, f32[256,2048]{1,0:T(8,128)}) custom-call(s32[4]{0:T(128)} %refs_0_.17, s32[2,6]{1,0:T(2,128)} %refs_1_.13, bf16[256,2048]{1,0:T(8,128)(2,1)} %refs_2_.6, bf16[256,2048]{1,0:T(8,128)(2,1)} %refs_2_.7, bf16[256,2048]{1,0:T(8,128)(2,1)} %refs_3_.13, bf16[128,2048]{1,0:T(8,128)(2,1)} %get-tuple-element.31.refs_6_.refs_5_, ...), custom_call_target="tpu_custom_call" | custom-call | flops 399999991808 | bytes 9437184 | tf_op jit(solution)/shard_map/key_grads/pallas_call | solution.py:404
  103.3 5.1 %all-to-all-done.3 = bf16[32,64,128]{2,1,0:T(8,128)(2,1)} async-done(((bf16[32,64,128]{2,1,0:T(8,128)(2,1)}), bf16[32,64,128]{2,1,0:T(8,128)(2,1)}, u32[]{:S(2)}, u32[]{:S(2)}) %all-to-all-start.3) | async-done | bytes 524320 | tf_op jit(solution)/shard_map/all_to_all | solution.py:462
  108.4 0.0 copy-done.2
  108.4 0.0 copy-done.3
  108.4 5.1 %last.1 = (bf16[256,2048]{1,0:T(8,128)(2,1)}, bf16[256,2048]{1,0:T(8,128)(2,1)}) custom-call(s32[4]{0:T(128)S(1)} %copy-done.2, s32[2,6]{1,0:T(2,128)S(1)} %copy-done.3, bf16[256,2048]{1,0:T(8,128)(2,1)} %refs_2_.7, bf16[256,2048]{1,0:T(8,128)(2,1)} %refs_3_.13, f32[256,2048]{1,0:T(8,128)} %get-tuple-element.45.refs_4_, ...), custom_call_target="tpu_custom_call" | custom-call | flops 268435456 | bytes 8912896 | tf_op jit(solution)/shard_map/last/pallas_call | solution.py:404
Async XLA Ops:
  0.6 26.4 %copy-start = (s32[4]{0:T(128)S(1)}, s32[4]{0:T(128)}, u32[]{:S(2)}) copy-start(s32[4]{0:T(128)} %refs_0_.17) | copy-start | bytes 52
  4.6 22.4 %all-to-all-start = ((bf16[32,64,128]{2,1,0:T(8,128)(2,1)}), bf16[32,64,128]{2,1,0:T(8,128)(2,1)S(1)}, u32[]{:S(2)}, u32[]{:S(2)}) async-start(bf16[32,64,128]{2,1,0:T(8,128)(2,1)} %bitcast.6), calls=%async_computation | async-start | bytes 1048576 | tf_op jit(solution)/shard_map/all_to_all | solution.py:462
  11.7 20.7 %collective-permute-start = (bf16[16,128,128]{2,1,0:T(8,128)(2,1)}, bf16[16,128,128]{2,1,0:T(8,128)(2,1)S(1)}, u32[]{:S(2)}, u32[]{:S(2)}) collective-permute-start(bf16[16,128,128]{2,1,0:T(8,128)(2,1)} %get-tuple-element.30), channel_id=1, source_target_pairs={{0,1},{2,3},{4,5},{6,7},{8,9},{10,11},{12,13},{14,15},{16,17},{18,... | collective-permute-start | bytes 1572872 | tf_op jit(solution)/shard_map/ppermute | solution.py:459
  15.0 42.2 %collective-permute-start.1 = (bf16[16,128,128]{2,1,0:T(8,128)(2,1)}, bf16[16,128,128]{2,1,0:T(8,128)(2,1)}, u32[]{:S(2)}, u32[]{:S(2)}) collective-permute-start(bf16[16,128,128]{2,1,0:T(8,128)(2,1)} %get-tuple-element.32), channel_id=1, source_target_pairs={{0,1},{2,3},{4,5},{6,7},{8,9},{10,11},{12,13},{14,15},{16,17},{18,... | collective-permute-start | bytes 1572872 | tf_op jit(solution)/shard_map/ppermute | solution.py:459
  28.5 0.6 copy-start.6
  29.1 22.2 %all-to-all-start.1 = ((bf16[32,64,128]{2,1,0:T(8,128)(2,1)}), bf16[32,64,128]{2,1,0:T(8,128)(2,1)}, u32[]{:S(2)}, u32[]{:S(2)}) async-start(bf16[32,64,128]{2,1,0:T(8,128)(2,1)} %get-tuple-element.28), calls=%async_computation.1 | async-start | bytes 1048576 | tf_op jit(solution)/shard_map/all_to_all | solution.py:462
  32.4 0.8 copy-start.7
  55.9 17.3 %collective-permute-start.2 = (bf16[16,128,128]{2,1,0:T(8,128)(2,1)}, bf16[16,128,128]{2,1,0:T(8,128)(2,1)}, u32[]{:S(2)}, u32[]{:S(2)}) collective-permute-start(bf16[16,128,128]{2,1,0:T(8,128)(2,1)} %get-tuple-element.33.refs_8_), channel_id=1, source_target_pairs={{1,0},{3,2},{5,4},{7,6},{9,8},{11,10},{13,12},{15,14},{17,16},{19,... | collective-permute-start | bytes 1572872 | tf_op jit(solution)/shard_map/ppermute | solution.py:459
  62.3 24.3 %all-to-all-start.2 = ((bf16[32,64,128]{2,1,0:T(8,128)(2,1)}), bf16[32,64,128]{2,1,0:T(8,128)(2,1)}, u32[]{:S(2)}, u32[]{:S(2)}) async-start(bf16[32,64,128]{2,1,0:T(8,128)(2,1)} %bitcast.5), calls=%async_computation.2 | async-start | bytes 1048576 | tf_op jit(solution)/shard_map/all_to_all | solution.py:462
  71.2 22.0 %collective-permute-start.3 = (bf16[16,128,128]{2,1,0:T(8,128)(2,1)}, bf16[16,128,128]{2,1,0:T(8,128)(2,1)}, u32[]{:S(2)}, u32[]{:S(2)}) collective-permute-start(bf16[16,128,128]{2,1,0:T(8,128)(2,1)} %get-tuple-element.41), channel_id=1, source_target_pairs={{1,0},{3,2},{5,4},{7,6},{9,8},{11,10},{13,12},{15,14},{17,16},{19,... | collective-permute-start | bytes 1572872 | tf_op jit(solution)/shard_map/ppermute | solution.py:459
  73.2 13.4 %copy-start.1 = (s32[4]{0:T(128)S(1)}, s32[4]{0:T(128)}, u32[]{:S(2)}) copy-start(s32[4]{0:T(128)} %refs_0_.17) | copy-start | bytes 52
  86.6 0.7 copy-start.4
  89.3 0.6 copy-start.5
  89.9 18.5 %all-to-all-start.3 = ((bf16[32,64,128]{2,1,0:T(8,128)(2,1)}), bf16[32,64,128]{2,1,0:T(8,128)(2,1)}, u32[]{:S(2)}, u32[]{:S(2)}) async-start(bf16[32,64,128]{2,1,0:T(8,128)(2,1)} %get-tuple-element.47), calls=%async_computation.3 | async-start | bytes 1048576 | tf_op jit(solution)/shard_map/all_to_all | solution.py:462
  93.2 15.3 %copy-start.2 = (s32[4]{0:T(128)S(1)}, s32[4]{0:T(128)}, u32[]{:S(2)}) copy-start(s32[4]{0:T(128)} %refs_0_.17) | copy-start | bytes 52
  93.2 15.3 %copy-start.3 = (s32[2,6]{1,0:T(2,128)S(1)}, s32[2,6]{1,0:T(2,128)}, u32[]{:S(2)}) copy-start(s32[2,6]{1,0:T(2,128)} %refs_1_.13) | copy-start | bytes 148

commit v9 on v8

--- a/solution.py
+++ b/solution.py
@@ -130,6 +130,25 @@
     return total.astype(BF)
 
 
+class Joined:
+    def __init__(self, refs):
+        self.refs, self.each = refs, refs[0].shape[0]
+
+    def __getitem__(self, head):
+        return self.refs[head // self.each][head % self.each]
+
+    def __setitem__(self, head, value):
+        self.refs[head // self.each][head % self.each] = value
+
+
+def joined(refs, counts):
+    result, at = [], 0
+    for count in counts:
+        result.append(Joined(refs[at : at + count]))
+        at += count
+    return result
+
+
 def columns(head):
     return pl.ds(head * DH, DH)
 
@@ -138,8 +157,9 @@
     return pl.ds(block * BLOCK, BLOCK)
 
 
-def state_body(place_of, ins, outs, scratch, arrive, leave, chunks):
+def state_body(place_of, ins, outs, scratch, arrive, leave, chunks, *, counts):
     k_ref, v_ref = ins
+    outs = joined(outs, counts)
     rows, width = k_ref.shape
     place = place_of(rows)
     last = place.seg(place.start(place.blocks) - 1)
@@ -211,9 +231,10 @@
         leave(c)
 
 
-def norm_body(place_of, ins, outs, scratch, arrive, leave, chunks, *, rows, block, peers):
+def norm_body(place_of, ins, outs, scratch, arrive, leave, chunks, *, rows, block, counts):
     gain_ref, q_ref, raw_ref, grad_ref = ins[:4]
-    state_refs, earlier_refs = ins[4 : 5 + peers], ins[5 + peers :]
+    held = 4 + sum(counts)
+    state_refs, earlier_refs = joined(ins[4:held], counts), ins[held:]
     scale_ref, held_ref, d_ref, w_ref, *t_refs = outs
     width = q_ref.shape[1]
     place = place_of(rows)
@@ -257,14 +278,14 @@
         leave(c, range(2, len(outs)))
 
 
-def query_grads_body(place_of, ins, outs, scratch, arrive, leave, chunks, *, peers):
+def query_grads_body(place_of, ins, outs, scratch, arrive, leave, chunks, *, peers, counts):
     gain_ref, k_ref, v_ref, kv_ref = ins[:4]
     rows, width = k_ref.shape
     place = place_of(rows)
     blocks = place.blocks
     rest = ins[4:]
     d_refs, raw_refs, scale_refs = rest[:blocks], rest[blocks : 2 * blocks], rest[2 * blocks : 3 * blocks]
-    peer_refs = rest[3 * blocks :]
+    peer_refs = joined(rest[3 * blocks :], counts)
     out_ref, gq_ref, token_ref = outs
     (weight_ref,) = scratch
     token_ref[...] = jnp.zeros_like(token_ref)
@@ -336,8 +357,9 @@
 
 
 class Part:
-    def __init__(self, array, axis=None, block=None, near=False):
+    def __init__(self, array, axis=None, block=None, near=False, lead=0, parts=None):
         self.array, self.axis, self.block, self.near = array, axis, block, near
+        self.lead, self.parts = lead, parts
         self.shape = array.shape if block is None else (BLOCK, *array.shape[1:])
         self.spec = pl.BlockSpec(memory_space=pltpu.VMEM if near else pltpu.HBM)
 
@@ -345,8 +367,9 @@
         far = far if self.block is None else far.at[rows_of(self.block)]
         if self.axis is None:
             return [(far, near, sems.at[0])]
+        count = self.parts or count
         size = self.shape[self.axis] // count
-        result = []
+        result = [None] * self.lead
         for c in range(count):
             at = [slice(None)] * len(self.shape)
             at[self.axis] = pl.ds(c * size, size)
@@ -378,7 +401,7 @@
 
         def copies(parts, c, which=None):
             for i, pieces in enumerate(parts):
-                if c < len(pieces) and (which is None or i in which):
+                if c < len(pieces) and pieces[c] is not None and (which is None or i in which):
                     yield pieces[c]
 
         def arrive(c):
@@ -452,6 +475,10 @@
     def states(array):
         return Part(array, 0)
 
+    def split_states(arrays):
+        count = chunks // len(arrays)
+        return [Part(a, 0, lead=i * count, parts=count) for i, a in enumerate(arrays)]
+
     def to_peers(array, away, backward):
         pairs = [(z, z + away) for z in range(head_count - away) if z % devices + away < devices]
         if backward:
@@ -478,17 +505,22 @@
         return slices, token
 
     gain_row = Part(gain.reshape(1, width))
+    halves = [2 if b > 0 and chunks % 2 == 0 else 1 for b in range(blocks) for _ in range(peers)]
+    later = [[shape((heads // n, DH, DH), BF)] * n for n in halves]
     sum_kv, *later = call(
-        state_body,
+        functools.partial(state_body, counts=[1, *halves]),
         "states",
         scalars,
         [wide(keys), wide(values)],
-        [states(state)] * (1 + blocks * peers),
+        [states(state), *[part for arrays in later for part in split_states(arrays)]],
         heads,
         chunks,
         flops=unit,
     )
-    from_peers = [to_peers(x, 1 + at % peers, False) for at, x in enumerate(later)]
+    later = iter(later)
+    from_peers = [[next(later) for _ in range(n)] for n in halves]
+    for at, arrays in enumerate(from_peers):
+        arrays[0] = to_peers(arrays[0], 1 + at % peers, False)
     slices, token = scanned(sum_kv, False)
     (raw_inner,) = call(
         inner_body,
@@ -500,15 +532,19 @@
         chunks,
         square,
         flops=LONG,
-        after=[token, *from_peers[:peers]],
+        after=[token, *[x for arrays in from_peers[:peers] for x in arrays]],
     )
     kv_state = exchanged(slices).reshape(heads, DH, DH)
+    for at, arrays in enumerate(from_peers):
+        if len(arrays) > 1:
+            later_half, kv_state = lax.optimization_barrier((arrays[1], kv_state))
+            arrays[1] = to_peers(later_half, 1 + at % peers, False)
 
     scales, raws, grads, updates, back = [], [], [], [], []
     for b in range(blocks):
         ends = [states(state)] if b == blocks - 1 and blocks > 1 else []
         scale, raw, grad, update, *sums = call(
-            functools.partial(norm_body, rows=rows, block=b, peers=peers),
+            functools.partial(norm_body, rows=rows, block=b, counts=[1, *halves[b * peers : (b + 1) * peers]]),
             "norm",
             scalars,
             [
@@ -517,7 +553,7 @@
                 wide(raw_inner, b),
                 wide(grad_out, b),
                 states(kv_state),
-                *[states(x) for x in from_peers[b * peers : (b + 1) * peers]],
+                *[p for arrays in from_peers[b * peers : (b + 1) * peers] for p in split_states(arrays)],
                 *[states(w) for w in (updates if ends else [])],
             ],
             [Part(shape((BLOCK, DH), F32)), wide(block_tokens), wide(block_tokens), states(state), *ends],
@@ -531,7 +567,7 @@
         updates.append(update)
         back += [to_peers(update, away, True) for away in range(1, devices)]
     output, grad_q, token = call(
-        functools.partial(query_grads_body, peers=peers),
+        functools.partial(query_grads_body, peers=peers, counts=halves),
         "query_grads",
         scalars,
         [
@@ -542,7 +578,7 @@
             *[wide(d) for d in grads],
             *[wide(r) for r in raws],
             *[Part(s) for s in scales],
-            *[states(x) for x in from_peers],
+            *[part for arrays in from_peers for part in split_states(arrays)],
         ],
         [wide(tokens), wide(tokens), token_part],
         heads,

time: 115 us -> 121 us (1.052)
  blocking collectives: 0 us -> 22.4 us
  waiting for transfers between devices: 33.6 us -> 22.8 us
  starting transfers between devices: 30.5 us -> 25.2 us
    all_to_all x0 -> x1, blocking collectives: none -> 22.4 us  [exchanged(): return lax.all_to_all(slices, AXES, split_axis=0, concat_axis=0, tiled=True)]
    all_to_all x4 -> x3, waiting for transfers between devices: 32.9 us -> 20.6 us  [exchanged(): return lax.all_to_all(slices, AXES, split_axis=0, concat_axis=0, tiled=True)]
    all_to_all x4 -> x3, starting transfers between devices: 22.5 us -> 14.8 us  [exchanged(): return lax.all_to_all(slices, AXES, split_axis=0, concat_axis=0, tiled=True)]
    ppermute x4 -> x5, starting transfers between devices: 8 us -> 10.4 us  [to_peers(): return lax.ppermute(array, 'head', pairs)]
    ppermute x4 -> x5, waiting for transfers between devices: 0.71 us -> 2.22 us  [to_peers(): return lax.ppermute(array, 'head', pairs)]
    unnamed x16 -> x20, local copies, waits for them, and re-layouts: 2.66 us -> 2.67 us
  transfers between devices with their start and end apart: 8 -> 8, of which waited for: 5 -> 4; matrix products, arithmetic and copies ran while one was open for 0% -> 0% of each run, Pallas kernels for 32% -> 29%
where the time goes in v9:
time: 121 us; the launch traced here: 120 us
  Pallas kernels  46 us (38%)
  starting transfers between devices  25.2 us (21%)
  waiting for transfers between devices  22.8 us (19%)
  blocking collectives  22.4 us (19%)
  local copies, waits for them, and re-layouts  2.67 us (2%)
    pallas_call x9, Pallas kernels, call(): pl.pallas_call(kernel, name=name, in_specs=[*[pl.BlockSpec(memory_space=p...  46 us
    all_to_all x1, blocking collectives, exchanged(): return lax.all_to_all(slices, AXES, split_axis=0, concat_axis=0, tiled=True)  22.4 us
    all_to_all x3, waiting for transfers between devices, exchanged(): return lax.all_to_all(slices, AXES, split_axis=0, concat_axis=0, tiled=True)  20.6 us
    all_to_all x3, starting transfers between devices, exchanged(): return lax.all_to_all(slices, AXES, split_axis=0, concat_axis=0, tiled=True)  14.8 us
    ppermute x5, starting transfers between devices, to_peers(): return lax.ppermute(array, 'head', pairs)  10.4 us
    unnamed x20, local copies, waits for them, and re-layouts  2.67 us
  transfers between devices with their start and end apart: 8, of which 4 were waited for; matrix products, arithmetic and copies ran while one was open for 0% of the time, Pallas kernels for 29%

profile of v9, /device:TPU:1, one launch (start us, length us, event | category | flops | bytes accessed | tf_op | source)
XLA Modules:
  0.0 120.1 jit_solution(13838534445930695434)
XLA Ops:
  0.6 0.0 copy-start
  0.6 4.0 %states.1 = (bf16[16,128,128]{2,1,0:T(8,128)(2,1)}, bf16[16,128,128]{2,1,0:T(8,128)(2,1)}, bf16[8,128,128]{2,1,0:T(8,128)(2,1)}, bf16[8,128,128]{2,1,0:T(8,128)(2,1)}) custom-call(s32[4]{0:T(128)} %refs_0_.17, s32[2,6]{1,0:T(2,128)} %refs_1_.13, bf16[256,2048]{1,0:T(8,128)(2,1)} %refs_2_.7, bf16[256,2048]{1,0:T(8,128)(2,1)} %refs_3_.13), custom_call_target="tpu_custom_call" | custom-call | flops 134217728 | bytes 3670016 | tf_op jit(solution)/shard_map/states/pallas_call | solution.py:427
  4.6 0.0 copy-start.9
  4.7 22.4 %all_to_all.20.refs_1_ = bf16[32,64,128]{2,1,0:T(8,128)(2,1)S(1)} all-to-all(bf16[32,64,128]{2,1,0:T(8,128)(2,1)} %bitcast.9), channel_id=1, replica_groups=mesh['ctx'=8,'head'=4] {'ctx','head'}, dimensions={0} | all-to-all | bytes 1048576 | tf_op jit(solution)/shard_map/all_to_all | solution.py:489
  27.1 0.0 copy-done
  27.1 1.5 %scan.2 = (bf16[32,64,128]{2,1,0:T(8,128)(2,1)}, f32[8,128]{1,0:T(8,128)S(1)}) custom-call(s32[4]{0:T(128)S(1)} %copy-done, bf16[32,64,128]{2,1,0:T(8,128)(2,1)S(1)} %all_to_all.20.refs_1_), custom_call_target="tpu_custom_call" | custom-call | bytes 1052672 | tf_op jit(solution)/shard_map/scan/pallas_call | solution.py:427
  28.6 0.0 copy-start.5
  28.6 0.6 copy-done.5
  29.2 3.2 %all-to-all-start.1 = ((bf16[32,64,128]{2,1,0:T(8,128)(2,1)}), bf16[32,64,128]{2,1,0:T(8,128)(2,1)S(1)}, u32[]{:S(2)}, u32[]{:S(2)}) async-start(bf16[32,64,128]{2,1,0:T(8,128)(2,1)} %get-tuple-element.32), calls=%async_computation.1 | async-start | bytes 1048576 | tf_op jit(solution)/shard_map/all_to_all | solution.py:489
  32.4 0.0 copy-done.9
  32.4 3.3 %collective-permute-start = (bf16[16,128,128]{2,1,0:T(8,128)(2,1)S(1)}, bf16[16,128,128]{2,1,0:T(8,128)(2,1)S(1)}, u32[]{:S(2)}, u32[]{:S(2)}) collective-permute-start(bf16[16,128,128]{2,1,0:T(8,128)(2,1)S(1)} %copy-done.9), channel_id=1, source_target_pairs={{0,1},{2,3},{4,5},{6,7},{8,9},{10,11},{12,13},{14,15},{16,17},{18,... | collective-permute-start | bytes 1572872 | tf_op jit(solution)/shard_map/ppermute | solution.py:486
  35.7 2.0 %collective-permute-start.1 = (bf16[8,128,128]{2,1,0:T(8,128)(2,1)}, bf16[8,128,128]{2,1,0:T(8,128)(2,1)}, u32[]{:S(2)}, u32[]{:S(2)}) collective-permute-start(bf16[8,128,128]{2,1,0:T(8,128)(2,1)} %get-tuple-element.37), channel_id=1, source_target_pairs={{0,1},{2,3},{4,5},{6,7},{8,9},{10,11},{12,13},{14,15},{16,17},{18,... | collective-permute-start | bytes 786440 | tf_op jit(solution)/shard_map/ppermute | solution.py:486
  37.7 10.0 %all-to-all-done.1 = bf16[32,64,128]{2,1,0:T(8,128)(2,1)S(1)} async-done(((bf16[32,64,128]{2,1,0:T(8,128)(2,1)}), bf16[32,64,128]{2,1,0:T(8,128)(2,1)S(1)}, u32[]{:S(2)}, u32[]{:S(2)}) %all-to-all-start.1) | async-done | bytes 524320 | tf_op jit(solution)/shard_map/all_to_all | solution.py:489
  47.7 0.0 copy-start.7
  47.7 2.5 %collective-permute-start.2 = (bf16[8,128,128]{2,1,0:T(8,128)(2,1)}, bf16[8,128,128]{2,1,0:T(8,128)(2,1)}, u32[]{:S(2)}, u32[]{:S(2)}) collective-permute-start(bf16[8,128,128]{2,1,0:T(8,128)(2,1)} %get-tuple-element.38), channel_id=1, source_target_pairs={{0,1},{2,3},{4,5},{6,7},{8,9},{10,11},{12,13},{14,15},{16,17},{18,... | collective-permute-start | bytes 786440 | tf_op jit(solution)/shard_map/ppermute | solution.py:486
  50.1 2.2 %collective-permute-done.refs_6_.refs_7_.refs_12_ = bf16[16,128,128]{2,1,0:T(8,128)(2,1)S(1)} collective-permute-done((bf16[16,128,128]{2,1,0:T(8,128)(2,1)S(1)}, bf16[16,128,128]{2,1,0:T(8,128)(2,1)S(1)}, u32[]{:S(2)}, u32[]{:S(2)}) %collective-permute-start) | collective-permute-done | bytes 524320 | tf_op jit(solution)/shard_map/ppermute | solution.py:486
  52.3 0.0 copy-start.8
  52.3 0.8 copy-done.8
  53.1 5.1 %inner.1.refs_4_ = f32[256,2048]{1,0:T(8,128)} custom-call(s32[4]{0:T(128)} %refs_0_.17, s32[2,6]{1,0:T(2,128)} %refs_1_.13, bf16[256,2048]{1,0:T(8,128)(2,1)} %refs_2_.6, bf16[256,2048]{1,0:T(8,128)(2,1)} %refs_2_.7, bf16[256,2048]{1,0:T(8,128)(2,1)} %refs_3_.13, f32[8,128]{1,0:T(8,128)} %copy-done.5, bf16[16,128,128]{2,1,0:T(8,128)(2,1)} %copy-done.8), custom_call_target="tpu_custom_call" | custom-call | flops 399999991808 | bytes 5242880 | tf_op jit(solution)/shard_map/inner/pallas_call | solution.py:427
  58.2 0.0 copy-done.7
  58.2 4.6 %norm.2 = (f32[128,128]{1,0:T(8,128)}, bf16[128,2048]{1,0:T(8,128)(2,1)}, bf16[128,2048]{1,0:T(8,128)(2,1)}, bf16[16,128,128]{2,1,0:T(8,128)(2,1)}) custom-call(s32[4]{0:T(128)} %refs_0_.17, s32[2,6]{1,0:T(2,128)} %refs_1_.13, f32[1,2048]{1,0:T(1,128)} %bitcast.10, bf16[256,2048]{1,0:T(8,128)(2,1)} %refs_2_.6, f32[256,2048]{1,0:T(8,128)} %inner.1.refs_4_, ...), custom_call_target="tpu_custom_call" | custom-call | flops 134217728 | bytes 6889472 | tf_op jit(solution)/shard_map/norm/pallas_call | solution.py:427
  62.8 1.3 %collective-permute-start.3 = (bf16[16,128,128]{2,1,0:T(8,128)(2,1)}, bf16[16,128,128]{2,1,0:T(8,128)(2,1)}, u32[]{:S(2)}, u32[]{:S(2)}) collective-permute-start(bf16[16,128,128]{2,1,0:T(8,128)(2,1)} %get-tuple-element.39.refs_9_), channel_id=1, source_target_pairs={{1,0},{3,2},{5,4},{7,6},{9,8},{11,10},{13,12},{15,14},{17,16},{19,... | collective-permute-start | bytes 1572872 | tf_op jit(solution)/shard_map/ppermute | solution.py:486
  64.1 0.0 collective-permute-done.1.refs_7_.refs_13_
  64.1 0.0 collective-permute-done.2.refs_8_.refs_14_
  64.1 5.1 %norm.3 = (f32[128,128]{1,0:T(8,128)}, bf16[128,2048]{1,0:T(8,128)(2,1)}, bf16[128,2048]{1,0:T(8,128)(2,1)}, bf16[16,128,128]{2,1,0:T(8,128)(2,1)}, bf16[16,128,128]{2,1,0:T(8,128)(2,1)}) custom-call(s32[4]{0:T(128)} %refs_0_.17, s32[2,6]{1,0:T(2,128)} %refs_1_.13, f32[1,2048]{1,0:T(1,128)} %bitcast.11, bf16[256,2048]{1,0:T(8,128)(2,1)} %refs_2_.6, ...), custom_call_target="tpu_custom_call" | custom-call | flops 399999991808 | bytes 7938048 | tf_op jit(solution)/shard_map/norm/pallas_call | solution.py:427
  69.2 8.4 %all-to-all-start.2 = ((bf16[32,64,128]{2,1,0:T(8,128)(2,1)}), bf16[32,64,128]{2,1,0:T(8,128)(2,1)}, u32[]{:S(2)}, u32[]{:S(2)}) async-start(bf16[32,64,128]{2,1,0:T(8,128)(2,1)} %bitcast.8), calls=%async_computation.2 | async-start | bytes 1048576 | tf_op jit(solution)/shard_map/all_to_all | solution.py:489
  77.6 1.3 %collective-permute-start.4 = (bf16[16,128,128]{2,1,0:T(8,128)(2,1)}, bf16[16,128,128]{2,1,0:T(8,128)(2,1)}, u32[]{:S(2)}, u32[]{:S(2)}) collective-permute-start(bf16[16,128,128]{2,1,0:T(8,128)(2,1)} %get-tuple-element.47), channel_id=1, source_target_pairs={{1,0},{3,2},{5,4},{7,6},{9,8},{11,10},{13,12},{15,14},{17,16},{19,... | collective-permute-start | bytes 1572872 | tf_op jit(solution)/shard_map/ppermute | solution.py:486
  78.9 0.0 collective-permute-done.3.refs_15_.refs_7_
  78.9 0.0 copy-start.1
  78.9 8.4 %query_grads.1 = (bf16[256,2048]{1,0:T(8,128)(2,1)}, bf16[256,2048]{1,0:T(8,128)(2,1)}, f32[8,128]{1,0:T(8,128)}) custom-call(s32[4]{0:T(128)} %refs_0_.17, s32[2,6]{1,0:T(2,128)} %refs_1_.13, f32[1,2048]{1,0:T(1,128)} %bitcast.12, bf16[256,2048]{1,0:T(8,128)(2,1)} %refs_2_.7, bf16[256,2048]{1,0:T(8,128)(2,1)} %refs_3_.13, bf16[16,128,128]{2,1,0:T(8,128)(2,1)} %bitcast.7, ...), custom_call_target="tpu_custom_call" | custom-call | flops 399999991808 | bytes 8007680 | tf_op jit(solution)/shard_map/query_grads/pallas_call | solution.py:427
  87.3 5.6 %all-to-all-done.2.refs_1_ = bf16[32,64,128]{2,1,0:T(8,128)(2,1)} async-done(((bf16[32,64,128]{2,1,0:T(8,128)(2,1)}), bf16[32,64,128]{2,1,0:T(8,128)(2,1)}, u32[]{:S(2)}, u32[]{:S(2)}) %all-to-all-start.2) | async-done | bytes 524320 | tf_op jit(solution)/shard_map/all_to_all | solution.py:489
  93.0 0.0 copy-done.1
  93.0 0.0 copy-start.4
  93.0 0.7 copy-done.4
  93.7 2.0 %scan.3 = (bf16[32,64,128]{2,1,0:T(8,128)(2,1)}, f32[8,128]{1,0:T(8,128)S(1)}) custom-call(s32[4]{0:T(128)S(1)} %copy-done.1, bf16[32,64,128]{2,1,0:T(8,128)(2,1)} %all-to-all-done.2.refs_1_, f32[8,128]{1,0:T(8,128)S(1)} %copy-done.4), custom_call_target="tpu_custom_call" | custom-call | bytes 1052672 | tf_op jit(solution)/shard_map/scan/pallas_call | solution.py:427
  95.7 0.0 copy-start.6
  95.7 0.6 copy-done.6
  96.3 3.3 %all-to-all-start.3 = ((bf16[32,64,128]{2,1,0:T(8,128)(2,1)}), bf16[32,64,128]{2,1,0:T(8,128)(2,1)}, u32[]{:S(2)}, u32[]{:S(2)}) async-start(bf16[32,64,128]{2,1,0:T(8,128)(2,1)} %get-tuple-element.53), calls=%async_computation.3 | async-start | bytes 1048576 | tf_op jit(solution)/shard_map/all_to_all | solution.py:489
  99.6 0.0 collective-permute-done.4.refs_8_
  99.6 0.0 copy-start.2
  99.6 0.0 copy-start.3
  99.6 10.2 %key_grads.1 = (f32[256,2048]{1,0:T(8,128)}, f32[256,2048]{1,0:T(8,128)}) custom-call(s32[4]{0:T(128)} %refs_0_.17, s32[2,6]{1,0:T(2,128)} %refs_1_.13, bf16[256,2048]{1,0:T(8,128)(2,1)} %refs_2_.6, bf16[256,2048]{1,0:T(8,128)(2,1)} %refs_2_.7, bf16[256,2048]{1,0:T(8,128)(2,1)} %refs_3_.13, bf16[128,2048]{1,0:T(8,128)(2,1)} %get-tuple-element.36.refs_6_.refs_5_, ...), custom_call_target="tpu_custom_call" | custom-call | flops 399999991808 | bytes 9437184 | tf_op jit(solution)/shard_map/key_grads/pallas_call | solution.py:427
  109.8 5.0 %all-to-all-done.3 = bf16[32,64,128]{2,1,0:T(8,128)(2,1)} async-done(((bf16[32,64,128]{2,1,0:T(8,128)(2,1)}), bf16[32,64,128]{2,1,0:T(8,128)(2,1)}, u32[]{:S(2)}, u32[]{:S(2)}) %all-to-all-start.3) | async-done | bytes 524320 | tf_op jit(solution)/shard_map/all_to_all | solution.py:489
  114.8 0.0 copy-done.2
  114.8 0.0 copy-done.3
  114.8 5.1 %last.1 = (bf16[256,2048]{1,0:T(8,128)(2,1)}, bf16[256,2048]{1,0:T(8,128)(2,1)}) custom-call(s32[4]{0:T(128)S(1)} %copy-done.2, s32[2,6]{1,0:T(2,128)S(1)} %copy-done.3, bf16[256,2048]{1,0:T(8,128)(2,1)} %refs_2_.7, bf16[256,2048]{1,0:T(8,128)(2,1)} %refs_3_.13, f32[256,2048]{1,0:T(8,128)} %get-tuple-element.51.refs_4_, ...), custom_call_target="tpu_custom_call" | custom-call | flops 268435456 | bytes 8912896 | tf_op jit(solution)/shard_map/last/pallas_call | solution.py:427
Async XLA Ops:
  0.6 26.4 %copy-start = (s32[4]{0:T(128)S(1)}, s32[4]{0:T(128)}, u32[]{:S(2)}) copy-start(s32[4]{0:T(128)} %refs_0_.17) | copy-start | bytes 52
  4.6 27.7 %copy-start.9 = (bf16[16,128,128]{2,1,0:T(8,128)(2,1)S(1)}, bf16[16,128,128]{2,1,0:T(8,128)(2,1)}, u32[]{:S(2)}) copy-start(bf16[16,128,128]{2,1,0:T(8,128)(2,1)} %get-tuple-element.35) | copy-start | bytes 1572868
  28.6 0.6 copy-start.5
  29.2 18.5 %all-to-all-start.1 = ((bf16[32,64,128]{2,1,0:T(8,128)(2,1)}), bf16[32,64,128]{2,1,0:T(8,128)(2,1)S(1)}, u32[]{:S(2)}, u32[]{:S(2)}) async-start(bf16[32,64,128]{2,1,0:T(8,128)(2,1)} %get-tuple-element.32), calls=%async_computation.1 | async-start | bytes 1048576 | tf_op jit(solution)/shard_map/all_to_all | solution.py:489
  32.4 19.9 %collective-permute-start = (bf16[16,128,128]{2,1,0:T(8,128)(2,1)S(1)}, bf16[16,128,128]{2,1,0:T(8,128)(2,1)S(1)}, u32[]{:S(2)}, u32[]{:S(2)}) collective-permute-start(bf16[16,128,128]{2,1,0:T(8,128)(2,1)S(1)} %copy-done.9), channel_id=1, source_target_pairs={{0,1},{2,3},{4,5},{6,7},{8,9},{10,11},{12,13},{14,15},{16,17},{18,... | collective-permute-start | bytes 1572872 | tf_op jit(solution)/shard_map/ppermute | solution.py:486
  35.7 28.4 %collective-permute-start.1 = (bf16[8,128,128]{2,1,0:T(8,128)(2,1)}, bf16[8,128,128]{2,1,0:T(8,128)(2,1)}, u32[]{:S(2)}, u32[]{:S(2)}) collective-permute-start(bf16[8,128,128]{2,1,0:T(8,128)(2,1)} %get-tuple-element.37), channel_id=1, source_target_pairs={{0,1},{2,3},{4,5},{6,7},{8,9},{10,11},{12,13},{14,15},{16,17},{18,... | collective-permute-start | bytes 786440 | tf_op jit(solution)/shard_map/ppermute | solution.py:486
  47.7 10.5 %copy-start.7 = (bf16[32,64,128]{2,1,0:T(8,128)(2,1)}, bf16[32,64,128]{2,1,0:T(8,128)(2,1)S(1)}, u32[]{:S(2)}) copy-start(bf16[32,64,128]{2,1,0:T(8,128)(2,1)S(1)} %all-to-all-done.1) | copy-start | bytes 1572868
  47.7 16.4 %collective-permute-start.2 = (bf16[8,128,128]{2,1,0:T(8,128)(2,1)}, bf16[8,128,128]{2,1,0:T(8,128)(2,1)}, u32[]{:S(2)}, u32[]{:S(2)}) collective-permute-start(bf16[8,128,128]{2,1,0:T(8,128)(2,1)} %get-tuple-element.38), channel_id=1, source_target_pairs={{0,1},{2,3},{4,5},{6,7},{8,9},{10,11},{12,13},{14,15},{16,17},{18,... | collective-permute-start | bytes 786440 | tf_op jit(solution)/shard_map/ppermute | solution.py:486
  52.3 0.8 copy-start.8
  62.8 16.1 %collective-permute-start.3 = (bf16[16,128,128]{2,1,0:T(8,128)(2,1)}, bf16[16,128,128]{2,1,0:T(8,128)(2,1)}, u32[]{:S(2)}, u32[]{:S(2)}) collective-permute-start(bf16[16,128,128]{2,1,0:T(8,128)(2,1)} %get-tuple-element.39.refs_9_), channel_id=1, source_target_pairs={{1,0},{3,2},{5,4},{7,6},{9,8},{11,10},{13,12},{15,14},{17,16},{19,... | collective-permute-start | bytes 1572872 | tf_op jit(solution)/shard_map/ppermute | solution.py:486
  69.2 23.8 %all-to-all-start.2 = ((bf16[32,64,128]{2,1,0:T(8,128)(2,1)}), bf16[32,64,128]{2,1,0:T(8,128)(2,1)}, u32[]{:S(2)}, u32[]{:S(2)}) async-start(bf16[32,64,128]{2,1,0:T(8,128)(2,1)} %bitcast.8), calls=%async_computation.2 | async-start | bytes 1048576 | tf_op jit(solution)/shard_map/all_to_all | solution.py:489
  77.6 22.0 %collective-permute-start.4 = (bf16[16,128,128]{2,1,0:T(8,128)(2,1)}, bf16[16,128,128]{2,1,0:T(8,128)(2,1)}, u32[]{:S(2)}, u32[]{:S(2)}) collective-permute-start(bf16[16,128,128]{2,1,0:T(8,128)(2,1)} %get-tuple-element.47), channel_id=1, source_target_pairs={{1,0},{3,2},{5,4},{7,6},{9,8},{11,10},{13,12},{15,14},{17,16},{19,... | collective-permute-start | bytes 1572872 | tf_op jit(solution)/shard_map/ppermute | solution.py:486
  78.9 14.1 %copy-start.1 = (s32[4]{0:T(128)S(1)}, s32[4]{0:T(128)}, u32[]{:S(2)}) copy-start(s32[4]{0:T(128)} %refs_0_.17) | copy-start | bytes 52
  93.0 0.7 copy-start.4
  95.7 0.6 copy-start.6
  96.3 18.5 %all-to-all-start.3 = ((bf16[32,64,128]{2,1,0:T(8,128)(2,1)}), bf16[32,64,128]{2,1,0:T(8,128)(2,1)}, u32[]{:S(2)}, u32[]{:S(2)}) async-start(bf16[32,64,128]{2,1,0:T(8,128)(2,1)} %get-tuple-element.53), calls=%async_computation.3 | async-start | bytes 1048576 | tf_op jit(solution)/shard_map/all_to_all | solution.py:489
  99.6 15.3 %copy-start.2 = (s32[4]{0:T(128)S(1)}, s32[4]{0:T(128)}, u32[]{:S(2)}) copy-start(s32[4]{0:T(128)} %refs_0_.17) | copy-start | bytes 52
  99.6 15.3 %copy-start.3 = (s32[2,6]{1,0:T(2,128)S(1)}, s32[2,6]{1,0:T(2,128)}, u32[]{:S(2)}) copy-start(s32[2,6]{1,0:T(2,128)} %refs_1_.13) | copy-start | bytes 148

commit v10 on v9

--- a/solution.py
+++ b/solution.py
@@ -537,7 +537,8 @@
     kv_state = exchanged(slices).reshape(heads, DH, DH)
     for at, arrays in enumerate(from_peers):
         if len(arrays) > 1:
-            later_half, kv_state = lax.optimization_barrier((arrays[1], kv_state))
+            held = lax.optimization_barrier((arrays[1], kv_state, raw_inner))
+            later_half, kv_state, raw_inner = held
             arrays[1] = to_peers(later_half, 1 + at % peers, False)
 
     scales, raws, grads, updates, back = [], [], [], [], []

time: 121 us -> 114 us (0.942)
  blocking collectives: 22.4 us -> 0 us
  waiting for transfers between devices: 22.8 us -> 29.9 us
  starting transfers between devices: 25.2 us -> 32.2 us
    all_to_all x1 -> x0, blocking collectives: 22.4 us -> none  [exchanged(): return lax.all_to_all(slices, AXES, split_axis=0, concat_axis=0, tiled=True)]
    all_to_all x3 -> x4, waiting for transfers between devices: 20.6 us -> 29.7 us  [exchanged(): return lax.all_to_all(slices, AXES, split_axis=0, concat_axis=0, tiled=True)]
    all_to_all x3 -> x4, starting transfers between devices: 14.8 us -> 20.6 us  [exchanged(): return lax.all_to_all(slices, AXES, split_axis=0, concat_axis=0, tiled=True)]
    ppermute x5, waiting for transfers between devices: 2.22 us -> 0.17 us  [to_peers(): return lax.ppermute(array, 'head', pairs)]
  transfers between devices with their start and end apart: 8 -> 9, of which waited for: 4 -> 5; matrix products, arithmetic and copies ran while one was open for 0% -> 0% of each run, Pallas kernels for 29% -> 33%
where the time goes in v10:
time: 114 us; the launch traced here: 113 us
  Pallas kernels  46.2 us (41%)
  starting transfers between devices  32.2 us (28%)
  waiting for transfers between devices  29.9 us (26%)
  local copies, waits for them, and re-layouts  3.37 us (3%)
    pallas_call x9, Pallas kernels, call(): pl.pallas_call(kernel, name=name, in_specs=[*[pl.BlockSpec(memory_space=p...  46.2 us
    all_to_all x4, waiting for transfers between devices, exchanged(): return lax.all_to_all(slices, AXES, split_axis=0, concat_axis=0, tiled=True)  29.7 us
    all_to_all x4, starting transfers between devices, exchanged(): return lax.all_to_all(slices, AXES, split_axis=0, concat_axis=0, tiled=True)  20.6 us
    ppermute x5, starting transfers between devices, to_peers(): return lax.ppermute(array, 'head', pairs)  11.6 us
    unnamed x20, local copies, waits for them, and re-layouts  3.37 us
  transfers between devices with their start and end apart: 9, of which 5 were waited for; matrix products, arithmetic and copies ran while one was open for 0% of the time, Pallas kernels for 33%

profile of v10, /device:TPU:1, one launch (start us, length us, event | category | flops | bytes accessed | tf_op | source)
XLA Modules:
  0.0 112.6 jit_solution(13118355575297152517)
XLA Ops:
  0.6 0.0 copy-start
  0.6 4.0 %states.1 = (bf16[16,128,128]{2,1,0:T(8,128)(2,1)}, bf16[16,128,128]{2,1,0:T(8,128)(2,1)}, bf16[8,128,128]{2,1,0:T(8,128)(2,1)}, bf16[8,128,128]{2,1,0:T(8,128)(2,1)}) custom-call(s32[4]{0:T(128)} %refs_0_.17, s32[2,6]{1,0:T(2,128)} %refs_1_.13, bf16[256,2048]{1,0:T(8,128)(2,1)} %refs_2_.7, bf16[256,2048]{1,0:T(8,128)(2,1)} %refs_3_.13), custom_call_target="tpu_custom_call" | custom-call | flops 134217728 | bytes 3670016 | tf_op jit(solution)/shard_map/states/pallas_call | solution.py:427
  4.6 7.1 %all-to-all-start = ((bf16[32,64,128]{2,1,0:T(8,128)(2,1)}), bf16[32,64,128]{2,1,0:T(8,128)(2,1)S(1)}, u32[]{:S(2)}, u32[]{:S(2)}) async-start(bf16[32,64,128]{2,1,0:T(8,128)(2,1)} %bitcast.6), calls=%async_computation | async-start | bytes 1048576 | tf_op jit(solution)/shard_map/all_to_all | solution.py:489
  11.7 3.3 %collective-permute-start = (bf16[16,128,128]{2,1,0:T(8,128)(2,1)}, bf16[16,128,128]{2,1,0:T(8,128)(2,1)S(1)}, u32[]{:S(2)}, u32[]{:S(2)}) collective-permute-start(bf16[16,128,128]{2,1,0:T(8,128)(2,1)} %get-tuple-element.35), channel_id=1, source_target_pairs={{0,1},{2,3},{4,5},{6,7},{8,9},{10,11},{12,13},{14,15},{16,17},{18,... | collective-permute-start | bytes 1572872 | tf_op jit(solution)/shard_map/ppermute | solution.py:486
  15.1 2.0 %collective-permute-start.1 = (bf16[8,128,128]{2,1,0:T(8,128)(2,1)}, bf16[8,128,128]{2,1,0:T(8,128)(2,1)}, u32[]{:S(2)}, u32[]{:S(2)}) collective-permute-start(bf16[8,128,128]{2,1,0:T(8,128)(2,1)} %get-tuple-element.39), channel_id=1, source_target_pairs={{0,1},{2,3},{4,5},{6,7},{8,9},{10,11},{12,13},{14,15},{16,17},{18,... | collective-permute-start | bytes 786440 | tf_op jit(solution)/shard_map/ppermute | solution.py:486
  17.1 10.0 %all-to-all-done.refs_1_ = bf16[32,64,128]{2,1,0:T(8,128)(2,1)S(1)} async-done(((bf16[32,64,128]{2,1,0:T(8,128)(2,1)}), bf16[32,64,128]{2,1,0:T(8,128)(2,1)S(1)}, u32[]{:S(2)}, u32[]{:S(2)}) %all-to-all-start) | async-done | bytes 524320 | tf_op jit(solution)/shard_map/all_to_all | solution.py:489
  27.0 0.0 copy-done
  27.0 1.5 %scan.2 = (bf16[32,64,128]{2,1,0:T(8,128)(2,1)}, f32[8,128]{1,0:T(8,128)S(1)}) custom-call(s32[4]{0:T(128)S(1)} %copy-done, bf16[32,64,128]{2,1,0:T(8,128)(2,1)S(1)} %all-to-all-done.refs_1_), custom_call_target="tpu_custom_call" | custom-call | bytes 1052672 | tf_op jit(solution)/shard_map/scan/pallas_call | solution.py:427
  28.6 0.0 copy-start.6
  28.6 0.6 copy-done.6
  29.2 3.2 %all-to-all-start.1 = ((bf16[32,64,128]{2,1,0:T(8,128)(2,1)}), bf16[32,64,128]{2,1,0:T(8,128)(2,1)}, u32[]{:S(2)}, u32[]{:S(2)}) async-start(bf16[32,64,128]{2,1,0:T(8,128)(2,1)} %get-tuple-element.33), calls=%async_computation.1 | async-start | bytes 1048576 | tf_op jit(solution)/shard_map/all_to_all | solution.py:489
  32.4 0.0 collective-permute-done.refs_6_.refs_7_.refs_12_
  32.4 0.0 copy-start.7
  32.4 0.8 copy-done.7
  33.2 0.0 copy-start.8
  33.2 5.2 %inner.1.refs_4_ = f32[256,2048]{1,0:T(8,128)} custom-call(s32[4]{0:T(128)} %refs_0_.17, s32[2,6]{1,0:T(2,128)} %refs_1_.13, bf16[256,2048]{1,0:T(8,128)(2,1)} %refs_2_.6, bf16[256,2048]{1,0:T(8,128)(2,1)} %refs_2_.7, bf16[256,2048]{1,0:T(8,128)(2,1)} %refs_3_.13, f32[8,128]{1,0:T(8,128)} %copy-done.6, bf16[16,128,128]{2,1,0:T(8,128)(2,1)} %copy-done.7), custom_call_target="tpu_custom_call" | custom-call | flops 399999991808 | bytes 5242880 | tf_op jit(solution)/shard_map/inner/pallas_call | solution.py:427
  38.4 9.3 %all-to-all-done.1 = bf16[32,64,128]{2,1,0:T(8,128)(2,1)} async-done(((bf16[32,64,128]{2,1,0:T(8,128)(2,1)}), bf16[32,64,128]{2,1,0:T(8,128)(2,1)}, u32[]{:S(2)}, u32[]{:S(2)}) %all-to-all-start.1) | async-done | bytes 524320 | tf_op jit(solution)/shard_map/all_to_all | solution.py:489
  47.7 0.0 copy-done.8
  47.7 3.7 %collective-permute-start.2 = (bf16[8,128,128]{2,1,0:T(8,128)(2,1)S(1)}, bf16[8,128,128]{2,1,0:T(8,128)(2,1)S(1)}, u32[]{:S(2)}, u32[]{:S(2)}) collective-permute-start(bf16[8,128,128]{2,1,0:T(8,128)(2,1)S(1)} %copy-done.8), channel_id=1, source_target_pairs={{0,1},{2,3},{4,5},{6,7},{8,9},{10,11},{12,13},{14,15},{16,17},{18,... | collective-permute-start | bytes 786440 | tf_op jit(solution)/shard_map/ppermute | solution.py:486
  51.4 4.6 %norm.2 = (f32[128,128]{1,0:T(8,128)}, bf16[128,2048]{1,0:T(8,128)(2,1)}, bf16[128,2048]{1,0:T(8,128)(2,1)}, bf16[16,128,128]{2,1,0:T(8,128)(2,1)}) custom-call(s32[4]{0:T(128)} %refs_0_.17, s32[2,6]{1,0:T(2,128)} %refs_1_.13, f32[1,2048]{1,0:T(1,128)} %bitcast.7, bf16[256,2048]{1,0:T(8,128)(2,1)} %refs_2_.6, f32[256,2048]{1,0:T(8,128)} %inner.1.refs_4_, ...), custom_call_target="tpu_custom_call" | custom-call | flops 134217728 | bytes 6889472 | tf_op jit(solution)/shard_map/norm/pallas_call | solution.py:427
  56.0 1.3 %collective-permute-start.3 = (bf16[16,128,128]{2,1,0:T(8,128)(2,1)}, bf16[16,128,128]{2,1,0:T(8,128)(2,1)}, u32[]{:S(2)}, u32[]{:S(2)}) collective-permute-start(bf16[16,128,128]{2,1,0:T(8,128)(2,1)} %get-tuple-element.41.refs_9_), channel_id=1, source_target_pairs={{1,0},{3,2},{5,4},{7,6},{9,8},{11,10},{13,12},{15,14},{17,16},{19,... | collective-permute-start | bytes 1572872 | tf_op jit(solution)/shard_map/ppermute | solution.py:486
  57.3 0.0 collective-permute-done.1.refs_7_.refs_13_
  57.3 0.0 collective-permute-done.2.refs_8_.refs_14_
  57.3 0.0 copy-start.9
  57.3 0.7 copy-done.9
  58.0 5.1 %norm.3 = (f32[128,128]{1,0:T(8,128)}, bf16[128,2048]{1,0:T(8,128)(2,1)}, bf16[128,2048]{1,0:T(8,128)(2,1)}, bf16[16,128,128]{2,1,0:T(8,128)(2,1)}, bf16[16,128,128]{2,1,0:T(8,128)(2,1)}) custom-call(s32[4]{0:T(128)} %refs_0_.17, s32[2,6]{1,0:T(2,128)} %refs_1_.13, f32[1,2048]{1,0:T(1,128)} %bitcast.8, bf16[256,2048]{1,0:T(8,128)(2,1)} %refs_2_.6, ...), custom_call_target="tpu_custom_call" | custom-call | flops 399999991808 | bytes 7938048 | tf_op jit(solution)/shard_map/norm/pallas_call | solution.py:427
  63.1 7.0 %all-to-all-start.2 = ((bf16[32,64,128]{2,1,0:T(8,128)(2,1)}), bf16[32,64,128]{2,1,0:T(8,128)(2,1)}, u32[]{:S(2)}, u32[]{:S(2)}) async-start(bf16[32,64,128]{2,1,0:T(8,128)(2,1)} %bitcast.5), calls=%async_computation.2 | async-start | bytes 1048576 | tf_op jit(solution)/shard_map/all_to_all | solution.py:489
  70.1 1.3 %collective-permute-start.4 = (bf16[16,128,128]{2,1,0:T(8,128)(2,1)}, bf16[16,128,128]{2,1,0:T(8,128)(2,1)}, u32[]{:S(2)}, u32[]{:S(2)}) collective-permute-start(bf16[16,128,128]{2,1,0:T(8,128)(2,1)} %get-tuple-element.49), channel_id=1, source_target_pairs={{1,0},{3,2},{5,4},{7,6},{9,8},{11,10},{13,12},{15,14},{17,16},{19,... | collective-permute-start | bytes 1572872 | tf_op jit(solution)/shard_map/ppermute | solution.py:486
  71.4 0.2 collective-permute-done.3.refs_15_.refs_7_
  71.6 0.0 copy-start.1
  71.6 8.5 %query_grads.1 = (bf16[256,2048]{1,0:T(8,128)(2,1)}, bf16[256,2048]{1,0:T(8,128)(2,1)}, f32[8,128]{1,0:T(8,128)}) custom-call(s32[4]{0:T(128)} %refs_0_.17, s32[2,6]{1,0:T(2,128)} %refs_1_.13, f32[1,2048]{1,0:T(1,128)} %bitcast.9, bf16[256,2048]{1,0:T(8,128)(2,1)} %refs_2_.7, bf16[256,2048]{1,0:T(8,128)(2,1)} %refs_3_.13, ...), custom_call_target="tpu_custom_call" | custom-call | flops 399999991808 | bytes 8007680 | tf_op jit(solution)/shard_map/query_grads/pallas_call | solution.py:427
  80.1 5.4 %all-to-all-done.2.refs_1_ = bf16[32,64,128]{2,1,0:T(8,128)(2,1)} async-done(((bf16[32,64,128]{2,1,0:T(8,128)(2,1)}), bf16[32,64,128]{2,1,0:T(8,128)(2,1)}, u32[]{:S(2)}, u32[]{:S(2)}) %all-to-all-start.2) | async-done | bytes 524320 | tf_op jit(solution)/shard_map/all_to_all | solution.py:489
  85.5 0.0 copy-done.1
  85.5 0.0 copy-start.4
  85.5 0.7 copy-done.4
  86.2 2.0 %scan.3 = (bf16[32,64,128]{2,1,0:T(8,128)(2,1)}, f32[8,128]{1,0:T(8,128)S(1)}) custom-call(s32[4]{0:T(128)S(1)} %copy-done.1, bf16[32,64,128]{2,1,0:T(8,128)(2,1)} %all-to-all-done.2.refs_1_, f32[8,128]{1,0:T(8,128)S(1)} %copy-done.4), custom_call_target="tpu_custom_call" | custom-call | bytes 1052672 | tf_op jit(solution)/shard_map/scan/pallas_call | solution.py:427
  88.2 0.0 copy-start.5
  88.2 0.6 copy-done.5
  88.8 3.3 %all-to-all-start.3 = ((bf16[32,64,128]{2,1,0:T(8,128)(2,1)}), bf16[32,64,128]{2,1,0:T(8,128)(2,1)}, u32[]{:S(2)}, u32[]{:S(2)}) async-start(bf16[32,64,128]{2,1,0:T(8,128)(2,1)} %get-tuple-element.55), calls=%async_computation.3 | async-start | bytes 1048576 | tf_op jit(solution)/shard_map/all_to_all | solution.py:489
  92.1 0.0 collective-permute-done.4.refs_8_
  92.1 0.0 copy-start.2
  92.1 0.0 copy-start.3
  92.1 10.2 %key_grads.1 = (f32[256,2048]{1,0:T(8,128)}, f32[256,2048]{1,0:T(8,128)}) custom-call(s32[4]{0:T(128)} %refs_0_.17, s32[2,6]{1,0:T(2,128)} %refs_1_.13, bf16[256,2048]{1,0:T(8,128)(2,1)} %refs_2_.6, bf16[256,2048]{1,0:T(8,128)(2,1)} %refs_2_.7, bf16[256,2048]{1,0:T(8,128)(2,1)} %refs_3_.13, bf16[128,2048]{1,0:T(8,128)(2,1)} %get-tuple-element.38.refs_6_.refs_5_, ...), custom_call_target="tpu_custom_call" | custom-call | flops 399999991808 | bytes 9437184 | tf_op jit(solution)/shard_map/key_grads/pallas_call | solution.py:427
  102.3 5.0 %all-to-all-done.3 = bf16[32,64,128]{2,1,0:T(8,128)(2,1)} async-done(((bf16[32,64,128]{2,1,0:T(8,128)(2,1)}), bf16[32,64,128]{2,1,0:T(8,128)(2,1)}, u32[]{:S(2)}, u32[]{:S(2)}) %all-to-all-start.3) | async-done | bytes 524320 | tf_op jit(solution)/shard_map/all_to_all | solution.py:489
  107.4 0.0 copy-done.2
  107.4 0.0 copy-done.3
  107.4 5.1 %last.1 = (bf16[256,2048]{1,0:T(8,128)(2,1)}, bf16[256,2048]{1,0:T(8,128)(2,1)}) custom-call(s32[4]{0:T(128)S(1)} %copy-done.2, s32[2,6]{1,0:T(2,128)S(1)} %copy-done.3, bf16[256,2048]{1,0:T(8,128)(2,1)} %refs_2_.7, bf16[256,2048]{1,0:T(8,128)(2,1)} %refs_3_.13, f32[256,2048]{1,0:T(8,128)} %get-tuple-element.53.refs_4_, ...), custom_call_target="tpu_custom_call" | custom-call | flops 268435456 | bytes 8912896 | tf_op jit(solution)/shard_map/last/pallas_call | solution.py:427
Async XLA Ops:
  0.6 26.4 %copy-start = (s32[4]{0:T(128)S(1)}, s32[4]{0:T(128)}, u32[]{:S(2)}) copy-start(s32[4]{0:T(128)} %refs_0_.17) | copy-start | bytes 52
  4.6 22.4 %all-to-all-start = ((bf16[32,64,128]{2,1,0:T(8,128)(2,1)}), bf16[32,64,128]{2,1,0:T(8,128)(2,1)S(1)}, u32[]{:S(2)}, u32[]{:S(2)}) async-start(bf16[32,64,128]{2,1,0:T(8,128)(2,1)} %bitcast.6), calls=%async_computation | async-start | bytes 1048576 | tf_op jit(solution)/shard_map/all_to_all | solution.py:489
  11.7 20.6 %collective-permute-start = (bf16[16,128,128]{2,1,0:T(8,128)(2,1)}, bf16[16,128,128]{2,1,0:T(8,128)(2,1)S(1)}, u32[]{:S(2)}, u32[]{:S(2)}) collective-permute-start(bf16[16,128,128]{2,1,0:T(8,128)(2,1)} %get-tuple-element.35), channel_id=1, source_target_pairs={{0,1},{2,3},{4,5},{6,7},{8,9},{10,11},{12,13},{14,15},{16,17},{18,... | collective-permute-start | bytes 1572872 | tf_op jit(solution)/shard_map/ppermute | solution.py:486
  15.1 42.2 %collective-permute-start.1 = (bf16[8,128,128]{2,1,0:T(8,128)(2,1)}, bf16[8,128,128]{2,1,0:T(8,128)(2,1)}, u32[]{:S(2)}, u32[]{:S(2)}) collective-permute-start(bf16[8,128,128]{2,1,0:T(8,128)(2,1)} %get-tuple-element.39), channel_id=1, source_target_pairs={{0,1},{2,3},{4,5},{6,7},{8,9},{10,11},{12,13},{14,15},{16,17},{18,... | collective-permute-start | bytes 786440 | tf_op jit(solution)/shard_map/ppermute | solution.py:486
  28.6 0.6 copy-start.6
  29.2 18.6 %all-to-all-start.1 = ((bf16[32,64,128]{2,1,0:T(8,128)(2,1)}), bf16[32,64,128]{2,1,0:T(8,128)(2,1)}, u32[]{:S(2)}, u32[]{:S(2)}) async-start(bf16[32,64,128]{2,1,0:T(8,128)(2,1)} %get-tuple-element.33), calls=%async_computation.1 | async-start | bytes 1048576 | tf_op jit(solution)/shard_map/all_to_all | solution.py:489
  32.4 0.8 copy-start.7
  33.2 14.5 %copy-start.8 = (bf16[8,128,128]{2,1,0:T(8,128)(2,1)S(1)}, bf16[8,128,128]{2,1,0:T(8,128)(2,1)}, u32[]{:S(2)}) copy-start(bf16[8,128,128]{2,1,0:T(8,128)(2,1)} %get-tuple-element.40) | copy-start | bytes 786436
  47.7 9.6 %collective-permute-start.2 = (bf16[8,128,128]{2,1,0:T(8,128)(2,1)S(1)}, bf16[8,128,128]{2,1,0:T(8,128)(2,1)S(1)}, u32[]{:S(2)}, u32[]{:S(2)}) collective-permute-start(bf16[8,128,128]{2,1,0:T(8,128)(2,1)S(1)} %copy-done.8), channel_id=1, source_target_pairs={{0,1},{2,3},{4,5},{6,7},{8,9},{10,11},{12,13},{14,15},{16,17},{18,... | collective-permute-start | bytes 786440 | tf_op jit(solution)/shard_map/ppermute | solution.py:486
  56.0 15.6 %collective-permute-start.3 = (bf16[16,128,128]{2,1,0:T(8,128)(2,1)}, bf16[16,128,128]{2,1,0:T(8,128)(2,1)}, u32[]{:S(2)}, u32[]{:S(2)}) collective-permute-start(bf16[16,128,128]{2,1,0:T(8,128)(2,1)} %get-tuple-element.41.refs_9_), channel_id=1, source_target_pairs={{1,0},{3,2},{5,4},{7,6},{9,8},{11,10},{13,12},{15,14},{17,16},{19,... | collective-permute-start | bytes 1572872 | tf_op jit(solution)/shard_map/ppermute | solution.py:486
  57.3 0.7 copy-start.9
  63.1 22.4 %all-to-all-start.2 = ((bf16[32,64,128]{2,1,0:T(8,128)(2,1)}), bf16[32,64,128]{2,1,0:T(8,128)(2,1)}, u32[]{:S(2)}, u32[]{:S(2)}) async-start(bf16[32,64,128]{2,1,0:T(8,128)(2,1)} %bitcast.5), calls=%async_computation.2 | async-start | bytes 1048576 | tf_op jit(solution)/shard_map/all_to_all | solution.py:489
  70.1 22.0 %collective-permute-start.4 = (bf16[16,128,128]{2,1,0:T(8,128)(2,1)}, bf16[16,128,128]{2,1,0:T(8,128)(2,1)}, u32[]{:S(2)}, u32[]{:S(2)}) collective-permute-start(bf16[16,128,128]{2,1,0:T(8,128)(2,1)} %get-tuple-element.49), channel_id=1, source_target_pairs={{1,0},{3,2},{5,4},{7,6},{9,8},{11,10},{13,12},{15,14},{17,16},{19,... | collective-permute-start | bytes 1572872 | tf_op jit(solution)/shard_map/ppermute | solution.py:486
  71.6 13.9 %copy-start.1 = (s32[4]{0:T(128)S(1)}, s32[4]{0:T(128)}, u32[]{:S(2)}) copy-start(s32[4]{0:T(128)} %refs_0_.17) | copy-start | bytes 52
  85.5 0.7 copy-start.4
  88.2 0.6 copy-start.5
  88.8 18.5 %all-to-all-start.3 = ((bf16[32,64,128]{2,1,0:T(8,128)(2,1)}), bf16[32,64,128]{2,1,0:T(8,128)(2,1)}, u32[]{:S(2)}, u32[]{:S(2)}) async-start(bf16[32,64,128]{2,1,0:T(8,128)(2,1)} %get-tuple-element.55), calls=%async_computation.3 | async-start | bytes 1048576 | tf_op jit(solution)/shard_map/all_to_all | solution.py:489
  92.1 15.3 %copy-start.2 = (s32[4]{0:T(128)S(1)}, s32[4]{0:T(128)}, u32[]{:S(2)}) copy-start(s32[4]{0:T(128)} %refs_0_.17) | copy-start | bytes 52
  92.1 15.3 %copy-start.3 = (s32[2,6]{1,0:T(2,128)S(1)}, s32[2,6]{1,0:T(2,128)}, u32[]{:S(2)}) copy-start(s32[2,6]{1,0:T(2,128)} %refs_1_.13) | copy-start | bytes 148

commit v11 on v10

--- a/solution.py
+++ b/solution.py
@@ -198,8 +198,7 @@
 
 
 def scan_body(place_of, ins, outs, scratch, arrive, leave, chunks, *, rows, backward):
-    (t_ref,), (out_ref, token_ref) = ins, outs
-    token_ref[...] = jnp.zeros_like(token_ref)
+    (t_ref,), (out_ref,) = ins, outs
     count, height, _ = t_ref.shape
     devices = GROUP // rows
     bounds = place_of(rows).bounds
@@ -286,9 +285,8 @@
     rest = ins[4:]
     d_refs, raw_refs, scale_refs = rest[:blocks], rest[blocks : 2 * blocks], rest[2 * blocks : 3 * blocks]
     peer_refs = joined(rest[3 * blocks :], counts)
-    out_ref, gq_ref, token_ref = outs
+    out_ref, gq_ref = outs
     (weight_ref,) = scratch
-    token_ref[...] = jnp.zeros_like(token_ref)
     weight_ref[...] = place.weights()
     factors = [place.before(b) for b in range(blocks)]
     for c, heads in enumerate(chunks):
@@ -458,6 +456,7 @@
     head_count = lax.axis_size("head")
     total = lax.axis_size("ctx") * head_count
     chunks = CHUNKS if heads % CHUNKS == 0 else 1
+    few = min(chunks, 2)
     shape = jax.ShapeDtypeStruct
     state = shape((heads, DH, DH), BF)
     tokens = shape((rows, width), BF)
@@ -467,7 +466,6 @@
     unit = 2 * rows * width * DH
     inner = 2 * rows * rows * width
     scalars = [lengths, block_mask]
-    token_part = Part(shape((8, DH), F32), near=True)
 
     def wide(array, block=None):
         return Part(array, 1, block)
@@ -475,7 +473,7 @@
     def states(array):
         return Part(array, 0)
 
-    def split_states(arrays):
+    def split_states(arrays, chunks):
         count = chunks // len(arrays)
         return [Part(a, 0, lead=i * count, parts=count) for i, a in enumerate(arrays)]
 
@@ -488,21 +486,18 @@
     def exchanged(slices):
         return lax.all_to_all(slices, AXES, split_axis=0, concat_axis=0, tiled=True)
 
-    def scanned(sums, backward, after=()):
-        height = heads * DH // total
-        slices = exchanged(sums.reshape(total, height, DH))
-        slices, token = call(
+    def scanned(slices, backward):
+        (slices,) = call(
             functools.partial(scan_body, rows=rows, backward=backward),
             "scan",
             [lengths],
             [Part(slices, near=True)],
-            [Part(shape(slices.shape, BF), 1), token_part],
+            [Part(shape(slices.shape, BF), 1)],
             heads,
-            2 if height % 32 == 0 else 1,
-            after=after,
+            2 if slices.shape[1] % 32 == 0 else 1,
             limit=SOME_BYTES,
         )
-        return slices, token
+        return slices
 
     gain_row = Part(gain.reshape(1, width))
     halves = [2 if b > 0 and chunks % 2 == 0 else 1 for b in range(blocks) for _ in range(peers)]
@@ -512,27 +507,28 @@
         "states",
         scalars,
         [wide(keys), wide(values)],
-        [states(state), *[part for arrays in later for part in split_states(arrays)]],
+        [states(state), *[part for arrays in later for part in split_states(arrays, few)]],
         heads,
-        chunks,
+        few,
         flops=unit,
     )
     later = iter(later)
     from_peers = [[next(later) for _ in range(n)] for n in halves]
     for at, arrays in enumerate(from_peers):
         arrays[0] = to_peers(arrays[0], 1 + at % peers, False)
-    slices, token = scanned(sum_kv, False)
+    slices = scanned(exchanged(sum_kv.reshape(total, -1, DH)), False)
+    slices, late_queries = lax.optimization_barrier((slices, queries))
     (raw_inner,) = call(
         inner_body,
         "inner",
         scalars,
-        [wide(queries), wide(keys), wide(values)],
+        [wide(late_queries), wide(keys), wide(values)],
         [wide(partial)],
         heads,
         chunks,
         square,
         flops=LONG,
-        after=[token, *[x for arrays in from_peers[:peers] for x in arrays]],
+        after=[x for arrays in from_peers[:peers] for x in arrays],
     )
     kv_state = exchanged(slices).reshape(heads, DH, DH)
     for at, arrays in enumerate(from_peers):
@@ -554,12 +550,12 @@
                 wide(raw_inner, b),
                 wide(grad_out, b),
                 states(kv_state),
-                *[p for arrays in from_peers[b * peers : (b + 1) * peers] for p in split_states(arrays)],
+                *[p for arrays in from_peers[b * peers : (b + 1) * peers] for p in split_states(arrays, few)],
                 *[states(w) for w in (updates if ends else [])],
             ],
             [Part(shape((BLOCK, DH), F32)), wide(block_tokens), wide(block_tokens), states(state), *ends],
             heads,
-            chunks,
+            few,
             flops=LONG if b > 0 else 2 * unit // blocks,
         )
         scales.append(scale)
@@ -567,7 +563,7 @@
         grads.append(grad)
         updates.append(update)
         back += [to_peers(update, away, True) for away in range(1, devices)]
-    output, grad_q, token = call(
+    output, grad_q = call(
         functools.partial(query_grads_body, peers=peers, counts=halves),
         "query_grads",
         scalars,
@@ -579,22 +575,25 @@
             *[wide(d) for d in grads],
             *[wide(r) for r in raws],
             *[Part(s) for s in scales],
-            *[part for arrays in from_peers for part in split_states(arrays)],
+            *[part for arrays in from_peers for part in split_states(arrays, chunks)],
         ],
-        [wide(tokens), wide(tokens), token_part],
+        [wide(tokens), wide(tokens)],
         heads,
         chunks,
         square,
         flops=LONG,
         after=back[:peers],
     )
-    slices, token = scanned(sums[0] if sums else updates[0], True, [token])
+    slices = exchanged((sums[0] if sums else updates[0]).reshape(total, -1, DH))
+    slices, grad_q = lax.optimization_barrier((slices, grad_q))
+    slices = scanned(slices, True)
+    slices, late_queries = lax.optimization_barrier((slices, queries))
     part_k, part_v = call(
         functools.partial(key_grads_body, peers=peers),
         "key_grads",
         scalars,
         [
-            wide(queries),
+            wide(late_queries),
             wide(keys),
             wide(values),
             *[wide(d) for d in grads],
@@ -605,7 +604,6 @@
         chunks,
         square,
         flops=LONG,
-        after=[token],
     )
     grad_state = exchanged(slices).reshape(heads, DH, DH)
     grad_k, grad_v = call(

time: 114 us -> 112 us (0.982)
  local copies, waits for them, and re-layouts: 3.37 us -> 1.51 us
  Pallas kernels: 46.2 us -> 44.9 us
    ppermute x5, waiting for transfers between devices: 0.17 us -> 2.36 us  [to_peers(): return lax.ppermute(array, 'head', pairs)]
    unnamed x20 -> x14, local copies, waits for them, and re-layouts: 3.37 us -> 1.51 us
    pallas_call x9, Pallas kernels: 46.2 us -> 44.9 us  [call(): pl.pallas_call(kernel, name=name, in_specs=[*[pl.BlockSpec(memory_space=p...]
    all_to_all x4, waiting for transfers between devices: 29.7 us -> 28.5 us  [exchanged(): return lax.all_to_all(slices, AXES, split_axis=0, concat_axis=0, tiled=True)]
  transfers between devices with their start and end apart: 9 -> 9, of which waited for: 5 -> 7; matrix products, arithmetic and copies ran while one was open for 0% -> 0% of each run, Pallas kernels for 33% -> 33%
where the time goes in v11:
time: 112 us; the launch traced here: 111 us
  Pallas kernels  44.9 us (40%)
  starting transfers between devices  32.4 us (29%)
  waiting for transfers between devices  30.8 us (28%)
  local copies, waits for them, and re-layouts  1.51 us (1%)
    pallas_call x9, Pallas kernels, call(): pl.pallas_call(kernel, name=name, in_specs=[*[pl.BlockSpec(memory_space=p...  44.9 us
    all_to_all x4, waiting for transfers between devices, exchanged(): return lax.all_to_all(slices, AXES, split_axis=0, concat_axis=0, tiled=True)  28.5 us
    all_to_all x4, starting transfers between devices, exchanged(): return lax.all_to_all(slices, AXES, split_axis=0, concat_axis=0, tiled=True)  20.3 us
    ppermute x5, starting transfers between devices, to_peers(): return lax.ppermute(array, 'head', pairs)  12.2 us
    ppermute x5, waiting for transfers between devices, to_peers(): return lax.ppermute(array, 'head', pairs)  2.36 us
  transfers between devices with their start and end apart: 9, of which 7 were waited for; matrix products, arithmetic and copies ran while one was open for 0% of the time, Pallas kernels for 33%

profile of v11, /device:TPU:1, one launch (start us, length us, event | category | flops | bytes accessed | tf_op | source)
XLA Modules:
  0.0 110.6 jit_solution(9009954748066855433)
XLA Ops:
  0.6 0.0 copy-start
  0.6 3.8 %states.1 = (bf16[16,128,128]{2,1,0:T(8,128)(2,1)}, bf16[16,128,128]{2,1,0:T(8,128)(2,1)}, bf16[8,128,128]{2,1,0:T(8,128)(2,1)}, bf16[8,128,128]{2,1,0:T(8,128)(2,1)}) custom-call(s32[4]{0:T(128)} %refs_0_.17, s32[2,6]{1,0:T(2,128)} %refs_1_.13, bf16[256,2048]{1,0:T(8,128)(2,1)} %refs_2_.5, bf16[256,2048]{1,0:T(8,128)(2,1)} %refs_3_.13), custom_call_target="tpu_custom_call" | custom-call | flops 134217728 | bytes 3670016 | tf_op jit(solution)/shard_map/states/pallas_call | solution.py:425
  4.4 7.1 %all-to-all-start = ((bf16[32,64,128]{2,1,0:T(8,128)(2,1)}), bf16[32,64,128]{2,1,0:T(8,128)(2,1)S(1)}, u32[]{:S(2)}, u32[]{:S(2)}) async-start(bf16[32,64,128]{2,1,0:T(8,128)(2,1)} %bitcast.6), calls=%async_computation | async-start | bytes 1048576 | tf_op jit(solution)/shard_map/all_to_all | solution.py:487
  11.5 3.3 %collective-permute-start = (bf16[16,128,128]{2,1,0:T(8,128)(2,1)}, bf16[16,128,128]{2,1,0:T(8,128)(2,1)S(1)}, u32[]{:S(2)}, u32[]{:S(2)}) collective-permute-start(bf16[16,128,128]{2,1,0:T(8,128)(2,1)} %get-tuple-element.36), channel_id=1, source_target_pairs={{0,1},{2,3},{4,5},{6,7},{8,9},{10,11},{12,13},{14,15},{16,17},{18,... | collective-permute-start | bytes 1572872 | tf_op jit(solution)/shard_map/ppermute | solution.py:484
  14.9 2.0 %collective-permute-start.1 = (bf16[8,128,128]{2,1,0:T(8,128)(2,1)}, bf16[8,128,128]{2,1,0:T(8,128)(2,1)}, u32[]{:S(2)}, u32[]{:S(2)}) collective-permute-start(bf16[8,128,128]{2,1,0:T(8,128)(2,1)} %get-tuple-element.40), channel_id=1, source_target_pairs={{0,1},{2,3},{4,5},{6,7},{8,9},{10,11},{12,13},{14,15},{16,17},{18,... | collective-permute-start | bytes 786440 | tf_op jit(solution)/shard_map/ppermute | solution.py:484
  16.9 9.9 %all-to-all-done.refs_1_ = bf16[32,64,128]{2,1,0:T(8,128)(2,1)S(1)} async-done(((bf16[32,64,128]{2,1,0:T(8,128)(2,1)}), bf16[32,64,128]{2,1,0:T(8,128)(2,1)S(1)}, u32[]{:S(2)}, u32[]{:S(2)}) %all-to-all-start) | async-done | bytes 524320 | tf_op jit(solution)/shard_map/all_to_all | solution.py:487
  26.8 0.0 copy-done
  26.8 1.5 %scan.2 = bf16[32,64,128]{2,1,0:T(8,128)(2,1)} custom-call(s32[4]{0:T(128)S(1)} %copy-done, bf16[32,64,128]{2,1,0:T(8,128)(2,1)S(1)} %all-to-all-done.refs_1_), custom_call_target="tpu_custom_call" | custom-call | bytes 1048576 | tf_op jit(solution)/shard_map/scan/pallas_call | solution.py:425
  28.3 3.2 %all-to-all-start.1 = ((bf16[32,64,128]{2,1,0:T(8,128)(2,1)}), bf16[32,64,128]{2,1,0:T(8,128)(2,1)}, u32[]{:S(2)}, u32[]{:S(2)}) async-start(bf16[32,64,128]{2,1,0:T(8,128)(2,1)} %scan.2), calls=%async_computation.1 | async-start | bytes 1048576 | tf_op jit(solution)/shard_map/all_to_all | solution.py:487
  31.6 0.0 collective-permute-done.refs_5_.refs_7_.refs_12_
  31.6 0.0 copy-start.4
  31.6 0.8 copy-done.4
  32.4 0.0 copy-start.5
  32.4 5.2 %inner.1.refs_4_ = f32[256,2048]{1,0:T(8,128)} custom-call(s32[4]{0:T(128)} %refs_0_.17, s32[2,6]{1,0:T(2,128)} %refs_1_.13, bf16[256,2048]{1,0:T(8,128)(2,1)} %refs_2_.4, bf16[256,2048]{1,0:T(8,128)(2,1)} %refs_2_.5, bf16[256,2048]{1,0:T(8,128)(2,1)} %refs_3_.13, bf16[16,128,128]{2,1,0:T(8,128)(2,1)} %copy-done.4), custom_call_target="tpu_custom_call" | custom-call | flops 399999991808 | bytes 5242880 | tf_op jit(solution)/shard_map/inner/pallas_call | solution.py:425
  37.6 9.3 %all-to-all-done.1 = bf16[32,64,128]{2,1,0:T(8,128)(2,1)} async-done(((bf16[32,64,128]{2,1,0:T(8,128)(2,1)}), bf16[32,64,128]{2,1,0:T(8,128)(2,1)}, u32[]{:S(2)}, u32[]{:S(2)}) %all-to-all-start.1) | async-done | bytes 524320 | tf_op jit(solution)/shard_map/all_to_all | solution.py:487
  46.9 0.0 copy-done.5
  46.9 4.3 %collective-permute-start.2 = (bf16[8,128,128]{2,1,0:T(8,128)(2,1)S(1)}, bf16[8,128,128]{2,1,0:T(8,128)(2,1)S(1)}, u32[]{:S(2)}, u32[]{:S(2)}) collective-permute-start(bf16[8,128,128]{2,1,0:T(8,128)(2,1)S(1)} %copy-done.5), channel_id=1, source_target_pairs={{0,1},{2,3},{4,5},{6,7},{8,9},{10,11},{12,13},{14,15},{16,17},{18,... | collective-permute-start | bytes 786440 | tf_op jit(solution)/shard_map/ppermute | solution.py:484
  51.2 4.4 %norm.2 = (f32[128,128]{1,0:T(8,128)}, bf16[128,2048]{1,0:T(8,128)(2,1)}, bf16[128,2048]{1,0:T(8,128)(2,1)}, bf16[16,128,128]{2,1,0:T(8,128)(2,1)}) custom-call(s32[4]{0:T(128)} %refs_0_.17, s32[2,6]{1,0:T(2,128)} %refs_1_.13, f32[1,2048]{1,0:T(1,128)} %bitcast.7, bf16[256,2048]{1,0:T(8,128)(2,1)} %refs_2_.4, f32[256,2048]{1,0:T(8,128)} %inner.1.refs_4_, ...), custom_call_target="tpu_custom_call" | custom-call | flops 134217728 | bytes 6889472 | tf_op jit(solution)/shard_map/norm/pallas_call | solution.py:425
  55.6 1.3 %collective-permute-start.3 = (bf16[16,128,128]{2,1,0:T(8,128)(2,1)}, bf16[16,128,128]{2,1,0:T(8,128)(2,1)}, u32[]{:S(2)}, u32[]{:S(2)}) collective-permute-start(bf16[16,128,128]{2,1,0:T(8,128)(2,1)} %get-tuple-element.42.refs_9_), channel_id=1, source_target_pairs={{1,0},{3,2},{5,4},{7,6},{9,8},{11,10},{13,12},{15,14},{17,16},{19,... | collective-permute-start | bytes 1572872 | tf_op jit(solution)/shard_map/ppermute | solution.py:484
  56.9 0.0 collective-permute-done.1.refs_7_.refs_13_
  56.9 0.3 collective-permute-done.2.refs_8_.refs_14_
  57.3 0.0 copy-start.6
  57.3 0.7 copy-done.6
  58.0 4.8 %norm.3 = (f32[128,128]{1,0:T(8,128)}, bf16[128,2048]{1,0:T(8,128)(2,1)}, bf16[128,2048]{1,0:T(8,128)(2,1)}, bf16[16,128,128]{2,1,0:T(8,128)(2,1)}, bf16[16,128,128]{2,1,0:T(8,128)(2,1)}) custom-call(s32[4]{0:T(128)} %refs_0_.17, s32[2,6]{1,0:T(2,128)} %refs_1_.13, f32[1,2048]{1,0:T(1,128)} %bitcast.8, bf16[256,2048]{1,0:T(8,128)(2,1)} %refs_2_.4, ...), custom_call_target="tpu_custom_call" | custom-call | flops 399999991808 | bytes 7938048 | tf_op jit(solution)/shard_map/norm/pallas_call | solution.py:425
  62.8 6.7 %all-to-all-start.2 = ((bf16[32,64,128]{2,1,0:T(8,128)(2,1)}), bf16[32,64,128]{2,1,0:T(8,128)(2,1)}, u32[]{:S(2)}, u32[]{:S(2)}) async-start(bf16[32,64,128]{2,1,0:T(8,128)(2,1)} %bitcast.5), calls=%async_computation.2 | async-start | bytes 1048576 | tf_op jit(solution)/shard_map/all_to_all | solution.py:487
  69.5 1.3 %collective-permute-start.4 = (bf16[16,128,128]{2,1,0:T(8,128)(2,1)}, bf16[16,128,128]{2,1,0:T(8,128)(2,1)}, u32[]{:S(2)}, u32[]{:S(2)}) collective-permute-start(bf16[16,128,128]{2,1,0:T(8,128)(2,1)} %get-tuple-element.54), channel_id=1, source_target_pairs={{1,0},{3,2},{5,4},{7,6},{9,8},{11,10},{13,12},{15,14},{17,16},{19,... | collective-permute-start | bytes 1572872 | tf_op jit(solution)/shard_map/ppermute | solution.py:484
  70.8 0.7 collective-permute-done.3.refs_15_.refs_7_
  71.5 0.0 copy-start.1
  71.5 7.9 %query_grads.1 = (bf16[256,2048]{1,0:T(8,128)(2,1)}, bf16[256,2048]{1,0:T(8,128)(2,1)}) custom-call(s32[4]{0:T(128)} %refs_0_.17, s32[2,6]{1,0:T(2,128)} %refs_1_.13, f32[1,2048]{1,0:T(1,128)} %bitcast.9, bf16[256,2048]{1,0:T(8,128)(2,1)} %refs_2_.5, bf16[256,2048]{1,0:T(8,128)(2,1)} %refs_3_.13, bf16[16,128,128]{2,1,0:T(8,128)(2,1)} %bitcast.2.refs_6_.refs_5_, ...), custom_call_target="tpu_custom_call" | custom-call | flops 399999991808 | bytes 8003584 | tf_op jit(solution)/shard_map/query_grads/pallas_call | solution.py:425
  79.4 5.5 %all-to-all-done.2.refs_1_ = bf16[32,64,128]{2,1,0:T(8,128)(2,1)} async-done(((bf16[32,64,128]{2,1,0:T(8,128)(2,1)}), bf16[32,64,128]{2,1,0:T(8,128)(2,1)}, u32[]{:S(2)}, u32[]{:S(2)}) %all-to-all-start.2) | async-done | bytes 524320 | tf_op jit(solution)/shard_map/all_to_all | solution.py:487
  84.8 0.0 copy-done.1
  84.8 2.0 %scan.3 = bf16[32,64,128]{2,1,0:T(8,128)(2,1)} custom-call(s32[4]{0:T(128)S(1)} %copy-done.1, bf16[32,64,128]{2,1,0:T(8,128)(2,1)} %all-to-all-done.2.refs_1_), custom_call_target="tpu_custom_call" | custom-call | bytes 1048576 | tf_op jit(solution)/shard_map/scan/pallas_call | solution.py:425
  86.9 3.3 %all-to-all-start.3 = ((bf16[32,64,128]{2,1,0:T(8,128)(2,1)}), bf16[32,64,128]{2,1,0:T(8,128)(2,1)}, u32[]{:S(2)}, u32[]{:S(2)}) async-start(bf16[32,64,128]{2,1,0:T(8,128)(2,1)} %scan.3), calls=%async_computation.3 | async-start | bytes 1048576 | tf_op jit(solution)/shard_map/all_to_all | solution.py:487
  90.1 1.3 %collective-permute-done.4.refs_8_ = bf16[16,128,128]{2,1,0:T(8,128)(2,1)} collective-permute-done((bf16[16,128,128]{2,1,0:T(8,128)(2,1)}, bf16[16,128,128]{2,1,0:T(8,128)(2,1)}, u32[]{:S(2)}, u32[]{:S(2)}) %collective-permute-start.4) | collective-permute-done | bytes 524320 | tf_op jit(solution)/shard_map/ppermute | solution.py:484
  91.4 0.0 copy-start.2
  91.4 0.0 copy-start.3
  91.4 10.3 %key_grads.1 = (f32[256,2048]{1,0:T(8,128)}, f32[256,2048]{1,0:T(8,128)}) custom-call(s32[4]{0:T(128)} %refs_0_.17, s32[2,6]{1,0:T(2,128)} %refs_1_.13, bf16[256,2048]{1,0:T(8,128)(2,1)} %refs_2_.4, bf16[256,2048]{1,0:T(8,128)(2,1)} %refs_2_.5, bf16[256,2048]{1,0:T(8,128)(2,1)} %refs_3_.13, bf16[128,2048]{1,0:T(8,128)(2,1)} %get-tuple-element.39.refs_6_.refs_5_, ...), custom_call_target="tpu_custom_call" | custom-call | flops 399999991808 | bytes 9437184 | tf_op jit(solution)/shard_map/key_grads/pallas_call | solution.py:425
  101.7 3.7 %all-to-all-done.3 = bf16[32,64,128]{2,1,0:T(8,128)(2,1)} async-done(((bf16[32,64,128]{2,1,0:T(8,128)(2,1)}), bf16[32,64,128]{2,1,0:T(8,128)(2,1)}, u32[]{:S(2)}, u32[]{:S(2)}) %all-to-all-start.3) | async-done | bytes 524320 | tf_op jit(solution)/shard_map/all_to_all | solution.py:487
  105.4 0.0 copy-done.2
  105.4 0.0 copy-done.3
  105.4 5.1 %last.1 = (bf16[256,2048]{1,0:T(8,128)(2,1)}, bf16[256,2048]{1,0:T(8,128)(2,1)}) custom-call(s32[4]{0:T(128)S(1)} %copy-done.2, s32[2,6]{1,0:T(2,128)S(1)} %copy-done.3, bf16[256,2048]{1,0:T(8,128)(2,1)} %refs_2_.5, bf16[256,2048]{1,0:T(8,128)(2,1)} %refs_3_.13, f32[256,2048]{1,0:T(8,128)} %get-tuple-element.55.refs_4_, ...), custom_call_target="tpu_custom_call" | custom-call | flops 268435456 | bytes 8912896 | tf_op jit(solution)/shard_map/last/pallas_call | solution.py:425
Async XLA Ops:
  0.6 26.2 %copy-start = (s32[4]{0:T(128)S(1)}, s32[4]{0:T(128)}, u32[]{:S(2)}) copy-start(s32[4]{0:T(128)} %refs_0_.17) | copy-start | bytes 52
  4.4 22.4 %all-to-all-start = ((bf16[32,64,128]{2,1,0:T(8,128)(2,1)}), bf16[32,64,128]{2,1,0:T(8,128)(2,1)S(1)}, u32[]{:S(2)}, u32[]{:S(2)}) async-start(bf16[32,64,128]{2,1,0:T(8,128)(2,1)} %bitcast.6), calls=%async_computation | async-start | bytes 1048576 | tf_op jit(solution)/shard_map/all_to_all | solution.py:487
  11.5 20.1 %collective-permute-start = (bf16[16,128,128]{2,1,0:T(8,128)(2,1)}, bf16[16,128,128]{2,1,0:T(8,128)(2,1)S(1)}, u32[]{:S(2)}, u32[]{:S(2)}) collective-permute-start(bf16[16,128,128]{2,1,0:T(8,128)(2,1)} %get-tuple-element.36), channel_id=1, source_target_pairs={{0,1},{2,3},{4,5},{6,7},{8,9},{10,11},{12,13},{14,15},{16,17},{18,... | collective-permute-start | bytes 1572872 | tf_op jit(solution)/shard_map/ppermute | solution.py:484
  14.9 42.1 %collective-permute-start.1 = (bf16[8,128,128]{2,1,0:T(8,128)(2,1)}, bf16[8,128,128]{2,1,0:T(8,128)(2,1)}, u32[]{:S(2)}, u32[]{:S(2)}) collective-permute-start(bf16[8,128,128]{2,1,0:T(8,128)(2,1)} %get-tuple-element.40), channel_id=1, source_target_pairs={{0,1},{2,3},{4,5},{6,7},{8,9},{10,11},{12,13},{14,15},{16,17},{18,... | collective-permute-start | bytes 786440 | tf_op jit(solution)/shard_map/ppermute | solution.py:484
  28.3 18.6 %all-to-all-start.1 = ((bf16[32,64,128]{2,1,0:T(8,128)(2,1)}), bf16[32,64,128]{2,1,0:T(8,128)(2,1)}, u32[]{:S(2)}, u32[]{:S(2)}) async-start(bf16[32,64,128]{2,1,0:T(8,128)(2,1)} %scan.2), calls=%async_computation.1 | async-start | bytes 1048576 | tf_op jit(solution)/shard_map/all_to_all | solution.py:487
  31.6 0.8 copy-start.4
  32.4 14.5 %copy-start.5 = (bf16[8,128,128]{2,1,0:T(8,128)(2,1)S(1)}, bf16[8,128,128]{2,1,0:T(8,128)(2,1)}, u32[]{:S(2)}) copy-start(bf16[8,128,128]{2,1,0:T(8,128)(2,1)} %get-tuple-element.41) | copy-start | bytes 786436
  46.9 10.4 %collective-permute-start.2 = (bf16[8,128,128]{2,1,0:T(8,128)(2,1)S(1)}, bf16[8,128,128]{2,1,0:T(8,128)(2,1)S(1)}, u32[]{:S(2)}, u32[]{:S(2)}) collective-permute-start(bf16[8,128,128]{2,1,0:T(8,128)(2,1)S(1)} %copy-done.5), channel_id=1, source_target_pairs={{0,1},{2,3},{4,5},{6,7},{8,9},{10,11},{12,13},{14,15},{16,17},{18,... | collective-permute-start | bytes 786440 | tf_op jit(solution)/shard_map/ppermute | solution.py:484
  55.6 15.9 %collective-permute-start.3 = (bf16[16,128,128]{2,1,0:T(8,128)(2,1)}, bf16[16,128,128]{2,1,0:T(8,128)(2,1)}, u32[]{:S(2)}, u32[]{:S(2)}) collective-permute-start(bf16[16,128,128]{2,1,0:T(8,128)(2,1)} %get-tuple-element.42.refs_9_), channel_id=1, source_target_pairs={{1,0},{3,2},{5,4},{7,6},{9,8},{11,10},{13,12},{15,14},{17,16},{19,... | collective-permute-start | bytes 1572872 | tf_op jit(solution)/shard_map/ppermute | solution.py:484
  57.3 0.7 copy-start.6
  62.8 22.0 %all-to-all-start.2 = ((bf16[32,64,128]{2,1,0:T(8,128)(2,1)}), bf16[32,64,128]{2,1,0:T(8,128)(2,1)}, u32[]{:S(2)}, u32[]{:S(2)}) async-start(bf16[32,64,128]{2,1,0:T(8,128)(2,1)} %bitcast.5), calls=%async_computation.2 | async-start | bytes 1048576 | tf_op jit(solution)/shard_map/all_to_all | solution.py:487
  69.5 22.0 %collective-permute-start.4 = (bf16[16,128,128]{2,1,0:T(8,128)(2,1)}, bf16[16,128,128]{2,1,0:T(8,128)(2,1)}, u32[]{:S(2)}, u32[]{:S(2)}) collective-permute-start(bf16[16,128,128]{2,1,0:T(8,128)(2,1)} %get-tuple-element.54), channel_id=1, source_target_pairs={{1,0},{3,2},{5,4},{7,6},{9,8},{11,10},{13,12},{15,14},{17,16},{19,... | collective-permute-start | bytes 1572872 | tf_op jit(solution)/shard_map/ppermute | solution.py:484
  71.5 13.4 %copy-start.1 = (s32[4]{0:T(128)S(1)}, s32[4]{0:T(128)}, u32[]{:S(2)}) copy-start(s32[4]{0:T(128)} %refs_0_.17) | copy-start | bytes 52
  86.9 18.6 %all-to-all-start.3 = ((bf16[32,64,128]{2,1,0:T(8,128)(2,1)}), bf16[32,64,128]{2,1,0:T(8,128)(2,1)}, u32[]{:S(2)}, u32[]{:S(2)}) async-start(bf16[32,64,128]{2,1,0:T(8,128)(2,1)} %scan.3), calls=%async_computation.3 | async-start | bytes 1048576 | tf_op jit(solution)/shard_map/all_to_all | solution.py:487
  91.4 14.0 %copy-start.2 = (s32[4]{0:T(128)S(1)}, s32[4]{0:T(128)}, u32[]{:S(2)}) copy-start(s32[4]{0:T(128)} %refs_0_.17) | copy-start | bytes 52
  91.4 14.0 %copy-start.3 = (s32[2,6]{1,0:T(2,128)S(1)}, s32[2,6]{1,0:T(2,128)}, u32[]{:S(2)}) copy-start(s32[2,6]{1,0:T(2,128)} %refs_1_.13) | copy-start | bytes 148

commit v12 on v11

--- a/solution.py
+++ b/solution.py
@@ -157,7 +157,7 @@
     return pl.ds(block * BLOCK, BLOCK)
 
 
-def state_body(place_of, ins, outs, scratch, arrive, leave, chunks, *, counts):
+def state_body(place_of, ins, outs, scratch, arrive, leave, chunks, *, counts, own):
     k_ref, v_ref = ins
     outs = joined(outs, counts)
     rows, width = k_ref.shape
@@ -165,10 +165,12 @@
     last = place.seg(place.start(place.blocks) - 1)
     ends = [place.seg(place.start(b + 1) - 1) for b in range(place.blocks)]
     masks = [(place.row_segments(b) == ends[b]).astype(BF) for b in range(place.blocks)]
-    wanted = [[same(e, last) for e in ends]]
-    for b in range(place.blocks):
-        for away in range(1, place.devices):
-            wanted.append(place.to_later(away, b))
+    if own:
+        wanted = [[same(e, last) for e in ends]]
+    else:
+        wanted = [
+            place.to_later(away, b) for b in range(place.blocks) for away in range(1, place.devices)
+        ]
     for c, heads in enumerate(chunks):
         arrive(c)
         for head in heads:
@@ -502,21 +504,35 @@
     gain_row = Part(gain.reshape(1, width))
     halves = [2 if b > 0 and chunks % 2 == 0 else 1 for b in range(blocks) for _ in range(peers)]
     later = [[shape((heads // n, DH, DH), BF)] * n for n in halves]
-    sum_kv, *later = call(
-        functools.partial(state_body, counts=[1, *halves]),
-        "states",
+    (sum_kv,) = call(
+        functools.partial(state_body, counts=[1], own=True),
+        "total",
         scalars,
         [wide(keys), wide(values)],
-        [states(state), *[part for arrays in later for part in split_states(arrays, few)]],
+        [states(state)],
         heads,
         few,
         flops=unit,
     )
+    slices = sum_kv.reshape(total, -1, DH)
+    slices, late_keys = lax.optimization_barrier((slices, keys))
+    slices = exchanged(slices)
+    if later:
+        later = call(
+            functools.partial(state_body, counts=halves, own=False),
+            "states",
+            scalars,
+            [wide(late_keys), wide(values)],
+            [part for arrays in later for part in split_states(arrays, few)],
+            heads,
+            few,
+            flops=LONG,
+        )
     later = iter(later)
     from_peers = [[next(later) for _ in range(n)] for n in halves]
     for at, arrays in enumerate(from_peers):
         arrays[0] = to_peers(arrays[0], 1 + at % peers, False)
-    slices = scanned(exchanged(sum_kv.reshape(total, -1, DH)), False)
+    slices = scanned(slices, False)
     slices, late_queries = lax.optimization_barrier((slices, queries))
     (raw_inner,) = call(
         inner_body,
@@ -613,7 +629,7 @@
         [wide(keys), wide(values), wide(part_k), wide(part_v), states(grad_state)],
         [wide(tokens), wide(tokens)],
         heads,
-        chunks,
+        few,
         flops=2 * unit,
         limit=NARROW_BYTES,
     )

time: 112 us -> 112 us (level)
  waiting for transfers between devices: 30.8 us -> 27 us
  Pallas kernels: 44.9 us -> 48.5 us
    pallas_call x9 -> x10, Pallas kernels: 44.9 us -> 48.5 us  [call(): pl.pallas_call(kernel, name=name, in_specs=[*[pl.BlockSpec(memory_space=p...]
    all_to_all x4, waiting for transfers between devices: 28.5 us -> 25.7 us  [exchanged(): return lax.all_to_all(slices, AXES, split_axis=0, concat_axis=0, tiled=True)]
  transfers between devices with their start and end apart: 9 -> 9, of which waited for: 7 -> 5; matrix products, arithmetic and copies ran while one was open for 0% -> 0% of each run, Pallas kernels for 33% -> 36%
where the time goes in v12:
time: 112 us; the launch traced here: 111 us
  Pallas kernels  48.5 us (43%)
  starting transfers between devices  32.6 us (29%)
  waiting for transfers between devices  27 us (24%)
  local copies, waits for them, and re-layouts  1.52 us (1%)
    pallas_call x10, Pallas kernels, call(): pl.pallas_call(kernel, name=name, in_specs=[*[pl.BlockSpec(memory_space=p...  48.5 us
    all_to_all x4, waiting for transfers between devices, exchanged(): return lax.all_to_all(slices, AXES, split_axis=0, concat_axis=0, tiled=True)  25.7 us
    all_to_all x4, starting transfers between devices, exchanged(): return lax.all_to_all(slices, AXES, split_axis=0, concat_axis=0, tiled=True)  21.1 us
    ppermute x5, starting transfers between devices, to_peers(): return lax.ppermute(array, 'head', pairs)  11.6 us
  transfers between devices with their start and end apart: 9, of which 5 were waited for; matrix products, arithmetic and copies ran while one was open for 0% of the time, Pallas kernels for 36%

profile of v12, /device:TPU:1, one launch (start us, length us, event | category | flops | bytes accessed | tf_op | source)
XLA Modules:
  0.0 110.7 jit_solution(2180575915794751340)
XLA Ops:
  0.6 3.3 %total.1 = bf16[16,128,128]{2,1,0:T(8,128)(2,1)} custom-call(s32[4]{0:T(128)} %refs_0_.19, s32[2,6]{1,0:T(2,128)} %refs_1_.15, bf16[256,2048]{1,0:T(8,128)(2,1)} %refs_2_.6, bf16[256,2048]{1,0:T(8,128)(2,1)} %refs_3_.15), custom_call_target="tpu_custom_call" | custom-call | flops 134217728 | bytes 2621440 | tf_op jit(solution)/shard_map/total/pallas_call | solution.py:427
  4.0 7.2 %all-to-all-start = ((bf16[32,64,128]{2,1,0:T(8,128)(2,1)}), bf16[32,64,128]{2,1,0:T(8,128)(2,1)}, u32[]{:S(2)}, u32[]{:S(2)}) async-start(bf16[32,64,128]{2,1,0:T(8,128)(2,1)} %bitcast.5), calls=%async_computation | async-start | bytes 1048576 | tf_op jit(solution)/shard_map/all_to_all | solution.py:489
  11.2 0.0 copy-start
  11.2 3.6 %states.1 = (bf16[16,128,128]{2,1,0:T(8,128)(2,1)}, bf16[8,128,128]{2,1,0:T(8,128)(2,1)}, bf16[8,128,128]{2,1,0:T(8,128)(2,1)}) custom-call(s32[4]{0:T(128)} %refs_0_.19, s32[2,6]{1,0:T(2,128)} %refs_1_.15, bf16[256,2048]{1,0:T(8,128)(2,1)} %refs_2_.6, bf16[256,2048]{1,0:T(8,128)(2,1)} %refs_3_.15), custom_call_target="tpu_custom_call" | custom-call | flops 399999991808 | bytes 3145728 | tf_op jit(solution)/shard_map/states/pallas_call | solution.py:427
  14.8 3.3 %collective-permute-start = (bf16[16,128,128]{2,1,0:T(8,128)(2,1)}, bf16[16,128,128]{2,1,0:T(8,128)(2,1)S(1)}, u32[]{:S(2)}, u32[]{:S(2)}) collective-permute-start(bf16[16,128,128]{2,1,0:T(8,128)(2,1)} %get-tuple-element.38), channel_id=1, source_target_pairs={{0,1},{2,3},{4,5},{6,7},{8,9},{10,11},{12,13},{14,15},{16,17},{18,... | collective-permute-start | bytes 1572872 | tf_op jit(solution)/shard_map/ppermute | solution.py:486
  18.1 2.0 %collective-permute-start.1 = (bf16[8,128,128]{2,1,0:T(8,128)(2,1)}, bf16[8,128,128]{2,1,0:T(8,128)(2,1)}, u32[]{:S(2)}, u32[]{:S(2)}) collective-permute-start(bf16[8,128,128]{2,1,0:T(8,128)(2,1)} %get-tuple-element.42), channel_id=1, source_target_pairs={{0,1},{2,3},{4,5},{6,7},{8,9},{10,11},{12,13},{14,15},{16,17},{18,... | collective-permute-start | bytes 786440 | tf_op jit(solution)/shard_map/ppermute | solution.py:486
  20.1 6.4 %all-to-all-done.refs_1_ = bf16[32,64,128]{2,1,0:T(8,128)(2,1)} async-done(((bf16[32,64,128]{2,1,0:T(8,128)(2,1)}), bf16[32,64,128]{2,1,0:T(8,128)(2,1)}, u32[]{:S(2)}, u32[]{:S(2)}) %all-to-all-start) | async-done | bytes 524320 | tf_op jit(solution)/shard_map/all_to_all | solution.py:489
  26.5 0.0 copy-done
  26.5 2.0 %scan.2 = bf16[32,64,128]{2,1,0:T(8,128)(2,1)} custom-call(s32[4]{0:T(128)S(1)} %copy-done, bf16[32,64,128]{2,1,0:T(8,128)(2,1)} %all-to-all-done.refs_1_), custom_call_target="tpu_custom_call" | custom-call | bytes 1048576 | tf_op jit(solution)/shard_map/scan/pallas_call | solution.py:427
  28.5 3.2 %all-to-all-start.1 = ((bf16[32,64,128]{2,1,0:T(8,128)(2,1)}), bf16[32,64,128]{2,1,0:T(8,128)(2,1)}, u32[]{:S(2)}, u32[]{:S(2)}) async-start(bf16[32,64,128]{2,1,0:T(8,128)(2,1)} %scan.2), calls=%async_computation.1 | async-start | bytes 1048576 | tf_op jit(solution)/shard_map/all_to_all | solution.py:489
  31.8 0.0 collective-permute-done.refs_5_.refs_7_.refs_12_
  31.8 0.0 copy-start.4
  31.8 0.8 copy-done.4
  32.6 0.0 copy-start.5
  32.6 5.2 %inner.1.refs_4_ = f32[256,2048]{1,0:T(8,128)} custom-call(s32[4]{0:T(128)} %refs_0_.19, s32[2,6]{1,0:T(2,128)} %refs_1_.15, bf16[256,2048]{1,0:T(8,128)(2,1)} %refs_2_.5, bf16[256,2048]{1,0:T(8,128)(2,1)} %refs_2_.6, bf16[256,2048]{1,0:T(8,128)(2,1)} %refs_3_.15, bf16[16,128,128]{2,1,0:T(8,128)(2,1)} %copy-done.4), custom_call_target="tpu_custom_call" | custom-call | flops 399999991808 | bytes 5242880 | tf_op jit(solution)/shard_map/inner/pallas_call | solution.py:427
  37.8 9.3 %all-to-all-done.1 = bf16[32,64,128]{2,1,0:T(8,128)(2,1)} async-done(((bf16[32,64,128]{2,1,0:T(8,128)(2,1)}), bf16[32,64,128]{2,1,0:T(8,128)(2,1)}, u32[]{:S(2)}, u32[]{:S(2)}) %all-to-all-start.1) | async-done | bytes 524320 | tf_op jit(solution)/shard_map/all_to_all | solution.py:489
  47.1 0.0 copy-done.5
  47.1 3.7 %collective-permute-start.2 = (bf16[8,128,128]{2,1,0:T(8,128)(2,1)S(1)}, bf16[8,128,128]{2,1,0:T(8,128)(2,1)S(1)}, u32[]{:S(2)}, u32[]{:S(2)}) collective-permute-start(bf16[8,128,128]{2,1,0:T(8,128)(2,1)S(1)} %copy-done.5), channel_id=1, source_target_pairs={{0,1},{2,3},{4,5},{6,7},{8,9},{10,11},{12,13},{14,15},{16,17},{18,... | collective-permute-start | bytes 786440 | tf_op jit(solution)/shard_map/ppermute | solution.py:486
  50.8 4.4 %norm.2 = (f32[128,128]{1,0:T(8,128)}, bf16[128,2048]{1,0:T(8,128)(2,1)}, bf16[128,2048]{1,0:T(8,128)(2,1)}, bf16[16,128,128]{2,1,0:T(8,128)(2,1)}) custom-call(s32[4]{0:T(128)} %refs_0_.19, s32[2,6]{1,0:T(2,128)} %refs_1_.15, f32[1,2048]{1,0:T(1,128)} %bitcast.7, bf16[256,2048]{1,0:T(8,128)(2,1)} %refs_2_.5, f32[256,2048]{1,0:T(8,128)} %inner.1.refs_4_, ...), custom_call_target="tpu_custom_call" | custom-call | flops 134217728 | bytes 6889472 | tf_op jit(solution)/shard_map/norm/pallas_call | solution.py:427
  55.2 1.3 %collective-permute-start.3 = (bf16[16,128,128]{2,1,0:T(8,128)(2,1)}, bf16[16,128,128]{2,1,0:T(8,128)(2,1)}, u32[]{:S(2)}, u32[]{:S(2)}) collective-permute-start(bf16[16,128,128]{2,1,0:T(8,128)(2,1)} %get-tuple-element.44.refs_9_), channel_id=1, source_target_pairs={{1,0},{3,2},{5,4},{7,6},{9,8},{11,10},{13,12},{15,14},{17,16},{19,... | collective-permute-start | bytes 1572872 | tf_op jit(solution)/shard_map/ppermute | solution.py:486
  56.5 0.0 collective-permute-done.1.refs_7_.refs_13_
  56.5 0.0 collective-permute-done.2.refs_8_.refs_14_
  56.5 0.0 copy-start.6
  56.5 0.7 copy-done.6
  57.2 4.8 %norm.3 = (f32[128,128]{1,0:T(8,128)}, bf16[128,2048]{1,0:T(8,128)(2,1)}, bf16[128,2048]{1,0:T(8,128)(2,1)}, bf16[16,128,128]{2,1,0:T(8,128)(2,1)}, bf16[16,128,128]{2,1,0:T(8,128)(2,1)}) custom-call(s32[4]{0:T(128)} %refs_0_.19, s32[2,6]{1,0:T(2,128)} %refs_1_.15, f32[1,2048]{1,0:T(1,128)} %bitcast.8, bf16[256,2048]{1,0:T(8,128)(2,1)} %refs_2_.5, ...), custom_call_target="tpu_custom_call" | custom-call | flops 399999991808 | bytes 7938048 | tf_op jit(solution)/shard_map/norm/pallas_call | solution.py:427
  62.1 7.4 %all-to-all-start.2 = ((bf16[32,64,128]{2,1,0:T(8,128)(2,1)}), bf16[32,64,128]{2,1,0:T(8,128)(2,1)}, u32[]{:S(2)}, u32[]{:S(2)}) async-start(bf16[32,64,128]{2,1,0:T(8,128)(2,1)} %bitcast.6), calls=%async_computation.2 | async-start | bytes 1048576 | tf_op jit(solution)/shard_map/all_to_all | solution.py:489
  69.5 1.3 %collective-permute-start.4 = (bf16[16,128,128]{2,1,0:T(8,128)(2,1)}, bf16[16,128,128]{2,1,0:T(8,128)(2,1)}, u32[]{:S(2)}, u32[]{:S(2)}) collective-permute-start(bf16[16,128,128]{2,1,0:T(8,128)(2,1)} %get-tuple-element.56), channel_id=1, source_target_pairs={{1,0},{3,2},{5,4},{7,6},{9,8},{11,10},{13,12},{15,14},{17,16},{19,... | collective-permute-start | bytes 1572872 | tf_op jit(solution)/shard_map/ppermute | solution.py:486
  70.8 0.0 collective-permute-done.3.refs_15_.refs_7_
  70.8 0.0 copy-start.1
  70.8 7.8 %query_grads.1 = (bf16[256,2048]{1,0:T(8,128)(2,1)}, bf16[256,2048]{1,0:T(8,128)(2,1)}) custom-call(s32[4]{0:T(128)} %refs_0_.19, s32[2,6]{1,0:T(2,128)} %refs_1_.15, f32[1,2048]{1,0:T(1,128)} %bitcast.9, bf16[256,2048]{1,0:T(8,128)(2,1)} %refs_2_.6, bf16[256,2048]{1,0:T(8,128)(2,1)} %refs_3_.15, bf16[16,128,128]{2,1,0:T(8,128)(2,1)} %bitcast.2.refs_6_.refs_5_, ...), custom_call_target="tpu_custom_call" | custom-call | flops 399999991808 | bytes 8003584 | tf_op jit(solution)/shard_map/query_grads/pallas_call | solution.py:427
  78.6 6.3 %all-to-all-done.2.refs_1_ = bf16[32,64,128]{2,1,0:T(8,128)(2,1)} async-done(((bf16[32,64,128]{2,1,0:T(8,128)(2,1)}), bf16[32,64,128]{2,1,0:T(8,128)(2,1)}, u32[]{:S(2)}, u32[]{:S(2)}) %all-to-all-start.2) | async-done | bytes 524320 | tf_op jit(solution)/shard_map/all_to_all | solution.py:489
  84.9 0.0 copy-done.1
  84.9 2.0 %scan.3 = bf16[32,64,128]{2,1,0:T(8,128)(2,1)} custom-call(s32[4]{0:T(128)S(1)} %copy-done.1, bf16[32,64,128]{2,1,0:T(8,128)(2,1)} %all-to-all-done.2.refs_1_), custom_call_target="tpu_custom_call" | custom-call | bytes 1048576 | tf_op jit(solution)/shard_map/scan/pallas_call | solution.py:427
  86.9 3.3 %all-to-all-start.3 = ((bf16[32,64,128]{2,1,0:T(8,128)(2,1)}), bf16[32,64,128]{2,1,0:T(8,128)(2,1)}, u32[]{:S(2)}, u32[]{:S(2)}) async-start(bf16[32,64,128]{2,1,0:T(8,128)(2,1)} %scan.3), calls=%async_computation.3 | async-start | bytes 1048576 | tf_op jit(solution)/shard_map/all_to_all | solution.py:489
  90.2 1.3 %collective-permute-done.4.refs_8_ = bf16[16,128,128]{2,1,0:T(8,128)(2,1)} collective-permute-done((bf16[16,128,128]{2,1,0:T(8,128)(2,1)}, bf16[16,128,128]{2,1,0:T(8,128)(2,1)}, u32[]{:S(2)}, u32[]{:S(2)}) %collective-permute-start.4) | collective-permute-done | bytes 524320 | tf_op jit(solution)/shard_map/ppermute | solution.py:486
  91.5 0.0 copy-start.2
  91.5 0.0 copy-start.3
  91.5 10.3 %key_grads.1 = (f32[256,2048]{1,0:T(8,128)}, f32[256,2048]{1,0:T(8,128)}) custom-call(s32[4]{0:T(128)} %refs_0_.19, s32[2,6]{1,0:T(2,128)} %refs_1_.15, bf16[256,2048]{1,0:T(8,128)(2,1)} %refs_2_.5, bf16[256,2048]{1,0:T(8,128)(2,1)} %refs_2_.6, bf16[256,2048]{1,0:T(8,128)(2,1)} %refs_3_.15, bf16[128,2048]{1,0:T(8,128)(2,1)} %get-tuple-element.41.refs_6_.refs_5_, ...), custom_call_target="tpu_custom_call" | custom-call | flops 399999991808 | bytes 9437184 | tf_op jit(solution)/shard_map/key_grads/pallas_call | solution.py:427
  101.7 3.7 %all-to-all-done.3 = bf16[32,64,128]{2,1,0:T(8,128)(2,1)} async-done(((bf16[32,64,128]{2,1,0:T(8,128)(2,1)}), bf16[32,64,128]{2,1,0:T(8,128)(2,1)}, u32[]{:S(2)}, u32[]{:S(2)}) %all-to-all-start.3) | async-done | bytes 524320 | tf_op jit(solution)/shard_map/all_to_all | solution.py:489
  105.4 0.0 copy-done.2
  105.4 0.0 copy-done.3
  105.5 5.0 %last.1 = (bf16[256,2048]{1,0:T(8,128)(2,1)}, bf16[256,2048]{1,0:T(8,128)(2,1)}) custom-call(s32[4]{0:T(128)S(1)} %copy-done.2, s32[2,6]{1,0:T(2,128)S(1)} %copy-done.3, bf16[256,2048]{1,0:T(8,128)(2,1)} %refs_2_.6, bf16[256,2048]{1,0:T(8,128)(2,1)} %refs_3_.15, f32[256,2048]{1,0:T(8,128)} %get-tuple-element.57.refs_4_, ...), custom_call_target="tpu_custom_call" | custom-call | flops 268435456 | bytes 8912896 | tf_op jit(solution)/shard_map/last/pallas_call | solution.py:427
Async XLA Ops:
  4.0 22.5 %all-to-all-start = ((bf16[32,64,128]{2,1,0:T(8,128)(2,1)}), bf16[32,64,128]{2,1,0:T(8,128)(2,1)}, u32[]{:S(2)}, u32[]{:S(2)}) async-start(bf16[32,64,128]{2,1,0:T(8,128)(2,1)} %bitcast.5), calls=%async_computation | async-start | bytes 1048576 | tf_op jit(solution)/shard_map/all_to_all | solution.py:489
  11.2 15.3 %copy-start = (s32[4]{0:T(128)S(1)}, s32[4]{0:T(128)}, u32[]{:S(2)}) copy-start(s32[4]{0:T(128)} %refs_0_.19) | copy-start | bytes 52
  14.8 17.0 %collective-permute-start = (bf16[16,128,128]{2,1,0:T(8,128)(2,1)}, bf16[16,128,128]{2,1,0:T(8,128)(2,1)S(1)}, u32[]{:S(2)}, u32[]{:S(2)}) collective-permute-start(bf16[16,128,128]{2,1,0:T(8,128)(2,1)} %get-tuple-element.38), channel_id=1, source_target_pairs={{0,1},{2,3},{4,5},{6,7},{8,9},{10,11},{12,13},{14,15},{16,17},{18,... | collective-permute-start | bytes 1572872 | tf_op jit(solution)/shard_map/ppermute | solution.py:486
  18.1 38.4 %collective-permute-start.1 = (bf16[8,128,128]{2,1,0:T(8,128)(2,1)}, bf16[8,128,128]{2,1,0:T(8,128)(2,1)}, u32[]{:S(2)}, u32[]{:S(2)}) collective-permute-start(bf16[8,128,128]{2,1,0:T(8,128)(2,1)} %get-tuple-element.42), channel_id=1, source_target_pairs={{0,1},{2,3},{4,5},{6,7},{8,9},{10,11},{12,13},{14,15},{16,17},{18,... | collective-permute-start | bytes 786440 | tf_op jit(solution)/shard_map/ppermute | solution.py:486
  28.5 18.6 %all-to-all-start.1 = ((bf16[32,64,128]{2,1,0:T(8,128)(2,1)}), bf16[32,64,128]{2,1,0:T(8,128)(2,1)}, u32[]{:S(2)}, u32[]{:S(2)}) async-start(bf16[32,64,128]{2,1,0:T(8,128)(2,1)} %scan.2), calls=%async_computation.1 | async-start | bytes 1048576 | tf_op jit(solution)/shard_map/all_to_all | solution.py:489
  31.8 0.8 copy-start.4
  32.6 14.5 %copy-start.5 = (bf16[8,128,128]{2,1,0:T(8,128)(2,1)S(1)}, bf16[8,128,128]{2,1,0:T(8,128)(2,1)}, u32[]{:S(2)}) copy-start(bf16[8,128,128]{2,1,0:T(8,128)(2,1)} %get-tuple-element.43) | copy-start | bytes 786436
  47.1 9.4 %collective-permute-start.2 = (bf16[8,128,128]{2,1,0:T(8,128)(2,1)S(1)}, bf16[8,128,128]{2,1,0:T(8,128)(2,1)S(1)}, u32[]{:S(2)}, u32[]{:S(2)}) collective-permute-start(bf16[8,128,128]{2,1,0:T(8,128)(2,1)S(1)} %copy-done.5), channel_id=1, source_target_pairs={{0,1},{2,3},{4,5},{6,7},{8,9},{10,11},{12,13},{14,15},{16,17},{18,... | collective-permute-start | bytes 786440 | tf_op jit(solution)/shard_map/ppermute | solution.py:486
  55.2 15.6 %collective-permute-start.3 = (bf16[16,128,128]{2,1,0:T(8,128)(2,1)}, bf16[16,128,128]{2,1,0:T(8,128)(2,1)}, u32[]{:S(2)}, u32[]{:S(2)}) collective-permute-start(bf16[16,128,128]{2,1,0:T(8,128)(2,1)} %get-tuple-element.44.refs_9_), channel_id=1, source_target_pairs={{1,0},{3,2},{5,4},{7,6},{9,8},{11,10},{13,12},{15,14},{17,16},{19,... | collective-permute-start | bytes 1572872 | tf_op jit(solution)/shard_map/ppermute | solution.py:486
  56.5 0.7 copy-start.6
  62.1 22.8 %all-to-all-start.2 = ((bf16[32,64,128]{2,1,0:T(8,128)(2,1)}), bf16[32,64,128]{2,1,0:T(8,128)(2,1)}, u32[]{:S(2)}, u32[]{:S(2)}) async-start(bf16[32,64,128]{2,1,0:T(8,128)(2,1)} %bitcast.6), calls=%async_computation.2 | async-start | bytes 1048576 | tf_op jit(solution)/shard_map/all_to_all | solution.py:489
  69.5 22.0 %collective-permute-start.4 = (bf16[16,128,128]{2,1,0:T(8,128)(2,1)}, bf16[16,128,128]{2,1,0:T(8,128)(2,1)}, u32[]{:S(2)}, u32[]{:S(2)}) collective-permute-start(bf16[16,128,128]{2,1,0:T(8,128)(2,1)} %get-tuple-element.56), channel_id=1, source_target_pairs={{1,0},{3,2},{5,4},{7,6},{9,8},{11,10},{13,12},{15,14},{17,16},{19,... | collective-permute-start | bytes 1572872 | tf_op jit(solution)/shard_map/ppermute | solution.py:486
  70.8 14.1 %copy-start.1 = (s32[4]{0:T(128)S(1)}, s32[4]{0:T(128)}, u32[]{:S(2)}) copy-start(s32[4]{0:T(128)} %refs_0_.19) | copy-start | bytes 52
  86.9 18.6 %all-to-all-start.3 = ((bf16[32,64,128]{2,1,0:T(8,128)(2,1)}), bf16[32,64,128]{2,1,0:T(8,128)(2,1)}, u32[]{:S(2)}, u32[]{:S(2)}) async-start(bf16[32,64,128]{2,1,0:T(8,128)(2,1)} %scan.3), calls=%async_computation.3 | async-start | bytes 1048576 | tf_op jit(solution)/shard_map/all_to_all | solution.py:489
  91.5 14.0 %copy-start.2 = (s32[4]{0:T(128)S(1)}, s32[4]{0:T(128)}, u32[]{:S(2)}) copy-start(s32[4]{0:T(128)} %refs_0_.19) | copy-start | bytes 52
  91.5 14.0 %copy-start.3 = (s32[2,6]{1,0:T(2,128)S(1)}, s32[2,6]{1,0:T(2,128)}, u32[]{:S(2)}) copy-start(s32[2,6]{1,0:T(2,128)} %refs_1_.15) | copy-start | bytes 148

commit v13 on v12

--- a/solution.py
+++ b/solution.py
@@ -157,20 +157,31 @@
     return pl.ds(block * BLOCK, BLOCK)
 
 
-def state_body(place_of, ins, outs, scratch, arrive, leave, chunks, *, counts, own):
+def total_body(place_of, ins, outs, scratch, arrive, leave, chunks):
+    k_ref, v_ref = ins
+    (t_ref,) = outs
+    place = place_of(k_ref.shape[0])
+    last = place.seg(place.start(place.blocks) - 1)
+    segments = [place.row_segments(b) for b in range(place.blocks)]
+    mask = (jnp.concatenate(segments, axis=0) == last).astype(BF)
+    for c, heads in enumerate(chunks):
+        arrive(c)
+        for head in heads:
+            at = columns(head)
+            t_ref[head] = dot(k_ref[:, at] * mask, v_ref[:, at], TN).astype(BF)
+        leave(c)
+
+
+def state_body(place_of, ins, outs, scratch, arrive, leave, chunks, *, counts):
     k_ref, v_ref = ins
     outs = joined(outs, counts)
     rows, width = k_ref.shape
     place = place_of(rows)
-    last = place.seg(place.start(place.blocks) - 1)
     ends = [place.seg(place.start(b + 1) - 1) for b in range(place.blocks)]
     masks = [(place.row_segments(b) == ends[b]).astype(BF) for b in range(place.blocks)]
-    if own:
-        wanted = [[same(e, last) for e in ends]]
-    else:
-        wanted = [
-            place.to_later(away, b) for b in range(place.blocks) for away in range(1, place.devices)
-        ]
+    wanted = [
+        place.to_later(away, b) for b in range(place.blocks) for away in range(1, place.devices)
+    ]
     for c, heads in enumerate(chunks):
         arrive(c)
         for head in heads:
@@ -505,13 +516,13 @@
     halves = [2 if b > 0 and chunks % 2 == 0 else 1 for b in range(blocks) for _ in range(peers)]
     later = [[shape((heads // n, DH, DH), BF)] * n for n in halves]
     (sum_kv,) = call(
-        functools.partial(state_body, counts=[1], own=True),
+        total_body,
         "total",
         scalars,
         [wide(keys), wide(values)],
         [states(state)],
         heads,
-        few,
+        chunks,
         flops=unit,
     )
     slices = sum_kv.reshape(total, -1, DH)
@@ -519,7 +530,7 @@
     slices = exchanged(slices)
     if later:
         later = call(
-            functools.partial(state_body, counts=halves, own=False),
+            functools.partial(state_body, counts=halves),
             "states",
             scalars,
             [wide(late_keys), wide(values)],
@@ -549,8 +560,7 @@
     kv_state = exchanged(slices).reshape(heads, DH, DH)
     for at, arrays in enumerate(from_peers):
         if len(arrays) > 1:
-            held = lax.optimization_barrier((arrays[1], kv_state, raw_inner))
-            later_half, kv_state, raw_inner = held
+            later_half, raw_inner = lax.optimization_barrier((arrays[1], raw_inner))
             arrays[1] = to_peers(later_half, 1 + at % peers, False)
 
     scales, raws, grads, updates, back = [], [], [], [], []

time: 112 us -> 108 us (0.964)
  waiting for transfers between devices: 27 us -> 23.5 us
    all_to_all x4, waiting for transfers between devices: 25.7 us -> 21.7 us  [exchanged(): return lax.all_to_all(slices, AXES, split_axis=0, concat_axis=0, tiled=True)]
  transfers between devices with their start and end apart: 9 -> 9, of which waited for: 5 -> 6; matrix products, arithmetic and copies ran while one was open for 0% -> 0% of each run, Pallas kernels for 36% -> 38%
where the time goes in v13:
time: 108 us; the launch traced here: 107 us
  Pallas kernels  48.9 us (45%)
  starting transfers between devices  32.1 us (30%)
  waiting for transfers between devices  23.5 us (22%)
  local copies, waits for them, and re-layouts  1.51 us (1%)
    pallas_call x10, Pallas kernels, call(): pl.pallas_call(kernel, name=name, in_specs=[*[pl.BlockSpec(memory_space=p...  48.9 us
    all_to_all x4, waiting for transfers between devices, exchanged(): return lax.all_to_all(slices, AXES, split_axis=0, concat_axis=0, tiled=True)  21.7 us
    all_to_all x4, starting transfers between devices, exchanged(): return lax.all_to_all(slices, AXES, split_axis=0, concat_axis=0, tiled=True)  20.8 us
    ppermute x5, starting transfers between devices, to_peers(): return lax.ppermute(array, 'head', pairs)  11.3 us
  transfers between devices with their start and end apart: 9, of which 6 were waited for; matrix products, arithmetic and copies ran while one was open for 0% of the time, Pallas kernels for 38%

profile of v13, /device:TPU:1, one launch (start us, length us, event | category | flops | bytes accessed | tf_op | source)
XLA Modules:
  0.0 107.0 jit_solution(7032059735947006064)
XLA Ops:
  0.6 3.7 %total.1 = bf16[16,128,128]{2,1,0:T(8,128)(2,1)} custom-call(s32[4]{0:T(128)} %refs_0_.19, s32[2,6]{1,0:T(2,128)} %refs_1_.15, bf16[256,2048]{1,0:T(8,128)(2,1)} %refs_2_.6, bf16[256,2048]{1,0:T(8,128)(2,1)} %refs_3_.15), custom_call_target="tpu_custom_call" | custom-call | flops 134217728 | bytes 2621440 | tf_op jit(solution)/shard_map/total/pallas_call | solution.py:438
  4.3 7.2 %all-to-all-start = ((bf16[32,64,128]{2,1,0:T(8,128)(2,1)}), bf16[32,64,128]{2,1,0:T(8,128)(2,1)}, u32[]{:S(2)}, u32[]{:S(2)}) async-start(bf16[32,64,128]{2,1,0:T(8,128)(2,1)} %bitcast.5), calls=%async_computation | async-start | bytes 1048576 | tf_op jit(solution)/shard_map/all_to_all | solution.py:500
  11.5 0.0 copy-start
  11.5 3.6 %states.1 = (bf16[16,128,128]{2,1,0:T(8,128)(2,1)}, bf16[8,128,128]{2,1,0:T(8,128)(2,1)}, bf16[8,128,128]{2,1,0:T(8,128)(2,1)}) custom-call(s32[4]{0:T(128)} %refs_0_.19, s32[2,6]{1,0:T(2,128)} %refs_1_.15, bf16[256,2048]{1,0:T(8,128)(2,1)} %refs_2_.6, bf16[256,2048]{1,0:T(8,128)(2,1)} %refs_3_.15), custom_call_target="tpu_custom_call" | custom-call | flops 399999991808 | bytes 3145728 | tf_op jit(solution)/shard_map/states/pallas_call | solution.py:438
  15.1 3.3 %collective-permute-start = (bf16[16,128,128]{2,1,0:T(8,128)(2,1)}, bf16[16,128,128]{2,1,0:T(8,128)(2,1)S(1)}, u32[]{:S(2)}, u32[]{:S(2)}) collective-permute-start(bf16[16,128,128]{2,1,0:T(8,128)(2,1)} %get-tuple-element.37), channel_id=1, source_target_pairs={{0,1},{2,3},{4,5},{6,7},{8,9},{10,11},{12,13},{14,15},{16,17},{18,... | collective-permute-start | bytes 1572872 | tf_op jit(solution)/shard_map/ppermute | solution.py:497
  18.4 2.0 %collective-permute-start.1 = (bf16[8,128,128]{2,1,0:T(8,128)(2,1)}, bf16[8,128,128]{2,1,0:T(8,128)(2,1)}, u32[]{:S(2)}, u32[]{:S(2)}) collective-permute-start(bf16[8,128,128]{2,1,0:T(8,128)(2,1)} %get-tuple-element.40), channel_id=1, source_target_pairs={{0,1},{2,3},{4,5},{6,7},{8,9},{10,11},{12,13},{14,15},{16,17},{18,... | collective-permute-start | bytes 786440 | tf_op jit(solution)/shard_map/ppermute | solution.py:497
  20.5 6.4 %all-to-all-done.refs_1_ = bf16[32,64,128]{2,1,0:T(8,128)(2,1)} async-done(((bf16[32,64,128]{2,1,0:T(8,128)(2,1)}), bf16[32,64,128]{2,1,0:T(8,128)(2,1)}, u32[]{:S(2)}, u32[]{:S(2)}) %all-to-all-start) | async-done | bytes 524320 | tf_op jit(solution)/shard_map/all_to_all | solution.py:500
  26.8 0.0 copy-done
  26.8 2.0 %scan.2 = bf16[32,64,128]{2,1,0:T(8,128)(2,1)} custom-call(s32[4]{0:T(128)S(1)} %copy-done, bf16[32,64,128]{2,1,0:T(8,128)(2,1)} %all-to-all-done.refs_1_), custom_call_target="tpu_custom_call" | custom-call | bytes 1048576 | tf_op jit(solution)/shard_map/scan/pallas_call | solution.py:438
  28.9 3.2 %all-to-all-start.1 = ((bf16[32,64,128]{2,1,0:T(8,128)(2,1)}), bf16[32,64,128]{2,1,0:T(8,128)(2,1)}, u32[]{:S(2)}, u32[]{:S(2)}) async-start(bf16[32,64,128]{2,1,0:T(8,128)(2,1)} %scan.2), calls=%async_computation.1 | async-start | bytes 1048576 | tf_op jit(solution)/shard_map/all_to_all | solution.py:500
  32.1 0.0 collective-permute-done.refs_5_.refs_7_.refs_12_
  32.1 0.0 copy-start.4
  32.1 0.8 copy-done.4
  32.9 0.0 copy-start.6
  32.9 5.2 %inner.1.refs_4_ = f32[256,2048]{1,0:T(8,128)} custom-call(s32[4]{0:T(128)} %refs_0_.19, s32[2,6]{1,0:T(2,128)} %refs_1_.15, bf16[256,2048]{1,0:T(8,128)(2,1)} %refs_2_.5, bf16[256,2048]{1,0:T(8,128)(2,1)} %refs_2_.6, bf16[256,2048]{1,0:T(8,128)(2,1)} %refs_3_.15, bf16[16,128,128]{2,1,0:T(8,128)(2,1)} %copy-done.4), custom_call_target="tpu_custom_call" | custom-call | flops 399999991808 | bytes 5242880 | tf_op jit(solution)/shard_map/inner/pallas_call | solution.py:438
  38.1 0.0 copy-done.6
  38.1 3.4 %collective-permute-start.2 = (bf16[8,128,128]{2,1,0:T(8,128)(2,1)S(1)}, bf16[8,128,128]{2,1,0:T(8,128)(2,1)S(1)}, u32[]{:S(2)}, u32[]{:S(2)}) collective-permute-start(bf16[8,128,128]{2,1,0:T(8,128)(2,1)S(1)} %copy-done.6), channel_id=1, source_target_pairs={{0,1},{2,3},{4,5},{6,7},{8,9},{10,11},{12,13},{14,15},{16,17},{18,... | collective-permute-start | bytes 786440 | tf_op jit(solution)/shard_map/ppermute | solution.py:497
  41.5 5.9 %all-to-all-done.1 = bf16[32,64,128]{2,1,0:T(8,128)(2,1)} async-done(((bf16[32,64,128]{2,1,0:T(8,128)(2,1)}), bf16[32,64,128]{2,1,0:T(8,128)(2,1)}, u32[]{:S(2)}, u32[]{:S(2)}) %all-to-all-start.1) | async-done | bytes 524320 | tf_op jit(solution)/shard_map/all_to_all | solution.py:500
  47.4 4.4 %norm.2 = (f32[128,128]{1,0:T(8,128)}, bf16[128,2048]{1,0:T(8,128)(2,1)}, bf16[128,2048]{1,0:T(8,128)(2,1)}, bf16[16,128,128]{2,1,0:T(8,128)(2,1)}) custom-call(s32[4]{0:T(128)} %refs_0_.19, s32[2,6]{1,0:T(2,128)} %refs_1_.15, f32[1,2048]{1,0:T(1,128)} %bitcast.7, bf16[256,2048]{1,0:T(8,128)(2,1)} %refs_2_.5, f32[256,2048]{1,0:T(8,128)} %inner.1.refs_4_, ...), custom_call_target="tpu_custom_call" | custom-call | flops 134217728 | bytes 6889472 | tf_op jit(solution)/shard_map/norm/pallas_call | solution.py:438
  51.9 1.3 %collective-permute-start.3 = (bf16[16,128,128]{2,1,0:T(8,128)(2,1)}, bf16[16,128,128]{2,1,0:T(8,128)(2,1)}, u32[]{:S(2)}, u32[]{:S(2)}) collective-permute-start(bf16[16,128,128]{2,1,0:T(8,128)(2,1)} %get-tuple-element.42.refs_9_), channel_id=1, source_target_pairs={{1,0},{3,2},{5,4},{7,6},{9,8},{11,10},{13,12},{15,14},{17,16},{19,... | collective-permute-start | bytes 1572872 | tf_op jit(solution)/shard_map/ppermute | solution.py:497
  53.2 0.0 collective-permute-done.1.refs_7_.refs_13_
  53.2 0.0 collective-permute-done.2.refs_8_.refs_14_
  53.2 0.0 copy-start.5
  53.2 0.7 copy-done.5
  53.9 4.8 %norm.3 = (f32[128,128]{1,0:T(8,128)}, bf16[128,2048]{1,0:T(8,128)(2,1)}, bf16[128,2048]{1,0:T(8,128)(2,1)}, bf16[16,128,128]{2,1,0:T(8,128)(2,1)}, bf16[16,128,128]{2,1,0:T(8,128)(2,1)}) custom-call(s32[4]{0:T(128)} %refs_0_.19, s32[2,6]{1,0:T(2,128)} %refs_1_.15, f32[1,2048]{1,0:T(1,128)} %bitcast.8, bf16[256,2048]{1,0:T(8,128)(2,1)} %refs_2_.5, ...), custom_call_target="tpu_custom_call" | custom-call | flops 399999991808 | bytes 7938048 | tf_op jit(solution)/shard_map/norm/pallas_call | solution.py:438
  58.7 7.1 %all-to-all-start.2 = ((bf16[32,64,128]{2,1,0:T(8,128)(2,1)}), bf16[32,64,128]{2,1,0:T(8,128)(2,1)}, u32[]{:S(2)}, u32[]{:S(2)}) async-start(bf16[32,64,128]{2,1,0:T(8,128)(2,1)} %bitcast.6), calls=%async_computation.2 | async-start | bytes 1048576 | tf_op jit(solution)/shard_map/all_to_all | solution.py:500
  65.9 1.3 %collective-permute-start.4 = (bf16[16,128,128]{2,1,0:T(8,128)(2,1)}, bf16[16,128,128]{2,1,0:T(8,128)(2,1)}, u32[]{:S(2)}, u32[]{:S(2)}) collective-permute-start(bf16[16,128,128]{2,1,0:T(8,128)(2,1)} %get-tuple-element.54), channel_id=1, source_target_pairs={{1,0},{3,2},{5,4},{7,6},{9,8},{11,10},{13,12},{15,14},{17,16},{19,... | collective-permute-start | bytes 1572872 | tf_op jit(solution)/shard_map/ppermute | solution.py:497
  67.2 0.4 collective-permute-done.3.refs_15_.refs_7_
  67.6 0.0 copy-start.1
  67.6 7.9 %query_grads.1 = (bf16[256,2048]{1,0:T(8,128)(2,1)}, bf16[256,2048]{1,0:T(8,128)(2,1)}) custom-call(s32[4]{0:T(128)} %refs_0_.19, s32[2,6]{1,0:T(2,128)} %refs_1_.15, f32[1,2048]{1,0:T(1,128)} %bitcast.9, bf16[256,2048]{1,0:T(8,128)(2,1)} %refs_2_.6, bf16[256,2048]{1,0:T(8,128)(2,1)} %refs_3_.15, bf16[16,128,128]{2,1,0:T(8,128)(2,1)} %bitcast.2.refs_6_.refs_5_, ...), custom_call_target="tpu_custom_call" | custom-call | flops 399999991808 | bytes 8003584 | tf_op jit(solution)/shard_map/query_grads/pallas_call | solution.py:438
  75.5 5.8 %all-to-all-done.2.refs_1_ = bf16[32,64,128]{2,1,0:T(8,128)(2,1)} async-done(((bf16[32,64,128]{2,1,0:T(8,128)(2,1)}), bf16[32,64,128]{2,1,0:T(8,128)(2,1)}, u32[]{:S(2)}, u32[]{:S(2)}) %all-to-all-start.2) | async-done | bytes 524320 | tf_op jit(solution)/shard_map/all_to_all | solution.py:500
  81.2 0.0 copy-done.1
  81.2 2.0 %scan.3 = bf16[32,64,128]{2,1,0:T(8,128)(2,1)} custom-call(s32[4]{0:T(128)S(1)} %copy-done.1, bf16[32,64,128]{2,1,0:T(8,128)(2,1)} %all-to-all-done.2.refs_1_), custom_call_target="tpu_custom_call" | custom-call | bytes 1048576 | tf_op jit(solution)/shard_map/scan/pallas_call | solution.py:438
  83.3 3.3 %all-to-all-start.3 = ((bf16[32,64,128]{2,1,0:T(8,128)(2,1)}), bf16[32,64,128]{2,1,0:T(8,128)(2,1)}, u32[]{:S(2)}, u32[]{:S(2)}) async-start(bf16[32,64,128]{2,1,0:T(8,128)(2,1)} %scan.3), calls=%async_computation.3 | async-start | bytes 1048576 | tf_op jit(solution)/shard_map/all_to_all | solution.py:500
  86.5 1.3 %collective-permute-done.4.refs_8_ = bf16[16,128,128]{2,1,0:T(8,128)(2,1)} collective-permute-done((bf16[16,128,128]{2,1,0:T(8,128)(2,1)}, bf16[16,128,128]{2,1,0:T(8,128)(2,1)}, u32[]{:S(2)}, u32[]{:S(2)}) %collective-permute-start.4) | collective-permute-done | bytes 524320 | tf_op jit(solution)/shard_map/ppermute | solution.py:497
  87.8 0.0 copy-start.2
  87.8 0.0 copy-start.3
  87.8 10.3 %key_grads.1 = (f32[256,2048]{1,0:T(8,128)}, f32[256,2048]{1,0:T(8,128)}) custom-call(s32[4]{0:T(128)} %refs_0_.19, s32[2,6]{1,0:T(2,128)} %refs_1_.15, bf16[256,2048]{1,0:T(8,128)(2,1)} %refs_2_.5, bf16[256,2048]{1,0:T(8,128)(2,1)} %refs_2_.6, bf16[256,2048]{1,0:T(8,128)(2,1)} %refs_3_.15, bf16[128,2048]{1,0:T(8,128)(2,1)} %get-tuple-element.39.refs_6_.refs_5_, ...), custom_call_target="tpu_custom_call" | custom-call | flops 399999991808 | bytes 9437184 | tf_op jit(solution)/shard_map/key_grads/pallas_call | solution.py:438
  98.1 3.7 %all-to-all-done.3 = bf16[32,64,128]{2,1,0:T(8,128)(2,1)} async-done(((bf16[32,64,128]{2,1,0:T(8,128)(2,1)}), bf16[32,64,128]{2,1,0:T(8,128)(2,1)}, u32[]{:S(2)}, u32[]{:S(2)}) %all-to-all-start.3) | async-done | bytes 524320 | tf_op jit(solution)/shard_map/all_to_all | solution.py:500
  101.8 0.0 copy-done.2
  101.8 0.0 copy-done.3
  101.8 5.0 %last.1 = (bf16[256,2048]{1,0:T(8,128)(2,1)}, bf16[256,2048]{1,0:T(8,128)(2,1)}) custom-call(s32[4]{0:T(128)S(1)} %copy-done.2, s32[2,6]{1,0:T(2,128)S(1)} %copy-done.3, bf16[256,2048]{1,0:T(8,128)(2,1)} %refs_2_.6, bf16[256,2048]{1,0:T(8,128)(2,1)} %refs_3_.15, f32[256,2048]{1,0:T(8,128)} %get-tuple-element.55.refs_4_, ...), custom_call_target="tpu_custom_call" | custom-call | flops 268435456 | bytes 8912896 | tf_op jit(solution)/shard_map/last/pallas_call | solution.py:438
Async XLA Ops:
  4.3 22.5 %all-to-all-start = ((bf16[32,64,128]{2,1,0:T(8,128)(2,1)}), bf16[32,64,128]{2,1,0:T(8,128)(2,1)}, u32[]{:S(2)}, u32[]{:S(2)}) async-start(bf16[32,64,128]{2,1,0:T(8,128)(2,1)} %bitcast.5), calls=%async_computation | async-start | bytes 1048576 | tf_op jit(solution)/shard_map/all_to_all | solution.py:500
  11.5 15.3 %copy-start = (s32[4]{0:T(128)S(1)}, s32[4]{0:T(128)}, u32[]{:S(2)}) copy-start(s32[4]{0:T(128)} %refs_0_.19) | copy-start | bytes 52
  15.1 17.0 %collective-permute-start = (bf16[16,128,128]{2,1,0:T(8,128)(2,1)}, bf16[16,128,128]{2,1,0:T(8,128)(2,1)S(1)}, u32[]{:S(2)}, u32[]{:S(2)}) collective-permute-start(bf16[16,128,128]{2,1,0:T(8,128)(2,1)} %get-tuple-element.37), channel_id=1, source_target_pairs={{0,1},{2,3},{4,5},{6,7},{8,9},{10,11},{12,13},{14,15},{16,17},{18,... | collective-permute-start | bytes 1572872 | tf_op jit(solution)/shard_map/ppermute | solution.py:497
  18.4 34.7 %collective-permute-start.1 = (bf16[8,128,128]{2,1,0:T(8,128)(2,1)}, bf16[8,128,128]{2,1,0:T(8,128)(2,1)}, u32[]{:S(2)}, u32[]{:S(2)}) collective-permute-start(bf16[8,128,128]{2,1,0:T(8,128)(2,1)} %get-tuple-element.40), channel_id=1, source_target_pairs={{0,1},{2,3},{4,5},{6,7},{8,9},{10,11},{12,13},{14,15},{16,17},{18,... | collective-permute-start | bytes 786440 | tf_op jit(solution)/shard_map/ppermute | solution.py:497
  28.9 18.6 %all-to-all-start.1 = ((bf16[32,64,128]{2,1,0:T(8,128)(2,1)}), bf16[32,64,128]{2,1,0:T(8,128)(2,1)}, u32[]{:S(2)}, u32[]{:S(2)}) async-start(bf16[32,64,128]{2,1,0:T(8,128)(2,1)} %scan.2), calls=%async_computation.1 | async-start | bytes 1048576 | tf_op jit(solution)/shard_map/all_to_all | solution.py:500
  32.1 0.8 copy-start.4
  32.9 5.2 %copy-start.6 = (bf16[8,128,128]{2,1,0:T(8,128)(2,1)S(1)}, bf16[8,128,128]{2,1,0:T(8,128)(2,1)}, u32[]{:S(2)}) copy-start(bf16[8,128,128]{2,1,0:T(8,128)(2,1)} %get-tuple-element.41) | copy-start | bytes 786436
  38.1 15.1 %collective-permute-start.2 = (bf16[8,128,128]{2,1,0:T(8,128)(2,1)S(1)}, bf16[8,128,128]{2,1,0:T(8,128)(2,1)S(1)}, u32[]{:S(2)}, u32[]{:S(2)}) collective-permute-start(bf16[8,128,128]{2,1,0:T(8,128)(2,1)S(1)} %copy-done.6), channel_id=1, source_target_pairs={{0,1},{2,3},{4,5},{6,7},{8,9},{10,11},{12,13},{14,15},{16,17},{18,... | collective-permute-start | bytes 786440 | tf_op jit(solution)/shard_map/ppermute | solution.py:497
  51.9 15.7 %collective-permute-start.3 = (bf16[16,128,128]{2,1,0:T(8,128)(2,1)}, bf16[16,128,128]{2,1,0:T(8,128)(2,1)}, u32[]{:S(2)}, u32[]{:S(2)}) collective-permute-start(bf16[16,128,128]{2,1,0:T(8,128)(2,1)} %get-tuple-element.42.refs_9_), channel_id=1, source_target_pairs={{1,0},{3,2},{5,4},{7,6},{9,8},{11,10},{13,12},{15,14},{17,16},{19,... | collective-permute-start | bytes 1572872 | tf_op jit(solution)/shard_map/ppermute | solution.py:497
  53.2 0.7 copy-start.5
  58.7 22.5 %all-to-all-start.2 = ((bf16[32,64,128]{2,1,0:T(8,128)(2,1)}), bf16[32,64,128]{2,1,0:T(8,128)(2,1)}, u32[]{:S(2)}, u32[]{:S(2)}) async-start(bf16[32,64,128]{2,1,0:T(8,128)(2,1)} %bitcast.6), calls=%async_computation.2 | async-start | bytes 1048576 | tf_op jit(solution)/shard_map/all_to_all | solution.py:500
  65.9 22.0 %collective-permute-start.4 = (bf16[16,128,128]{2,1,0:T(8,128)(2,1)}, bf16[16,128,128]{2,1,0:T(8,128)(2,1)}, u32[]{:S(2)}, u32[]{:S(2)}) collective-permute-start(bf16[16,128,128]{2,1,0:T(8,128)(2,1)} %get-tuple-element.54), channel_id=1, source_target_pairs={{1,0},{3,2},{5,4},{7,6},{9,8},{11,10},{13,12},{15,14},{17,16},{19,... | collective-permute-start | bytes 1572872 | tf_op jit(solution)/shard_map/ppermute | solution.py:497
  67.6 13.6 %copy-start.1 = (s32[4]{0:T(128)S(1)}, s32[4]{0:T(128)}, u32[]{:S(2)}) copy-start(s32[4]{0:T(128)} %refs_0_.19) | copy-start | bytes 52
  83.3 18.6 %all-to-all-start.3 = ((bf16[32,64,128]{2,1,0:T(8,128)(2,1)}), bf16[32,64,128]{2,1,0:T(8,128)(2,1)}, u32[]{:S(2)}, u32[]{:S(2)}) async-start(bf16[32,64,128]{2,1,0:T(8,128)(2,1)} %scan.3), calls=%async_computation.3 | async-start | bytes 1048576 | tf_op jit(solution)/shard_map/all_to_all | solution.py:500
  87.8 14.0 %copy-start.2 = (s32[4]{0:T(128)S(1)}, s32[4]{0:T(128)}, u32[]{:S(2)}) copy-start(s32[4]{0:T(128)} %refs_0_.19) | copy-start | bytes 52
  87.8 14.0 %copy-start.3 = (s32[2,6]{1,0:T(2,128)S(1)}, s32[2,6]{1,0:T(2,128)}, u32[]{:S(2)}) copy-start(s32[2,6]{1,0:T(2,128)} %refs_1_.15) | copy-start | bytes 148

commit v14 on v13

--- a/solution.py
+++ b/solution.py
@@ -513,7 +513,7 @@
         return slices
 
     gain_row = Part(gain.reshape(1, width))
-    halves = [2 if b > 0 and chunks % 2 == 0 else 1 for b in range(blocks) for _ in range(peers)]
+    halves = [1] * (blocks * peers)
     later = [[shape((heads // n, DH, DH), BF)] * n for n in halves]
     (sum_kv,) = call(
         total_body,
@@ -522,7 +522,7 @@
         [wide(keys), wide(values)],
         [states(state)],
         heads,
-        chunks,
+        few,
         flops=unit,
     )
     slices = sum_kv.reshape(total, -1, DH)
@@ -541,8 +541,8 @@
         )
     later = iter(later)
     from_peers = [[next(later) for _ in range(n)] for n in halves]
-    for at, arrays in enumerate(from_peers):
-        arrays[0] = to_peers(arrays[0], 1 + at % peers, False)
+    for away, arrays in enumerate(from_peers[:peers], 1):
+        arrays[0] = to_peers(arrays[0], away, False)
     slices = scanned(slices, False)
     slices, late_queries = lax.optimization_barrier((slices, queries))
     (raw_inner,) = call(
@@ -558,10 +558,9 @@
         after=[x for arrays in from_peers[:peers] for x in arrays],
     )
     kv_state = exchanged(slices).reshape(heads, DH, DH)
-    for at, arrays in enumerate(from_peers):
-        if len(arrays) > 1:
-            later_half, raw_inner = lax.optimization_barrier((arrays[1], raw_inner))
-            arrays[1] = to_peers(later_half, 1 + at % peers, False)
+    for at, arrays in enumerate(from_peers[peers:]):
+        delayed, raw_inner = lax.optimization_barrier((arrays[0], raw_inner))
+        arrays[0] = to_peers(delayed, 1 + at % peers, False)
 
     scales, raws, grads, updates, back = [], [], [], [], []
     for b in range(blocks):

time: 108 us -> 109 us (level)
  waiting for transfers between devices: 23.5 us -> 25.7 us
    all_to_all x4, waiting for transfers between devices: 21.7 us -> 24.4 us  [exchanged(): return lax.all_to_all(slices, AXES, split_axis=0, concat_axis=0, tiled=True)]
    ppermute x5 -> x4, starting transfers between devices: 11.3 us -> 9.34 us  [to_peers(): return lax.ppermute(array, 'head', pairs)]
  transfers between devices with their start and end apart: 9 -> 8, of which waited for: 6 -> 5; matrix products, arithmetic and copies ran while one was open for 0% -> 0% of each run, Pallas kernels for 38% -> 37%
where the time goes in v14:
time: 109 us; the launch traced here: 108 us
  Pallas kernels  48.5 us (44%)
  starting transfers between devices  31.2 us (29%)
  waiting for transfers between devices  25.7 us (24%)
  local copies, waits for them, and re-layouts  1.6 us (1%)
    pallas_call x10, Pallas kernels, call(): pl.pallas_call(kernel, name=name, in_specs=[*[pl.BlockSpec(memory_space=p...  48.5 us
    all_to_all x4, waiting for transfers between devices, exchanged(): return lax.all_to_all(slices, AXES, split_axis=0, concat_axis=0, tiled=True)  24.4 us
    all_to_all x4, starting transfers between devices, exchanged(): return lax.all_to_all(slices, AXES, split_axis=0, concat_axis=0, tiled=True)  21.8 us
    ppermute x4, starting transfers between devices, to_peers(): return lax.ppermute(array, 'head', pairs)  9.34 us
  transfers between devices with their start and end apart: 8, of which 5 were waited for; matrix products, arithmetic and copies ran while one was open for 0% of the time, Pallas kernels for 37%

profile of v14, /device:TPU:1, one launch (start us, length us, event | category | flops | bytes accessed | tf_op | source)
XLA Modules:
  0.0 107.9 jit_solution(5393966894915211918)
XLA Ops:
  0.6 3.4 %total.1 = bf16[16,128,128]{2,1,0:T(8,128)(2,1)} custom-call(s32[4]{0:T(128)} %refs_0_.19, s32[2,6]{1,0:T(2,128)} %refs_1_.15, bf16[256,2048]{1,0:T(8,128)(2,1)} %refs_2_.6, bf16[256,2048]{1,0:T(8,128)(2,1)} %refs_3_.15), custom_call_target="tpu_custom_call" | custom-call | flops 134217728 | bytes 2621440 | tf_op jit(solution)/shard_map/total/pallas_call | solution.py:438
  4.1 7.2 %all-to-all-start = ((bf16[32,64,128]{2,1,0:T(8,128)(2,1)}), bf16[32,64,128]{2,1,0:T(8,128)(2,1)}, u32[]{:S(2)}, u32[]{:S(2)}) async-start(bf16[32,64,128]{2,1,0:T(8,128)(2,1)} %bitcast.5), calls=%async_computation | async-start | bytes 1048576 | tf_op jit(solution)/shard_map/all_to_all | solution.py:500
  11.2 0.0 copy-start
  11.2 3.6 %states.1 = (bf16[16,128,128]{2,1,0:T(8,128)(2,1)}, bf16[16,128,128]{2,1,0:T(8,128)(2,1)}) custom-call(s32[4]{0:T(128)} %refs_0_.19, s32[2,6]{1,0:T(2,128)} %refs_1_.15, bf16[256,2048]{1,0:T(8,128)(2,1)} %refs_2_.6, bf16[256,2048]{1,0:T(8,128)(2,1)} %refs_3_.15), custom_call_target="tpu_custom_call" | custom-call | flops 399999991808 | bytes 3145728 | tf_op jit(solution)/shard_map/states/pallas_call | solution.py:438
  14.8 3.3 %collective-permute-start = (bf16[16,128,128]{2,1,0:T(8,128)(2,1)}, bf16[16,128,128]{2,1,0:T(8,128)(2,1)S(1)}, u32[]{:S(2)}, u32[]{:S(2)}) collective-permute-start(bf16[16,128,128]{2,1,0:T(8,128)(2,1)} %get-tuple-element.36), channel_id=1, source_target_pairs={{0,1},{2,3},{4,5},{6,7},{8,9},{10,11},{12,13},{14,15},{16,17},{18,... | collective-permute-start | bytes 1572872 | tf_op jit(solution)/shard_map/ppermute | solution.py:497
  18.2 8.4 %all-to-all-done.refs_1_ = bf16[32,64,128]{2,1,0:T(8,128)(2,1)} async-done(((bf16[32,64,128]{2,1,0:T(8,128)(2,1)}), bf16[32,64,128]{2,1,0:T(8,128)(2,1)}, u32[]{:S(2)}, u32[]{:S(2)}) %all-to-all-start) | async-done | bytes 524320 | tf_op jit(solution)/shard_map/all_to_all | solution.py:500
  26.6 0.0 copy-done
  26.6 2.0 %scan.2 = bf16[32,64,128]{2,1,0:T(8,128)(2,1)} custom-call(s32[4]{0:T(128)S(1)} %copy-done, bf16[32,64,128]{2,1,0:T(8,128)(2,1)} %all-to-all-done.refs_1_), custom_call_target="tpu_custom_call" | custom-call | bytes 1048576 | tf_op jit(solution)/shard_map/scan/pallas_call | solution.py:438
  28.6 3.2 %all-to-all-start.1 = ((bf16[32,64,128]{2,1,0:T(8,128)(2,1)}), bf16[32,64,128]{2,1,0:T(8,128)(2,1)}, u32[]{:S(2)}, u32[]{:S(2)}) async-start(bf16[32,64,128]{2,1,0:T(8,128)(2,1)} %scan.2), calls=%async_computation.1 | async-start | bytes 1048576 | tf_op jit(solution)/shard_map/all_to_all | solution.py:500
  31.8 0.0 collective-permute-done.refs_5_.refs_7_.refs_12_
  31.8 0.0 copy-start.4
  31.9 0.8 copy-done.4
  32.6 0.0 copy-start.6
  32.6 5.2 %inner.1.refs_4_ = f32[256,2048]{1,0:T(8,128)} custom-call(s32[4]{0:T(128)} %refs_0_.19, s32[2,6]{1,0:T(2,128)} %refs_1_.15, bf16[256,2048]{1,0:T(8,128)(2,1)} %refs_2_.5, bf16[256,2048]{1,0:T(8,128)(2,1)} %refs_2_.6, bf16[256,2048]{1,0:T(8,128)(2,1)} %refs_3_.15, bf16[16,128,128]{2,1,0:T(8,128)(2,1)} %copy-done.4), custom_call_target="tpu_custom_call" | custom-call | flops 399999991808 | bytes 5242880 | tf_op jit(solution)/shard_map/inner/pallas_call | solution.py:438
  37.9 0.0 copy-done.6
  37.9 3.4 %collective-permute-start.1 = (bf16[16,128,128]{2,1,0:T(8,128)(2,1)S(1)}, bf16[16,128,128]{2,1,0:T(8,128)(2,1)S(1)}, u32[]{:S(2)}, u32[]{:S(2)}) collective-permute-start(bf16[16,128,128]{2,1,0:T(8,128)(2,1)S(1)} %copy-done.6), channel_id=1, source_target_pairs={{0,1},{2,3},{4,5},{6,7},{8,9},{10,11},{12,13},{14,15},{16,17},{18,... | collective-permute-start | bytes 1572872 | tf_op jit(solution)/shard_map/ppermute | solution.py:497
  41.3 5.9 %all-to-all-done.1 = bf16[32,64,128]{2,1,0:T(8,128)(2,1)} async-done(((bf16[32,64,128]{2,1,0:T(8,128)(2,1)}), bf16[32,64,128]{2,1,0:T(8,128)(2,1)}, u32[]{:S(2)}, u32[]{:S(2)}) %all-to-all-start.1) | async-done | bytes 524320 | tf_op jit(solution)/shard_map/all_to_all | solution.py:500
  47.2 4.4 %norm.2 = (f32[128,128]{1,0:T(8,128)}, bf16[128,2048]{1,0:T(8,128)(2,1)}, bf16[128,2048]{1,0:T(8,128)(2,1)}, bf16[16,128,128]{2,1,0:T(8,128)(2,1)}) custom-call(s32[4]{0:T(128)} %refs_0_.19, s32[2,6]{1,0:T(2,128)} %refs_1_.15, f32[1,2048]{1,0:T(1,128)} %bitcast.7, bf16[256,2048]{1,0:T(8,128)(2,1)} %refs_2_.5, f32[256,2048]{1,0:T(8,128)} %inner.1.refs_4_, ...), custom_call_target="tpu_custom_call" | custom-call | flops 134217728 | bytes 6889472 | tf_op jit(solution)/shard_map/norm/pallas_call | solution.py:438
  51.6 1.3 %collective-permute-start.2 = (bf16[16,128,128]{2,1,0:T(8,128)(2,1)}, bf16[16,128,128]{2,1,0:T(8,128)(2,1)}, u32[]{:S(2)}, u32[]{:S(2)}) collective-permute-start(bf16[16,128,128]{2,1,0:T(8,128)(2,1)} %get-tuple-element.40.refs_8_), channel_id=1, source_target_pairs={{1,0},{3,2},{5,4},{7,6},{9,8},{11,10},{13,12},{15,14},{17,16},{19,... | collective-permute-start | bytes 1572872 | tf_op jit(solution)/shard_map/ppermute | solution.py:497
  52.9 0.0 collective-permute-done.1.refs_7_.refs_13_
  52.9 0.0 copy-start.5
  52.9 0.8 copy-done.5
  53.7 4.9 %norm.3 = (f32[128,128]{1,0:T(8,128)}, bf16[128,2048]{1,0:T(8,128)(2,1)}, bf16[128,2048]{1,0:T(8,128)(2,1)}, bf16[16,128,128]{2,1,0:T(8,128)(2,1)}, bf16[16,128,128]{2,1,0:T(8,128)(2,1)}) custom-call(s32[4]{0:T(128)} %refs_0_.19, s32[2,6]{1,0:T(2,128)} %refs_1_.15, f32[1,2048]{1,0:T(1,128)} %bitcast.8, bf16[256,2048]{1,0:T(8,128)(2,1)} %refs_2_.5, ...), custom_call_target="tpu_custom_call" | custom-call | flops 399999991808 | bytes 7938048 | tf_op jit(solution)/shard_map/norm/pallas_call | solution.py:438
  58.6 8.2 %all-to-all-start.2 = ((bf16[32,64,128]{2,1,0:T(8,128)(2,1)}), bf16[32,64,128]{2,1,0:T(8,128)(2,1)}, u32[]{:S(2)}, u32[]{:S(2)}) async-start(bf16[32,64,128]{2,1,0:T(8,128)(2,1)} %bitcast.6), calls=%async_computation.2 | async-start | bytes 1048576 | tf_op jit(solution)/shard_map/all_to_all | solution.py:500
  66.8 1.3 %collective-permute-start.3 = (bf16[16,128,128]{2,1,0:T(8,128)(2,1)}, bf16[16,128,128]{2,1,0:T(8,128)(2,1)}, u32[]{:S(2)}, u32[]{:S(2)}) collective-permute-start(bf16[16,128,128]{2,1,0:T(8,128)(2,1)} %get-tuple-element.52), channel_id=1, source_target_pairs={{1,0},{3,2},{5,4},{7,6},{9,8},{11,10},{13,12},{15,14},{17,16},{19,... | collective-permute-start | bytes 1572872 | tf_op jit(solution)/shard_map/ppermute | solution.py:497
  68.1 0.0 collective-permute-done.2.refs_14_.refs_7_
  68.1 0.0 copy-start.1
  68.1 7.7 %query_grads.1 = (bf16[256,2048]{1,0:T(8,128)(2,1)}, bf16[256,2048]{1,0:T(8,128)(2,1)}) custom-call(s32[4]{0:T(128)} %refs_0_.19, s32[2,6]{1,0:T(2,128)} %refs_1_.15, f32[1,2048]{1,0:T(1,128)} %bitcast.9, bf16[256,2048]{1,0:T(8,128)(2,1)} %refs_2_.6, bf16[256,2048]{1,0:T(8,128)(2,1)} %refs_3_.15, bf16[16,128,128]{2,1,0:T(8,128)(2,1)} %bitcast.2.refs_6_.refs_5_, ...), custom_call_target="tpu_custom_call" | custom-call | flops 399999991808 | bytes 8003584 | tf_op jit(solution)/shard_map/query_grads/pallas_call | solution.py:438
  75.8 6.3 %all-to-all-done.2.refs_1_ = bf16[32,64,128]{2,1,0:T(8,128)(2,1)} async-done(((bf16[32,64,128]{2,1,0:T(8,128)(2,1)}), bf16[32,64,128]{2,1,0:T(8,128)(2,1)}, u32[]{:S(2)}, u32[]{:S(2)}) %all-to-all-start.2) | async-done | bytes 524320 | tf_op jit(solution)/shard_map/all_to_all | solution.py:500
  82.1 0.0 copy-done.1
  82.2 2.0 %scan.3 = bf16[32,64,128]{2,1,0:T(8,128)(2,1)} custom-call(s32[4]{0:T(128)S(1)} %copy-done.1, bf16[32,64,128]{2,1,0:T(8,128)(2,1)} %all-to-all-done.2.refs_1_), custom_call_target="tpu_custom_call" | custom-call | bytes 1048576 | tf_op jit(solution)/shard_map/scan/pallas_call | solution.py:438
  84.2 3.3 %all-to-all-start.3 = ((bf16[32,64,128]{2,1,0:T(8,128)(2,1)}), bf16[32,64,128]{2,1,0:T(8,128)(2,1)}, u32[]{:S(2)}, u32[]{:S(2)}) async-start(bf16[32,64,128]{2,1,0:T(8,128)(2,1)} %scan.3), calls=%async_computation.3 | async-start | bytes 1048576 | tf_op jit(solution)/shard_map/all_to_all | solution.py:500
  87.5 1.3 %collective-permute-done.3.refs_8_ = bf16[16,128,128]{2,1,0:T(8,128)(2,1)} collective-permute-done((bf16[16,128,128]{2,1,0:T(8,128)(2,1)}, bf16[16,128,128]{2,1,0:T(8,128)(2,1)}, u32[]{:S(2)}, u32[]{:S(2)}) %collective-permute-start.3) | collective-permute-done | bytes 524320 | tf_op jit(solution)/shard_map/ppermute | solution.py:497
  88.7 0.0 copy-start.2
  88.7 0.0 copy-start.3
  88.8 10.2 %key_grads.1 = (f32[256,2048]{1,0:T(8,128)}, f32[256,2048]{1,0:T(8,128)}) custom-call(s32[4]{0:T(128)} %refs_0_.19, s32[2,6]{1,0:T(2,128)} %refs_1_.15, bf16[256,2048]{1,0:T(8,128)(2,1)} %refs_2_.5, bf16[256,2048]{1,0:T(8,128)(2,1)} %refs_2_.6, bf16[256,2048]{1,0:T(8,128)(2,1)} %refs_3_.15, bf16[128,2048]{1,0:T(8,128)(2,1)} %get-tuple-element.38.refs_6_.refs_5_, ...), custom_call_target="tpu_custom_call" | custom-call | flops 399999991808 | bytes 9437184 | tf_op jit(solution)/shard_map/key_grads/pallas_call | solution.py:438
  99.0 3.8 %all-to-all-done.3 = bf16[32,64,128]{2,1,0:T(8,128)(2,1)} async-done(((bf16[32,64,128]{2,1,0:T(8,128)(2,1)}), bf16[32,64,128]{2,1,0:T(8,128)(2,1)}, u32[]{:S(2)}, u32[]{:S(2)}) %all-to-all-start.3) | async-done | bytes 524320 | tf_op jit(solution)/shard_map/all_to_all | solution.py:500
  102.7 0.0 copy-done.2
  102.7 0.0 copy-done.3
  102.7 5.0 %last.1 = (bf16[256,2048]{1,0:T(8,128)(2,1)}, bf16[256,2048]{1,0:T(8,128)(2,1)}) custom-call(s32[4]{0:T(128)S(1)} %copy-done.2, s32[2,6]{1,0:T(2,128)S(1)} %copy-done.3, bf16[256,2048]{1,0:T(8,128)(2,1)} %refs_2_.6, bf16[256,2048]{1,0:T(8,128)(2,1)} %refs_3_.15, f32[256,2048]{1,0:T(8,128)} %get-tuple-element.53.refs_4_, ...), custom_call_target="tpu_custom_call" | custom-call | flops 268435456 | bytes 8912896 | tf_op jit(solution)/shard_map/last/pallas_call | solution.py:438
Async XLA Ops:
  4.1 22.5 %all-to-all-start = ((bf16[32,64,128]{2,1,0:T(8,128)(2,1)}), bf16[32,64,128]{2,1,0:T(8,128)(2,1)}, u32[]{:S(2)}, u32[]{:S(2)}) async-start(bf16[32,64,128]{2,1,0:T(8,128)(2,1)} %bitcast.5), calls=%async_computation | async-start | bytes 1048576 | tf_op jit(solution)/shard_map/all_to_all | solution.py:500
  11.2 15.3 %copy-start = (s32[4]{0:T(128)S(1)}, s32[4]{0:T(128)}, u32[]{:S(2)}) copy-start(s32[4]{0:T(128)} %refs_0_.19) | copy-start | bytes 52
  14.8 17.0 %collective-permute-start = (bf16[16,128,128]{2,1,0:T(8,128)(2,1)}, bf16[16,128,128]{2,1,0:T(8,128)(2,1)S(1)}, u32[]{:S(2)}, u32[]{:S(2)}) collective-permute-start(bf16[16,128,128]{2,1,0:T(8,128)(2,1)} %get-tuple-element.36), channel_id=1, source_target_pairs={{0,1},{2,3},{4,5},{6,7},{8,9},{10,11},{12,13},{14,15},{16,17},{18,... | collective-permute-start | bytes 1572872 | tf_op jit(solution)/shard_map/ppermute | solution.py:497
  28.6 18.6 %all-to-all-start.1 = ((bf16[32,64,128]{2,1,0:T(8,128)(2,1)}), bf16[32,64,128]{2,1,0:T(8,128)(2,1)}, u32[]{:S(2)}, u32[]{:S(2)}) async-start(bf16[32,64,128]{2,1,0:T(8,128)(2,1)} %scan.2), calls=%async_computation.1 | async-start | bytes 1048576 | tf_op jit(solution)/shard_map/all_to_all | solution.py:500
  31.8 0.8 copy-start.4
  32.6 5.2 %copy-start.6 = (bf16[16,128,128]{2,1,0:T(8,128)(2,1)S(1)}, bf16[16,128,128]{2,1,0:T(8,128)(2,1)}, u32[]{:S(2)}) copy-start(bf16[16,128,128]{2,1,0:T(8,128)(2,1)} %get-tuple-element.39) | copy-start | bytes 1572868
  37.9 15.1 %collective-permute-start.1 = (bf16[16,128,128]{2,1,0:T(8,128)(2,1)S(1)}, bf16[16,128,128]{2,1,0:T(8,128)(2,1)S(1)}, u32[]{:S(2)}, u32[]{:S(2)}) collective-permute-start(bf16[16,128,128]{2,1,0:T(8,128)(2,1)S(1)} %copy-done.6), channel_id=1, source_target_pairs={{0,1},{2,3},{4,5},{6,7},{8,9},{10,11},{12,13},{14,15},{16,17},{18,... | collective-permute-start | bytes 1572872 | tf_op jit(solution)/shard_map/ppermute | solution.py:497
  51.6 16.5 %collective-permute-start.2 = (bf16[16,128,128]{2,1,0:T(8,128)(2,1)}, bf16[16,128,128]{2,1,0:T(8,128)(2,1)}, u32[]{:S(2)}, u32[]{:S(2)}) collective-permute-start(bf16[16,128,128]{2,1,0:T(8,128)(2,1)} %get-tuple-element.40.refs_8_), channel_id=1, source_target_pairs={{1,0},{3,2},{5,4},{7,6},{9,8},{11,10},{13,12},{15,14},{17,16},{19,... | collective-permute-start | bytes 1572872 | tf_op jit(solution)/shard_map/ppermute | solution.py:497
  52.9 0.8 copy-start.5
  58.6 23.6 %all-to-all-start.2 = ((bf16[32,64,128]{2,1,0:T(8,128)(2,1)}), bf16[32,64,128]{2,1,0:T(8,128)(2,1)}, u32[]{:S(2)}, u32[]{:S(2)}) async-start(bf16[32,64,128]{2,1,0:T(8,128)(2,1)} %bitcast.6), calls=%async_computation.2 | async-start | bytes 1048576 | tf_op jit(solution)/shard_map/all_to_all | solution.py:500
  66.8 22.0 %collective-permute-start.3 = (bf16[16,128,128]{2,1,0:T(8,128)(2,1)}, bf16[16,128,128]{2,1,0:T(8,128)(2,1)}, u32[]{:S(2)}, u32[]{:S(2)}) collective-permute-start(bf16[16,128,128]{2,1,0:T(8,128)(2,1)} %get-tuple-element.52), channel_id=1, source_target_pairs={{1,0},{3,2},{5,4},{7,6},{9,8},{11,10},{13,12},{15,14},{17,16},{19,... | collective-permute-start | bytes 1572872 | tf_op jit(solution)/shard_map/ppermute | solution.py:497
  68.1 14.1 %copy-start.1 = (s32[4]{0:T(128)S(1)}, s32[4]{0:T(128)}, u32[]{:S(2)}) copy-start(s32[4]{0:T(128)} %refs_0_.19) | copy-start | bytes 52
  84.2 18.6 %all-to-all-start.3 = ((bf16[32,64,128]{2,1,0:T(8,128)(2,1)}), bf16[32,64,128]{2,1,0:T(8,128)(2,1)}, u32[]{:S(2)}, u32[]{:S(2)}) async-start(bf16[32,64,128]{2,1,0:T(8,128)(2,1)} %scan.3), calls=%async_computation.3 | async-start | bytes 1048576 | tf_op jit(solution)/shard_map/all_to_all | solution.py:500
  88.7 14.0 %copy-start.2 = (s32[4]{0:T(128)S(1)}, s32[4]{0:T(128)}, u32[]{:S(2)}) copy-start(s32[4]{0:T(128)} %refs_0_.19) | copy-start | bytes 52
  88.7 14.0 %copy-start.3 = (s32[2,6]{1,0:T(2,128)S(1)}, s32[2,6]{1,0:T(2,128)}, u32[]{:S(2)}) copy-start(s32[2,6]{1,0:T(2,128)} %refs_1_.15) | copy-start | bytes 148

commit v15 on v13

--- a/solution.py
+++ b/solution.py
@@ -132,13 +132,15 @@
 
 class Joined:
     def __init__(self, refs):
-        self.refs, self.each = refs, refs[0].shape[0]
+        self.spots = [(ref, k) for ref in refs for k in range(ref.shape[0])]
 
     def __getitem__(self, head):
-        return self.refs[head // self.each][head % self.each]
+        ref, at = self.spots[head]
+        return ref[at]
 
     def __setitem__(self, head, value):
-        self.refs[head // self.each][head % self.each] = value
+        ref, at = self.spots[head]
+        ref[at] = value
 
 
 def joined(refs, counts):
@@ -486,9 +488,13 @@
     def states(array):
         return Part(array, 0)
 
-    def split_states(arrays, chunks):
-        count = chunks // len(arrays)
-        return [Part(a, 0, lead=i * count, parts=count) for i, a in enumerate(arrays)]
+    def split_states(arrays):
+        result, lead = [], 0
+        for a in arrays:
+            count = a.shape[0] * chunks // heads
+            result.append(Part(a, 0, lead=lead, parts=count))
+            lead += count
+        return result
 
     def to_peers(array, away, backward):
         pairs = [(z, z + away) for z in range(head_count - away) if z % devices + away < devices]
@@ -513,8 +519,11 @@
         return slices
 
     gain_row = Part(gain.reshape(1, width))
-    halves = [2 if b > 0 and chunks % 2 == 0 else 1 for b in range(blocks) for _ in range(peers)]
-    later = [[shape((heads // n, DH, DH), BF)] * n for n in halves]
+    early = heads // chunks
+    sizes = [heads], [early, heads - early] if chunks > 1 else [heads]
+    sizes = [sizes[b > 0] for b in range(blocks) for _ in range(peers)]
+    halves = [len(n) for n in sizes]
+    later = [[shape((k, DH, DH), BF) for k in n] for n in sizes]
     (sum_kv,) = call(
         total_body,
         "total",
@@ -522,7 +531,7 @@
         [wide(keys), wide(values)],
         [states(state)],
         heads,
-        chunks,
+        few,
         flops=unit,
     )
     slices = sum_kv.reshape(total, -1, DH)
@@ -534,9 +543,9 @@
             "states",
             scalars,
             [wide(late_keys), wide(values)],
-            [part for arrays in later for part in split_states(arrays, few)],
+            [part for arrays in later for part in split_states(arrays)],
             heads,
-            few,
+            chunks,
             flops=LONG,
         )
     later = iter(later)
@@ -576,7 +585,7 @@
                 wide(raw_inner, b),
                 wide(grad_out, b),
                 states(kv_state),
-                *[p for arrays in from_peers[b * peers : (b + 1) * peers] for p in split_states(arrays, few)],
+                *[Part(x) for arrays in from_peers[b * peers : (b + 1) * peers] for x in arrays],
                 *[states(w) for w in (updates if ends else [])],
             ],
             [Part(shape((BLOCK, DH), F32)), wide(block_tokens), wide(block_tokens), states(state), *ends],
@@ -601,7 +610,7 @@
             *[wide(d) for d in grads],
             *[wide(r) for r in raws],
             *[Part(s) for s in scales],
-            *[part for arrays in from_peers for part in split_states(arrays, chunks)],
+            *[part for arrays in from_peers for part in split_states(arrays)],
         ],
         [wide(tokens), wide(tokens)],
         heads,

time: 108 us -> 109 us (level)
    all_to_all x4, starting transfers between devices: 20.8 us -> 21.9 us  [exchanged(): return lax.all_to_all(slices, AXES, split_axis=0, concat_axis=0, tiled=True)]
    unnamed x14 -> x18, local copies, waits for them, and re-layouts: 1.51 us -> 2.2 us
  transfers between devices with their start and end apart: 9 -> 9, of which waited for: 6 -> 5; matrix products, arithmetic and copies ran while one was open for 0% -> 0% of each run, Pallas kernels for 38% -> 37%
where the time goes in v15:
time: 109 us
  Pallas kernels  48.8 us (45%)
  starting transfers between devices  32.5 us (30%)
  waiting for transfers between devices  24.1 us (22%)
  local copies, waits for them, and re-layouts  2.2 us (2%)
    pallas_call x10, Pallas kernels, call(): pl.pallas_call(kernel, name=name, in_specs=[*[pl.BlockSpec(memory_space=p...  48.8 us
    all_to_all x4, waiting for transfers between devices, exchanged(): return lax.all_to_all(slices, AXES, split_axis=0, concat_axis=0, tiled=True)  22.8 us
    all_to_all x4, starting transfers between devices, exchanged(): return lax.all_to_all(slices, AXES, split_axis=0, concat_axis=0, tiled=True)  21.9 us
    ppermute x5, starting transfers between devices, to_peers(): return lax.ppermute(array, 'head', pairs)  10.6 us
    unnamed x18, local copies, waits for them, and re-layouts  2.2 us
  transfers between devices with their start and end apart: 9, of which 5 were waited for; matrix products, arithmetic and copies ran while one was open for 0% of the time, Pallas kernels for 37%

profile of v15, /device:TPU:1, one launch (start us, length us, event | category | flops | bytes accessed | tf_op | source)
XLA Modules:
  0.0 108.6 jit_solution(10651552864377998943)
XLA Ops:
  0.6 3.4 %total.1 = bf16[16,128,128]{2,1,0:T(8,128)(2,1)} custom-call(s32[4]{0:T(128)} %refs_0_.19, s32[2,6]{1,0:T(2,128)} %refs_1_.15, bf16[256,2048]{1,0:T(8,128)(2,1)} %refs_2_.6, bf16[256,2048]{1,0:T(8,128)(2,1)} %refs_3_.15), custom_call_target="tpu_custom_call" | custom-call | flops 134217728 | bytes 2621440 | tf_op jit(solution)/shard_map/total/pallas_call | solution.py:440
  4.1 7.2 %all-to-all-start = ((bf16[32,64,128]{2,1,0:T(8,128)(2,1)}), bf16[32,64,128]{2,1,0:T(8,128)(2,1)}, u32[]{:S(2)}, u32[]{:S(2)}) async-start(bf16[32,64,128]{2,1,0:T(8,128)(2,1)} %bitcast.5), calls=%async_computation | async-start | bytes 1048576 | tf_op jit(solution)/shard_map/all_to_all | solution.py:506
  11.2 0.0 copy-start
  11.2 3.8 %states.1 = (bf16[16,128,128]{2,1,0:T(8,128)(2,1)}, bf16[4,128,128]{2,1,0:T(8,128)(2,1)}, bf16[12,128,128]{2,1,0:T(8,128)(2,1)}) custom-call(s32[4]{0:T(128)} %refs_0_.19, s32[2,6]{1,0:T(2,128)} %refs_1_.15, bf16[256,2048]{1,0:T(8,128)(2,1)} %refs_2_.6, bf16[256,2048]{1,0:T(8,128)(2,1)} %refs_3_.15), custom_call_target="tpu_custom_call" | custom-call | flops 399999991808 | bytes 3145728 | tf_op jit(solution)/shard_map/states/pallas_call | solution.py:440
  15.1 3.3 %collective-permute-start = (bf16[16,128,128]{2,1,0:T(8,128)(2,1)}, bf16[16,128,128]{2,1,0:T(8,128)(2,1)S(1)}, u32[]{:S(2)}, u32[]{:S(2)}) collective-permute-start(bf16[16,128,128]{2,1,0:T(8,128)(2,1)} %get-tuple-element.37), channel_id=1, source_target_pairs={{0,1},{2,3},{4,5},{6,7},{8,9},{10,11},{12,13},{14,15},{16,17},{18,... | collective-permute-start | bytes 1572872 | tf_op jit(solution)/shard_map/ppermute | solution.py:503
  18.4 8.1 %all-to-all-done.refs_1_ = bf16[32,64,128]{2,1,0:T(8,128)(2,1)} async-done(((bf16[32,64,128]{2,1,0:T(8,128)(2,1)}), bf16[32,64,128]{2,1,0:T(8,128)(2,1)}, u32[]{:S(2)}, u32[]{:S(2)}) %all-to-all-start) | async-done | bytes 524320 | tf_op jit(solution)/shard_map/all_to_all | solution.py:506
  26.6 0.0 copy-done
  26.6 2.0 %scan.2 = bf16[32,64,128]{2,1,0:T(8,128)(2,1)} custom-call(s32[4]{0:T(128)S(1)} %copy-done, bf16[32,64,128]{2,1,0:T(8,128)(2,1)} %all-to-all-done.refs_1_), custom_call_target="tpu_custom_call" | custom-call | bytes 1048576 | tf_op jit(solution)/shard_map/scan/pallas_call | solution.py:440
  28.6 3.2 %all-to-all-start.1 = ((bf16[32,64,128]{2,1,0:T(8,128)(2,1)}), bf16[32,64,128]{2,1,0:T(8,128)(2,1)}, u32[]{:S(2)}, u32[]{:S(2)}) async-start(bf16[32,64,128]{2,1,0:T(8,128)(2,1)} %scan.2), calls=%async_computation.1 | async-start | bytes 1048576 | tf_op jit(solution)/shard_map/all_to_all | solution.py:506
  31.8 0.0 collective-permute-done.refs_5_.refs_7_.refs_12_
  31.8 0.0 copy-start.4
  31.9 0.8 copy-done.4
  32.6 0.0 copy-start.6
  32.6 0.0 copy-start.8
  32.6 5.2 %inner.1.refs_4_ = f32[256,2048]{1,0:T(8,128)} custom-call(s32[4]{0:T(128)} %refs_0_.19, s32[2,6]{1,0:T(2,128)} %refs_1_.15, bf16[256,2048]{1,0:T(8,128)(2,1)} %refs_2_.5, bf16[256,2048]{1,0:T(8,128)(2,1)} %refs_2_.6, bf16[256,2048]{1,0:T(8,128)(2,1)} %refs_3_.15, bf16[16,128,128]{2,1,0:T(8,128)(2,1)} %copy-done.4), custom_call_target="tpu_custom_call" | custom-call | flops 399999991808 | bytes 5242880 | tf_op jit(solution)/shard_map/inner/pallas_call | solution.py:440
  37.9 0.0 copy-done.6
  37.9 3.4 %collective-permute-start.2 = (bf16[12,128,128]{2,1,0:T(8,128)(2,1)S(1)}, bf16[12,128,128]{2,1,0:T(8,128)(2,1)S(1)}, u32[]{:S(2)}, u32[]{:S(2)}) collective-permute-start(bf16[12,128,128]{2,1,0:T(8,128)(2,1)S(1)} %copy-done.6), channel_id=1, source_target_pairs={{0,1},{2,3},{4,5},{6,7},{8,9},{10,11},{12,13},{14,15},{16,17},{18,... | collective-permute-start | bytes 1179656 | tf_op jit(solution)/shard_map/ppermute | solution.py:503
  41.3 0.0 copy-done.8
  41.3 1.3 %collective-permute-start.1 = (bf16[4,128,128]{2,1,0:T(8,128)(2,1)S(1)}, bf16[4,128,128]{2,1,0:T(8,128)(2,1)S(1)}, u32[]{:S(2)}, u32[]{:S(2)}) collective-permute-start(bf16[4,128,128]{2,1,0:T(8,128)(2,1)S(1)} %copy-done.8), channel_id=1, source_target_pairs={{0,1},{2,3},{4,5},{6,7},{8,9},{10,11},{12,13},{14,15},{16,17},{18,... | collective-permute-start | bytes 393224 | tf_op jit(solution)/shard_map/ppermute | solution.py:503
  42.6 4.6 %all-to-all-done.1 = bf16[32,64,128]{2,1,0:T(8,128)(2,1)} async-done(((bf16[32,64,128]{2,1,0:T(8,128)(2,1)}), bf16[32,64,128]{2,1,0:T(8,128)(2,1)}, u32[]{:S(2)}, u32[]{:S(2)}) %all-to-all-start.1) | async-done | bytes 524320 | tf_op jit(solution)/shard_map/all_to_all | solution.py:506
  47.2 4.4 %norm.2 = (f32[128,128]{1,0:T(8,128)}, bf16[128,2048]{1,0:T(8,128)(2,1)}, bf16[128,2048]{1,0:T(8,128)(2,1)}, bf16[16,128,128]{2,1,0:T(8,128)(2,1)}) custom-call(s32[4]{0:T(128)} %refs_0_.19, s32[2,6]{1,0:T(2,128)} %refs_1_.15, f32[1,2048]{1,0:T(1,128)} %bitcast.7, bf16[256,2048]{1,0:T(8,128)(2,1)} %refs_2_.5, f32[256,2048]{1,0:T(8,128)} %inner.1.refs_4_, ...), custom_call_target="tpu_custom_call" | custom-call | flops 134217728 | bytes 6889472 | tf_op jit(solution)/shard_map/norm/pallas_call | solution.py:440
  51.6 1.3 %collective-permute-start.3 = (bf16[16,128,128]{2,1,0:T(8,128)(2,1)}, bf16[16,128,128]{2,1,0:T(8,128)(2,1)}, u32[]{:S(2)}, u32[]{:S(2)}) collective-permute-start(bf16[16,128,128]{2,1,0:T(8,128)(2,1)} %get-tuple-element.42.refs_9_), channel_id=1, source_target_pairs={{1,0},{3,2},{5,4},{7,6},{9,8},{11,10},{13,12},{15,14},{17,16},{19,... | collective-permute-start | bytes 1572872 | tf_op jit(solution)/shard_map/ppermute | solution.py:503
  52.9 0.0 collective-permute-done.1.refs_7_.refs_13_
  52.9 0.0 copy-start.7
  52.9 0.0 collective-permute-done.2.refs_8_.refs_14_
  52.9 0.6 copy-done.7
  53.6 0.0 copy-start.5
  53.6 0.8 copy-done.5
  54.3 4.9 %norm.3 = (f32[128,128]{1,0:T(8,128)}, bf16[128,2048]{1,0:T(8,128)(2,1)}, bf16[128,2048]{1,0:T(8,128)(2,1)}, bf16[16,128,128]{2,1,0:T(8,128)(2,1)}, bf16[16,128,128]{2,1,0:T(8,128)(2,1)}) custom-call(s32[4]{0:T(128)} %refs_0_.19, s32[2,6]{1,0:T(2,128)} %refs_1_.15, f32[1,2048]{1,0:T(1,128)} %bitcast.8, bf16[256,2048]{1,0:T(8,128)(2,1)} %refs_2_.5, ...), custom_call_target="tpu_custom_call" | custom-call | flops 399999991808 | bytes 7938048 | tf_op jit(solution)/shard_map/norm/pallas_call | solution.py:440
  59.2 8.3 %all-to-all-start.2 = ((bf16[32,64,128]{2,1,0:T(8,128)(2,1)}), bf16[32,64,128]{2,1,0:T(8,128)(2,1)}, u32[]{:S(2)}, u32[]{:S(2)}) async-start(bf16[32,64,128]{2,1,0:T(8,128)(2,1)} %bitcast.6), calls=%async_computation.2 | async-start | bytes 1048576 | tf_op jit(solution)/shard_map/all_to_all | solution.py:506
  67.4 1.3 %collective-permute-start.4 = (bf16[16,128,128]{2,1,0:T(8,128)(2,1)}, bf16[16,128,128]{2,1,0:T(8,128)(2,1)}, u32[]{:S(2)}, u32[]{:S(2)}) collective-permute-start(bf16[16,128,128]{2,1,0:T(8,128)(2,1)} %get-tuple-element.54), channel_id=1, source_target_pairs={{1,0},{3,2},{5,4},{7,6},{9,8},{11,10},{13,12},{15,14},{17,16},{19,... | collective-permute-start | bytes 1572872 | tf_op jit(solution)/shard_map/ppermute | solution.py:503
  68.7 0.0 collective-permute-done.3.refs_15_.refs_7_
  68.8 0.0 copy-start.1
  68.8 7.8 %query_grads.1 = (bf16[256,2048]{1,0:T(8,128)(2,1)}, bf16[256,2048]{1,0:T(8,128)(2,1)}) custom-call(s32[4]{0:T(128)} %refs_0_.19, s32[2,6]{1,0:T(2,128)} %refs_1_.15, f32[1,2048]{1,0:T(1,128)} %bitcast.9, bf16[256,2048]{1,0:T(8,128)(2,1)} %refs_2_.6, bf16[256,2048]{1,0:T(8,128)(2,1)} %refs_3_.15, bf16[16,128,128]{2,1,0:T(8,128)(2,1)} %bitcast.2.refs_6_.refs_5_, ...), custom_call_target="tpu_custom_call" | custom-call | flops 399999991808 | bytes 8003584 | tf_op jit(solution)/shard_map/query_grads/pallas_call | solution.py:440
  76.5 6.3 %all-to-all-done.2.refs_1_ = bf16[32,64,128]{2,1,0:T(8,128)(2,1)} async-done(((bf16[32,64,128]{2,1,0:T(8,128)(2,1)}), bf16[32,64,128]{2,1,0:T(8,128)(2,1)}, u32[]{:S(2)}, u32[]{:S(2)}) %all-to-all-start.2) | async-done | bytes 524320 | tf_op jit(solution)/shard_map/all_to_all | solution.py:506
  82.8 0.0 copy-done.1
  82.8 2.0 %scan.3 = bf16[32,64,128]{2,1,0:T(8,128)(2,1)} custom-call(s32[4]{0:T(128)S(1)} %copy-done.1, bf16[32,64,128]{2,1,0:T(8,128)(2,1)} %all-to-all-done.2.refs_1_), custom_call_target="tpu_custom_call" | custom-call | bytes 1048576 | tf_op jit(solution)/shard_map/scan/pallas_call | solution.py:440
  84.8 3.3 %all-to-all-start.3 = ((bf16[32,64,128]{2,1,0:T(8,128)(2,1)}), bf16[32,64,128]{2,1,0:T(8,128)(2,1)}, u32[]{:S(2)}, u32[]{:S(2)}) async-start(bf16[32,64,128]{2,1,0:T(8,128)(2,1)} %scan.3), calls=%async_computation.3 | async-start | bytes 1048576 | tf_op jit(solution)/shard_map/all_to_all | solution.py:506
  88.1 1.3 %collective-permute-done.4.refs_8_ = bf16[16,128,128]{2,1,0:T(8,128)(2,1)} collective-permute-done((bf16[16,128,128]{2,1,0:T(8,128)(2,1)}, bf16[16,128,128]{2,1,0:T(8,128)(2,1)}, u32[]{:S(2)}, u32[]{:S(2)}) %collective-permute-start.4) | collective-permute-done | bytes 524320 | tf_op jit(solution)/shard_map/ppermute | solution.py:503
  89.4 0.0 copy-start.2
  89.4 0.0 copy-start.3
  89.4 10.2 %key_grads.1 = (f32[256,2048]{1,0:T(8,128)}, f32[256,2048]{1,0:T(8,128)}) custom-call(s32[4]{0:T(128)} %refs_0_.19, s32[2,6]{1,0:T(2,128)} %refs_1_.15, bf16[256,2048]{1,0:T(8,128)(2,1)} %refs_2_.5, bf16[256,2048]{1,0:T(8,128)(2,1)} %refs_2_.6, bf16[256,2048]{1,0:T(8,128)(2,1)} %refs_3_.15, bf16[128,2048]{1,0:T(8,128)(2,1)} %get-tuple-element.39.refs_6_.refs_5_, ...), custom_call_target="tpu_custom_call" | custom-call | flops 399999991808 | bytes 9437184 | tf_op jit(solution)/shard_map/key_grads/pallas_call | solution.py:440
  99.6 3.8 %all-to-all-done.3 = bf16[32,64,128]{2,1,0:T(8,128)(2,1)} async-done(((bf16[32,64,128]{2,1,0:T(8,128)(2,1)}), bf16[32,64,128]{2,1,0:T(8,128)(2,1)}, u32[]{:S(2)}, u32[]{:S(2)}) %all-to-all-start.3) | async-done | bytes 524320 | tf_op jit(solution)/shard_map/all_to_all | solution.py:506
  103.4 0.0 copy-done.2
  103.4 0.0 copy-done.3
  103.4 5.0 %last.1 = (bf16[256,2048]{1,0:T(8,128)(2,1)}, bf16[256,2048]{1,0:T(8,128)(2,1)}) custom-call(s32[4]{0:T(128)S(1)} %copy-done.2, s32[2,6]{1,0:T(2,128)S(1)} %copy-done.3, bf16[256,2048]{1,0:T(8,128)(2,1)} %refs_2_.6, bf16[256,2048]{1,0:T(8,128)(2,1)} %refs_3_.15, f32[256,2048]{1,0:T(8,128)} %get-tuple-element.55.refs_4_, ...), custom_call_target="tpu_custom_call" | custom-call | flops 268435456 | bytes 8912896 | tf_op jit(solution)/shard_map/last/pallas_call | solution.py:440
Async XLA Ops:
  4.1 22.5 %all-to-all-start = ((bf16[32,64,128]{2,1,0:T(8,128)(2,1)}), bf16[32,64,128]{2,1,0:T(8,128)(2,1)}, u32[]{:S(2)}, u32[]{:S(2)}) async-start(bf16[32,64,128]{2,1,0:T(8,128)(2,1)} %bitcast.5), calls=%async_computation | async-start | bytes 1048576 | tf_op jit(solution)/shard_map/all_to_all | solution.py:506
  11.2 15.3 %copy-start = (s32[4]{0:T(128)S(1)}, s32[4]{0:T(128)}, u32[]{:S(2)}) copy-start(s32[4]{0:T(128)} %refs_0_.19) | copy-start | bytes 52
  15.1 16.7 %collective-permute-start = (bf16[16,128,128]{2,1,0:T(8,128)(2,1)}, bf16[16,128,128]{2,1,0:T(8,128)(2,1)S(1)}, u32[]{:S(2)}, u32[]{:S(2)}) collective-permute-start(bf16[16,128,128]{2,1,0:T(8,128)(2,1)} %get-tuple-element.37), channel_id=1, source_target_pairs={{0,1},{2,3},{4,5},{6,7},{8,9},{10,11},{12,13},{14,15},{16,17},{18,... | collective-permute-start | bytes 1572872 | tf_op jit(solution)/shard_map/ppermute | solution.py:503
  28.6 18.6 %all-to-all-start.1 = ((bf16[32,64,128]{2,1,0:T(8,128)(2,1)}), bf16[32,64,128]{2,1,0:T(8,128)(2,1)}, u32[]{:S(2)}, u32[]{:S(2)}) async-start(bf16[32,64,128]{2,1,0:T(8,128)(2,1)} %scan.2), calls=%async_computation.1 | async-start | bytes 1048576 | tf_op jit(solution)/shard_map/all_to_all | solution.py:506
  31.8 0.8 copy-start.4
  32.6 5.2 %copy-start.6 = (bf16[12,128,128]{2,1,0:T(8,128)(2,1)S(1)}, bf16[12,128,128]{2,1,0:T(8,128)(2,1)}, u32[]{:S(2)}) copy-start(bf16[12,128,128]{2,1,0:T(8,128)(2,1)} %get-tuple-element.41) | copy-start | bytes 1179652
  32.6 8.7 %copy-start.8 = (bf16[4,128,128]{2,1,0:T(8,128)(2,1)S(1)}, bf16[4,128,128]{2,1,0:T(8,128)(2,1)}, u32[]{:S(2)}) copy-start(bf16[4,128,128]{2,1,0:T(8,128)(2,1)} %get-tuple-element.40) | copy-start | bytes 393220
  37.9 15.1 %collective-permute-start.2 = (bf16[12,128,128]{2,1,0:T(8,128)(2,1)S(1)}, bf16[12,128,128]{2,1,0:T(8,128)(2,1)S(1)}, u32[]{:S(2)}, u32[]{:S(2)}) collective-permute-start(bf16[12,128,128]{2,1,0:T(8,128)(2,1)S(1)} %copy-done.6), channel_id=1, source_target_pairs={{0,1},{2,3},{4,5},{6,7},{8,9},{10,11},{12,13},{14,15},{16,17},{18,... | collective-permute-start | bytes 1179656 | tf_op jit(solution)/shard_map/ppermute | solution.py:503
  41.3 11.6 %collective-permute-start.1 = (bf16[4,128,128]{2,1,0:T(8,128)(2,1)S(1)}, bf16[4,128,128]{2,1,0:T(8,128)(2,1)S(1)}, u32[]{:S(2)}, u32[]{:S(2)}) collective-permute-start(bf16[4,128,128]{2,1,0:T(8,128)(2,1)S(1)} %copy-done.8), channel_id=1, source_target_pairs={{0,1},{2,3},{4,5},{6,7},{8,9},{10,11},{12,13},{14,15},{16,17},{18,... | collective-permute-start | bytes 393224 | tf_op jit(solution)/shard_map/ppermute | solution.py:503
  51.6 17.1 %collective-permute-start.3 = (bf16[16,128,128]{2,1,0:T(8,128)(2,1)}, bf16[16,128,128]{2,1,0:T(8,128)(2,1)}, u32[]{:S(2)}, u32[]{:S(2)}) collective-permute-start(bf16[16,128,128]{2,1,0:T(8,128)(2,1)} %get-tuple-element.42.refs_9_), channel_id=1, source_target_pairs={{1,0},{3,2},{5,4},{7,6},{9,8},{11,10},{13,12},{15,14},{17,16},{19,... | collective-permute-start | bytes 1572872 | tf_op jit(solution)/shard_map/ppermute | solution.py:503
  52.9 0.6 copy-start.7
  53.6 0.8 copy-start.5
  59.2 23.6 %all-to-all-start.2 = ((bf16[32,64,128]{2,1,0:T(8,128)(2,1)}), bf16[32,64,128]{2,1,0:T(8,128)(2,1)}, u32[]{:S(2)}, u32[]{:S(2)}) async-start(bf16[32,64,128]{2,1,0:T(8,128)(2,1)} %bitcast.6), calls=%async_computation.2 | async-start | bytes 1048576 | tf_op jit(solution)/shard_map/all_to_all | solution.py:506
  67.4 22.0 %collective-permute-start.4 = (bf16[16,128,128]{2,1,0:T(8,128)(2,1)}, bf16[16,128,128]{2,1,0:T(8,128)(2,1)}, u32[]{:S(2)}, u32[]{:S(2)}) collective-permute-start(bf16[16,128,128]{2,1,0:T(8,128)(2,1)} %get-tuple-element.54), channel_id=1, source_target_pairs={{1,0},{3,2},{5,4},{7,6},{9,8},{11,10},{13,12},{15,14},{17,16},{19,... | collective-permute-start | bytes 1572872 | tf_op jit(solution)/shard_map/ppermute | solution.py:503
  68.8 14.1 %copy-start.1 = (s32[4]{0:T(128)S(1)}, s32[4]{0:T(128)}, u32[]{:S(2)}) copy-start(s32[4]{0:T(128)} %refs_0_.19) | copy-start | bytes 52
  84.8 18.6 %all-to-all-start.3 = ((bf16[32,64,128]{2,1,0:T(8,128)(2,1)}), bf16[32,64,128]{2,1,0:T(8,128)(2,1)}, u32[]{:S(2)}, u32[]{:S(2)}) async-start(bf16[32,64,128]{2,1,0:T(8,128)(2,1)} %scan.3), calls=%async_computation.3 | async-start | bytes 1048576 | tf_op jit(solution)/shard_map/all_to_all | solution.py:506
  89.4 14.0 %copy-start.2 = (s32[4]{0:T(128)S(1)}, s32[4]{0:T(128)}, u32[]{:S(2)}) copy-start(s32[4]{0:T(128)} %refs_0_.19) | copy-start | bytes 52
  89.4 14.0 %copy-start.3 = (s32[2,6]{1,0:T(2,128)S(1)}, s32[2,6]{1,0:T(2,128)}, u32[]{:S(2)}) copy-start(s32[2,6]{1,0:T(2,128)} %refs_1_.15) | copy-start | bytes 148

commit v16 on v13

--- a/solution.py
+++ b/solution.py
@@ -522,7 +522,7 @@
         [wide(keys), wide(values)],
         [states(state)],
         heads,
-        chunks,
+        few,
         flops=unit,
     )
     slices = sum_kv.reshape(total, -1, DH)

time: 108 us -> 108 us (level)
  no operation moved by 1% of the time
where the time goes in v16:
time: 108 us; the launch traced here: 107 us
  Pallas kernels  48.7 us (45%)
  starting transfers between devices  32.1 us (30%)
  waiting for transfers between devices  23.5 us (22%)
  local copies, waits for them, and re-layouts  1.51 us (1%)
    pallas_call x10, Pallas kernels, call(): pl.pallas_call(kernel, name=name, in_specs=[*[pl.BlockSpec(memory_space=p...  48.7 us
    all_to_all x4, waiting for transfers between devices, exchanged(): return lax.all_to_all(slices, AXES, split_axis=0, concat_axis=0, tiled=True)  21.7 us
    all_to_all x4, starting transfers between devices, exchanged(): return lax.all_to_all(slices, AXES, split_axis=0, concat_axis=0, tiled=True)  20.8 us
    ppermute x5, starting transfers between devices, to_peers(): return lax.ppermute(array, 'head', pairs)  11.3 us
  transfers between devices with their start and end apart: 9, of which 6 were waited for; matrix products, arithmetic and copies ran while one was open for 0% of the time, Pallas kernels for 38%

profile of v16, /device:TPU:1, one launch (start us, length us, event | category | flops | bytes accessed | tf_op | source)
XLA Modules:
  0.0 106.8 jit_solution(5615958029463867605)
XLA Ops:
  0.6 3.4 %total.1 = bf16[16,128,128]{2,1,0:T(8,128)(2,1)} custom-call(s32[4]{0:T(128)} %refs_0_.19, s32[2,6]{1,0:T(2,128)} %refs_1_.15, bf16[256,2048]{1,0:T(8,128)(2,1)} %refs_2_.6, bf16[256,2048]{1,0:T(8,128)(2,1)} %refs_3_.15), custom_call_target="tpu_custom_call" | custom-call | flops 134217728 | bytes 2621440 | tf_op jit(solution)/shard_map/total/pallas_call | solution.py:438
  4.1 7.2 %all-to-all-start = ((bf16[32,64,128]{2,1,0:T(8,128)(2,1)}), bf16[32,64,128]{2,1,0:T(8,128)(2,1)}, u32[]{:S(2)}, u32[]{:S(2)}) async-start(bf16[32,64,128]{2,1,0:T(8,128)(2,1)} %bitcast.5), calls=%async_computation | async-start | bytes 1048576 | tf_op jit(solution)/shard_map/all_to_all | solution.py:500
  11.2 0.0 copy-start
  11.2 3.6 %states.1 = (bf16[16,128,128]{2,1,0:T(8,128)(2,1)}, bf16[8,128,128]{2,1,0:T(8,128)(2,1)}, bf16[8,128,128]{2,1,0:T(8,128)(2,1)}) custom-call(s32[4]{0:T(128)} %refs_0_.19, s32[2,6]{1,0:T(2,128)} %refs_1_.15, bf16[256,2048]{1,0:T(8,128)(2,1)} %refs_2_.6, bf16[256,2048]{1,0:T(8,128)(2,1)} %refs_3_.15), custom_call_target="tpu_custom_call" | custom-call | flops 399999991808 | bytes 3145728 | tf_op jit(solution)/shard_map/states/pallas_call | solution.py:438
  14.9 3.3 %collective-permute-start = (bf16[16,128,128]{2,1,0:T(8,128)(2,1)}, bf16[16,128,128]{2,1,0:T(8,128)(2,1)S(1)}, u32[]{:S(2)}, u32[]{:S(2)}) collective-permute-start(bf16[16,128,128]{2,1,0:T(8,128)(2,1)} %get-tuple-element.37), channel_id=1, source_target_pairs={{0,1},{2,3},{4,5},{6,7},{8,9},{10,11},{12,13},{14,15},{16,17},{18,... | collective-permute-start | bytes 1572872 | tf_op jit(solution)/shard_map/ppermute | solution.py:497
  18.2 2.0 %collective-permute-start.1 = (bf16[8,128,128]{2,1,0:T(8,128)(2,1)}, bf16[8,128,128]{2,1,0:T(8,128)(2,1)}, u32[]{:S(2)}, u32[]{:S(2)}) collective-permute-start(bf16[8,128,128]{2,1,0:T(8,128)(2,1)} %get-tuple-element.40), channel_id=1, source_target_pairs={{0,1},{2,3},{4,5},{6,7},{8,9},{10,11},{12,13},{14,15},{16,17},{18,... | collective-permute-start | bytes 786440 | tf_op jit(solution)/shard_map/ppermute | solution.py:497
  20.2 6.4 %all-to-all-done.refs_1_ = bf16[32,64,128]{2,1,0:T(8,128)(2,1)} async-done(((bf16[32,64,128]{2,1,0:T(8,128)(2,1)}), bf16[32,64,128]{2,1,0:T(8,128)(2,1)}, u32[]{:S(2)}, u32[]{:S(2)}) %all-to-all-start) | async-done | bytes 524320 | tf_op jit(solution)/shard_map/all_to_all | solution.py:500
  26.6 0.0 copy-done
  26.6 2.0 %scan.2 = bf16[32,64,128]{2,1,0:T(8,128)(2,1)} custom-call(s32[4]{0:T(128)S(1)} %copy-done, bf16[32,64,128]{2,1,0:T(8,128)(2,1)} %all-to-all-done.refs_1_), custom_call_target="tpu_custom_call" | custom-call | bytes 1048576 | tf_op jit(solution)/shard_map/scan/pallas_call | solution.py:438
  28.6 3.2 %all-to-all-start.1 = ((bf16[32,64,128]{2,1,0:T(8,128)(2,1)}), bf16[32,64,128]{2,1,0:T(8,128)(2,1)}, u32[]{:S(2)}, u32[]{:S(2)}) async-start(bf16[32,64,128]{2,1,0:T(8,128)(2,1)} %scan.2), calls=%async_computation.1 | async-start | bytes 1048576 | tf_op jit(solution)/shard_map/all_to_all | solution.py:500
  31.8 0.0 collective-permute-done.refs_5_.refs_7_.refs_12_
  31.8 0.0 copy-start.4
  31.9 0.8 copy-done.4
  32.6 0.0 copy-start.6
  32.6 5.2 %inner.1.refs_4_ = f32[256,2048]{1,0:T(8,128)} custom-call(s32[4]{0:T(128)} %refs_0_.19, s32[2,6]{1,0:T(2,128)} %refs_1_.15, bf16[256,2048]{1,0:T(8,128)(2,1)} %refs_2_.5, bf16[256,2048]{1,0:T(8,128)(2,1)} %refs_2_.6, bf16[256,2048]{1,0:T(8,128)(2,1)} %refs_3_.15, bf16[16,128,128]{2,1,0:T(8,128)(2,1)} %copy-done.4), custom_call_target="tpu_custom_call" | custom-call | flops 399999991808 | bytes 5242880 | tf_op jit(solution)/shard_map/inner/pallas_call | solution.py:438
  37.9 0.0 copy-done.6
  37.9 3.4 %collective-permute-start.2 = (bf16[8,128,128]{2,1,0:T(8,128)(2,1)S(1)}, bf16[8,128,128]{2,1,0:T(8,128)(2,1)S(1)}, u32[]{:S(2)}, u32[]{:S(2)}) collective-permute-start(bf16[8,128,128]{2,1,0:T(8,128)(2,1)S(1)} %copy-done.6), channel_id=1, source_target_pairs={{0,1},{2,3},{4,5},{6,7},{8,9},{10,11},{12,13},{14,15},{16,17},{18,... | collective-permute-start | bytes 786440 | tf_op jit(solution)/shard_map/ppermute | solution.py:497
  41.3 5.9 %all-to-all-done.1 = bf16[32,64,128]{2,1,0:T(8,128)(2,1)} async-done(((bf16[32,64,128]{2,1,0:T(8,128)(2,1)}), bf16[32,64,128]{2,1,0:T(8,128)(2,1)}, u32[]{:S(2)}, u32[]{:S(2)}) %all-to-all-start.1) | async-done | bytes 524320 | tf_op jit(solution)/shard_map/all_to_all | solution.py:500
  47.2 4.4 %norm.2 = (f32[128,128]{1,0:T(8,128)}, bf16[128,2048]{1,0:T(8,128)(2,1)}, bf16[128,2048]{1,0:T(8,128)(2,1)}, bf16[16,128,128]{2,1,0:T(8,128)(2,1)}) custom-call(s32[4]{0:T(128)} %refs_0_.19, s32[2,6]{1,0:T(2,128)} %refs_1_.15, f32[1,2048]{1,0:T(1,128)} %bitcast.7, bf16[256,2048]{1,0:T(8,128)(2,1)} %refs_2_.5, f32[256,2048]{1,0:T(8,128)} %inner.1.refs_4_, ...), custom_call_target="tpu_custom_call" | custom-call | flops 134217728 | bytes 6889472 | tf_op jit(solution)/shard_map/norm/pallas_call | solution.py:438
  51.6 1.3 %collective-permute-start.3 = (bf16[16,128,128]{2,1,0:T(8,128)(2,1)}, bf16[16,128,128]{2,1,0:T(8,128)(2,1)}, u32[]{:S(2)}, u32[]{:S(2)}) collective-permute-start(bf16[16,128,128]{2,1,0:T(8,128)(2,1)} %get-tuple-element.42.refs_9_), channel_id=1, source_target_pairs={{1,0},{3,2},{5,4},{7,6},{9,8},{11,10},{13,12},{15,14},{17,16},{19,... | collective-permute-start | bytes 1572872 | tf_op jit(solution)/shard_map/ppermute | solution.py:497
  52.9 0.0 collective-permute-done.1.refs_7_.refs_13_
  52.9 0.0 collective-permute-done.2.refs_8_.refs_14_
  52.9 0.0 copy-start.5
  52.9 0.7 copy-done.5
  53.6 4.8 %norm.3 = (f32[128,128]{1,0:T(8,128)}, bf16[128,2048]{1,0:T(8,128)(2,1)}, bf16[128,2048]{1,0:T(8,128)(2,1)}, bf16[16,128,128]{2,1,0:T(8,128)(2,1)}, bf16[16,128,128]{2,1,0:T(8,128)(2,1)}) custom-call(s32[4]{0:T(128)} %refs_0_.19, s32[2,6]{1,0:T(2,128)} %refs_1_.15, f32[1,2048]{1,0:T(1,128)} %bitcast.8, bf16[256,2048]{1,0:T(8,128)(2,1)} %refs_2_.5, ...), custom_call_target="tpu_custom_call" | custom-call | flops 399999991808 | bytes 7938048 | tf_op jit(solution)/shard_map/norm/pallas_call | solution.py:438
  58.5 7.1 %all-to-all-start.2 = ((bf16[32,64,128]{2,1,0:T(8,128)(2,1)}), bf16[32,64,128]{2,1,0:T(8,128)(2,1)}, u32[]{:S(2)}, u32[]{:S(2)}) async-start(bf16[32,64,128]{2,1,0:T(8,128)(2,1)} %bitcast.6), calls=%async_computation.2 | async-start | bytes 1048576 | tf_op jit(solution)/shard_map/all_to_all | solution.py:500
  65.6 1.3 %collective-permute-start.4 = (bf16[16,128,128]{2,1,0:T(8,128)(2,1)}, bf16[16,128,128]{2,1,0:T(8,128)(2,1)}, u32[]{:S(2)}, u32[]{:S(2)}) collective-permute-start(bf16[16,128,128]{2,1,0:T(8,128)(2,1)} %get-tuple-element.54), channel_id=1, source_target_pairs={{1,0},{3,2},{5,4},{7,6},{9,8},{11,10},{13,12},{15,14},{17,16},{19,... | collective-permute-start | bytes 1572872 | tf_op jit(solution)/shard_map/ppermute | solution.py:497
  66.9 0.4 collective-permute-done.3.refs_15_.refs_7_
  67.4 0.0 copy-start.1
  67.4 7.9 %query_grads.1 = (bf16[256,2048]{1,0:T(8,128)(2,1)}, bf16[256,2048]{1,0:T(8,128)(2,1)}) custom-call(s32[4]{0:T(128)} %refs_0_.19, s32[2,6]{1,0:T(2,128)} %refs_1_.15, f32[1,2048]{1,0:T(1,128)} %bitcast.9, bf16[256,2048]{1,0:T(8,128)(2,1)} %refs_2_.6, bf16[256,2048]{1,0:T(8,128)(2,1)} %refs_3_.15, bf16[16,128,128]{2,1,0:T(8,128)(2,1)} %bitcast.2.refs_6_.refs_5_, ...), custom_call_target="tpu_custom_call" | custom-call | flops 399999991808 | bytes 8003584 | tf_op jit(solution)/shard_map/query_grads/pallas_call | solution.py:438
  75.2 5.8 %all-to-all-done.2.refs_1_ = bf16[32,64,128]{2,1,0:T(8,128)(2,1)} async-done(((bf16[32,64,128]{2,1,0:T(8,128)(2,1)}), bf16[32,64,128]{2,1,0:T(8,128)(2,1)}, u32[]{:S(2)}, u32[]{:S(2)}) %all-to-all-start.2) | async-done | bytes 524320 | tf_op jit(solution)/shard_map/all_to_all | solution.py:500
  81.0 0.0 copy-done.1
  81.0 2.0 %scan.3 = bf16[32,64,128]{2,1,0:T(8,128)(2,1)} custom-call(s32[4]{0:T(128)S(1)} %copy-done.1, bf16[32,64,128]{2,1,0:T(8,128)(2,1)} %all-to-all-done.2.refs_1_), custom_call_target="tpu_custom_call" | custom-call | bytes 1048576 | tf_op jit(solution)/shard_map/scan/pallas_call | solution.py:438
  83.0 3.3 %all-to-all-start.3 = ((bf16[32,64,128]{2,1,0:T(8,128)(2,1)}), bf16[32,64,128]{2,1,0:T(8,128)(2,1)}, u32[]{:S(2)}, u32[]{:S(2)}) async-start(bf16[32,64,128]{2,1,0:T(8,128)(2,1)} %scan.3), calls=%async_computation.3 | async-start | bytes 1048576 | tf_op jit(solution)/shard_map/all_to_all | solution.py:500
  86.3 1.3 %collective-permute-done.4.refs_8_ = bf16[16,128,128]{2,1,0:T(8,128)(2,1)} collective-permute-done((bf16[16,128,128]{2,1,0:T(8,128)(2,1)}, bf16[16,128,128]{2,1,0:T(8,128)(2,1)}, u32[]{:S(2)}, u32[]{:S(2)}) %collective-permute-start.4) | collective-permute-done | bytes 524320 | tf_op jit(solution)/shard_map/ppermute | solution.py:497
  87.6 0.0 copy-start.2
  87.6 0.0 copy-start.3
  87.6 10.3 %key_grads.1 = (f32[256,2048]{1,0:T(8,128)}, f32[256,2048]{1,0:T(8,128)}) custom-call(s32[4]{0:T(128)} %refs_0_.19, s32[2,6]{1,0:T(2,128)} %refs_1_.15, bf16[256,2048]{1,0:T(8,128)(2,1)} %refs_2_.5, bf16[256,2048]{1,0:T(8,128)(2,1)} %refs_2_.6, bf16[256,2048]{1,0:T(8,128)(2,1)} %refs_3_.15, bf16[128,2048]{1,0:T(8,128)(2,1)} %get-tuple-element.39.refs_6_.refs_5_, ...), custom_call_target="tpu_custom_call" | custom-call | flops 399999991808 | bytes 9437184 | tf_op jit(solution)/shard_map/key_grads/pallas_call | solution.py:438
  97.9 3.7 %all-to-all-done.3 = bf16[32,64,128]{2,1,0:T(8,128)(2,1)} async-done(((bf16[32,64,128]{2,1,0:T(8,128)(2,1)}), bf16[32,64,128]{2,1,0:T(8,128)(2,1)}, u32[]{:S(2)}, u32[]{:S(2)}) %all-to-all-start.3) | async-done | bytes 524320 | tf_op jit(solution)/shard_map/all_to_all | solution.py:500
  101.6 0.0 copy-done.2
  101.6 0.0 copy-done.3
  101.6 5.0 %last.1 = (bf16[256,2048]{1,0:T(8,128)(2,1)}, bf16[256,2048]{1,0:T(8,128)(2,1)}) custom-call(s32[4]{0:T(128)S(1)} %copy-done.2, s32[2,6]{1,0:T(2,128)S(1)} %copy-done.3, bf16[256,2048]{1,0:T(8,128)(2,1)} %refs_2_.6, bf16[256,2048]{1,0:T(8,128)(2,1)} %refs_3_.15, f32[256,2048]{1,0:T(8,128)} %get-tuple-element.55.refs_4_, ...), custom_call_target="tpu_custom_call" | custom-call | flops 268435456 | bytes 8912896 | tf_op jit(solution)/shard_map/last/pallas_call | solution.py:438
Async XLA Ops:
  4.1 22.5 %all-to-all-start = ((bf16[32,64,128]{2,1,0:T(8,128)(2,1)}), bf16[32,64,128]{2,1,0:T(8,128)(2,1)}, u32[]{:S(2)}, u32[]{:S(2)}) async-start(bf16[32,64,128]{2,1,0:T(8,128)(2,1)} %bitcast.5), calls=%async_computation | async-start | bytes 1048576 | tf_op jit(solution)/shard_map/all_to_all | solution.py:500
  11.2 15.3 %copy-start = (s32[4]{0:T(128)S(1)}, s32[4]{0:T(128)}, u32[]{:S(2)}) copy-start(s32[4]{0:T(128)} %refs_0_.19) | copy-start | bytes 52
  14.9 17.0 %collective-permute-start = (bf16[16,128,128]{2,1,0:T(8,128)(2,1)}, bf16[16,128,128]{2,1,0:T(8,128)(2,1)S(1)}, u32[]{:S(2)}, u32[]{:S(2)}) collective-permute-start(bf16[16,128,128]{2,1,0:T(8,128)(2,1)} %get-tuple-element.37), channel_id=1, source_target_pairs={{0,1},{2,3},{4,5},{6,7},{8,9},{10,11},{12,13},{14,15},{16,17},{18,... | collective-permute-start | bytes 1572872 | tf_op jit(solution)/shard_map/ppermute | solution.py:497
  18.2 34.7 %collective-permute-start.1 = (bf16[8,128,128]{2,1,0:T(8,128)(2,1)}, bf16[8,128,128]{2,1,0:T(8,128)(2,1)}, u32[]{:S(2)}, u32[]{:S(2)}) collective-permute-start(bf16[8,128,128]{2,1,0:T(8,128)(2,1)} %get-tuple-element.40), channel_id=1, source_target_pairs={{0,1},{2,3},{4,5},{6,7},{8,9},{10,11},{12,13},{14,15},{16,17},{18,... | collective-permute-start | bytes 786440 | tf_op jit(solution)/shard_map/ppermute | solution.py:497
  28.6 18.6 %all-to-all-start.1 = ((bf16[32,64,128]{2,1,0:T(8,128)(2,1)}), bf16[32,64,128]{2,1,0:T(8,128)(2,1)}, u32[]{:S(2)}, u32[]{:S(2)}) async-start(bf16[32,64,128]{2,1,0:T(8,128)(2,1)} %scan.2), calls=%async_computation.1 | async-start | bytes 1048576 | tf_op jit(solution)/shard_map/all_to_all | solution.py:500
  31.8 0.8 copy-start.4
  32.6 5.2 %copy-start.6 = (bf16[8,128,128]{2,1,0:T(8,128)(2,1)S(1)}, bf16[8,128,128]{2,1,0:T(8,128)(2,1)}, u32[]{:S(2)}) copy-start(bf16[8,128,128]{2,1,0:T(8,128)(2,1)} %get-tuple-element.41) | copy-start | bytes 786436
  37.9 15.1 %collective-permute-start.2 = (bf16[8,128,128]{2,1,0:T(8,128)(2,1)S(1)}, bf16[8,128,128]{2,1,0:T(8,128)(2,1)S(1)}, u32[]{:S(2)}, u32[]{:S(2)}) collective-permute-start(bf16[8,128,128]{2,1,0:T(8,128)(2,1)S(1)} %copy-done.6), channel_id=1, source_target_pairs={{0,1},{2,3},{4,5},{6,7},{8,9},{10,11},{12,13},{14,15},{16,17},{18,... | collective-permute-start | bytes 786440 | tf_op jit(solution)/shard_map/ppermute | solution.py:497
  51.6 15.7 %collective-permute-start.3 = (bf16[16,128,128]{2,1,0:T(8,128)(2,1)}, bf16[16,128,128]{2,1,0:T(8,128)(2,1)}, u32[]{:S(2)}, u32[]{:S(2)}) collective-permute-start(bf16[16,128,128]{2,1,0:T(8,128)(2,1)} %get-tuple-element.42.refs_9_), channel_id=1, source_target_pairs={{1,0},{3,2},{5,4},{7,6},{9,8},{11,10},{13,12},{15,14},{17,16},{19,... | collective-permute-start | bytes 1572872 | tf_op jit(solution)/shard_map/ppermute | solution.py:497
  52.9 0.7 copy-start.5
  58.5 22.5 %all-to-all-start.2 = ((bf16[32,64,128]{2,1,0:T(8,128)(2,1)}), bf16[32,64,128]{2,1,0:T(8,128)(2,1)}, u32[]{:S(2)}, u32[]{:S(2)}) async-start(bf16[32,64,128]{2,1,0:T(8,128)(2,1)} %bitcast.6), calls=%async_computation.2 | async-start | bytes 1048576 | tf_op jit(solution)/shard_map/all_to_all | solution.py:500
  65.6 22.0 %collective-permute-start.4 = (bf16[16,128,128]{2,1,0:T(8,128)(2,1)}, bf16[16,128,128]{2,1,0:T(8,128)(2,1)}, u32[]{:S(2)}, u32[]{:S(2)}) collective-permute-start(bf16[16,128,128]{2,1,0:T(8,128)(2,1)} %get-tuple-element.54), channel_id=1, source_target_pairs={{1,0},{3,2},{5,4},{7,6},{9,8},{11,10},{13,12},{15,14},{17,16},{19,... | collective-permute-start | bytes 1572872 | tf_op jit(solution)/shard_map/ppermute | solution.py:497
  67.4 13.6 %copy-start.1 = (s32[4]{0:T(128)S(1)}, s32[4]{0:T(128)}, u32[]{:S(2)}) copy-start(s32[4]{0:T(128)} %refs_0_.19) | copy-start | bytes 52
  83.0 18.6 %all-to-all-start.3 = ((bf16[32,64,128]{2,1,0:T(8,128)(2,1)}), bf16[32,64,128]{2,1,0:T(8,128)(2,1)}, u32[]{:S(2)}, u32[]{:S(2)}) async-start(bf16[32,64,128]{2,1,0:T(8,128)(2,1)} %scan.3), calls=%async_computation.3 | async-start | bytes 1048576 | tf_op jit(solution)/shard_map/all_to_all | solution.py:500
  87.6 14.0 %copy-start.2 = (s32[4]{0:T(128)S(1)}, s32[4]{0:T(128)}, u32[]{:S(2)}) copy-start(s32[4]{0:T(128)} %refs_0_.19) | copy-start | bytes 52
  87.6 14.0 %copy-start.3 = (s32[2,6]{1,0:T(2,128)S(1)}, s32[2,6]{1,0:T(2,128)}, u32[]{:S(2)}) copy-start(s32[2,6]{1,0:T(2,128)} %refs_1_.15) | copy-start | bytes 148

commit v17 on v16

--- a/solution.py
+++ b/solution.py
@@ -507,7 +507,7 @@
             [Part(slices, near=True)],
             [Part(shape(slices.shape, BF), 1)],
             heads,
-            2 if slices.shape[1] % 32 == 0 else 1,
+            1,
             limit=SOME_BYTES,
         )
         return slices
@@ -522,7 +522,7 @@
         [wide(keys), wide(values)],
         [states(state)],
         heads,
-        few,
+        1,
         flops=unit,
     )
     slices = sum_kv.reshape(total, -1, DH)

time: 108 us -> 108 us (level)
  no operation moved by 1% of the time
where the time goes in v17:
time: 108 us; the launch traced here: 107 us
  Pallas kernels  48.9 us (45%)
  starting transfers between devices  32.1 us (30%)
  waiting for transfers between devices  23.5 us (22%)
  local copies, waits for them, and re-layouts  1.51 us (1%)
    pallas_call x10, Pallas kernels, call(): pl.pallas_call(kernel, name=name, in_specs=[*[pl.BlockSpec(memory_space=p...  48.9 us
    all_to_all x4, waiting for transfers between devices, exchanged(): return lax.all_to_all(slices, AXES, split_axis=0, concat_axis=0, tiled=True)  21.7 us
    all_to_all x4, starting transfers between devices, exchanged(): return lax.all_to_all(slices, AXES, split_axis=0, concat_axis=0, tiled=True)  20.8 us
    ppermute x5, starting transfers between devices, to_peers(): return lax.ppermute(array, 'head', pairs)  11.3 us
  transfers between devices with their start and end apart: 9, of which 6 were waited for; matrix products, arithmetic and copies ran while one was open for 0% of the time, Pallas kernels for 38%

profile of v17, /device:TPU:1, one launch (start us, length us, event | category | flops | bytes accessed | tf_op | source)
XLA Modules:
  0.0 107.0 jit_solution(491709011141830368)
XLA Ops:
  0.6 3.6 %total.1 = bf16[16,128,128]{2,1,0:T(8,128)(2,1)} custom-call(s32[4]{0:T(128)} %refs_0_.19, s32[2,6]{1,0:T(2,128)} %refs_1_.15, bf16[256,2048]{1,0:T(8,128)(2,1)} %refs_2_.6, bf16[256,2048]{1,0:T(8,128)(2,1)} %refs_3_.15), custom_call_target="tpu_custom_call" | custom-call | flops 134217728 | bytes 2621440 | tf_op jit(solution)/shard_map/total/pallas_call | solution.py:438
  4.3 7.2 %all-to-all-start = ((bf16[32,64,128]{2,1,0:T(8,128)(2,1)}), bf16[32,64,128]{2,1,0:T(8,128)(2,1)}, u32[]{:S(2)}, u32[]{:S(2)}) async-start(bf16[32,64,128]{2,1,0:T(8,128)(2,1)} %bitcast.5), calls=%async_computation | async-start | bytes 1048576 | tf_op jit(solution)/shard_map/all_to_all | solution.py:500
  11.4 0.0 copy-start
  11.4 3.6 %states.1 = (bf16[16,128,128]{2,1,0:T(8,128)(2,1)}, bf16[8,128,128]{2,1,0:T(8,128)(2,1)}, bf16[8,128,128]{2,1,0:T(8,128)(2,1)}) custom-call(s32[4]{0:T(128)} %refs_0_.19, s32[2,6]{1,0:T(2,128)} %refs_1_.15, bf16[256,2048]{1,0:T(8,128)(2,1)} %refs_2_.6, bf16[256,2048]{1,0:T(8,128)(2,1)} %refs_3_.15), custom_call_target="tpu_custom_call" | custom-call | flops 399999991808 | bytes 3145728 | tf_op jit(solution)/shard_map/states/pallas_call | solution.py:438
  15.0 3.3 %collective-permute-start = (bf16[16,128,128]{2,1,0:T(8,128)(2,1)}, bf16[16,128,128]{2,1,0:T(8,128)(2,1)S(1)}, u32[]{:S(2)}, u32[]{:S(2)}) collective-permute-start(bf16[16,128,128]{2,1,0:T(8,128)(2,1)} %get-tuple-element.37), channel_id=1, source_target_pairs={{0,1},{2,3},{4,5},{6,7},{8,9},{10,11},{12,13},{14,15},{16,17},{18,... | collective-permute-start | bytes 1572872 | tf_op jit(solution)/shard_map/ppermute | solution.py:497
  18.4 2.0 %collective-permute-start.1 = (bf16[8,128,128]{2,1,0:T(8,128)(2,1)}, bf16[8,128,128]{2,1,0:T(8,128)(2,1)}, u32[]{:S(2)}, u32[]{:S(2)}) collective-permute-start(bf16[8,128,128]{2,1,0:T(8,128)(2,1)} %get-tuple-element.40), channel_id=1, source_target_pairs={{0,1},{2,3},{4,5},{6,7},{8,9},{10,11},{12,13},{14,15},{16,17},{18,... | collective-permute-start | bytes 786440 | tf_op jit(solution)/shard_map/ppermute | solution.py:497
  20.4 6.4 %all-to-all-done.refs_1_ = bf16[32,64,128]{2,1,0:T(8,128)(2,1)} async-done(((bf16[32,64,128]{2,1,0:T(8,128)(2,1)}), bf16[32,64,128]{2,1,0:T(8,128)(2,1)}, u32[]{:S(2)}, u32[]{:S(2)}) %all-to-all-start) | async-done | bytes 524320 | tf_op jit(solution)/shard_map/all_to_all | solution.py:500
  26.8 0.0 copy-done
  26.8 2.0 %scan.2 = bf16[32,64,128]{2,1,0:T(8,128)(2,1)} custom-call(s32[4]{0:T(128)S(1)} %copy-done, bf16[32,64,128]{2,1,0:T(8,128)(2,1)} %all-to-all-done.refs_1_), custom_call_target="tpu_custom_call" | custom-call | bytes 1048576 | tf_op jit(solution)/shard_map/scan/pallas_call | solution.py:438
  28.8 3.2 %all-to-all-start.1 = ((bf16[32,64,128]{2,1,0:T(8,128)(2,1)}), bf16[32,64,128]{2,1,0:T(8,128)(2,1)}, u32[]{:S(2)}, u32[]{:S(2)}) async-start(bf16[32,64,128]{2,1,0:T(8,128)(2,1)} %scan.2), calls=%async_computation.1 | async-start | bytes 1048576 | tf_op jit(solution)/shard_map/all_to_all | solution.py:500
  32.0 0.0 collective-permute-done.refs_5_.refs_7_.refs_12_
  32.0 0.0 copy-start.4
  32.0 0.8 copy-done.4
  32.8 0.0 copy-start.6
  32.8 5.2 %inner.1.refs_4_ = f32[256,2048]{1,0:T(8,128)} custom-call(s32[4]{0:T(128)} %refs_0_.19, s32[2,6]{1,0:T(2,128)} %refs_1_.15, bf16[256,2048]{1,0:T(8,128)(2,1)} %refs_2_.5, bf16[256,2048]{1,0:T(8,128)(2,1)} %refs_2_.6, bf16[256,2048]{1,0:T(8,128)(2,1)} %refs_3_.15, bf16[16,128,128]{2,1,0:T(8,128)(2,1)} %copy-done.4), custom_call_target="tpu_custom_call" | custom-call | flops 399999991808 | bytes 5242880 | tf_op jit(solution)/shard_map/inner/pallas_call | solution.py:438
  38.0 0.0 copy-done.6
  38.0 3.4 %collective-permute-start.2 = (bf16[8,128,128]{2,1,0:T(8,128)(2,1)S(1)}, bf16[8,128,128]{2,1,0:T(8,128)(2,1)S(1)}, u32[]{:S(2)}, u32[]{:S(2)}) collective-permute-start(bf16[8,128,128]{2,1,0:T(8,128)(2,1)S(1)} %copy-done.6), channel_id=1, source_target_pairs={{0,1},{2,3},{4,5},{6,7},{8,9},{10,11},{12,13},{14,15},{16,17},{18,... | collective-permute-start | bytes 786440 | tf_op jit(solution)/shard_map/ppermute | solution.py:497
  41.5 5.9 %all-to-all-done.1 = bf16[32,64,128]{2,1,0:T(8,128)(2,1)} async-done(((bf16[32,64,128]{2,1,0:T(8,128)(2,1)}), bf16[32,64,128]{2,1,0:T(8,128)(2,1)}, u32[]{:S(2)}, u32[]{:S(2)}) %all-to-all-start.1) | async-done | bytes 524320 | tf_op jit(solution)/shard_map/all_to_all | solution.py:500
  47.4 4.4 %norm.2 = (f32[128,128]{1,0:T(8,128)}, bf16[128,2048]{1,0:T(8,128)(2,1)}, bf16[128,2048]{1,0:T(8,128)(2,1)}, bf16[16,128,128]{2,1,0:T(8,128)(2,1)}) custom-call(s32[4]{0:T(128)} %refs_0_.19, s32[2,6]{1,0:T(2,128)} %refs_1_.15, f32[1,2048]{1,0:T(1,128)} %bitcast.7, bf16[256,2048]{1,0:T(8,128)(2,1)} %refs_2_.5, f32[256,2048]{1,0:T(8,128)} %inner.1.refs_4_, ...), custom_call_target="tpu_custom_call" | custom-call | flops 134217728 | bytes 6889472 | tf_op jit(solution)/shard_map/norm/pallas_call | solution.py:438
  51.8 1.3 %collective-permute-start.3 = (bf16[16,128,128]{2,1,0:T(8,128)(2,1)}, bf16[16,128,128]{2,1,0:T(8,128)(2,1)}, u32[]{:S(2)}, u32[]{:S(2)}) collective-permute-start(bf16[16,128,128]{2,1,0:T(8,128)(2,1)} %get-tuple-element.42.refs_9_), channel_id=1, source_target_pairs={{1,0},{3,2},{5,4},{7,6},{9,8},{11,10},{13,12},{15,14},{17,16},{19,... | collective-permute-start | bytes 1572872 | tf_op jit(solution)/shard_map/ppermute | solution.py:497
  53.1 0.0 collective-permute-done.1.refs_7_.refs_13_
  53.1 0.0 collective-permute-done.2.refs_8_.refs_14_
  53.1 0.0 copy-start.5
  53.1 0.7 copy-done.5
  53.8 4.8 %norm.3 = (f32[128,128]{1,0:T(8,128)}, bf16[128,2048]{1,0:T(8,128)(2,1)}, bf16[128,2048]{1,0:T(8,128)(2,1)}, bf16[16,128,128]{2,1,0:T(8,128)(2,1)}, bf16[16,128,128]{2,1,0:T(8,128)(2,1)}) custom-call(s32[4]{0:T(128)} %refs_0_.19, s32[2,6]{1,0:T(2,128)} %refs_1_.15, f32[1,2048]{1,0:T(1,128)} %bitcast.8, bf16[256,2048]{1,0:T(8,128)(2,1)} %refs_2_.5, ...), custom_call_target="tpu_custom_call" | custom-call | flops 399999991808 | bytes 7938048 | tf_op jit(solution)/shard_map/norm/pallas_call | solution.py:438
  58.7 7.2 %all-to-all-start.2 = ((bf16[32,64,128]{2,1,0:T(8,128)(2,1)}), bf16[32,64,128]{2,1,0:T(8,128)(2,1)}, u32[]{:S(2)}, u32[]{:S(2)}) async-start(bf16[32,64,128]{2,1,0:T(8,128)(2,1)} %bitcast.6), calls=%async_computation.2 | async-start | bytes 1048576 | tf_op jit(solution)/shard_map/all_to_all | solution.py:500
  65.8 1.3 %collective-permute-start.4 = (bf16[16,128,128]{2,1,0:T(8,128)(2,1)}, bf16[16,128,128]{2,1,0:T(8,128)(2,1)}, u32[]{:S(2)}, u32[]{:S(2)}) collective-permute-start(bf16[16,128,128]{2,1,0:T(8,128)(2,1)} %get-tuple-element.54), channel_id=1, source_target_pairs={{1,0},{3,2},{5,4},{7,6},{9,8},{11,10},{13,12},{15,14},{17,16},{19,... | collective-permute-start | bytes 1572872 | tf_op jit(solution)/shard_map/ppermute | solution.py:497
  67.1 0.4 collective-permute-done.3.refs_15_.refs_7_
  67.5 0.0 copy-start.1
  67.5 7.9 %query_grads.1 = (bf16[256,2048]{1,0:T(8,128)(2,1)}, bf16[256,2048]{1,0:T(8,128)(2,1)}) custom-call(s32[4]{0:T(128)} %refs_0_.19, s32[2,6]{1,0:T(2,128)} %refs_1_.15, f32[1,2048]{1,0:T(1,128)} %bitcast.9, bf16[256,2048]{1,0:T(8,128)(2,1)} %refs_2_.6, bf16[256,2048]{1,0:T(8,128)(2,1)} %refs_3_.15, bf16[16,128,128]{2,1,0:T(8,128)(2,1)} %bitcast.2.refs_6_.refs_5_, ...), custom_call_target="tpu_custom_call" | custom-call | flops 399999991808 | bytes 8003584 | tf_op jit(solution)/shard_map/query_grads/pallas_call | solution.py:438
  75.4 5.8 %all-to-all-done.2.refs_1_ = bf16[32,64,128]{2,1,0:T(8,128)(2,1)} async-done(((bf16[32,64,128]{2,1,0:T(8,128)(2,1)}), bf16[32,64,128]{2,1,0:T(8,128)(2,1)}, u32[]{:S(2)}, u32[]{:S(2)}) %all-to-all-start.2) | async-done | bytes 524320 | tf_op jit(solution)/shard_map/all_to_all | solution.py:500
  81.2 0.0 copy-done.1
  81.2 2.0 %scan.3 = bf16[32,64,128]{2,1,0:T(8,128)(2,1)} custom-call(s32[4]{0:T(128)S(1)} %copy-done.1, bf16[32,64,128]{2,1,0:T(8,128)(2,1)} %all-to-all-done.2.refs_1_), custom_call_target="tpu_custom_call" | custom-call | bytes 1048576 | tf_op jit(solution)/shard_map/scan/pallas_call | solution.py:438
  83.2 3.3 %all-to-all-start.3 = ((bf16[32,64,128]{2,1,0:T(8,128)(2,1)}), bf16[32,64,128]{2,1,0:T(8,128)(2,1)}, u32[]{:S(2)}, u32[]{:S(2)}) async-start(bf16[32,64,128]{2,1,0:T(8,128)(2,1)} %scan.3), calls=%async_computation.3 | async-start | bytes 1048576 | tf_op jit(solution)/shard_map/all_to_all | solution.py:500
  86.5 1.3 %collective-permute-done.4.refs_8_ = bf16[16,128,128]{2,1,0:T(8,128)(2,1)} collective-permute-done((bf16[16,128,128]{2,1,0:T(8,128)(2,1)}, bf16[16,128,128]{2,1,0:T(8,128)(2,1)}, u32[]{:S(2)}, u32[]{:S(2)}) %collective-permute-start.4) | collective-permute-done | bytes 524320 | tf_op jit(solution)/shard_map/ppermute | solution.py:497
  87.8 0.0 copy-start.2
  87.8 0.0 copy-start.3
  87.8 10.3 %key_grads.1 = (f32[256,2048]{1,0:T(8,128)}, f32[256,2048]{1,0:T(8,128)}) custom-call(s32[4]{0:T(128)} %refs_0_.19, s32[2,6]{1,0:T(2,128)} %refs_1_.15, bf16[256,2048]{1,0:T(8,128)(2,1)} %refs_2_.5, bf16[256,2048]{1,0:T(8,128)(2,1)} %refs_2_.6, bf16[256,2048]{1,0:T(8,128)(2,1)} %refs_3_.15, bf16[128,2048]{1,0:T(8,128)(2,1)} %get-tuple-element.39.refs_6_.refs_5_, ...), custom_call_target="tpu_custom_call" | custom-call | flops 399999991808 | bytes 9437184 | tf_op jit(solution)/shard_map/key_grads/pallas_call | solution.py:438
  98.0 3.7 %all-to-all-done.3 = bf16[32,64,128]{2,1,0:T(8,128)(2,1)} async-done(((bf16[32,64,128]{2,1,0:T(8,128)(2,1)}), bf16[32,64,128]{2,1,0:T(8,128)(2,1)}, u32[]{:S(2)}, u32[]{:S(2)}) %all-to-all-start.3) | async-done | bytes 524320 | tf_op jit(solution)/shard_map/all_to_all | solution.py:500
  101.7 0.0 copy-done.2
  101.7 0.0 copy-done.3
  101.7 5.0 %last.1 = (bf16[256,2048]{1,0:T(8,128)(2,1)}, bf16[256,2048]{1,0:T(8,128)(2,1)}) custom-call(s32[4]{0:T(128)S(1)} %copy-done.2, s32[2,6]{1,0:T(2,128)S(1)} %copy-done.3, bf16[256,2048]{1,0:T(8,128)(2,1)} %refs_2_.6, bf16[256,2048]{1,0:T(8,128)(2,1)} %refs_3_.15, f32[256,2048]{1,0:T(8,128)} %get-tuple-element.55.refs_4_, ...), custom_call_target="tpu_custom_call" | custom-call | flops 268435456 | bytes 8912896 | tf_op jit(solution)/shard_map/last/pallas_call | solution.py:438
Async XLA Ops:
  4.3 22.5 %all-to-all-start = ((bf16[32,64,128]{2,1,0:T(8,128)(2,1)}), bf16[32,64,128]{2,1,0:T(8,128)(2,1)}, u32[]{:S(2)}, u32[]{:S(2)}) async-start(bf16[32,64,128]{2,1,0:T(8,128)(2,1)} %bitcast.5), calls=%async_computation | async-start | bytes 1048576 | tf_op jit(solution)/shard_map/all_to_all | solution.py:500
  11.4 15.3 %copy-start = (s32[4]{0:T(128)S(1)}, s32[4]{0:T(128)}, u32[]{:S(2)}) copy-start(s32[4]{0:T(128)} %refs_0_.19) | copy-start | bytes 52
  15.0 17.0 %collective-permute-start = (bf16[16,128,128]{2,1,0:T(8,128)(2,1)}, bf16[16,128,128]{2,1,0:T(8,128)(2,1)S(1)}, u32[]{:S(2)}, u32[]{:S(2)}) collective-permute-start(bf16[16,128,128]{2,1,0:T(8,128)(2,1)} %get-tuple-element.37), channel_id=1, source_target_pairs={{0,1},{2,3},{4,5},{6,7},{8,9},{10,11},{12,13},{14,15},{16,17},{18,... | collective-permute-start | bytes 1572872 | tf_op jit(solution)/shard_map/ppermute | solution.py:497
  18.4 34.7 %collective-permute-start.1 = (bf16[8,128,128]{2,1,0:T(8,128)(2,1)}, bf16[8,128,128]{2,1,0:T(8,128)(2,1)}, u32[]{:S(2)}, u32[]{:S(2)}) collective-permute-start(bf16[8,128,128]{2,1,0:T(8,128)(2,1)} %get-tuple-element.40), channel_id=1, source_target_pairs={{0,1},{2,3},{4,5},{6,7},{8,9},{10,11},{12,13},{14,15},{16,17},{18,... | collective-permute-start | bytes 786440 | tf_op jit(solution)/shard_map/ppermute | solution.py:497
  28.8 18.6 %all-to-all-start.1 = ((bf16[32,64,128]{2,1,0:T(8,128)(2,1)}), bf16[32,64,128]{2,1,0:T(8,128)(2,1)}, u32[]{:S(2)}, u32[]{:S(2)}) async-start(bf16[32,64,128]{2,1,0:T(8,128)(2,1)} %scan.2), calls=%async_computation.1 | async-start | bytes 1048576 | tf_op jit(solution)/shard_map/all_to_all | solution.py:500
  32.0 0.8 copy-start.4
  32.8 5.2 %copy-start.6 = (bf16[8,128,128]{2,1,0:T(8,128)(2,1)S(1)}, bf16[8,128,128]{2,1,0:T(8,128)(2,1)}, u32[]{:S(2)}) copy-start(bf16[8,128,128]{2,1,0:T(8,128)(2,1)} %get-tuple-element.41) | copy-start | bytes 786436
  38.0 15.1 %collective-permute-start.2 = (bf16[8,128,128]{2,1,0:T(8,128)(2,1)S(1)}, bf16[8,128,128]{2,1,0:T(8,128)(2,1)S(1)}, u32[]{:S(2)}, u32[]{:S(2)}) collective-permute-start(bf16[8,128,128]{2,1,0:T(8,128)(2,1)S(1)} %copy-done.6), channel_id=1, source_target_pairs={{0,1},{2,3},{4,5},{6,7},{8,9},{10,11},{12,13},{14,15},{16,17},{18,... | collective-permute-start | bytes 786440 | tf_op jit(solution)/shard_map/ppermute | solution.py:497
  51.8 15.7 %collective-permute-start.3 = (bf16[16,128,128]{2,1,0:T(8,128)(2,1)}, bf16[16,128,128]{2,1,0:T(8,128)(2,1)}, u32[]{:S(2)}, u32[]{:S(2)}) collective-permute-start(bf16[16,128,128]{2,1,0:T(8,128)(2,1)} %get-tuple-element.42.refs_9_), channel_id=1, source_target_pairs={{1,0},{3,2},{5,4},{7,6},{9,8},{11,10},{13,12},{15,14},{17,16},{19,... | collective-permute-start | bytes 1572872 | tf_op jit(solution)/shard_map/ppermute | solution.py:497
  53.1 0.7 copy-start.5
  58.7 22.5 %all-to-all-start.2 = ((bf16[32,64,128]{2,1,0:T(8,128)(2,1)}), bf16[32,64,128]{2,1,0:T(8,128)(2,1)}, u32[]{:S(2)}, u32[]{:S(2)}) async-start(bf16[32,64,128]{2,1,0:T(8,128)(2,1)} %bitcast.6), calls=%async_computation.2 | async-start | bytes 1048576 | tf_op jit(solution)/shard_map/all_to_all | solution.py:500
  65.8 22.0 %collective-permute-start.4 = (bf16[16,128,128]{2,1,0:T(8,128)(2,1)}, bf16[16,128,128]{2,1,0:T(8,128)(2,1)}, u32[]{:S(2)}, u32[]{:S(2)}) collective-permute-start(bf16[16,128,128]{2,1,0:T(8,128)(2,1)} %get-tuple-element.54), channel_id=1, source_target_pairs={{1,0},{3,2},{5,4},{7,6},{9,8},{11,10},{13,12},{15,14},{17,16},{19,... | collective-permute-start | bytes 1572872 | tf_op jit(solution)/shard_map/ppermute | solution.py:497
  67.5 13.7 %copy-start.1 = (s32[4]{0:T(128)S(1)}, s32[4]{0:T(128)}, u32[]{:S(2)}) copy-start(s32[4]{0:T(128)} %refs_0_.19) | copy-start | bytes 52
  83.2 18.6 %all-to-all-start.3 = ((bf16[32,64,128]{2,1,0:T(8,128)(2,1)}), bf16[32,64,128]{2,1,0:T(8,128)(2,1)}, u32[]{:S(2)}, u32[]{:S(2)}) async-start(bf16[32,64,128]{2,1,0:T(8,128)(2,1)} %scan.3), calls=%async_computation.3 | async-start | bytes 1048576 | tf_op jit(solution)/shard_map/all_to_all | solution.py:500
  87.8 14.0 %copy-start.2 = (s32[4]{0:T(128)S(1)}, s32[4]{0:T(128)}, u32[]{:S(2)}) copy-start(s32[4]{0:T(128)} %refs_0_.19) | copy-start | bytes 52
  87.8 14.0 %copy-start.3 = (s32[2,6]{1,0:T(2,128)S(1)}, s32[2,6]{1,0:T(2,128)}, u32[]{:S(2)}) copy-start(s32[2,6]{1,0:T(2,128)} %refs_1_.15) | copy-start | bytes 148

commit v18 on v16

--- a/solution.py
+++ b/solution.py
@@ -575,8 +575,8 @@
                 wide(queries, b),
                 wide(raw_inner, b),
                 wide(grad_out, b),
-                states(kv_state),
-                *[p for arrays in from_peers[b * peers : (b + 1) * peers] for p in split_states(arrays, few)],
+                Part(kv_state),
+                *[Part(x) for arrays in from_peers[b * peers : (b + 1) * peers] for x in arrays],
                 *[states(w) for w in (updates if ends else [])],
             ],
             [Part(shape((BLOCK, DH), F32)), wide(block_tokens), wide(block_tokens), states(state), *ends],

time: 108 us -> 108 us (level)
  no operation moved by 1% of the time
where the time goes in v18:
time: 108 us; the launch traced here: 107 us
  Pallas kernels  48.7 us (45%)
  starting transfers between devices  32.1 us (30%)
  waiting for transfers between devices  23.5 us (22%)
  local copies, waits for them, and re-layouts  1.51 us (1%)
    pallas_call x10, Pallas kernels, call(): pl.pallas_call(kernel, name=name, in_specs=[*[pl.BlockSpec(memory_space=p...  48.7 us
    all_to_all x4, waiting for transfers between devices, exchanged(): return lax.all_to_all(slices, AXES, split_axis=0, concat_axis=0, tiled=True)  21.7 us
    all_to_all x4, starting transfers between devices, exchanged(): return lax.all_to_all(slices, AXES, split_axis=0, concat_axis=0, tiled=True)  20.8 us
    ppermute x5, starting transfers between devices, to_peers(): return lax.ppermute(array, 'head', pairs)  11.3 us
  transfers between devices with their start and end apart: 9, of which 6 were waited for; matrix products, arithmetic and copies ran while one was open for 0% of the time, Pallas kernels for 38%

profile of v18, /device:TPU:1, one launch (start us, length us, event | category | flops | bytes accessed | tf_op | source)
XLA Modules:
  0.0 106.8 jit_solution(7557693090849996792)
XLA Ops:
  0.6 3.4 %total.1 = bf16[16,128,128]{2,1,0:T(8,128)(2,1)} custom-call(s32[4]{0:T(128)} %refs_0_.19, s32[2,6]{1,0:T(2,128)} %refs_1_.15, bf16[256,2048]{1,0:T(8,128)(2,1)} %refs_2_.6, bf16[256,2048]{1,0:T(8,128)(2,1)} %refs_3_.15), custom_call_target="tpu_custom_call" | custom-call | flops 134217728 | bytes 2621440 | tf_op jit(solution)/shard_map/total/pallas_call | solution.py:438
  4.1 7.2 %all-to-all-start = ((bf16[32,64,128]{2,1,0:T(8,128)(2,1)}), bf16[32,64,128]{2,1,0:T(8,128)(2,1)}, u32[]{:S(2)}, u32[]{:S(2)}) async-start(bf16[32,64,128]{2,1,0:T(8,128)(2,1)} %bitcast.5), calls=%async_computation | async-start | bytes 1048576 | tf_op jit(solution)/shard_map/all_to_all | solution.py:500
  11.2 0.0 copy-start
  11.2 3.6 %states.1 = (bf16[16,128,128]{2,1,0:T(8,128)(2,1)}, bf16[8,128,128]{2,1,0:T(8,128)(2,1)}, bf16[8,128,128]{2,1,0:T(8,128)(2,1)}) custom-call(s32[4]{0:T(128)} %refs_0_.19, s32[2,6]{1,0:T(2,128)} %refs_1_.15, bf16[256,2048]{1,0:T(8,128)(2,1)} %refs_2_.6, bf16[256,2048]{1,0:T(8,128)(2,1)} %refs_3_.15), custom_call_target="tpu_custom_call" | custom-call | flops 399999991808 | bytes 3145728 | tf_op jit(solution)/shard_map/states/pallas_call | solution.py:438
  14.9 3.3 %collective-permute-start = (bf16[16,128,128]{2,1,0:T(8,128)(2,1)}, bf16[16,128,128]{2,1,0:T(8,128)(2,1)S(1)}, u32[]{:S(2)}, u32[]{:S(2)}) collective-permute-start(bf16[16,128,128]{2,1,0:T(8,128)(2,1)} %get-tuple-element.37), channel_id=1, source_target_pairs={{0,1},{2,3},{4,5},{6,7},{8,9},{10,11},{12,13},{14,15},{16,17},{18,... | collective-permute-start | bytes 1572872 | tf_op jit(solution)/shard_map/ppermute | solution.py:497
  18.2 2.0 %collective-permute-start.1 = (bf16[8,128,128]{2,1,0:T(8,128)(2,1)}, bf16[8,128,128]{2,1,0:T(8,128)(2,1)}, u32[]{:S(2)}, u32[]{:S(2)}) collective-permute-start(bf16[8,128,128]{2,1,0:T(8,128)(2,1)} %get-tuple-element.40), channel_id=1, source_target_pairs={{0,1},{2,3},{4,5},{6,7},{8,9},{10,11},{12,13},{14,15},{16,17},{18,... | collective-permute-start | bytes 786440 | tf_op jit(solution)/shard_map/ppermute | solution.py:497
  20.2 6.4 %all-to-all-done.refs_1_ = bf16[32,64,128]{2,1,0:T(8,128)(2,1)} async-done(((bf16[32,64,128]{2,1,0:T(8,128)(2,1)}), bf16[32,64,128]{2,1,0:T(8,128)(2,1)}, u32[]{:S(2)}, u32[]{:S(2)}) %all-to-all-start) | async-done | bytes 524320 | tf_op jit(solution)/shard_map/all_to_all | solution.py:500
  26.6 0.0 copy-done
  26.6 2.0 %scan.2 = bf16[32,64,128]{2,1,0:T(8,128)(2,1)} custom-call(s32[4]{0:T(128)S(1)} %copy-done, bf16[32,64,128]{2,1,0:T(8,128)(2,1)} %all-to-all-done.refs_1_), custom_call_target="tpu_custom_call" | custom-call | bytes 1048576 | tf_op jit(solution)/shard_map/scan/pallas_call | solution.py:438
  28.6 3.2 %all-to-all-start.1 = ((bf16[32,64,128]{2,1,0:T(8,128)(2,1)}), bf16[32,64,128]{2,1,0:T(8,128)(2,1)}, u32[]{:S(2)}, u32[]{:S(2)}) async-start(bf16[32,64,128]{2,1,0:T(8,128)(2,1)} %scan.2), calls=%async_computation.1 | async-start | bytes 1048576 | tf_op jit(solution)/shard_map/all_to_all | solution.py:500
  31.8 0.0 collective-permute-done.refs_5_.refs_7_.refs_12_
  31.8 0.0 copy-start.4
  31.9 0.8 copy-done.4
  32.6 0.0 copy-start.6
  32.6 5.2 %inner.1.refs_4_ = f32[256,2048]{1,0:T(8,128)} custom-call(s32[4]{0:T(128)} %refs_0_.19, s32[2,6]{1,0:T(2,128)} %refs_1_.15, bf16[256,2048]{1,0:T(8,128)(2,1)} %refs_2_.5, bf16[256,2048]{1,0:T(8,128)(2,1)} %refs_2_.6, bf16[256,2048]{1,0:T(8,128)(2,1)} %refs_3_.15, bf16[16,128,128]{2,1,0:T(8,128)(2,1)} %copy-done.4), custom_call_target="tpu_custom_call" | custom-call | flops 399999991808 | bytes 5242880 | tf_op jit(solution)/shard_map/inner/pallas_call | solution.py:438
  37.9 0.0 copy-done.6
  37.9 3.4 %collective-permute-start.2 = (bf16[8,128,128]{2,1,0:T(8,128)(2,1)S(1)}, bf16[8,128,128]{2,1,0:T(8,128)(2,1)S(1)}, u32[]{:S(2)}, u32[]{:S(2)}) collective-permute-start(bf16[8,128,128]{2,1,0:T(8,128)(2,1)S(1)} %copy-done.6), channel_id=1, source_target_pairs={{0,1},{2,3},{4,5},{6,7},{8,9},{10,11},{12,13},{14,15},{16,17},{18,... | collective-permute-start | bytes 786440 | tf_op jit(solution)/shard_map/ppermute | solution.py:497
  41.3 5.9 %all-to-all-done.1 = bf16[32,64,128]{2,1,0:T(8,128)(2,1)} async-done(((bf16[32,64,128]{2,1,0:T(8,128)(2,1)}), bf16[32,64,128]{2,1,0:T(8,128)(2,1)}, u32[]{:S(2)}, u32[]{:S(2)}) %all-to-all-start.1) | async-done | bytes 524320 | tf_op jit(solution)/shard_map/all_to_all | solution.py:500
  47.2 4.4 %norm.2 = (f32[128,128]{1,0:T(8,128)}, bf16[128,2048]{1,0:T(8,128)(2,1)}, bf16[128,2048]{1,0:T(8,128)(2,1)}, bf16[16,128,128]{2,1,0:T(8,128)(2,1)}) custom-call(s32[4]{0:T(128)} %refs_0_.19, s32[2,6]{1,0:T(2,128)} %refs_1_.15, f32[1,2048]{1,0:T(1,128)} %bitcast.7, bf16[256,2048]{1,0:T(8,128)(2,1)} %refs_2_.5, f32[256,2048]{1,0:T(8,128)} %inner.1.refs_4_, ...), custom_call_target="tpu_custom_call" | custom-call | flops 134217728 | bytes 6889472 | tf_op jit(solution)/shard_map/norm/pallas_call | solution.py:438
  51.6 1.3 %collective-permute-start.3 = (bf16[16,128,128]{2,1,0:T(8,128)(2,1)}, bf16[16,128,128]{2,1,0:T(8,128)(2,1)}, u32[]{:S(2)}, u32[]{:S(2)}) collective-permute-start(bf16[16,128,128]{2,1,0:T(8,128)(2,1)} %get-tuple-element.42.refs_9_), channel_id=1, source_target_pairs={{1,0},{3,2},{5,4},{7,6},{9,8},{11,10},{13,12},{15,14},{17,16},{19,... | collective-permute-start | bytes 1572872 | tf_op jit(solution)/shard_map/ppermute | solution.py:497
  52.9 0.0 collective-permute-done.1.refs_7_.refs_13_
  52.9 0.0 collective-permute-done.2.refs_8_.refs_14_
  53.0 0.0 copy-start.5
  53.0 0.7 copy-done.5
  53.7 4.8 %norm.3 = (f32[128,128]{1,0:T(8,128)}, bf16[128,2048]{1,0:T(8,128)(2,1)}, bf16[128,2048]{1,0:T(8,128)(2,1)}, bf16[16,128,128]{2,1,0:T(8,128)(2,1)}, bf16[16,128,128]{2,1,0:T(8,128)(2,1)}) custom-call(s32[4]{0:T(128)} %refs_0_.19, s32[2,6]{1,0:T(2,128)} %refs_1_.15, f32[1,2048]{1,0:T(1,128)} %bitcast.8, bf16[256,2048]{1,0:T(8,128)(2,1)} %refs_2_.5, ...), custom_call_target="tpu_custom_call" | custom-call | flops 399999991808 | bytes 7938048 | tf_op jit(solution)/shard_map/norm/pallas_call | solution.py:438
  58.5 7.1 %all-to-all-start.2 = ((bf16[32,64,128]{2,1,0:T(8,128)(2,1)}), bf16[32,64,128]{2,1,0:T(8,128)(2,1)}, u32[]{:S(2)}, u32[]{:S(2)}) async-start(bf16[32,64,128]{2,1,0:T(8,128)(2,1)} %bitcast.6), calls=%async_computation.2 | async-start | bytes 1048576 | tf_op jit(solution)/shard_map/all_to_all | solution.py:500
  65.7 1.3 %collective-permute-start.4 = (bf16[16,128,128]{2,1,0:T(8,128)(2,1)}, bf16[16,128,128]{2,1,0:T(8,128)(2,1)}, u32[]{:S(2)}, u32[]{:S(2)}) collective-permute-start(bf16[16,128,128]{2,1,0:T(8,128)(2,1)} %get-tuple-element.54), channel_id=1, source_target_pairs={{1,0},{3,2},{5,4},{7,6},{9,8},{11,10},{13,12},{15,14},{17,16},{19,... | collective-permute-start | bytes 1572872 | tf_op jit(solution)/shard_map/ppermute | solution.py:497
  67.0 0.4 collective-permute-done.3.refs_15_.refs_7_
  67.4 0.0 copy-start.1
  67.4 7.9 %query_grads.1 = (bf16[256,2048]{1,0:T(8,128)(2,1)}, bf16[256,2048]{1,0:T(8,128)(2,1)}) custom-call(s32[4]{0:T(128)} %refs_0_.19, s32[2,6]{1,0:T(2,128)} %refs_1_.15, f32[1,2048]{1,0:T(1,128)} %bitcast.9, bf16[256,2048]{1,0:T(8,128)(2,1)} %refs_2_.6, bf16[256,2048]{1,0:T(8,128)(2,1)} %refs_3_.15, bf16[16,128,128]{2,1,0:T(8,128)(2,1)} %bitcast.2.refs_6_.refs_5_, ...), custom_call_target="tpu_custom_call" | custom-call | flops 399999991808 | bytes 8003584 | tf_op jit(solution)/shard_map/query_grads/pallas_call | solution.py:438
  75.3 5.8 %all-to-all-done.2.refs_1_ = bf16[32,64,128]{2,1,0:T(8,128)(2,1)} async-done(((bf16[32,64,128]{2,1,0:T(8,128)(2,1)}), bf16[32,64,128]{2,1,0:T(8,128)(2,1)}, u32[]{:S(2)}, u32[]{:S(2)}) %all-to-all-start.2) | async-done | bytes 524320 | tf_op jit(solution)/shard_map/all_to_all | solution.py:500
  81.0 0.0 copy-done.1
  81.0 2.0 %scan.3 = bf16[32,64,128]{2,1,0:T(8,128)(2,1)} custom-call(s32[4]{0:T(128)S(1)} %copy-done.1, bf16[32,64,128]{2,1,0:T(8,128)(2,1)} %all-to-all-done.2.refs_1_), custom_call_target="tpu_custom_call" | custom-call | bytes 1048576 | tf_op jit(solution)/shard_map/scan/pallas_call | solution.py:438
  83.0 3.3 %all-to-all-start.3 = ((bf16[32,64,128]{2,1,0:T(8,128)(2,1)}), bf16[32,64,128]{2,1,0:T(8,128)(2,1)}, u32[]{:S(2)}, u32[]{:S(2)}) async-start(bf16[32,64,128]{2,1,0:T(8,128)(2,1)} %scan.3), calls=%async_computation.3 | async-start | bytes 1048576 | tf_op jit(solution)/shard_map/all_to_all | solution.py:500
  86.3 1.3 %collective-permute-done.4.refs_8_ = bf16[16,128,128]{2,1,0:T(8,128)(2,1)} collective-permute-done((bf16[16,128,128]{2,1,0:T(8,128)(2,1)}, bf16[16,128,128]{2,1,0:T(8,128)(2,1)}, u32[]{:S(2)}, u32[]{:S(2)}) %collective-permute-start.4) | collective-permute-done | bytes 524320 | tf_op jit(solution)/shard_map/ppermute | solution.py:497
  87.6 0.0 copy-start.2
  87.6 0.0 copy-start.3
  87.6 10.3 %key_grads.1 = (f32[256,2048]{1,0:T(8,128)}, f32[256,2048]{1,0:T(8,128)}) custom-call(s32[4]{0:T(128)} %refs_0_.19, s32[2,6]{1,0:T(2,128)} %refs_1_.15, bf16[256,2048]{1,0:T(8,128)(2,1)} %refs_2_.5, bf16[256,2048]{1,0:T(8,128)(2,1)} %refs_2_.6, bf16[256,2048]{1,0:T(8,128)(2,1)} %refs_3_.15, bf16[128,2048]{1,0:T(8,128)(2,1)} %get-tuple-element.39.refs_6_.refs_5_, ...), custom_call_target="tpu_custom_call" | custom-call | flops 399999991808 | bytes 9437184 | tf_op jit(solution)/shard_map/key_grads/pallas_call | solution.py:438
  97.9 3.7 %all-to-all-done.3 = bf16[32,64,128]{2,1,0:T(8,128)(2,1)} async-done(((bf16[32,64,128]{2,1,0:T(8,128)(2,1)}), bf16[32,64,128]{2,1,0:T(8,128)(2,1)}, u32[]{:S(2)}, u32[]{:S(2)}) %all-to-all-start.3) | async-done | bytes 524320 | tf_op jit(solution)/shard_map/all_to_all | solution.py:500
  101.6 0.0 copy-done.2
  101.6 0.0 copy-done.3
  101.6 5.0 %last.1 = (bf16[256,2048]{1,0:T(8,128)(2,1)}, bf16[256,2048]{1,0:T(8,128)(2,1)}) custom-call(s32[4]{0:T(128)S(1)} %copy-done.2, s32[2,6]{1,0:T(2,128)S(1)} %copy-done.3, bf16[256,2048]{1,0:T(8,128)(2,1)} %refs_2_.6, bf16[256,2048]{1,0:T(8,128)(2,1)} %refs_3_.15, f32[256,2048]{1,0:T(8,128)} %get-tuple-element.55.refs_4_, ...), custom_call_target="tpu_custom_call" | custom-call | flops 268435456 | bytes 8912896 | tf_op jit(solution)/shard_map/last/pallas_call | solution.py:438
Async XLA Ops:
  4.1 22.5 %all-to-all-start = ((bf16[32,64,128]{2,1,0:T(8,128)(2,1)}), bf16[32,64,128]{2,1,0:T(8,128)(2,1)}, u32[]{:S(2)}, u32[]{:S(2)}) async-start(bf16[32,64,128]{2,1,0:T(8,128)(2,1)} %bitcast.5), calls=%async_computation | async-start | bytes 1048576 | tf_op jit(solution)/shard_map/all_to_all | solution.py:500
  11.2 15.3 %copy-start = (s32[4]{0:T(128)S(1)}, s32[4]{0:T(128)}, u32[]{:S(2)}) copy-start(s32[4]{0:T(128)} %refs_0_.19) | copy-start | bytes 52
  14.9 17.0 %collective-permute-start = (bf16[16,128,128]{2,1,0:T(8,128)(2,1)}, bf16[16,128,128]{2,1,0:T(8,128)(2,1)S(1)}, u32[]{:S(2)}, u32[]{:S(2)}) collective-permute-start(bf16[16,128,128]{2,1,0:T(8,128)(2,1)} %get-tuple-element.37), channel_id=1, source_target_pairs={{0,1},{2,3},{4,5},{6,7},{8,9},{10,11},{12,13},{14,15},{16,17},{18,... | collective-permute-start | bytes 1572872 | tf_op jit(solution)/shard_map/ppermute | solution.py:497
  18.2 34.7 %collective-permute-start.1 = (bf16[8,128,128]{2,1,0:T(8,128)(2,1)}, bf16[8,128,128]{2,1,0:T(8,128)(2,1)}, u32[]{:S(2)}, u32[]{:S(2)}) collective-permute-start(bf16[8,128,128]{2,1,0:T(8,128)(2,1)} %get-tuple-element.40), channel_id=1, source_target_pairs={{0,1},{2,3},{4,5},{6,7},{8,9},{10,11},{12,13},{14,15},{16,17},{18,... | collective-permute-start | bytes 786440 | tf_op jit(solution)/shard_map/ppermute | solution.py:497
  28.6 18.6 %all-to-all-start.1 = ((bf16[32,64,128]{2,1,0:T(8,128)(2,1)}), bf16[32,64,128]{2,1,0:T(8,128)(2,1)}, u32[]{:S(2)}, u32[]{:S(2)}) async-start(bf16[32,64,128]{2,1,0:T(8,128)(2,1)} %scan.2), calls=%async_computation.1 | async-start | bytes 1048576 | tf_op jit(solution)/shard_map/all_to_all | solution.py:500
  31.8 0.8 copy-start.4
  32.6 5.2 %copy-start.6 = (bf16[8,128,128]{2,1,0:T(8,128)(2,1)S(1)}, bf16[8,128,128]{2,1,0:T(8,128)(2,1)}, u32[]{:S(2)}) copy-start(bf16[8,128,128]{2,1,0:T(8,128)(2,1)} %get-tuple-element.41) | copy-start | bytes 786436
  37.9 15.1 %collective-permute-start.2 = (bf16[8,128,128]{2,1,0:T(8,128)(2,1)S(1)}, bf16[8,128,128]{2,1,0:T(8,128)(2,1)S(1)}, u32[]{:S(2)}, u32[]{:S(2)}) collective-permute-start(bf16[8,128,128]{2,1,0:T(8,128)(2,1)S(1)} %copy-done.6), channel_id=1, source_target_pairs={{0,1},{2,3},{4,5},{6,7},{8,9},{10,11},{12,13},{14,15},{16,17},{18,... | collective-permute-start | bytes 786440 | tf_op jit(solution)/shard_map/ppermute | solution.py:497
  51.6 15.7 %collective-permute-start.3 = (bf16[16,128,128]{2,1,0:T(8,128)(2,1)}, bf16[16,128,128]{2,1,0:T(8,128)(2,1)}, u32[]{:S(2)}, u32[]{:S(2)}) collective-permute-start(bf16[16,128,128]{2,1,0:T(8,128)(2,1)} %get-tuple-element.42.refs_9_), channel_id=1, source_target_pairs={{1,0},{3,2},{5,4},{7,6},{9,8},{11,10},{13,12},{15,14},{17,16},{19,... | collective-permute-start | bytes 1572872 | tf_op jit(solution)/shard_map/ppermute | solution.py:497
  53.0 0.7 copy-start.5
  58.5 22.5 %all-to-all-start.2 = ((bf16[32,64,128]{2,1,0:T(8,128)(2,1)}), bf16[32,64,128]{2,1,0:T(8,128)(2,1)}, u32[]{:S(2)}, u32[]{:S(2)}) async-start(bf16[32,64,128]{2,1,0:T(8,128)(2,1)} %bitcast.6), calls=%async_computation.2 | async-start | bytes 1048576 | tf_op jit(solution)/shard_map/all_to_all | solution.py:500
  65.7 22.0 %collective-permute-start.4 = (bf16[16,128,128]{2,1,0:T(8,128)(2,1)}, bf16[16,128,128]{2,1,0:T(8,128)(2,1)}, u32[]{:S(2)}, u32[]{:S(2)}) collective-permute-start(bf16[16,128,128]{2,1,0:T(8,128)(2,1)} %get-tuple-element.54), channel_id=1, source_target_pairs={{1,0},{3,2},{5,4},{7,6},{9,8},{11,10},{13,12},{15,14},{17,16},{19,... | collective-permute-start | bytes 1572872 | tf_op jit(solution)/shard_map/ppermute | solution.py:497
  67.4 13.6 %copy-start.1 = (s32[4]{0:T(128)S(1)}, s32[4]{0:T(128)}, u32[]{:S(2)}) copy-start(s32[4]{0:T(128)} %refs_0_.19) | copy-start | bytes 52
  83.0 18.6 %all-to-all-start.3 = ((bf16[32,64,128]{2,1,0:T(8,128)(2,1)}), bf16[32,64,128]{2,1,0:T(8,128)(2,1)}, u32[]{:S(2)}, u32[]{:S(2)}) async-start(bf16[32,64,128]{2,1,0:T(8,128)(2,1)} %scan.3), calls=%async_computation.3 | async-start | bytes 1048576 | tf_op jit(solution)/shard_map/all_to_all | solution.py:500
  87.6 14.0 %copy-start.2 = (s32[4]{0:T(128)S(1)}, s32[4]{0:T(128)}, u32[]{:S(2)}) copy-start(s32[4]{0:T(128)} %refs_0_.19) | copy-start | bytes 52
  87.6 14.0 %copy-start.3 = (s32[2,6]{1,0:T(2,128)S(1)}, s32[2,6]{1,0:T(2,128)}, u32[]{:S(2)}) copy-start(s32[2,6]{1,0:T(2,128)} %refs_1_.15) | copy-start | bytes 148
